TPU v7x, 32 devices: a whole 2x2x4 slice. The times are simulated.
32 devices in a mesh: groups: 2 (over y), seq: 4 (over z), head: 2 (over x), sub: 2 (over core).
Axes of the slice: x: 2, y: 2, z: 4, core: 2. Of those that a mesh axis runs over, the one named last changes fastest.
Arguments:
- queries: bfloat16 [4096, 4096], P(('groups', 'seq'), ('head', 'sub')), parts along dimension 0, may hold values from -33 to 33
- keys: bfloat16 [4096, 4096], P(('groups', 'seq'), ('head', 'sub')), parts along dimension 0, may hold values from -6 to 6
- values: bfloat16 [4096, 4096], P(('groups', 'seq'), ('head', 'sub')), parts along dimension 0, may hold values from -6 to 6
- latent_keys: bfloat16 [1024, 4096], P('groups', ('head', 'sub')), parts along dimension 0, may hold values from -6 to 6
- latent_values: bfloat16 [1024, 4096], P('groups', ('head', 'sub')), parts along dimension 0, may hold values from -6 to 6
- pattern: int32 [16, 8], P(('groups', 'seq')), parts along dimension 0, may hold values 0 or 1
- doc_starts: int32 [64], P('groups'), parts along dimension 0, may hold values from 0 to 2047, as said below
- doc_owner: int32 [64], P('groups'), parts along dimension 0, may hold values from 0 to 3, as said below
Outputs:
- context: bfloat16 [4096, 4096], P(('groups', 'seq'), ('head', 'sub')), parts along dimension 0
- pooled: bfloat16 [8, 4, 2, 4096], P(('groups', 'seq'), None, None, ('head', 'sub')), parts along dimension 0
There are 2 independent parts, one for each index of `groups`. A program takes and returns all parts, laid end to end along the dimension named above; each array names one. Nothing has to cross between parts.
Inputs may be any that keep to these rules, and one draw needn't show every extreme that they name: `doc_starts`: document 2i starts at i * 128, the start of the i-th piece of 128 tokens, and document 2i + 1 starts 1 to 127 tokens later. `doc_owner`: documents 2i and 2i + 1 have one owner; the 4 pieces of one shard of 512 tokens have different owners; in every draw some owner owns a piece of every shard.
All inputs are finite; a program needn't handle non-finite values. No bound on the sum of `pattern` on one device may be relied on, other than what follows from the above.
Results may differ from a plain program's by a relative error of at most 0.0085.
Values may be sent and summed in bfloat16 or wider, within the bound.
No kernel may reach another device: no remote copies, remote signals or barrier semaphores. Data moves between devices by JAX's collectives and lax.ppermute only.
A program may use at most 128 MiB of HBM per device.

v0:
```python
import math

import jax
import jax.numpy as jnp
from jax import lax
from jax.sharding import PartitionSpec as P

HD = 128
LEVELS = 4
BLK = 256
PIECES = 4


def from_behind(value, axis, steps):
    count = lax.axis_size(axis)
    first, last = (max(0, -steps), min(count, count - steps))
    return lax.ppermute(value, axis, [(source, source + steps) for source in range(first, last)])


def heads_first(matrix, head_size):
    row_count, column_count = matrix.shape
    return jnp.transpose(matrix.reshape(row_count, column_count // head_size, head_size), (1, 0, 2))


def latent_mix(query_heads, latent_heads, latent_vals, score_scale):
    scores = (
        jnp.einsum("hqd,hld->hql", query_heads, latent_heads, preferred_element_type=jnp.float32)
        * score_scale
    )
    row_peak = jnp.max(scores, axis=2)
    exp_terms = jnp.exp(scores - row_peak[:, :, None])
    totals = jnp.sum(exp_terms, axis=2)
    blended = jnp.einsum(
        "hql,hld->hqd",
        exp_terms.astype(jnp.bfloat16),
        latent_vals,
        preferred_element_type=jnp.float32,
    )
    return blended / totals[:, :, None]


def body(queries, keys, values, latent_keys, latent_values, pattern, doc_starts, doc_owner):
    tok_rows, columns = queries.shape
    heads_here = columns // HD
    score_scale = 1.0 / math.sqrt(HD)
    blocks_here = tok_rows // BLK
    seq_index = lax.axis_index("seq")
    seq_count = lax.axis_size("seq")
    query_heads = heads_first(queries, HD)
    key_heads = heads_first(keys, HD)
    value_heads = heads_first(values, HD)
    rows_step = 512
    block_count = tok_rows // rows_step

    def own_block(block_index):
        scores = (
            jnp.einsum("hqd,hkd->hqk", query_heads, key_heads, preferred_element_type=jnp.float32)
            * score_scale
        )
        row_peak = jnp.max(scores, axis=2)
        exp_terms = jnp.exp(scores - row_peak[:, :, None])
        totals = jnp.sum(exp_terms, axis=2)
        gathered = jnp.einsum(
            "hqk,hkd->hqd",
            exp_terms.astype(jnp.bfloat16),
            value_heads,
            preferred_element_type=jnp.float32,
        )
        return (row_peak, totals, gathered)

    block_peaks, block_totals, accums = lax.map(own_block, jnp.arange(block_count, dtype=jnp.int32))
    running = (
        jnp.moveaxis(block_peaks, 0, 1).reshape(heads_here, tok_rows),
        jnp.moveaxis(block_totals, 0, 1).reshape(heads_here, tok_rows),
        jnp.moveaxis(accums, 0, 1).reshape(heads_here, tok_rows, HD),
    )
    query_blocks = query_heads.reshape(heads_here, blocks_here, BLK, HD)
    stacked = jnp.stack((key_heads, value_heads))
    for level_index in range(LEVELS):
        distance = 2**level_index
        if distance < seq_count:
            for side_index in range(2):
                toward = distance if side_index == 0 else -distance
                panel_data = from_behind(stacked, "seq", toward)
                partner = seq_index - toward
                inside = (partner >= 0) & (partner < seq_count)
                slot_live = (pattern[:, 2 * level_index + side_index] == 1) & inside
                peak_old, total_old, accum_old = running
                panel_keys = panel_data[0].reshape(heads_here, blocks_here, BLK, HD)
                panel_vals = panel_data[1].reshape(heads_here, blocks_here, BLK, HD)
                add_scores = (
                    jnp.einsum(
                        "hbqd,hbkd->hbqk",
                        query_blocks,
                        panel_keys,
                        preferred_element_type=jnp.float32,
                    )
                    * score_scale
                )
                add_scores = jnp.where(slot_live[None, :, None, None], add_scores, -jnp.inf)
                add_scores = add_scores.reshape(heads_here, tok_rows, BLK)
                peak_new = jnp.maximum(peak_old, jnp.max(add_scores, axis=2))
                add_exp_terms = jnp.exp(add_scores - peak_new[:, :, None])
                shrink = jnp.exp(peak_old - peak_new)
                total_new = total_old * shrink + jnp.sum(add_exp_terms, axis=2)
                weights = add_exp_terms.astype(jnp.bfloat16).reshape(
                    heads_here, blocks_here, BLK, BLK
                )
                fresh_terms = jnp.einsum(
                    "hbqk,hbkd->hbqd", weights, panel_vals, preferred_element_type=jnp.float32
                )
                accum_new = accum_old * shrink[:, :, None] + fresh_terms.reshape(
                    heads_here, tok_rows, HD
                )
                running = (peak_new, total_new, accum_new)
    peak_now, total_now, accum_now = running
    context_heads = (accum_now / total_now[:, :, None]).astype(jnp.bfloat16)
    context = jnp.transpose(context_heads, (1, 0, 2)).reshape(tok_rows, columns)
    latent_heads = heads_first(latent_keys, HD)
    latent_vals = heads_first(latent_values, HD)
    piece_rows = tok_rows // PIECES
    owner_pairs = doc_owner.reshape(-1, 2)
    owners = owner_pairs[:, 0].reshape(seq_count, PIECES)
    bounds = doc_starts.reshape(-1, 2)
    splits = (bounds[:, 1] - bounds[:, 0]).reshape(seq_count, PIECES)
    targets = jnp.arange(seq_count, dtype=jnp.int32)
    positions = jnp.arange(piece_rows, dtype=jnp.int32)
    matched = owners == seq_index
    present = jnp.any(matched, axis=1).astype(jnp.float32)
    split_got = jnp.sum(jnp.where(matched, splits, 0), axis=1)
    counts = jnp.stack(
        (
            split_got.astype(jnp.float32) * present,
            (piece_rows - split_got).astype(jnp.float32) * present,
        ),
        axis=1,
    )
    my_owners = lax.dynamic_index_in_dim(owners, seq_index, 0, keepdims=False)
    route_hits = my_owners[None, :] == targets[:, None]

    def local_block(block_index):
        return latent_mix(
            query_heads, latent_heads, latent_vals, score_scale
        ) + context_heads.astype(jnp.float32)

    mixed_local = lax.map(local_block, jnp.arange(block_count, dtype=jnp.int32))
    mixed_local = jnp.moveaxis(mixed_local, 0, 1).reshape(heads_here, PIECES, piece_rows, HD)
    my_splits = lax.dynamic_index_in_dim(splits, seq_index, 0, keepdims=False)
    local_first = (positions[None, :] < my_splits[:, None]).astype(jnp.float32)
    local_masks = jnp.stack((local_first, 1.0 - local_first), axis=1)
    local_sums = jnp.einsum(
        "pjn,hpnd->pjhd", local_masks, mixed_local, precision=lax.Precision.HIGHEST
    ).reshape(PIECES, 2, columns)
    outgoing = jnp.einsum(
        "rp,pjc->rjc", route_hits.astype(jnp.float32), local_sums, precision=lax.Precision.HIGHEST
    )
    doc_sums = lax.all_to_all(
        outgoing.astype(jnp.bfloat16), "seq", split_axis=0, concat_axis=0, tiled=True
    ).astype(outgoing.dtype)
    pooled = (doc_sums / jnp.maximum(counts, 1.0)[:, :, None]).astype(jnp.bfloat16)[None]
    return (context, pooled)


def solution(mesh):
    in_specs = (
        P(("groups", "seq"), ("head", "sub")),
        P(("groups", "seq"), ("head", "sub")),
        P(("groups", "seq"), ("head", "sub")),
        P("groups", ("head", "sub")),
        P("groups", ("head", "sub")),
        P(("groups", "seq"), None),
        P("groups"),
        P("groups"),
    )
    out_specs = (
        P(("groups", "seq"), ("head", "sub")),
        P(("groups", "seq"), None, None, ("head", "sub")),
    )
    return jax.shard_map(body, mesh=mesh, in_specs=in_specs, out_specs=out_specs, check_vma=False)
```

profile of v0, /device:TPU:0, one launch (start us, length us, event | category | flops | bytes accessed | tf_op | source)
XLA Modules:
  0.0 183.0 jit_solution(6355597071163609764)
XLA Ops:
  0.7 2.2 %bitcast_bitcast_fusion.4 = (bf16[1,8,512,128]{3,2,1,0:T(8,128)(2,1)S(1)}, bf16[1,8,512,128]{3,2,1,0:T(8,128)(2,1)S(1)}) fusion(bf16[512,1024]{1,0:T(8,128)(2,1)} %param.9, bf16[512,1024]{1,0:T(8,128)(2,1)} %param.10), kind=kLoop, calls=%fused_computation.78 | loop fusion | bytes 4194304 | tf_op jit(solution)/shard_map/stack | solution.py:78
  2.9 1.5 pad_maximum_fusion
  4.4 7.3 %collective-permute-start.2 = (bf16[2,8,512,128]{3,2,1,0:T(8,128)(2,1)}, bf16[2,8,512,128]{3,2,1,0:T(8,128)(2,1)}, u32[]{:S(2)}, u32[]{:S(2)}) collective-permute-start(bf16[2,8,512,128]{3,2,1,0:T(8,128)(2,1)} %pad_maximum_fusion), channel_id=1, source_target_pairs={{0,8},{4,12},{1,9},{5,13},{2,10},{6,14},{3,11},{7,15},{16,24},{20,... | collective-permute-start | bytes 6291464 | tf_op jit(solution)/shard_map/ppermute | solution.py:17
  11.7 1.3 collective-permute-start.1
  12.9 5.9 %collective-permute-start = (bf16[2,8,512,128]{3,2,1,0:T(8,128)(2,1)}, bf16[2,8,512,128]{3,2,1,0:T(8,128)(2,1)}, u32[]{:S(2)}, u32[]{:S(2)}) collective-permute-start(bf16[2,8,512,128]{3,2,1,0:T(8,128)(2,1)} %pad_maximum_fusion), channel_id=1, source_target_pairs={{0,4},{4,8},{8,12},{1,5},{5,9},{9,13},{2,6},{6,10},{10,14},{3,7},{... | collective-permute-start | bytes 6291464 | tf_op jit(solution)/shard_map/ppermute | solution.py:17
  18.9 1.3 collective-permute-start.3
  20.2 4.5 %multiply_reduce_fusion.1 = (f32[8,512]{1,0:T(8,128)S(1)}, f32[8,512,512]{1,2,0:T(8,128)}) fusion(bf16[512,1024]{1,0:T(8,128)(2,1)S(1)} %copy-done.3, bf16[512,1024]{1,0:T(8,128)(2,1)S(1)} %copy-done), kind=kOutput, calls=%fused_computation.3 | convolution fusion | flops 541061120 | bytes 10502144 | tf_op jit(solution)/shard_map/while/body/eval_jaxpr/hqd,hkd->hqk/dot_general | solution.py:57
  24.7 4.5 %multiply_reduce_fusion = (f32[8,512]{1,0:T(8,128)S(1)}, f32[8,512,512]{1,2,0:T(8,128)}) fusion(bf16[512,1024]{1,0:T(8,128)(2,1)S(1)} %copy-done.4, bf16[512,1024]{1,0:T(8,128)(2,1)S(1)} %copy-done), kind=kOutput, calls=%fused_computation.2 | convolution fusion | flops 541061120 | bytes 10502144 | tf_op jit(solution)/shard_map/while/body/eval_jaxpr/hqd,hld->hql/dot_general | solution.py:27
  30.5 4.9 %fusion = f32[8,512]{1,0:T(8,128)S(1)} fusion(f32[8,512,512]{1,2,0:T(8,128)} %get-tuple-element.81, f32[8,512]{1,0:T(8,128)S(1)} %get-tuple-element.80), kind=kLoop, calls=%fused_computation.4 | loop fusion | flops 6287360 | bytes 8421376 | tf_op jit(solution)/shard_map/while/body/eval_jaxpr/reduce_sum | solution.py:62
  36.2 1.4 fusion.2
  37.8 18.9 %collective-permute-done.2 = bf16[2,8,512,128]{3,2,1,0:T(8,128)(2,1)} collective-permute-done((bf16[2,8,512,128]{3,2,1,0:T(8,128)(2,1)}, bf16[2,8,512,128]{3,2,1,0:T(8,128)(2,1)}, u32[]{:S(2)}, u32[]{:S(2)}) %collective-permute-start.2) | collective-permute-done | bytes 2097184 | tf_op jit(solution)/shard_map/ppermute | solution.py:17
  56.7 1.7 fusion.95
  58.4 2.6 %collective-permute-done.1 = bf16[2,8,512,128]{3,2,1,0:T(8,128)(2,1)} collective-permute-done((bf16[2,8,512,128]{3,2,1,0:T(8,128)(2,1)}, bf16[2,8,512,128]{3,2,1,0:T(8,128)(2,1)}, u32[]{:S(2)}, u32[]{:S(2)}) %collective-permute-start.1) | collective-permute-done | bytes 2097184 | tf_op jit(solution)/shard_map/ppermute | solution.py:17
  60.9 1.7 fusion.94
  62.6 37.9 %collective-permute-done = bf16[2,8,512,128]{3,2,1,0:T(8,128)(2,1)} collective-permute-done((bf16[2,8,512,128]{3,2,1,0:T(8,128)(2,1)}, bf16[2,8,512,128]{3,2,1,0:T(8,128)(2,1)}, u32[]{:S(2)}, u32[]{:S(2)}) %collective-permute-start) | collective-permute-done | bytes 2097184 | tf_op jit(solution)/shard_map/ppermute | solution.py:17
  100.5 1.7 fusion.93
  104.4 47.4 %collective-permute-done.3 = bf16[2,8,512,128]{3,2,1,0:T(8,128)(2,1)} collective-permute-done((bf16[2,8,512,128]{3,2,1,0:T(8,128)(2,1)}, bf16[2,8,512,128]{3,2,1,0:T(8,128)(2,1)}, u32[]{:S(2)}, u32[]{:S(2)}) %collective-permute-start.3) | collective-permute-done | bytes 2097184 | tf_op jit(solution)/shard_map/ppermute | solution.py:17
  151.8 1.7 fusion.96
  159.5 1.2 fusion.28
  163.3 5.5 %fusion.33 = bf16[8,512,128]{2,1,0:T(8,128)(2,1)S(1)} fusion(f32[8,2,256,128]{3,2,1,0:T(8,128)S(1)} %fusion.24, f32[8,2,256,128]{3,2,1,0:T(8,128)S(1)} %fusion.26, f32[8,2,256,128]{3,2,1,0:T(8,128)S(1)} %fusion.28, f32[8,2,256,128]{3,2,1,0:T(8,128)S(1)} %fusion.30, f32[8,512,512]{1,2,0:T(8,128)S(1)} %bitcast.221, f32[8,512]{1,0:T(8,128)S(1)} %get-tuple-element.80, ...), kind=kOutput, calls=%fused_computation.45 | convolution fusion | flops 548405248 | bytes 18972672 | tf_op jit(solution)/shard_map/while/body/eval_jaxpr/hqk,hkd->hqd/dot_general | solution.py:63
  168.8 2.8 %convert_add_fusion = f32[8,512,128]{2,1,0:T(8,128)S(1)} fusion(bf16[8,512,128]{2,1,0:T(8,128)(2,1)S(1)} %fusion.33, f32[8,512]{1,0:T(8,128)S(1)} %fusion.2, f32[8,512,512]{1,2,0:T(8,128)S(1)} %copy-done.2, f32[8,512]{1,0:T(8,128)S(1)} %get-tuple-element.82, bf16[512,1024]{1,0:T(8,128)(2,1)S(1)} %copy-done.9), kind=kOutput, calls=%fused_computation.54 | convolution fusion | flops 544735232 | bytes 12615680 | tf_op jit(solution)/shard_map/while/body/eval_jaxpr/hql,hld->hqd/dot_general | solution.py:33
  173.5 3.3 %all-to-all-start = ((bf16[4,2,1024]{2,1,0:T(2,128)(2,1)}), bf16[4,2,1024]{2,1,0:T(2,128)(2,1)S(1)}, u32[]{:S(2)}, u32[]{:S(2)}) async-start(bf16[4,2,1024]{2,1,0:T(2,128)(2,1)} %copy.56), calls=%async_computation | async-start | bytes 32768 | tf_op jit(solution)/shard_map/all_to_all | solution.py:157
  177.4 1.3 copy.58
  178.7 3.6 %all-to-all-done = bf16[4,2,1024]{2,1,0:T(2,128)(2,1)S(1)} async-done(((bf16[4,2,1024]{2,1,0:T(2,128)(2,1)}), bf16[4,2,1024]{2,1,0:T(2,128)(2,1)S(1)}, u32[]{:S(2)}, u32[]{:S(2)}) %all-to-all-start) | async-done | bytes 16416 | tf_op jit(solution)/shard_map/all_to_all | solution.py:157
  (67 shorter events, 16.2 us)
Async XLA Ops:
  0.6 19.6 %copy-start = (bf16[512,1024]{1,0:T(8,128)(2,1)S(1)}, bf16[512,1024]{1,0:T(8,128)(2,1)}, u32[]{:S(2)}) copy-start(bf16[512,1024]{1,0:T(8,128)(2,1)} %param.8) | copy-start | bytes 3145732
  0.6 19.6 %copy-start.3 = (bf16[512,1024]{1,0:T(8,128)(2,1)S(1)}, bf16[512,1024]{1,0:T(8,128)(2,1)}, u32[]{:S(2)}) copy-start(bf16[512,1024]{1,0:T(8,128)(2,1)} %param.9) | copy-start | bytes 3145732
  4.4 52.3 %collective-permute-start.2 = (bf16[2,8,512,128]{3,2,1,0:T(8,128)(2,1)}, bf16[2,8,512,128]{3,2,1,0:T(8,128)(2,1)}, u32[]{:S(2)}, u32[]{:S(2)}) collective-permute-start(bf16[2,8,512,128]{3,2,1,0:T(8,128)(2,1)} %pad_maximum_fusion), channel_id=1, source_target_pairs={{0,8},{4,12},{1,9},{5,13},{2,10},{6,14},{3,11},{7,15},{16,24},{20,... | collective-permute-start | bytes 6291464 | tf_op jit(solution)/shard_map/ppermute | solution.py:17
  11.7 49.3 %collective-permute-start.1 = (bf16[2,8,512,128]{3,2,1,0:T(8,128)(2,1)}, bf16[2,8,512,128]{3,2,1,0:T(8,128)(2,1)}, u32[]{:S(2)}, u32[]{:S(2)}) collective-permute-start(bf16[2,8,512,128]{3,2,1,0:T(8,128)(2,1)} %pad_maximum_fusion), channel_id=1, source_target_pairs={{4,0},{8,4},{12,8},{5,1},{9,5},{13,9},{6,2},{10,6},{14,10},{7,3},{... | collective-permute-start | bytes 6291464 | tf_op jit(solution)/shard_map/ppermute | solution.py:17
  12.9 87.6 %collective-permute-start = (bf16[2,8,512,128]{3,2,1,0:T(8,128)(2,1)}, bf16[2,8,512,128]{3,2,1,0:T(8,128)(2,1)}, u32[]{:S(2)}, u32[]{:S(2)}) collective-permute-start(bf16[2,8,512,128]{3,2,1,0:T(8,128)(2,1)} %pad_maximum_fusion), channel_id=1, source_target_pairs={{0,4},{4,8},{8,12},{1,5},{5,9},{9,13},{2,6},{6,10},{10,14},{3,7},{... | collective-permute-start | bytes 6291464 | tf_op jit(solution)/shard_map/ppermute | solution.py:17
  18.9 132.9 %collective-permute-start.3 = (bf16[2,8,512,128]{3,2,1,0:T(8,128)(2,1)}, bf16[2,8,512,128]{3,2,1,0:T(8,128)(2,1)}, u32[]{:S(2)}, u32[]{:S(2)}) collective-permute-start(bf16[2,8,512,128]{3,2,1,0:T(8,128)(2,1)} %pad_maximum_fusion), channel_id=1, source_target_pairs={{8,0},{12,4},{9,1},{13,5},{10,2},{14,6},{11,3},{15,7},{24,16},{28,... | collective-permute-start | bytes 6291464 | tf_op jit(solution)/shard_map/ppermute | solution.py:17
  20.2 4.5 %copy-start.4 = (bf16[512,1024]{1,0:T(8,128)(2,1)S(1)}, bf16[512,1024]{1,0:T(8,128)(2,1)}, u32[]{:S(2)}) copy-start(bf16[512,1024]{1,0:T(8,128)(2,1)} %param.11) | copy-start | bytes 3145732
  24.7 4.5 %copy-start.7 = (s32[32]{0:T(128)S(1)}, s32[32]{0:T(128)}, u32[]{:S(2)}) copy-start(s32[32]{0:T(128)} %param.15) | copy-start | bytes 388
  24.7 4.8 %copy-start.8 = (s32[32]{0:T(128)S(1)}, s32[32]{0:T(128)}, u32[]{:S(2)}) copy-start(s32[32]{0:T(128)} %param.14) | copy-start | bytes 388
  30.5 5.8 %copy-start.2 = (f32[8,512,512]{1,2,0:T(8,128)S(1)}, f32[8,512,512]{1,2,0:T(8,128)}, u32[]{:S(2)}) copy-start(f32[8,512,512]{1,2,0:T(8,128)} %get-tuple-element.83) | copy-start | bytes 25165828
  36.2 1.4 copy-start.6
  159.5 3.6 %slice-start = ((s8[8388608]{0:T(1024)(128)(4,1)}), s8[4194304]{0:T(1024)(128)(4,1)S(1)}, s32[]{:S(2)}) async-start(s8[8388608]{0:T(1024)(128)(4,1)} %bitcast.220), calls=%async_computation.1 | async-start | bytes 8388608
  160.6 2.5 %slice-start.1 = ((s8[8388608]{0:T(1024)(128)(4,1)}), s8[4194304]{0:T(1024)(128)(4,1)S(1)}, s32[]{:S(2)}) async-start(s8[8388608]{0:T(1024)(128)(4,1)} %bitcast.220), calls=%async_computation.2 | async-start | bytes 8388608
  161.8 1.5 copy-start.5
  163.3 5.5 %copy-start.9 = (bf16[512,1024]{1,0:T(8,128)(2,1)S(1)}, bf16[512,1024]{1,0:T(8,128)(2,1)}, u32[]{:S(2)}) copy-start(bf16[512,1024]{1,0:T(8,128)(2,1)} %param.12) | copy-start | bytes 3145732
  168.8 14.2 %copy-start.1 = (bf16[512,1024]{1,0:T(8,128)(2,1)S(1)}, bf16[512,1024]{1,0:T(8,128)(2,1)}, u32[]{:S(2)}) copy-start(bf16[512,1024]{1,0:T(8,128)(2,1)} %param.8) | copy-start | bytes 3145732
  173.5 8.8 %all-to-all-start = ((bf16[4,2,1024]{2,1,0:T(2,128)(2,1)}), bf16[4,2,1024]{2,1,0:T(2,128)(2,1)S(1)}, u32[]{:S(2)}, u32[]{:S(2)}) async-start(bf16[4,2,1024]{2,1,0:T(2,128)(2,1)} %copy.56), calls=%async_computation | async-start | bytes 32768 | tf_op jit(solution)/shard_map/all_to_all | solution.py:157
where the time goes:
time: 183 us
  waiting for transfers between devices  110 us (60%)
  matrix products  26 us (14%)
  starting transfers between devices  19 us (10%)
  local copies, waits for them, and re-layouts  13.3 us (7%)
  other arithmetic  13.3 us (7%)
    ppermute x4, waiting for transfers between devices, from_behind(): lax.ppermute(value, axis, [(source, source + steps) for source in range(f...  107 us
    ppermute x4, starting transfers between devices, from_behind(): lax.ppermute(value, axis, [(source, source + steps) for source in range(f...  15.8 us
    dot_general x1, matrix products, own_block(): jnp.einsum('hqk,hkd->hqd', exp_terms.astype(jnp.bfloat16), value_heads, p...  5.47 us
    slice x3, local copies, waits for them, and re-layouts, body(): panel_vals = panel_data[1].reshape(heads_here, blocks_here, BLK, HD)  5.04 us
    reduce_sum x1, other arithmetic, own_block(): totals = jnp.sum(exp_terms, axis=2)  4.94 us
    dot_general x4, matrix products, body(): jnp.einsum('hbqk,hbkd->hbqd', weights, panel_vals, preferred_element_type...  4.64 us
    dot_general x1, matrix products, own_block(): jnp.einsum('hqd,hkd->hqk', query_heads, key_heads, preferred_element_type...  4.49 us
    dot_general x1, matrix products, latent_mix(): jnp.einsum('hqd,hld->hql', query_heads, latent_heads, preferred_element_t...  4.47 us
  transfers between devices with their start and end apart: 5, of which 5 were waited for; matrix products, arithmetic and copies ran while one was open for 14% of the time, Pallas kernels for 0%

commit v1 on v0

v1 whole, which is shorter than its diff:
```python
import functools
import math

import jax
import jax.numpy as jnp
from jax import lax
from jax.experimental import pallas as pl
from jax.experimental.pallas import tpu as pltpu
from jax.sharding import PartitionSpec as P

HD = 128
LEVELS = 4
BLK = 256
PIECES = 4
SCALE = math.log2(math.e) / math.sqrt(HD)
PARAMS = pltpu.CompilerParams(vmem_limit_bytes=40 * 1024 * 1024)
F32 = jnp.float32
BF16 = jnp.bfloat16


def dot_t(a, b):
    return lax.dot_general(a, b, (((1,), (1,)), ((), ())), preferred_element_type=F32)


def dot(a, b):
    return jnp.dot(a, b, preferred_element_type=F32)


def doc_rows(rows, split):
    place = lax.broadcasted_iota(jnp.int32, rows.shape, 0)
    first = jnp.sum(jnp.where(place < split, rows, 0.0), axis=0, keepdims=True)
    second = jnp.sum(jnp.where(place < split, 0.0, rows), axis=0, keepdims=True)
    return jnp.concatenate((first, second), axis=0)


def own_kernel(splits, q_ref, k_ref, v_ref, lk_ref, lv_ref, acc_ref, top_ref, sum_ref, lat_ref):
    q = q_ref[...]
    s = dot_t(q, k_ref[...]) * SCALE
    top = jnp.max(s, axis=1, keepdims=True)
    e = jnp.exp2(s - top)
    acc_ref[...] = dot(e.astype(BF16), v_ref[...])
    top_ref[...] = jnp.broadcast_to(top, top_ref.shape)
    sum_ref[...] = jnp.broadcast_to(jnp.sum(e, axis=1, keepdims=True), sum_ref.shape)
    s = dot_t(q, lk_ref[...]) * SCALE
    e = jnp.exp2(s - jnp.max(s, axis=1, keepdims=True))
    out = dot(e.astype(BF16), lv_ref[...]) / jnp.sum(e, axis=1, keepdims=True)
    piece = out.shape[0] // PIECES
    for p in range(PIECES):
        lat_ref[2 * p : 2 * p + 2, :] = doc_rows(out[p * piece : (p + 1) * piece], splits[p])


def slot_scores(live, q, keys, rows, block):
    scores = []
    for source, k_ref in enumerate(keys):
        s = dot_t(q, k_ref[rows, :]) * SCALE
        scores.append(jnp.where(live[source, block] == 1, s, -jnp.inf))
    return scores


def update_kernel(sources, live, q_ref, *refs):
    keys, vals = refs[:sources], refs[sources : 2 * sources]
    acc_in, top_in, sum_in, acc_ref, top_ref, sum_ref = refs[2 * sources :]
    for block in range(q_ref.shape[0] // BLK):
        rows = pl.ds(block * BLK, BLK)
        scores = slot_scores(live, q_ref[rows, :], keys, rows, block)
        old = top_in[rows, :1]
        top = old
        for s in scores:
            top = jnp.maximum(top, jnp.max(s, axis=1, keepdims=True))
        shrink = jnp.exp2(old - top)
        total = sum_in[rows, :1] * shrink
        acc = acc_in[rows, :] * shrink
        for s, v_ref in zip(scores, vals):
            e = jnp.exp2(s - top)
            total = total + jnp.sum(e, axis=1, keepdims=True)
            acc = acc + dot(e.astype(BF16), v_ref[rows, :])
        acc_ref[rows, :] = acc
        top_ref[rows, :] = jnp.broadcast_to(top, acc.shape)
        sum_ref[rows, :] = jnp.broadcast_to(total, acc.shape)


def weigh_kernel(sources, live, q_ref, *refs):
    keys = refs[:sources]
    acc_in, top_in, sum_in, acc_ref = refs[sources : sources + 4]
    outs = refs[sources + 4 :]
    for block in range(q_ref.shape[0] // BLK):
        rows = pl.ds(block * BLK, BLK)
        scores = slot_scores(live, q_ref[rows, :], keys, rows, block)
        old = top_in[rows, :1]
        top = old
        for s in scores:
            top = jnp.maximum(top, jnp.max(s, axis=1, keepdims=True))
        shrink = jnp.exp2(old - top)
        total = sum_in[rows, :1] * shrink
        exps = []
        for s in scores:
            e = jnp.exp2(s - top)
            total = total + jnp.sum(e, axis=1, keepdims=True)
            exps.append(e)
        inverse = 1.0 / total
        acc_ref[rows, :] = acc_in[rows, :] * (shrink * inverse)
        for e, out in zip(exps, outs):
            out[rows, :] = (e * inverse).astype(BF16)


def finish_kernel(sources, shards, splits, places, acc_ref, lat_ref, *refs):
    weights, vals = refs[:sources], refs[sources : 2 * sources]
    ctx_ref = refs[2 * sources]
    outs = refs[2 * sources + 1 :]
    rows_here = acc_ref.shape[0]
    piece = rows_here // PIECES
    parts = []
    for block in range(rows_here // BLK):
        rows = pl.ds(block * BLK, BLK)
        acc = acc_ref[rows, :]
        for w_ref, v_ref in zip(weights, vals):
            acc = acc + dot(w_ref[rows, :], v_ref[rows, :])
        ctx = acc.astype(BF16)
        ctx_ref[rows, :] = ctx
        ctx = ctx.astype(F32)
        for start in range(0, BLK, piece):
            parts.append(ctx[start : start + piece])
    means = []
    side = lax.broadcasted_iota(jnp.int32, (2, HD), 0)
    for p in range(PIECES):
        count = jnp.where(side == 0, splits[p], piece - splits[p]).astype(F32)
        means.append((doc_rows(parts[p], splits[p]) + lat_ref[2 * p : 2 * p + 2, :]) / count)
    for r in range(shards):
        chosen = jnp.zeros((2, HD), F32)
        for p in range(PIECES):
            chosen = jnp.where(places[p] == r, means[p], chosen)
        chosen = chosen.astype(BF16)
        if len(outs) == 1:
            outs[0][r] = chosen
        else:
            outs[r][...] = chosen


def spec(rows, columns=HD):
    return pl.BlockSpec((rows, columns), lambda h: (0, h))


def smem():
    return pl.BlockSpec(memory_space=pltpu.SMEM)


def shape(rows, columns, kind=F32):
    return jax.ShapeDtypeStruct((rows, columns), kind)


def shift(value, pairs):
    return lax.ppermute(value, "seq", pairs)


def body(queries, keys, values, latent_keys, latent_values, pattern, doc_starts, doc_owner):
    rows, columns = queries.shape
    heads = columns // HD
    seq_index = lax.axis_index("seq")
    seq_count = lax.axis_size("seq")
    blocks = rows // BLK
    levels = [j for j in range(LEVELS) if 2**j < seq_count]

    def both_ways(value, distance):
        behind = shift(value, [(s, s + distance) for s in range(seq_count - distance)])
        ahead = shift(value, [(s, s - distance) for s in range(distance, seq_count)])
        return [behind, ahead]

    def live_flags(level, merged):
        distance = 2**level
        flags = []
        for side, partner in ((0, seq_index - distance), (1, seq_index + distance)):
            inside = (partner >= 0) & (partner < seq_count)
            flags.append((pattern[:, 2 * level + side] == 1) & inside)
        if merged:
            return jnp.where(seq_index >= distance, flags[0], flags[1])[None].astype(jnp.int32)
        return jnp.stack(flags).astype(jnp.int32)

    last = levels[-1]
    merged = 2 * 2**last >= seq_count
    near_keys = both_ways(keys, 1)
    near_vals = both_ways(values, 1)

    def far(value, near):
        distance = 2**last
        if not merged:
            return both_ways(value, distance)
        if seq_count == 4:
            sent = jnp.where(seq_index == 2, near[0], jnp.where(seq_index == 1, near[1], value))
            return [shift(sent, [(0, 2), (3, 1), (2, 3), (1, 0)])]
        pairs = [(s, s + distance) for s in range(seq_count - distance)]
        pairs += [(s, s - distance) for s in range(distance, seq_count)]
        return [shift(value, pairs)]

    my_pieces = lax.dynamic_index_in_dim(doc_starts.reshape(seq_count, PIECES, 2), seq_index, 0, keepdims=False)
    splits = my_pieces[:, 1] - my_pieces[:, 0]
    owners = lax.dynamic_index_in_dim(doc_owner.reshape(seq_count, PIECES, 2), seq_index, 0, keepdims=False)[:, 0]
    rotate = seq_count <= 4
    places = lax.rem(owners - seq_index + seq_count, seq_count) if rotate else owners

    state_shapes = (shape(rows, columns),) * 3
    acc, top, total, lat = pl.pallas_call(
        own_kernel,
        grid=(heads,),
        in_specs=[smem()] + [spec(rows)] * 3 + [spec(latent_keys.shape[0])] * 2,
        out_specs=[spec(rows)] * 3 + [spec(2 * PIECES)],
        out_shape=state_shapes + (shape(2 * PIECES, columns),),
        compiler_params=PARAMS,
        cost_estimate=pl.CostEstimate(
            flops=8 * rows * columns * rows, bytes_accessed=12 * rows * columns * 2, transcendentals=2 * heads * rows * rows
        ),
        name="own",
    )(splits, queries, keys, values, latent_keys, latent_values)

    state = (acc, top, total)
    for level in levels[:-1]:
        if level == 0:
            got_keys, got_vals = near_keys, near_vals
        else:
            got_keys, got_vals = both_ways(keys, 2**level), both_ways(values, 2**level)
        sources = len(got_keys)
        first = 2 + 2 * sources
        state = pl.pallas_call(
            functools.partial(update_kernel, sources),
            grid=(heads,),
            in_specs=[smem()] + [spec(rows)] * (4 + 2 * sources),
            out_specs=[spec(rows)] * 3,
            out_shape=state_shapes,
            input_output_aliases={first + i: i for i in range(3)},
            compiler_params=PARAMS,
            cost_estimate=pl.CostEstimate(
                flops=4 * sources * rows * columns * BLK,
                bytes_accessed=(12 + 4 * sources) * rows * columns * 2,
                transcendentals=sources * heads * rows * BLK,
            ),
            name="near",
        )(live_flags(level, False), queries, *got_keys, *got_vals, *state)

    far_keys = far(keys, near_keys)
    far_vals = far(values, near_vals)
    sources = len(far_keys)
    acc, *weights = pl.pallas_call(
        functools.partial(weigh_kernel, sources),
        grid=(heads,),
        in_specs=[smem()] + [spec(rows)] * (4 + sources),
        out_specs=[spec(rows)] + [spec(rows, BLK)] * sources,
        out_shape=(shape(rows, columns),) + (shape(rows, heads * BLK, BF16),) * sources,
        input_output_aliases={2 + sources: 0},
        compiler_params=PARAMS,
        cost_estimate=pl.CostEstimate(
            flops=2 * sources * rows * columns * BLK,
            bytes_accessed=(10 + 3 * sources) * rows * columns * 2,
            transcendentals=sources * heads * rows * BLK,
        ),
        name="weigh",
    )(live_flags(last, merged), queries, *far_keys, *state)

    if rotate:
        out_specs = [pl.BlockSpec((2, HD), lambda h: (0, h))] * seq_count
        out_shapes = (shape(2, columns, BF16),) * seq_count
    else:
        out_specs = [pl.BlockSpec((seq_count, 2, HD), lambda h: (0, 0, h))]
        out_shapes = (jax.ShapeDtypeStruct((seq_count, 2, columns), BF16),)
    context, *means = pl.pallas_call(
        functools.partial(finish_kernel, sources, seq_count),
        grid=(heads,),
        in_specs=[smem()] * 2 + [spec(rows), spec(2 * PIECES)] + [spec(rows, BLK)] * sources + [spec(rows)] * sources,
        out_specs=[spec(rows)] + out_specs,
        out_shape=(shape(rows, columns, BF16),) + out_shapes,
        compiler_params=PARAMS,
        cost_estimate=pl.CostEstimate(
            flops=2 * sources * rows * columns * BLK, bytes_accessed=(3 + 3 * sources) * rows * columns * 2, transcendentals=0
        ),
        name="finish",
    )(splits, places, acc, lat, *weights, *far_vals)

    if not rotate:
        return context, lax.all_to_all(means[0], "seq", split_axis=0, concat_axis=0, tiled=True)[None]
    got = [means[0]]
    for r in range(1, seq_count):
        got.append(shift(means[r], [(s, (s + r) % seq_count) for s in range(seq_count)]))
    pooled = []
    for s in range(seq_count):
        back = lax.rem(seq_index - s + seq_count, seq_count)
        row = got[0]
        for r in range(1, seq_count):
            row = jnp.where(back == r, got[r], row)
        pooled.append(row)
    return context, jnp.stack(pooled)[None]


def solution(mesh):
    in_specs = (
        P(("groups", "seq"), ("head", "sub")),
        P(("groups", "seq"), ("head", "sub")),
        P(("groups", "seq"), ("head", "sub")),
        P("groups", ("head", "sub")),
        P("groups", ("head", "sub")),
        P(("groups", "seq"), None),
        P("groups"),
        P("groups"),
    )
    out_specs = (
        P(("groups", "seq"), ("head", "sub")),
        P(("groups", "seq"), None, None, ("head", "sub")),
    )
    return jax.shard_map(body, mesh=mesh, in_specs=in_specs, out_specs=out_specs, check_vma=False)
```

time: 183 us -> 139 us (0.76)
  waiting for transfers between devices: 110 us -> 39.2 us
  Pallas kernels: 0 us -> 36.1 us
  starting transfers between devices: 19 us -> 50.5 us
  matrix products: 26 us -> 0 us
  other arithmetic: 13.3 us -> 5.32 us
  local copies, waits for them, and re-layouts: 13.3 us -> 6.59 us
    ppermute x4 -> x9, waiting for transfers between devices: 107 us -> 39.2 us  [shift(): return lax.ppermute(value, 'seq', pairs)]
    pallas_call x0 -> x4, Pallas kernels: none -> 36.1 us  [the longest x1 11.3 us: body(): pl.pallas_call(own_kernel, grid=(heads,), in_specs=[smem()] + [spec(rows)...]
    ppermute x4 -> x9, starting transfers between devices: 15.8 us -> 50.5 us  [shift(): return lax.ppermute(value, 'seq', pairs)]
    dot_general x14 -> x0, matrix products: 26 us -> none  [the longest x1 5.47 us: own_block(): jnp.einsum('hqk,hkd->hqd', exp_terms.astype(jnp.bfloat16), value_heads, p...]
    reduce_sum x7 -> x0, other arithmetic: 10.3 us -> none  [the longest x1 4.94 us: own_block(): totals = jnp.sum(exp_terms, axis=2)]
    slice x5 -> x0, local copies, waits for them, and re-layouts: 6.83 us -> none  [the longest x3 5.04 us: body(): panel_vals = panel_data[1].reshape(heads_here, blocks_here, BLK, HD)]
    all_to_all x1 -> x0, waiting for transfers between devices: 3.62 us -> none  [body(): lax.all_to_all(outgoing.astype(jnp.bfloat16), 'seq', split_axis=0, concat...]
    select_n x0 -> x2, other arithmetic: none -> 3.47 us  [far(): jnp.where(seq_index == 2, near[0], jnp.where(seq_index == 1, near[1], val...]
  transfers between devices with their start and end apart: 5 -> 9, of which waited for: 5 -> 7; matrix products, arithmetic and copies ran while one was open for 14% -> 5% of each run, Pallas kernels for 0% -> 22%
where the time goes in v1:
time: 139 us; the launch traced here: 138 us
  starting transfers between devices  50.5 us (36%)
  waiting for transfers between devices  39.2 us (28%)
  Pallas kernels  36.1 us (26%)
  local copies, waits for them, and re-layouts  6.59 us (5%)
  other arithmetic  5.32 us (4%)
    ppermute x9, starting transfers between devices, shift(): return lax.ppermute(value, 'seq', pairs)  50.5 us
    ppermute x9, waiting for transfers between devices, shift(): return lax.ppermute(value, 'seq', pairs)  39.2 us
    pallas_call x1, Pallas kernels, body(): pl.pallas_call(own_kernel, grid=(heads,), in_specs=[smem()] + [spec(rows)...  11.3 us
    pallas_call x1, Pallas kernels, body(): pl.pallas_call(functools.partial(update_kernel, sources), grid=(heads,),...  10.9 us
    pallas_call x1, Pallas kernels, body(): pl.pallas_call(functools.partial(weigh_kernel, sources), grid=(heads,), i...  7.6 us
    pallas_call x1, Pallas kernels, body(): pl.pallas_call(functools.partial(finish_kernel, sources, seq_count), grid...  6.29 us
    unnamed x14, local copies, waits for them, and re-layouts  4.91 us
    select_n x2, other arithmetic, far(): jnp.where(seq_index == 2, near[0], jnp.where(seq_index == 1, near[1], val...  3.47 us
  transfers between devices with their start and end apart: 9, of which 7 were waited for; matrix products, arithmetic and copies ran while one was open for 5% of the time, Pallas kernels for 22%

profile of v1, /device:TPU:0, one launch (start us, length us, event | category | flops | bytes accessed | tf_op | source)
XLA Modules:
  0.0 138.5 jit_solution(10369603540897817210)
XLA Ops:
  0.6 5.0 %collective-permute-start = (bf16[512,1024]{1,0:T(8,128)(2,1)}, bf16[512,1024]{1,0:T(8,128)(2,1)S(1)}, u32[]{:S(2)}, u32[]{:S(2)}) collective-permute-start(bf16[512,1024]{1,0:T(8,128)(2,1)} %k_ref.1), channel_id=1, source_target_pairs={{0,4},{4,8},{8,12},{1,5},{5,9},{9,13},{2,6},{6,10},{10,14},{3,7},{... | collective-permute-start | bytes 3145736 | tf_op jit(solution)/shard_map/ppermute | solution.py:152
  5.6 1.3 collective-permute-start.1
  6.9 5.6 %collective-permute-start.3 = (bf16[512,1024]{1,0:T(8,128)(2,1)}, bf16[512,1024]{1,0:T(8,128)(2,1)}, u32[]{:S(2)}, u32[]{:S(2)}) collective-permute-start(bf16[512,1024]{1,0:T(8,128)(2,1)} %v_ref.1), channel_id=1, source_target_pairs={{0,4},{4,8},{8,12},{1,5},{5,9},{9,13},{2,6},{6,10},{10,14},{3,7},{... | collective-permute-start | bytes 3145736 | tf_op jit(solution)/shard_map/ppermute | solution.py:152
  12.5 1.3 collective-permute-start.4
  15.3 1.0 and_reduce_fusion.1
  16.3 13.1 %collective-permute-done.refs_0_ = bf16[512,1024]{1,0:T(8,128)(2,1)S(1)} collective-permute-done((bf16[512,1024]{1,0:T(8,128)(2,1)}, bf16[512,1024]{1,0:T(8,128)(2,1)S(1)}, u32[]{:S(2)}, u32[]{:S(2)}) %collective-permute-start) | collective-permute-done | bytes 1048608 | tf_op jit(solution)/shard_map/ppermute | solution.py:152
  29.4 4.4 %collective-permute-done.1.refs_1_ = bf16[512,1024]{1,0:T(8,128)(2,1)S(1)} collective-permute-done((bf16[512,1024]{1,0:T(8,128)(2,1)}, bf16[512,1024]{1,0:T(8,128)(2,1)S(1)}, u32[]{:S(2)}, u32[]{:S(2)}) %collective-permute-start.1) | collective-permute-done | bytes 1048608 | tf_op jit(solution)/shard_map/ppermute | solution.py:152
  33.8 2.3 %select_select_fusion.1 = bf16[512,1024]{1,0:T(8,128)(2,1)} fusion(bf16[512,1024]{1,0:T(8,128)(2,1)S(1)} %collective-permute-done.refs_0_, bf16[512,1024]{1,0:T(8,128)(2,1)S(1)} %collective-permute-done.1.refs_1_, bf16[512,1024]{1,0:T(8,128)(2,1)} %k_ref.1, pred[]{:T(512)S(6)} %eq.91, pred[]{:T(512)S(6)} %eq.90), kind=kLoop, calls=%fused_computation.1 | loop fusion | flops 1048576 | bytes 4194306 | tf_op jit(solution)/shard_map/jit(_where)/select_n | solution.py:188
  36.2 2.5 %collective-permute-start.2 = (bf16[512,1024]{1,0:T(8,128)(2,1)}, bf16[512,1024]{1,0:T(8,128)(2,1)}, u32[]{:S(2)}, u32[]{:S(2)}) collective-permute-start(bf16[512,1024]{1,0:T(8,128)(2,1)} %select_select_fusion.1), channel_id=1, source_target_pairs={{0,8},{12,4},{8,12},{4,0},{1,9},{13,5},{9,13},{5,1},{2,10},{14,6},... | collective-permute-start | bytes 3145736 | tf_op jit(solution)/shard_map/ppermute | solution.py:152
  38.7 13.2 %collective-permute-done.3.refs_2_ = bf16[512,1024]{1,0:T(8,128)(2,1)} collective-permute-done((bf16[512,1024]{1,0:T(8,128)(2,1)}, bf16[512,1024]{1,0:T(8,128)(2,1)}, u32[]{:S(2)}, u32[]{:S(2)}) %collective-permute-start.3) | collective-permute-done | bytes 1048608 | tf_op jit(solution)/shard_map/ppermute | solution.py:152
  51.9 4.5 %collective-permute-done.4.refs_3_ = bf16[512,1024]{1,0:T(8,128)(2,1)} collective-permute-done((bf16[512,1024]{1,0:T(8,128)(2,1)}, bf16[512,1024]{1,0:T(8,128)(2,1)}, u32[]{:S(2)}, u32[]{:S(2)}) %collective-permute-start.4) | collective-permute-done | bytes 1048608 | tf_op jit(solution)/shard_map/ppermute | solution.py:152
  56.4 1.1 select_select_fusion
  57.5 32.8 %collective-permute-start.5 = (bf16[512,1024]{1,0:T(8,128)(2,1)}, bf16[512,1024]{1,0:T(8,128)(2,1)}, u32[]{:S(2)}, u32[]{:S(2)}) collective-permute-start(bf16[512,1024]{1,0:T(8,128)(2,1)} %select_select_fusion), channel_id=1, source_target_pairs={{0,8},{12,4},{8,12},{4,0},{1,9},{13,5},{9,13},{5,1},{2,10},{14,6},... | collective-permute-start | bytes 3145736 | tf_op jit(solution)/shard_map/ppermute | solution.py:152
  90.7 1.2 copy-done.1
  92.0 1.2 copy-done.3
  93.2 1.2 copy-done.4
  94.4 1.2 copy-done.5
  95.6 11.3 %own.1 = (f32[512,1024]{1,0:T(8,128)S(1)}, f32[512,1024]{1,0:T(8,128)S(1)}, f32[512,1024]{1,0:T(8,128)S(1)}, f32[8,1024]{1,0:T(8,128)S(1)}) custom-call(s32[4]{0:T(128)S(1)} %subtract_bitcast_fusion.splits, bf16[512,1024]{1,0:T(8,128)(2,1)S(1)} %copy-done, bf16[512,1024]{1,0:T(8,128)(2,1)S(1)} %copy-done.1, bf16[512,1024]{1,0:T(8,128)(2,1)S(1)} %copy-done.3, ...), custom_call_target="tpu_custom_call" | custom-call | flops 2147483648 | bytes 12582912 | tf_op jit(solution)/shard_map/own/pallas_call | solution.py:201
  107.0 10.9 %near.1 = (f32[512,1024]{1,0:T(8,128)S(1)}, f32[512,1024]{1,0:T(8,128)S(1)}, f32[512,1024]{1,0:T(8,128)S(1)}) custom-call(s32[2,2]{1,0:T(2,128)S(1)} %add_convert_fusion.live, bf16[512,1024]{1,0:T(8,128)(2,1)S(1)} %copy-done, bf16[512,1024]{1,0:T(8,128)(2,1)S(1)} %collective-permute-done.refs_0_, ...), custom_call_target="tpu_custom_call", output_to_operand_aliasing={{0}: (6, {}), {1}: (7, {}), {2}: (8, {})} | custom-call | flops 1073741824 | bytes 20971520 | tf_op jit(solution)/shard_map/near/pallas_call | solution.py:222
  117.9 7.6 %weigh.1 = (f32[512,1024]{1,0:T(8,128)S(1)}, bf16[512,2048]{1,0:T(8,128)(2,1)S(1)}) custom-call(s32[1,2]{1,0:T(1,128)S(1)} %bitcast.19, bf16[512,1024]{1,0:T(8,128)(2,1)S(1)} %copy-done, bf16[512,1024]{1,0:T(8,128)(2,1)} %collective-permute-done.2.refs_0_, f32[512,1024]{1,0:T(8,128)S(1)} %get-tuple-element.19.refs_1_, ...), custom_call_target="tpu_custom_call", output_to_operand_aliasing={{0}: (3, {})} | custom-call | flops 268435456 | bytes 13631488 | tf_op jit(solution)/shard_map/weigh/pallas_call | solution.py:241
  125.5 6.3 %finish.1 = (bf16[512,1024]{1,0:T(8,128)(2,1)}, bf16[2,1024]{1,0:T(2,128)(2,1)S(1)}, bf16[2,1024]{1,0:T(2,128)(2,1)S(1)}, bf16[2,1024]{1,0:T(2,128)(2,1)S(1)}, bf16[2,1024]{1,0:T(2,128)(2,1)S(1)}) custom-call(s32[4]{0:T(128)S(1)} %subtract_bitcast_fusion.splits, s32[4]{0:T(128)S(1)} %compare_select_fusion.places, f32[512,1024]{1,0:T(8,128)S(1)} %get-tuple-element.22.acc_ref, ...), custom_call_target="tpu_custom_call" | custom-call | flops 268435456 | bytes 6291456 | tf_op jit(solution)/shard_map/finish/pallas_call | solution.py:263
  131.8 2.0 %collective-permute-start.8 = (bf16[2,1024]{1,0:T(2,128)(2,1)S(1)}, bf16[2,1024]{1,0:T(2,128)(2,1)S(1)}, u32[]{:S(2)}, u32[]{:S(2)}) collective-permute-start(bf16[2,1024]{1,0:T(2,128)(2,1)S(1)} %get-tuple-element.28), channel_id=1, source_target_pairs={{0,4},{4,8},{8,12},{12,0},{1,5},{5,9},{9,13},{13,1},{2,6},{6,10},{... | collective-permute-start | bytes 12296 | tf_op jit(solution)/shard_map/ppermute | solution.py:152
  133.8 1.6 %collective-permute-done.6 = bf16[2,1024]{1,0:T(2,128)(2,1)S(1)} collective-permute-done((bf16[2,1024]{1,0:T(2,128)(2,1)S(1)}, bf16[2,1024]{1,0:T(2,128)(2,1)S(1)}, u32[]{:S(2)}, u32[]{:S(2)}) %collective-permute-start.6) | collective-permute-done | bytes 4128 | tf_op jit(solution)/shard_map/ppermute | solution.py:152
  136.3 1.5 %collective-permute-done.8 = bf16[2,1024]{1,0:T(2,128)(2,1)S(1)} collective-permute-done((bf16[2,1024]{1,0:T(2,128)(2,1)S(1)}, bf16[2,1024]{1,0:T(2,128)(2,1)S(1)}, u32[]{:S(2)}, u32[]{:S(2)}) %collective-permute-start.8) | collective-permute-done | bytes 4128 | tf_op jit(solution)/shard_map/ppermute | solution.py:152
  (26 shorter events, 3.5 us)
Async XLA Ops:
  0.6 28.8 %collective-permute-start = (bf16[512,1024]{1,0:T(8,128)(2,1)}, bf16[512,1024]{1,0:T(8,128)(2,1)S(1)}, u32[]{:S(2)}, u32[]{:S(2)}) collective-permute-start(bf16[512,1024]{1,0:T(8,128)(2,1)} %k_ref.1), channel_id=1, source_target_pairs={{0,4},{4,8},{8,12},{1,5},{5,9},{9,13},{2,6},{6,10},{10,14},{3,7},{... | collective-permute-start | bytes 3145736 | tf_op jit(solution)/shard_map/ppermute | solution.py:152
  5.6 28.2 %collective-permute-start.1 = (bf16[512,1024]{1,0:T(8,128)(2,1)}, bf16[512,1024]{1,0:T(8,128)(2,1)S(1)}, u32[]{:S(2)}, u32[]{:S(2)}) collective-permute-start(bf16[512,1024]{1,0:T(8,128)(2,1)} %k_ref.1), channel_id=1, source_target_pairs={{4,0},{8,4},{12,8},{5,1},{9,5},{13,9},{6,2},{10,6},{14,10},{7,3},{... | collective-permute-start | bytes 3145736 | tf_op jit(solution)/shard_map/ppermute | solution.py:152
  6.9 45.0 %collective-permute-start.3 = (bf16[512,1024]{1,0:T(8,128)(2,1)}, bf16[512,1024]{1,0:T(8,128)(2,1)}, u32[]{:S(2)}, u32[]{:S(2)}) collective-permute-start(bf16[512,1024]{1,0:T(8,128)(2,1)} %v_ref.1), channel_id=1, source_target_pairs={{0,4},{4,8},{8,12},{1,5},{5,9},{9,13},{2,6},{6,10},{10,14},{3,7},{... | collective-permute-start | bytes 3145736 | tf_op jit(solution)/shard_map/ppermute | solution.py:152
  12.5 43.9 %collective-permute-start.4 = (bf16[512,1024]{1,0:T(8,128)(2,1)}, bf16[512,1024]{1,0:T(8,128)(2,1)}, u32[]{:S(2)}, u32[]{:S(2)}) collective-permute-start(bf16[512,1024]{1,0:T(8,128)(2,1)} %v_ref.1), channel_id=1, source_target_pairs={{4,0},{8,4},{12,8},{5,1},{9,5},{13,9},{6,2},{10,6},{14,10},{7,3},{... | collective-permute-start | bytes 3145736 | tf_op jit(solution)/shard_map/ppermute | solution.py:152
  16.3 40.1 %copy-start.2 = (bf16[512,1024]{1,0:T(8,128)(2,1)S(1)}, bf16[512,1024]{1,0:T(8,128)(2,1)}, u32[]{:S(2)}) copy-start(bf16[512,1024]{1,0:T(8,128)(2,1)} %v_ref.1) | copy-start | bytes 3145732
  36.2 54.4 %copy-start.6 = (s32[2,8]{1,0:T(2,128)S(1)}, s32[2,8]{1,0:T(2,128)}, u32[]{:S(2)}) copy-start(s32[2,8]{1,0:T(2,128)} %param.13) | copy-start | bytes 196
  36.2 54.6 %copy-start = (bf16[512,1024]{1,0:T(8,128)(2,1)S(1)}, bf16[512,1024]{1,0:T(8,128)(2,1)}, u32[]{:S(2)}) copy-start(bf16[512,1024]{1,0:T(8,128)(2,1)} %q_ref.5) | copy-start | bytes 3145732
  36.2 81.7 %collective-permute-start.2 = (bf16[512,1024]{1,0:T(8,128)(2,1)}, bf16[512,1024]{1,0:T(8,128)(2,1)}, u32[]{:S(2)}, u32[]{:S(2)}) collective-permute-start(bf16[512,1024]{1,0:T(8,128)(2,1)} %select_select_fusion.1), channel_id=1, source_target_pairs={{0,8},{12,4},{8,12},{4,0},{1,9},{13,5},{9,13},{5,1},{2,10},{14,6},... | collective-permute-start | bytes 3145736 | tf_op jit(solution)/shard_map/ppermute | solution.py:152
  57.5 67.9 %collective-permute-start.5 = (bf16[512,1024]{1,0:T(8,128)(2,1)}, bf16[512,1024]{1,0:T(8,128)(2,1)}, u32[]{:S(2)}, u32[]{:S(2)}) collective-permute-start(bf16[512,1024]{1,0:T(8,128)(2,1)} %select_select_fusion), channel_id=1, source_target_pairs={{0,8},{12,4},{8,12},{4,0},{1,9},{13,5},{9,13},{5,1},{2,10},{14,6},... | collective-permute-start | bytes 3145736 | tf_op jit(solution)/shard_map/ppermute | solution.py:152
  90.7 1.2 copy-start.1
  92.0 1.2 copy-start.3
  93.2 1.2 copy-start.4
  94.4 1.2 copy-start.5
  131.8 3.6 %collective-permute-start.6 = (bf16[2,1024]{1,0:T(2,128)(2,1)S(1)}, bf16[2,1024]{1,0:T(2,128)(2,1)S(1)}, u32[]{:S(2)}, u32[]{:S(2)}) collective-permute-start(bf16[2,1024]{1,0:T(2,128)(2,1)S(1)} %get-tuple-element.26), channel_id=1, source_target_pairs={{0,12},{4,0},{8,4},{12,8},{1,13},{5,1},{9,5},{13,9},{2,14},{6,2},{... | collective-permute-start | bytes 12296 | tf_op jit(solution)/shard_map/ppermute | solution.py:152
  131.8 4.5 %collective-permute-start.7 = (bf16[2,1024]{1,0:T(2,128)(2,1)S(1)}, bf16[2,1024]{1,0:T(2,128)(2,1)S(1)}, u32[]{:S(2)}, u32[]{:S(2)}) collective-permute-start(bf16[2,1024]{1,0:T(2,128)(2,1)S(1)} %get-tuple-element.27), channel_id=1, source_target_pairs={{0,8},{4,12},{8,0},{12,4},{1,9},{5,13},{9,1},{13,5},{2,10},{6,14},... | collective-permute-start | bytes 12296 | tf_op jit(solution)/shard_map/ppermute | solution.py:152
  131.8 6.0 %collective-permute-start.8 = (bf16[2,1024]{1,0:T(2,128)(2,1)S(1)}, bf16[2,1024]{1,0:T(2,128)(2,1)S(1)}, u32[]{:S(2)}, u32[]{:S(2)}) collective-permute-start(bf16[2,1024]{1,0:T(2,128)(2,1)S(1)} %get-tuple-element.28), channel_id=1, source_target_pairs={{0,4},{4,8},{8,12},{12,0},{1,5},{5,9},{9,13},{13,1},{2,6},{6,10},{... | collective-permute-start | bytes 12296 | tf_op jit(solution)/shard_map/ppermute | solution.py:152

commit v2 on v1

v2 whole, which is shorter than its diff:
```python
import functools
import math

import jax
import jax.numpy as jnp
from jax import lax
from jax.experimental import pallas as pl
from jax.experimental.pallas import tpu as pltpu
from jax.sharding import PartitionSpec as P

HD = 128
LEVELS = 4
BLK = 256
PIECES = 4
SCALE = math.log2(math.e) / math.sqrt(HD)
PARAMS = pltpu.CompilerParams(vmem_limit_bytes=40 * 1024 * 1024)
F32 = jnp.float32
BF16 = jnp.bfloat16


def dot_t(a, b):
    return lax.dot_general(a, b, (((1,), (1,)), ((), ())), preferred_element_type=F32)


def dot(a, b):
    return jnp.dot(a, b, preferred_element_type=F32)


def doc_rows(rows, split):
    place = lax.broadcasted_iota(jnp.int32, rows.shape, 0)
    first = jnp.sum(jnp.where(place < split, rows, 0.0), axis=0, keepdims=True)
    second = jnp.sum(jnp.where(place < split, 0.0, rows), axis=0, keepdims=True)
    return jnp.concatenate((first, second), axis=0)


def own_kernel(where, starts, q_ref, k_ref, v_ref, lk_ref, lv_ref, acc_ref, top_ref, sum_ref, lat_ref):
    q = q_ref[...]
    s = dot_t(q, k_ref[...]) * SCALE
    top = jnp.max(s, axis=1, keepdims=True)
    e = jnp.exp2(s - top)
    acc_ref[...] = dot(e.astype(BF16), v_ref[...])
    top_ref[...] = jnp.broadcast_to(top, top_ref.shape)
    sum_ref[...] = jnp.broadcast_to(jnp.sum(e, axis=1, keepdims=True), sum_ref.shape)
    s = dot_t(q, lk_ref[...]) * SCALE
    e = jnp.exp2(s - jnp.max(s, axis=1, keepdims=True))
    out = dot(e.astype(BF16), lv_ref[...]) / jnp.sum(e, axis=1, keepdims=True)
    piece = out.shape[0] // PIECES
    for p in range(PIECES):
        split = split_of(where, starts, p)
        lat_ref[2 * p : 2 * p + 2, :] = doc_rows(out[p * piece : (p + 1) * piece], split)


def split_of(where, starts, p):
    first = 2 * (PIECES * where[0] + p)
    return starts[first + 1] - starts[first]


def slot_live(where, pattern, shards, level, side, block):
    partner = where[0] + (2 * side - 1) * 2**level
    return (pattern[block, 2 * level + side] == 1) & (partner >= 0) & (partner < shards)


def live_scores(live, q, k):
    return jnp.where(live, dot_t(q, k) * SCALE, -jnp.inf)


def near_kernel(shards, level, where, pattern, q_ref, kb_ref, ka_ref, vb_ref, va_ref, *refs):
    acc_in, top_in, sum_in, acc_ref, top_ref, sum_ref = refs
    for block in range(q_ref.shape[0] // BLK):
        rows = pl.ds(block * BLK, BLK)
        q = q_ref[rows, :]
        scores = [
            live_scores(slot_live(where, pattern, shards, level, side, block), q, k_ref[rows, :])
            for side, k_ref in enumerate((kb_ref, ka_ref))
        ]
        old = top_in[rows, :1]
        top = old
        for s in scores:
            top = jnp.maximum(top, jnp.max(s, axis=1, keepdims=True))
        shrink = jnp.exp2(old - top)
        total = sum_in[rows, :1] * shrink
        acc = acc_in[rows, :] * shrink
        for s, v_ref in zip(scores, (vb_ref, va_ref)):
            e = jnp.exp2(s - top)
            total = total + jnp.sum(e, axis=1, keepdims=True)
            acc = acc + dot(e.astype(BF16), v_ref[rows, :])
        acc_ref[rows, :] = acc
        top_ref[rows, :] = jnp.broadcast_to(top, acc.shape)
        sum_ref[rows, :] = jnp.broadcast_to(total, acc.shape)


def far_kernel(shards, level, merged, where, pattern, q_ref, kb_ref, ka_ref, acc_in, top_in, sum_in, acc_ref, *outs):
    behind = where[0] >= 2**level
    for block in range(q_ref.shape[0] // BLK):
        rows = pl.ds(block * BLK, BLK)
        q = q_ref[rows, :]
        live = [slot_live(where, pattern, shards, level, side, block) for side in range(2)]
        pair = [k_ref[rows, :] for k_ref in (kb_ref, ka_ref)]
        if merged:
            live = [(behind & live[0]) | (jnp.logical_not(behind) & live[1])]
            pair = [jnp.where(behind, pair[0], pair[1])]
        scores = [live_scores(on, q, k) for on, k in zip(live, pair)]
        old = top_in[rows, :1]
        top = old
        for s in scores:
            top = jnp.maximum(top, jnp.max(s, axis=1, keepdims=True))
        shrink = jnp.exp2(old - top)
        total = sum_in[rows, :1] * shrink
        exps = []
        for s in scores:
            e = jnp.exp2(s - top)
            total = total + jnp.sum(e, axis=1, keepdims=True)
            exps.append(e)
        inverse = 1.0 / total
        acc_ref[rows, :] = acc_in[rows, :] * (shrink * inverse)
        for e, out in zip(exps, outs):
            out[rows, :] = (e * inverse).astype(BF16)


def finish_kernel(shards, level, merged, where, starts, owners, acc_ref, lat_ref, *refs):
    sources = 1 if merged else 2
    weights, (vb_ref, va_ref) = refs[:sources], refs[sources : sources + 2]
    ctx_ref, outs = refs[sources + 2], refs[sources + 3 :]
    rows_here, columns = acc_ref.shape
    piece = rows_here // PIECES
    splits = [split_of(where, starts, p) for p in range(PIECES)]
    behind = where[0] >= 2**level
    sums = []
    for h in range(columns // HD):
        head = pl.ds(h * HD, HD)
        slots = pl.ds(h * BLK, BLK)
        found = []
        for block in range(rows_here // BLK):
            rows = pl.ds(block * BLK, BLK)
            pair = [v_ref[rows, head] for v_ref in (vb_ref, va_ref)]
            if merged:
                pair = [jnp.where(behind, pair[0], pair[1])]
            acc = acc_ref[rows, head]
            for w_ref, v in zip(weights, pair):
                acc = acc + dot(w_ref[rows, slots], v)
            ctx = acc.astype(BF16)
            ctx_ref[rows, head] = ctx
            ctx = ctx.astype(F32)
            for start in range(0, BLK, piece):
                found.append(doc_rows(ctx[start : start + piece], splits[len(found)]))
        sums.append(found)
    side = lax.broadcasted_iota(jnp.int32, (2, columns), 0)
    means = []
    for p in range(PIECES):
        count = jnp.where(side == 0, splits[p], piece - splits[p]).astype(F32)
        total = jnp.concatenate([found[p] for found in sums], axis=1) + lat_ref[2 * p : 2 * p + 2, :]
        means.append(total / count)
    for r in range(shards):
        if len(outs) == 1:
            target = r
        else:
            target = lax.rem(where[0] + r, shards)
        chosen = jnp.zeros((2, columns), F32)
        for p in range(PIECES):
            chosen = jnp.where(owners[2 * (PIECES * where[0] + p)] == target, means[p], chosen)
        if len(outs) == 1:
            outs[0][r] = chosen.astype(BF16)
        else:
            outs[r][...] = chosen.astype(BF16)


def spec(rows, columns=HD):
    return pl.BlockSpec((rows, columns), lambda h: (0, h))


def smem(count):
    return [pl.BlockSpec(memory_space=pltpu.SMEM)] * count


def vmem(count):
    return [pl.BlockSpec(memory_space=pltpu.VMEM)] * count


def shape(rows, columns, kind=F32):
    return jax.ShapeDtypeStruct((rows, columns), kind)


def body(queries, keys, values, latent_keys, latent_values, pattern, doc_starts, doc_owner):
    rows, columns = queries.shape
    heads = columns // HD
    shards = lax.axis_size("seq")
    seq_index = lax.axis_index("seq")
    where = seq_index.astype(jnp.int32).reshape(1)
    levels = [j for j in range(LEVELS) if 2**j < shards]
    last = levels[-1]
    merged = 2 * 2**last >= shards
    rotate = shards <= 4

    def both_ways(value, distance):
        behind = lax.ppermute(value, "seq", [(s, s + distance) for s in range(shards - distance)])
        ahead = lax.ppermute(value, "seq", [(s, s - distance) for s in range(distance, shards)])
        return [behind, ahead]

    def far(value, near):
        if last != 1:
            return both_ways(value, 2**last)
        behind = lax.ppermute(near[0], "seq", [(s, s + 1) for s in range(1, shards - 1)])
        ahead = lax.ppermute(near[1], "seq", [(s, s - 1) for s in range(1, shards - 1)])
        return [behind, ahead]

    near_keys = both_ways(keys, 1)
    near_vals = both_ways(values, 1)
    state_shapes = (shape(rows, columns),) * 3
    *state, lat = pl.pallas_call(
        own_kernel,
        grid=(heads,),
        in_specs=smem(2) + [spec(rows)] * 3 + [spec(latent_keys.shape[0])] * 2,
        out_specs=[spec(rows)] * 3 + [spec(2 * PIECES)],
        out_shape=state_shapes + (shape(2 * PIECES, columns),),
        compiler_params=PARAMS,
        cost_estimate=pl.CostEstimate(
            flops=8 * rows * columns * rows, bytes_accessed=12 * rows * columns * 2, transcendentals=2 * heads * rows * rows
        ),
        name="own",
    )(where, doc_starts, queries, keys, values, latent_keys, latent_values)
    near_keys, state = lax.optimization_barrier((near_keys, state))

    for level in levels[:-1]:
        if level == 0:
            got = near_keys + near_vals
        else:
            got = both_ways(keys, 2**level) + both_ways(values, 2**level)
        state = pl.pallas_call(
            functools.partial(near_kernel, shards, level),
            grid=(heads,),
            in_specs=smem(2) + [spec(rows)] * 8,
            out_specs=[spec(rows)] * 3,
            out_shape=state_shapes,
            input_output_aliases={7 + i: i for i in range(3)},
            compiler_params=PARAMS,
            cost_estimate=pl.CostEstimate(
                flops=8 * rows * columns * BLK, bytes_accessed=20 * rows * columns * 2, transcendentals=2 * heads * rows * BLK
            ),
            name="near",
        )(where, pattern, queries, *got, *state)

    far_keys = far(keys, near_keys)
    far_vals = far(values, near_vals)
    sources = 1 if merged else 2
    acc, *weights = pl.pallas_call(
        functools.partial(far_kernel, shards, last, merged),
        grid=(heads,),
        in_specs=smem(2) + [spec(rows)] * 6,
        out_specs=[spec(rows)] + [spec(rows, BLK)] * sources,
        out_shape=(shape(rows, columns),) + (shape(rows, heads * BLK, BF16),) * sources,
        input_output_aliases={5: 0},
        compiler_params=PARAMS,
        cost_estimate=pl.CostEstimate(
            flops=2 * sources * rows * columns * BLK,
            bytes_accessed=(10 + 3 * sources) * rows * columns * 2,
            transcendentals=sources * heads * rows * BLK,
        ),
        name="far",
    )(where, pattern, queries, *far_keys, *state)

    if rotate:
        sent = (shape(2, columns, BF16),) * shards
    else:
        sent = (jax.ShapeDtypeStruct((shards, 2, columns), BF16),)
    context, *means = pl.pallas_call(
        functools.partial(finish_kernel, shards, last, merged),
        in_specs=smem(3) + vmem(4 + sources),
        out_specs=vmem(1 + len(sent)),
        out_shape=(shape(rows, columns, BF16),) + sent,
        compiler_params=PARAMS,
        cost_estimate=pl.CostEstimate(
            flops=2 * sources * rows * columns * BLK, bytes_accessed=(3 + 3 * sources) * rows * columns * 2, transcendentals=0
        ),
        name="finish",
    )(where, doc_starts, doc_owner, acc, lat, *weights, *far_vals)

    if not rotate:
        return context, lax.all_to_all(means[0], "seq", split_axis=0, concat_axis=0, tiled=True)[None]
    got = [means[0]]
    for r in range(1, shards):
        got.append(lax.ppermute(means[r], "seq", [(s, (s + r) % shards) for s in range(shards)]))
    pooled = []
    for s in range(shards):
        back = lax.rem(seq_index - s + shards, shards)
        row = got[0]
        for r in range(1, shards):
            row = jnp.where(back == r, got[r], row)
        pooled.append(row)
    return context, jnp.stack(pooled)[None]


def solution(mesh):
    in_specs = (
        P(("groups", "seq"), ("head", "sub")),
        P(("groups", "seq"), ("head", "sub")),
        P(("groups", "seq"), ("head", "sub")),
        P("groups", ("head", "sub")),
        P("groups", ("head", "sub")),
        P(("groups", "seq"), None),
        P("groups"),
        P("groups"),
    )
    out_specs = (
        P(("groups", "seq"), ("head", "sub")),
        P(("groups", "seq"), None, None, ("head", "sub")),
    )
    return jax.shard_map(body, mesh=mesh, in_specs=in_specs, out_specs=out_specs, check_vma=False)
```

time: 139 us -> 112 us (0.81)
  starting transfers between devices: 50.5 us -> 20 us
  waiting for transfers between devices: 39.2 us -> 50.4 us
  other arithmetic: 5.32 us -> 0.67 us
  Pallas kernels: 36.1 us -> 33 us
    ppermute x9 -> x11, starting transfers between devices: 50.5 us -> 20 us  [the longest x2 9.61 us: both_ways(): lax.ppermute(value, 'seq', [(s, s + distance) for s in range(shards - dis...]
    ppermute x9 -> x11, waiting for transfers between devices: 39.2 us -> 50.4 us  [the longest x2 23.5 us: far(): lax.ppermute(near[1], 'seq', [(s, s - 1) for s in range(1, shards - 1)])]
    select_n x2 -> x0, other arithmetic: 3.47 us -> none  [far(): jnp.where(seq_index == 2, near[0], jnp.where(seq_index == 1, near[1], val...]
    pallas_call x4, Pallas kernels: 36.1 us -> 33 us  [the longest x1 11.4 us: body(): pl.pallas_call(own_kernel, grid=(heads,), in_specs=smem(2) + [spec(rows)]...]
    unnamed x14 -> x16, local copies, waits for them, and re-layouts: 4.91 us -> 6.78 us
    reshape x2 -> x0, local copies, waits for them, and re-layouts: 1.5 us -> none  [the longest x1 0.75 us: body(): doc_owner.reshape(seq_count, PIECES, 2)]
  transfers between devices with their start and end apart: 9 -> 11, of which waited for: 7 -> 7; matrix products, arithmetic and copies ran while one was open for 5% -> 0% of each run, Pallas kernels for 22% -> 27%
where the time goes in v2:
time: 112 us
  waiting for transfers between devices  50.4 us (45%)
  Pallas kernels  33 us (29%)
  starting transfers between devices  20 us (18%)
  local copies, waits for them, and re-layouts  6.78 us (6%)
    ppermute x2, waiting for transfers between devices, far(): lax.ppermute(near[1], 'seq', [(s, s - 1) for s in range(1, shards - 1)])  23.5 us
    ppermute x2, waiting for transfers between devices, both_ways(): lax.ppermute(value, 'seq', [(s, s + distance) for s in range(shards - dis...  14.8 us
    pallas_call x1, Pallas kernels, body(): pl.pallas_call(own_kernel, grid=(heads,), in_specs=smem(2) + [spec(rows)]...  11.4 us
    pallas_call x1, Pallas kernels, body(): pl.pallas_call(functools.partial(near_kernel, shards, level), grid=(heads...  10.9 us
    ppermute x2, starting transfers between devices, both_ways(): lax.ppermute(value, 'seq', [(s, s + distance) for s in range(shards - dis...  9.61 us
    pallas_call x1, Pallas kernels, body(): pl.pallas_call(functools.partial(far_kernel, shards, last, merged), grid=...  7.76 us
    ppermute x2, waiting for transfers between devices, both_ways(): lax.ppermute(value, 'seq', [(s, s - distance) for s in range(distance, sh...  7.66 us
    unnamed x16, local copies, waits for them, and re-layouts  6.78 us
  transfers between devices with their start and end apart: 11, of which 7 were waited for; matrix products, arithmetic and copies ran while one was open for 0% of the time, Pallas kernels for 27%

profile of v2, /device:TPU:0, one launch (start us, length us, event | category | flops | bytes accessed | tf_op | source)
XLA Modules:
  0.0 111.7 jit_solution(17878960538365141779)
XLA Ops:
  0.6 5.0 %collective-permute-start = (bf16[512,1024]{1,0:T(8,128)(2,1)}, bf16[512,1024]{1,0:T(8,128)(2,1)S(1)}, u32[]{:S(2)}, u32[]{:S(2)}) collective-permute-start(bf16[512,1024]{1,0:T(8,128)(2,1)} %k_ref.1), channel_id=1, source_target_pairs={{0,4},{4,8},{8,12},{1,5},{5,9},{9,13},{2,6},{6,10},{10,14},{3,7},{... | collective-permute-start | bytes 3145736 | tf_op jit(solution)/shard_map/ppermute | solution.py:195
  5.6 1.3 %collective-permute-start.1 = (bf16[512,1024]{1,0:T(8,128)(2,1)}, bf16[512,1024]{1,0:T(8,128)(2,1)}, u32[]{:S(2)}, u32[]{:S(2)}) collective-permute-start(bf16[512,1024]{1,0:T(8,128)(2,1)} %k_ref.1), channel_id=1, source_target_pairs={{4,0},{8,4},{12,8},{5,1},{9,5},{13,9},{6,2},{10,6},{14,10},{7,3},{... | collective-permute-start | bytes 3145736 | tf_op jit(solution)/shard_map/ppermute | solution.py:196
  6.9 4.6 %collective-permute-start.4 = (bf16[512,1024]{1,0:T(8,128)(2,1)}, bf16[512,1024]{1,0:T(8,128)(2,1)S(1)}, u32[]{:S(2)}, u32[]{:S(2)}) collective-permute-start(bf16[512,1024]{1,0:T(8,128)(2,1)} %v_ref.1), channel_id=1, source_target_pairs={{0,4},{4,8},{8,12},{1,5},{5,9},{9,13},{2,6},{6,10},{10,14},{3,7},{... | collective-permute-start | bytes 3145736 | tf_op jit(solution)/shard_map/ppermute | solution.py:195
  11.6 1.3 %collective-permute-start.5 = (bf16[512,1024]{1,0:T(8,128)(2,1)}, bf16[512,1024]{1,0:T(8,128)(2,1)S(1)}, u32[]{:S(2)}, u32[]{:S(2)}) collective-permute-start(bf16[512,1024]{1,0:T(8,128)(2,1)} %v_ref.1), channel_id=1, source_target_pairs={{4,0},{8,4},{12,8},{5,1},{9,5},{13,9},{6,2},{10,6},{14,10},{7,3},{... | collective-permute-start | bytes 3145736 | tf_op jit(solution)/shard_map/ppermute | solution.py:196
  12.9 1.2 %copy-done = bf16[512,1024]{1,0:T(8,128)(2,1)S(1)} copy-done((bf16[512,1024]{1,0:T(8,128)(2,1)S(1)}, bf16[512,1024]{1,0:T(8,128)(2,1)}, u32[]{:S(2)}) %copy-start) | copy-done | bytes 1048600
  14.7 1.2 %copy-done.4 = bf16[512,1024]{1,0:T(8,128)(2,1)S(1)} copy-done((bf16[512,1024]{1,0:T(8,128)(2,1)S(1)}, bf16[512,1024]{1,0:T(8,128)(2,1)}, u32[]{:S(2)}) %copy-start.4) | copy-done | bytes 1048600
  16.0 1.2 %copy-done.5 = bf16[512,1024]{1,0:T(8,128)(2,1)S(1)} copy-done((bf16[512,1024]{1,0:T(8,128)(2,1)S(1)}, bf16[512,1024]{1,0:T(8,128)(2,1)}, u32[]{:S(2)}) %copy-start.5) | copy-done | bytes 1048600
  17.2 1.2 %copy-done.6 = bf16[512,1024]{1,0:T(8,128)(2,1)S(1)} copy-done((bf16[512,1024]{1,0:T(8,128)(2,1)S(1)}, bf16[512,1024]{1,0:T(8,128)(2,1)}, u32[]{:S(2)}) %copy-start.6) | copy-done | bytes 1048600
  18.4 1.2 %copy-done.7 = bf16[512,1024]{1,0:T(8,128)(2,1)S(1)} copy-done((bf16[512,1024]{1,0:T(8,128)(2,1)S(1)}, bf16[512,1024]{1,0:T(8,128)(2,1)}, u32[]{:S(2)}) %copy-start.7) | copy-done | bytes 1048600
  19.6 11.4 %own.1 = (f32[512,1024]{1,0:T(8,128)S(1)}, f32[512,1024]{1,0:T(8,128)S(1)}, f32[512,1024]{1,0:T(8,128)S(1)}, f32[8,1024]{1,0:T(8,128)S(1)}) custom-call(s32[1]{0:T(128)} %bitcast.where, s32[32]{0:T(128)S(1)} %copy-done.2, bf16[512,1024]{1,0:T(8,128)(2,1)S(1)} %copy-done, bf16[512,1024]{1,0:T(8,128)(2,1)S(1)} %copy-done.6, bf16[512,1024]{1,0:T(8,128)(2,1)S(1)} %copy-done.7, ...), custom_call_target="tpu_custom_call" | custom-call | flops 2147483648 | bytes 12582912 | tf_op jit(solution)/shard_map/own/pallas_call | solution.py:209
  31.1 2.8 %collective-permute-done.1.ka_ref = bf16[512,1024]{1,0:T(8,128)(2,1)} collective-permute-done((bf16[512,1024]{1,0:T(8,128)(2,1)}, bf16[512,1024]{1,0:T(8,128)(2,1)}, u32[]{:S(2)}, u32[]{:S(2)}) %collective-permute-start.1) | collective-permute-done | bytes 1048608 | tf_op jit(solution)/shard_map/ppermute | solution.py:196
  34.7 1.3 %collective-permute-start.3 = (bf16[512,1024]{1,0:T(8,128)(2,1)}, bf16[512,1024]{1,0:T(8,128)(2,1)S(1)}, u32[]{:S(2)}, u32[]{:S(2)}) collective-permute-start(bf16[512,1024]{1,0:T(8,128)(2,1)} %collective-permute-done.1.ka_ref), channel_id=1, source_target_pairs={{4,0},{8,4},{5,1},{9,5},{6,2},{10,6},{7,3},{11,7},{20,16},{24,20},... | collective-permute-start | bytes 3145736 | tf_op jit(solution)/shard_map/ppermute | solution.py:203
  36.0 14.8 %collective-permute-done.4.vb_ref = bf16[512,1024]{1,0:T(8,128)(2,1)S(1)} collective-permute-done((bf16[512,1024]{1,0:T(8,128)(2,1)}, bf16[512,1024]{1,0:T(8,128)(2,1)S(1)}, u32[]{:S(2)}, u32[]{:S(2)}) %collective-permute-start.4) | collective-permute-done | bytes 1048608 | tf_op jit(solution)/shard_map/ppermute | solution.py:195
  51.5 4.8 %collective-permute-done.5.va_ref = bf16[512,1024]{1,0:T(8,128)(2,1)S(1)} collective-permute-done((bf16[512,1024]{1,0:T(8,128)(2,1)}, bf16[512,1024]{1,0:T(8,128)(2,1)S(1)}, u32[]{:S(2)}, u32[]{:S(2)}) %collective-permute-start.5) | collective-permute-done | bytes 1048608 | tf_op jit(solution)/shard_map/ppermute | solution.py:196
  56.3 1.3 %collective-permute-start.7 = (bf16[512,1024]{1,0:T(8,128)(2,1)S(1)}, bf16[512,1024]{1,0:T(8,128)(2,1)S(1)}, u32[]{:S(2)}, u32[]{:S(2)}) collective-permute-start(bf16[512,1024]{1,0:T(8,128)(2,1)S(1)} %collective-permute-done.5.va_ref), channel_id=1, source_target_pairs={{4,0},{8,4},{5,1},{9,5},{6,2},{10,6},{7,3},{11,7},{20,16},{24,20},... | collective-permute-start | bytes 3145736 | tf_op jit(solution)/shard_map/ppermute | solution.py:203
  57.6 10.9 %near.1 = (f32[512,1024]{1,0:T(8,128)S(1)}, f32[512,1024]{1,0:T(8,128)S(1)}, f32[512,1024]{1,0:T(8,128)S(1)}) custom-call(s32[1]{0:T(128)} %bitcast.where, s32[2,8]{1,0:T(2,128)S(1)} %copy-done.1, bf16[512,1024]{1,0:T(8,128)(2,1)S(1)} %copy-done, ...), custom_call_target="tpu_custom_call", output_to_operand_aliasing={{0}: (7, {}), {1}: (8, {}), {2}: (9, {})} | custom-call | flops 1073741824 | bytes 20971520 | tf_op jit(solution)/shard_map/near/pallas_call | solution.py:228
  68.5 10.2 %collective-permute-done.3.ka_ref = bf16[512,1024]{1,0:T(8,128)(2,1)S(1)} collective-permute-done((bf16[512,1024]{1,0:T(8,128)(2,1)}, bf16[512,1024]{1,0:T(8,128)(2,1)S(1)}, u32[]{:S(2)}, u32[]{:S(2)}) %collective-permute-start.3) | collective-permute-done | bytes 1048608 | tf_op jit(solution)/shard_map/ppermute | solution.py:203
  78.8 7.8 %far.1 = (f32[512,1024]{1,0:T(8,128)S(1)}, bf16[512,2048]{1,0:T(8,128)(2,1)S(1)}) custom-call(s32[1]{0:T(128)} %bitcast.where, s32[2,8]{1,0:T(2,128)S(1)} %copy-done.1, bf16[512,1024]{1,0:T(8,128)(2,1)S(1)} %copy-done, bf16[512,1024]{1,0:T(8,128)(2,1)S(1)} %collective-permute-done.2.kb_ref, ...), custom_call_target="tpu_custom_call", output_to_operand_aliasing={{0}: (5, {})} | custom-call | flops 268435456 | bytes 13631488 | tf_op jit(solution)/shard_map/far/pallas_call | solution.py:245
  86.5 13.2 %collective-permute-done.7.refs_2_ = bf16[512,1024]{1,0:T(8,128)(2,1)S(1)} collective-permute-done((bf16[512,1024]{1,0:T(8,128)(2,1)S(1)}, bf16[512,1024]{1,0:T(8,128)(2,1)S(1)}, u32[]{:S(2)}, u32[]{:S(2)}) %collective-permute-start.7) | collective-permute-done | bytes 1048608 | tf_op jit(solution)/shard_map/ppermute | solution.py:203
  99.8 2.9 %finish.1 = (bf16[512,1024]{1,0:T(8,128)(2,1)}, bf16[2,1024]{1,0:T(2,128)(2,1)S(1)}, bf16[2,1024]{1,0:T(2,128)(2,1)S(1)}, bf16[2,1024]{1,0:T(2,128)(2,1)S(1)}, bf16[2,1024]{1,0:T(2,128)(2,1)S(1)}) custom-call(s32[1]{0:T(128)} %bitcast.where, s32[32]{0:T(128)S(1)} %copy-done.2, s32[32]{0:T(128)S(1)} %copy-done.3, f32[512,1024]{1,0:T(8,128)S(1)} %get-tuple-element.32.acc_ref, ...), custom_call_target="tpu_custom_call" | custom-call | flops 268435456 | bytes 6291456 | tf_op jit(solution)/shard_map/finish/pallas_call | solution.py:265
  102.7 1.5 %collective-permute-start.10 = (bf16[2,1024]{1,0:T(2,128)(2,1)S(1)}, bf16[2,1024]{1,0:T(2,128)(2,1)S(1)}, u32[]{:S(2)}, u32[]{:S(2)}) collective-permute-start(bf16[2,1024]{1,0:T(2,128)(2,1)S(1)} %get-tuple-element.38), channel_id=1, source_target_pairs={{0,4},{4,8},{8,12},{12,0},{1,5},{5,9},{9,13},{13,1},{2,6},{6,10},{... | collective-permute-start | bytes 12296 | tf_op jit(solution)/shard_map/ppermute | solution.py:281
  104.2 2.3 %collective-permute-start.8 = (bf16[2,1024]{1,0:T(2,128)(2,1)S(1)}, bf16[2,1024]{1,0:T(2,128)(2,1)S(1)}, u32[]{:S(2)}, u32[]{:S(2)}) collective-permute-start(bf16[2,1024]{1,0:T(2,128)(2,1)S(1)} %get-tuple-element.36), channel_id=1, source_target_pairs={{0,12},{4,0},{8,4},{12,8},{1,13},{5,1},{9,5},{13,9},{2,14},{6,2},{... | collective-permute-start | bytes 12296 | tf_op jit(solution)/shard_map/ppermute | solution.py:281
  106.5 1.6 %collective-permute-done.10 = bf16[2,1024]{1,0:T(2,128)(2,1)S(1)} collective-permute-done((bf16[2,1024]{1,0:T(2,128)(2,1)S(1)}, bf16[2,1024]{1,0:T(2,128)(2,1)S(1)}, u32[]{:S(2)}, u32[]{:S(2)}) %collective-permute-start.10) | collective-permute-done | bytes 4128 | tf_op jit(solution)/shard_map/ppermute | solution.py:281
  108.1 2.9 %collective-permute-done.9 = bf16[2,1024]{1,0:T(2,128)(2,1)S(1)} collective-permute-done((bf16[2,1024]{1,0:T(2,128)(2,1)S(1)}, bf16[2,1024]{1,0:T(2,128)(2,1)S(1)}, u32[]{:S(2)}, u32[]{:S(2)}) %collective-permute-start.9) | collective-permute-done | bytes 4128 | tf_op jit(solution)/shard_map/ppermute | solution.py:281
  (20 shorter events, 2.8 us)
Async XLA Ops:
  0.6 30.4 %collective-permute-start = (bf16[512,1024]{1,0:T(8,128)(2,1)}, bf16[512,1024]{1,0:T(8,128)(2,1)S(1)}, u32[]{:S(2)}, u32[]{:S(2)}) collective-permute-start(bf16[512,1024]{1,0:T(8,128)(2,1)} %k_ref.1), channel_id=1, source_target_pairs={{0,4},{4,8},{8,12},{1,5},{5,9},{9,13},{2,6},{6,10},{10,14},{3,7},{... | collective-permute-start | bytes 3145736 | tf_op jit(solution)/shard_map/ppermute | solution.py:195
  5.6 28.3 %collective-permute-start.1 = (bf16[512,1024]{1,0:T(8,128)(2,1)}, bf16[512,1024]{1,0:T(8,128)(2,1)}, u32[]{:S(2)}, u32[]{:S(2)}) collective-permute-start(bf16[512,1024]{1,0:T(8,128)(2,1)} %k_ref.1), channel_id=1, source_target_pairs={{4,0},{8,4},{12,8},{5,1},{9,5},{13,9},{6,2},{10,6},{14,10},{7,3},{... | collective-permute-start | bytes 3145736 | tf_op jit(solution)/shard_map/ppermute | solution.py:196
  6.9 43.8 %collective-permute-start.4 = (bf16[512,1024]{1,0:T(8,128)(2,1)}, bf16[512,1024]{1,0:T(8,128)(2,1)S(1)}, u32[]{:S(2)}, u32[]{:S(2)}) collective-permute-start(bf16[512,1024]{1,0:T(8,128)(2,1)} %v_ref.1), channel_id=1, source_target_pairs={{0,4},{4,8},{8,12},{1,5},{5,9},{9,13},{2,6},{6,10},{10,14},{3,7},{... | collective-permute-start | bytes 3145736 | tf_op jit(solution)/shard_map/ppermute | solution.py:195
  11.6 44.7 %collective-permute-start.5 = (bf16[512,1024]{1,0:T(8,128)(2,1)}, bf16[512,1024]{1,0:T(8,128)(2,1)S(1)}, u32[]{:S(2)}, u32[]{:S(2)}) collective-permute-start(bf16[512,1024]{1,0:T(8,128)(2,1)} %v_ref.1), channel_id=1, source_target_pairs={{4,0},{8,4},{12,8},{5,1},{9,5},{13,9},{6,2},{10,6},{14,10},{7,3},{... | collective-permute-start | bytes 3145736 | tf_op jit(solution)/shard_map/ppermute | solution.py:196
  12.9 1.2 %copy-start = (bf16[512,1024]{1,0:T(8,128)(2,1)S(1)}, bf16[512,1024]{1,0:T(8,128)(2,1)}, u32[]{:S(2)}) copy-start(bf16[512,1024]{1,0:T(8,128)(2,1)} %q_ref.5) | copy-start | bytes 3145732
  14.1 0.7 copy-start.2
  14.7 1.2 %copy-start.4 = (bf16[512,1024]{1,0:T(8,128)(2,1)S(1)}, bf16[512,1024]{1,0:T(8,128)(2,1)}, u32[]{:S(2)}) copy-start(bf16[512,1024]{1,0:T(8,128)(2,1)} %lk_ref.1) | copy-start | bytes 3145732
  16.0 1.2 %copy-start.5 = (bf16[512,1024]{1,0:T(8,128)(2,1)S(1)}, bf16[512,1024]{1,0:T(8,128)(2,1)}, u32[]{:S(2)}) copy-start(bf16[512,1024]{1,0:T(8,128)(2,1)} %lv_ref.1) | copy-start | bytes 3145732
  17.2 1.2 %copy-start.6 = (bf16[512,1024]{1,0:T(8,128)(2,1)S(1)}, bf16[512,1024]{1,0:T(8,128)(2,1)}, u32[]{:S(2)}) copy-start(bf16[512,1024]{1,0:T(8,128)(2,1)} %k_ref.1) | copy-start | bytes 3145732
  18.4 1.2 %copy-start.7 = (bf16[512,1024]{1,0:T(8,128)(2,1)S(1)}, bf16[512,1024]{1,0:T(8,128)(2,1)}, u32[]{:S(2)}) copy-start(bf16[512,1024]{1,0:T(8,128)(2,1)} %v_ref.1) | copy-start | bytes 3145732
  19.6 37.9 %copy-start.1 = (s32[2,8]{1,0:T(2,128)S(1)}, s32[2,8]{1,0:T(2,128)}, u32[]{:S(2)}) copy-start(s32[2,8]{1,0:T(2,128)} %pattern.3) | copy-start | bytes 196
  33.9 34.6 %collective-permute-start.2 = (bf16[512,1024]{1,0:T(8,128)(2,1)S(1)}, bf16[512,1024]{1,0:T(8,128)(2,1)S(1)}, u32[]{:S(2)}, u32[]{:S(2)}) collective-permute-start(bf16[512,1024]{1,0:T(8,128)(2,1)S(1)} %collective-permute-done.kb_ref), channel_id=1, source_target_pairs={{4,8},{8,12},{5,9},{9,13},{6,10},{10,14},{7,11},{11,15},{20,24},{2... | collective-permute-start | bytes 3145736 | tf_op jit(solution)/shard_map/ppermute | solution.py:202
  34.7 44.1 %collective-permute-start.3 = (bf16[512,1024]{1,0:T(8,128)(2,1)}, bf16[512,1024]{1,0:T(8,128)(2,1)S(1)}, u32[]{:S(2)}, u32[]{:S(2)}) collective-permute-start(bf16[512,1024]{1,0:T(8,128)(2,1)} %collective-permute-done.1.ka_ref), channel_id=1, source_target_pairs={{4,0},{8,4},{5,1},{9,5},{6,2},{10,6},{7,3},{11,7},{20,16},{24,20},... | collective-permute-start | bytes 3145736 | tf_op jit(solution)/shard_map/ppermute | solution.py:203
  50.8 35.8 %collective-permute-start.6 = (bf16[512,1024]{1,0:T(8,128)(2,1)S(1)}, bf16[512,1024]{1,0:T(8,128)(2,1)S(1)}, u32[]{:S(2)}, u32[]{:S(2)}) collective-permute-start(bf16[512,1024]{1,0:T(8,128)(2,1)S(1)} %collective-permute-done.4.vb_ref), channel_id=1, source_target_pairs={{4,8},{8,12},{5,9},{9,13},{6,10},{10,14},{7,11},{11,15},{20,24},{2... | collective-permute-start | bytes 3145736 | tf_op jit(solution)/shard_map/ppermute | solution.py:202
  56.3 43.5 %collective-permute-start.7 = (bf16[512,1024]{1,0:T(8,128)(2,1)S(1)}, bf16[512,1024]{1,0:T(8,128)(2,1)S(1)}, u32[]{:S(2)}, u32[]{:S(2)}) collective-permute-start(bf16[512,1024]{1,0:T(8,128)(2,1)S(1)} %collective-permute-done.5.va_ref), channel_id=1, source_target_pairs={{4,0},{8,4},{5,1},{9,5},{6,2},{10,6},{7,3},{11,7},{20,16},{24,20},... | collective-permute-start | bytes 3145736 | tf_op jit(solution)/shard_map/ppermute | solution.py:203
  78.8 21.0 %copy-start.3 = (s32[32]{0:T(128)S(1)}, s32[32]{0:T(128)}, u32[]{:S(2)}) copy-start(s32[32]{0:T(128)} %owners.1) | copy-start | bytes 388
  102.7 5.4 %collective-permute-start.10 = (bf16[2,1024]{1,0:T(2,128)(2,1)S(1)}, bf16[2,1024]{1,0:T(2,128)(2,1)S(1)}, u32[]{:S(2)}, u32[]{:S(2)}) collective-permute-start(bf16[2,1024]{1,0:T(2,128)(2,1)S(1)} %get-tuple-element.38), channel_id=1, source_target_pairs={{0,4},{4,8},{8,12},{12,0},{1,5},{5,9},{9,13},{13,1},{2,6},{6,10},{... | collective-permute-start | bytes 12296 | tf_op jit(solution)/shard_map/ppermute | solution.py:281
  104.2 3.9 %collective-permute-start.8 = (bf16[2,1024]{1,0:T(2,128)(2,1)S(1)}, bf16[2,1024]{1,0:T(2,128)(2,1)S(1)}, u32[]{:S(2)}, u32[]{:S(2)}) collective-permute-start(bf16[2,1024]{1,0:T(2,128)(2,1)S(1)} %get-tuple-element.36), channel_id=1, source_target_pairs={{0,12},{4,0},{8,4},{12,8},{1,13},{5,1},{9,5},{13,9},{2,14},{6,2},{... | collective-permute-start | bytes 12296 | tf_op jit(solution)/shard_map/ppermute | solution.py:281
  106.5 4.5 %collective-permute-start.9 = (bf16[2,1024]{1,0:T(2,128)(2,1)S(1)}, bf16[2,1024]{1,0:T(2,128)(2,1)S(1)}, u32[]{:S(2)}, u32[]{:S(2)}) collective-permute-start(bf16[2,1024]{1,0:T(2,128)(2,1)S(1)} %get-tuple-element.37), channel_id=1, source_target_pairs={{0,8},{4,12},{8,0},{12,4},{1,9},{5,13},{9,1},{13,5},{2,10},{6,14},... | collective-permute-start | bytes 12296 | tf_op jit(solution)/shard_map/ppermute | solution.py:281

commit v3 on v2

--- a/solution.py
+++ b/solution.py
@@ -13,7 +13,7 @@
 BLK = 256
 PIECES = 4
 SCALE = math.log2(math.e) / math.sqrt(HD)
-PARAMS = pltpu.CompilerParams(vmem_limit_bytes=40 * 1024 * 1024)
+PARAMS = pltpu.CompilerParams(vmem_limit_bytes=24 * 1024 * 1024)
 F32 = jnp.float32
 BF16 = jnp.bfloat16
 
@@ -33,25 +33,32 @@
     return jnp.concatenate((first, second), axis=0)
 
 
-def own_kernel(where, starts, q_ref, k_ref, v_ref, lk_ref, lv_ref, acc_ref, top_ref, sum_ref, lat_ref):
-    q = q_ref[...]
-    s = dot_t(q, k_ref[...]) * SCALE
-    top = jnp.max(s, axis=1, keepdims=True)
-    e = jnp.exp2(s - top)
-    acc_ref[...] = dot(e.astype(BF16), v_ref[...])
-    top_ref[...] = jnp.broadcast_to(top, top_ref.shape)
-    sum_ref[...] = jnp.broadcast_to(jnp.sum(e, axis=1, keepdims=True), sum_ref.shape)
-    s = dot_t(q, lk_ref[...]) * SCALE
-    e = jnp.exp2(s - jnp.max(s, axis=1, keepdims=True))
-    out = dot(e.astype(BF16), lv_ref[...]) / jnp.sum(e, axis=1, keepdims=True)
-    piece = out.shape[0] // PIECES
-    for p in range(PIECES):
-        split = split_of(where, starts, p)
-        lat_ref[2 * p : 2 * p + 2, :] = doc_rows(out[p * piece : (p + 1) * piece], split)
-
-
-def split_of(where, starts, p):
-    first = 2 * (PIECES * where[0] + p)
+def own_kernel(q_ref, k_ref, v_ref, acc_ref, top_ref, sum_ref):
+    for h in range(q_ref.shape[1] // HD):
+        head = slice(h * HD, (h + 1) * HD)
+        s = dot_t(q_ref[:, head], k_ref[:, head]) * SCALE
+        top = jnp.max(s, axis=1, keepdims=True)
+        e = jnp.exp2(s - top)
+        acc = dot(e.astype(BF16), v_ref[:, head])
+        acc_ref[:, head] = acc
+        top_ref[:, head] = jnp.broadcast_to(top, acc.shape)
+        sum_ref[:, head] = jnp.broadcast_to(jnp.sum(e, axis=1, keepdims=True), acc.shape)
+
+
+def latent_kernel(where, starts, q_ref, lk_ref, lv_ref, lat_ref):
+    for h in range(q_ref.shape[1] // HD):
+        head = slice(h * HD, (h + 1) * HD)
+        s = dot_t(q_ref[:, head], lk_ref[:, head]) * SCALE
+        e = jnp.exp2(s - jnp.max(s, axis=1, keepdims=True))
+        out = dot(e.astype(BF16), lv_ref[:, head]) / jnp.sum(e, axis=1, keepdims=True)
+        piece = out.shape[0] // PIECES
+        for p in range(PIECES):
+            split = split_of(where, starts, p)
+            lat_ref[2 * p : 2 * p + 2, head] = doc_rows(out[p * piece : (p + 1) * piece], split)
+
+
+def split_of(where, starts, p, shard=None):
+    first = 2 * (PIECES * (where[0] if shard is None else shard) + p)
     return starts[first + 1] - starts[first]
 
 
@@ -164,6 +171,99 @@
             outs[r][...] = chosen.astype(BF16)
 
 
+def weigh_kernel(block, shards, where, pattern, starts, q_ref, nb_ref, na_ref, fb_ref, fa_ref, *refs):
+    acc_in, top_in, sum_in, acc_ref, wb_ref, wa_ref, wf_ref, sums_ref = refs
+    behind = where[0] >= 2
+    far_live = [slot_live(where, pattern, shards, 1, side, block) for side in range(2)]
+    live = [slot_live(where, pattern, shards, 0, side, block) for side in range(2)]
+    live.append((behind & far_live[0]) | (jnp.logical_not(behind) & far_live[1]))
+    pieces = sums_ref.shape[0] // 2
+    piece = BLK // pieces
+    for h in range(q_ref.shape[1] // HD):
+        head = slice(h * HD, (h + 1) * HD)
+        slots = slice(h * BLK, (h + 1) * BLK)
+        q = q_ref[:, head]
+        keys = [nb_ref[:, head], na_ref[:, head], jnp.where(behind, fb_ref[:, head], fa_ref[:, head])]
+        scores = [live_scores(on, q, k) for on, k in zip(live, keys)]
+        old = top_in[:, h * HD : h * HD + 1]
+        top = jnp.max(jnp.maximum(jnp.maximum(scores[0], scores[1]), scores[2]), axis=1, keepdims=True)
+        top = jnp.maximum(top, old)
+        shrink = jnp.exp2(old - top)
+        exps = [jnp.exp2(s - top) for s in scores]
+        total = sum_in[:, h * HD : h * HD + 1] * shrink
+        total = total + jnp.sum(exps[0] + exps[1] + exps[2], axis=1, keepdims=True)
+        inverse = 1.0 / total
+        acc_ref[:, head] = acc_in[:, head] * (shrink * inverse)
+        wb_ref[:, slots] = (exps[0] * inverse).astype(BF16)
+        wa_ref[:, slots] = (exps[1] * inverse).astype(BF16)
+        far = exps[2] * inverse
+        wf_ref[:, slots] = far.astype(BF16)
+        for p in range(pieces):
+            split = split_of(where, starts, block * pieces + p)
+            sums_ref[2 * p : 2 * p + 2, slots] = doc_rows(far[p * piece : (p + 1) * piece], split)
+
+
+def mix_kernel(block, where, starts, acc_in, wb_ref, wa_ref, vb_ref, va_ref, v_ref, sums_ref, lat_ref, *refs):
+    acc_ref, mean_ref, part_ref = refs
+    pieces = mean_ref.shape[0] // 2
+    piece = BLK // pieces
+    partner = lax.rem(where[0] + 2, 4)
+    side = lax.broadcasted_iota(jnp.int32, (2, HD), 0)
+
+    def counts(split):
+        return jnp.where(side == 0, split, piece - split).astype(F32)
+
+    for h in range(acc_in.shape[1] // HD):
+        head = slice(h * HD, (h + 1) * HD)
+        slots = slice(h * BLK, (h + 1) * BLK)
+        acc = acc_in[:, head] + dot(wb_ref[:, slots], vb_ref[:, head]) + dot(wa_ref[:, slots], va_ref[:, head])
+        acc_ref[:, head] = acc
+        part = dot(sums_ref[:, slots].astype(BF16), v_ref[:, head])
+        for p in range(pieces):
+            rows = slice(2 * p, 2 * p + 2)
+            index = block * pieces + p
+            split = split_of(where, starts, index)
+            found = doc_rows(acc[p * piece : (p + 1) * piece], split)
+            mean_ref[rows, head] = (found + lat_ref[2 * index : 2 * index + 2, head]) / counts(split)
+            part_ref[rows, head] = part[2 * index : 2 * index + 2] / counts(split_of(where, starts, index, partner))
+
+
+def route_kernel(where, owners, *refs):
+    halves, out_ref = refs[:-1], refs[-1]
+    means, parts = halves[: len(halves) // 2], halves[len(halves) // 2 :]
+    pieces = means[0].shape[0] // 2
+    for target in range(out_ref.shape[0]):
+        for first, group, shard in ((0, means, where[0]), (2, parts, lax.rem(where[0] + 2, 4))):
+            chosen = jnp.zeros((2, out_ref.shape[2]), F32)
+            for p in range(PIECES):
+                row = 2 * (p % pieces)
+                mine = owners[2 * (PIECES * shard + p)] == target
+                chosen = jnp.where(mine, group[p // pieces][row : row + 2, :], chosen)
+            out_ref[target, first : first + 2, :] = chosen
+
+
+def pool_kernel(got_ref, out_ref):
+    for s in range(4):
+        out_ref[0, s] = (got_ref[s, :2, :] + got_ref[s ^ 2, 2:, :]).astype(BF16)
+
+
+def context_kernel(block, where, acc_ref, w_ref, vb_ref, va_ref, *refs):
+    out_ref, stage, sem = refs[-3:]
+    behind = where[0] >= 2
+    copies = []
+    for h in range(acc_ref.shape[1] // HD):
+        head = pl.ds(h * HD, HD)
+        v = jnp.where(behind, vb_ref[:, head], va_ref[:, head])
+        stage[:, head] = (acc_ref[:, head] + dot(w_ref[:, pl.ds(h * BLK, BLK)], v)).astype(BF16)
+        if h % 2:
+            pair = pl.ds((h - 1) * HD, 2 * HD)
+            copy = pltpu.make_async_copy(stage.at[:, pair], out_ref.at[pl.ds(block * BLK, BLK), pair], sem.at[h // 2])
+            copy.start()
+            copies.append(copy)
+    for copy in copies:
+        copy.wait()
+
+
 def spec(rows, columns=HD):
     return pl.BlockSpec((rows, columns), lambda h: (0, h))
 
@@ -178,6 +278,165 @@
 
 def shape(rows, columns, kind=F32):
     return jax.ShapeDtypeStruct((rows, columns), kind)
+
+
+def step_of(heads):
+    return 2 if heads % 2 == 0 else 1
+
+
+def own_call(queries, keys, values):
+    rows, columns = queries.shape
+    heads = columns // HD
+    wide = step_of(heads) * HD
+    return pl.pallas_call(
+        own_kernel,
+        grid=(columns // wide,),
+        in_specs=[spec(rows, wide)] * 3,
+        out_specs=[spec(rows, wide)] * 3,
+        out_shape=(shape(rows, columns),) * 3,
+        compiler_params=PARAMS,
+        cost_estimate=pl.CostEstimate(
+            flops=4 * rows * columns * rows, bytes_accessed=18 * rows * columns, transcendentals=heads * rows * rows
+        ),
+        name="own",
+    )(queries, keys, values)
+
+
+def latent_call(where, doc_starts, queries, latent_keys, latent_values):
+    rows, columns = queries.shape
+    latents = latent_keys.shape[0]
+    heads = columns // HD
+    wide = step_of(heads) * HD
+    return pl.pallas_call(
+        latent_kernel,
+        grid=(columns // wide,),
+        in_specs=smem(2) + [spec(rows, wide)] + [spec(latents, wide)] * 2,
+        out_specs=spec(2 * PIECES, wide),
+        out_shape=shape(2 * PIECES, columns),
+        compiler_params=PARAMS,
+        cost_estimate=pl.CostEstimate(
+            flops=4 * rows * columns * latents, bytes_accessed=6 * rows * columns, transcendentals=heads * rows * latents
+        ),
+        name="latent",
+    )(where, doc_starts, queries, latent_keys, latent_values)
+
+
+def four_shards(queries, keys, values, latent_keys, latent_values, pattern, doc_starts, doc_owner):
+    rows, columns = queries.shape
+    heads = columns // HD
+    step = step_of(heads)
+    wide = step * HD
+    slots = heads * BLK
+    blocks = rows // BLK
+    docs = 2 * PIECES // blocks
+    where = lax.axis_index("seq").astype(jnp.int32).reshape(1)
+    right, left = [(0, 1), (1, 2), (2, 3)], [(1, 0), (2, 1), (3, 2)]
+
+    def move(value, pairs):
+        return lax.ppermute(value, "seq", pairs)
+
+    def near(value):
+        return [move(value, right), move(value, left)]
+
+    def onward(pair):
+        return [move(pair[0], right[1:]), move(pair[1], left[:-1])]
+
+    def part(array, block):
+        return array[block * BLK : (block + 1) * BLK]
+
+    def row_spec(block, width=wide):
+        return pl.BlockSpec((BLK, width), lambda h: (block, h))
+
+    def weigh(block, near_keys, far_keys, state):
+        return pl.pallas_call(
+            functools.partial(weigh_kernel, block, 4),
+            grid=(heads // step,),
+            in_specs=smem(3) + [row_spec(block)] + [row_spec(0)] * 4 + [row_spec(block)] * 3,
+            out_specs=[row_spec(0)] + [row_spec(0, step * BLK)] * 3 + [spec(docs, step * BLK)],
+            out_shape=(shape(BLK, columns),) + (shape(BLK, slots, BF16),) * 3 + (shape(docs, slots),),
+            compiler_params=PARAMS,
+            cost_estimate=pl.CostEstimate(
+                flops=6 * BLK * columns * BLK, bytes_accessed=22 * BLK * columns, transcendentals=3 * heads * BLK * BLK
+            ),
+            name="weigh",
+        )(where, pattern, doc_starts, queries, *near_keys, *far_keys, *state)
+
+    def mix(block, acc, weights, near_vals, sums, lat):
+        return pl.pallas_call(
+            functools.partial(mix_kernel, block),
+            grid=(heads // step,),
+            in_specs=smem(2)
+            + [row_spec(0)]
+            + [row_spec(0, step * BLK)] * 2
+            + [row_spec(0)] * 2
+            + [row_spec(block), spec(2 * PIECES, step * BLK), spec(2 * PIECES, wide)],
+            out_specs=[row_spec(0)] + [spec(docs, wide)] * 2,
+            out_shape=(shape(BLK, columns),) + (shape(docs, columns),) * 2,
+            compiler_params=PARAMS,
+            cost_estimate=pl.CostEstimate(flops=5 * BLK * columns * BLK, bytes_accessed=22 * BLK * columns, transcendentals=0),
+            name="mix",
+        )(where, doc_starts, acc, *weights, *near_vals, values, sums, lat)
+
+    def finish(block, acc, weights, far_vals, context):
+        held = [] if context is None else [context]
+        return pl.pallas_call(
+            functools.partial(context_kernel, block),
+            in_specs=smem(1) + vmem(4) + [pl.BlockSpec(memory_space=pl.ANY)] * len(held),
+            out_specs=pl.BlockSpec(memory_space=pl.ANY),
+            out_shape=shape(rows, columns, BF16),
+            scratch_shapes=[pltpu.VMEM((BLK, columns), BF16), pltpu.SemaphoreType.DMA((heads // 2,))],
+            input_output_aliases={5: 0} if held else {},
+            compiler_params=PARAMS,
+            cost_estimate=pl.CostEstimate(flops=2 * BLK * columns * BLK, bytes_accessed=14 * BLK * columns, transcendentals=0),
+            name="finish",
+        )(where, acc, weights, *far_vals, *held)
+
+    near_keys = [near(part(keys, 0))]
+    lat = latent_call(where, doc_starts, queries, latent_keys, latent_values)
+    lat, late_keys = lax.optimization_barrier((lat, part(keys, 1)))
+    near_keys.append(near(late_keys))
+    state = own_call(queries, keys, values)
+    near_keys[0], state = lax.optimization_barrier((near_keys[0], state))
+    far_keys = [onward(pair) for pair in near_keys]
+    late_vals, near_keys[1] = lax.optimization_barrier(([part(values, block) for block in range(blocks)], near_keys[1]))
+    near_vals = [near(value) for value in late_vals]
+    acc, near_weights, far_weights, sums = [], [], [], []
+    for block in range(blocks):
+        out = weigh(block, near_keys[block], far_keys[block], state)
+        acc.append(out[0])
+        near_weights.append(out[1:3])
+        far_weights.append(out[3])
+        sums.append(out[4])
+    sums = move(jnp.concatenate(sums), [(s, s ^ 2) for s in range(4)])
+    far_vals = [onward(near_vals[0])]
+    means, parts = [], []
+    for block in range(blocks):
+        acc[block], mean, far_part = mix(block, acc[block], near_weights[block], near_vals[block], sums, lat)
+        means.append(mean)
+        parts.append(far_part)
+    sent = pl.pallas_call(
+        route_kernel,
+        in_specs=smem(2) + vmem(2 * blocks),
+        out_specs=pl.BlockSpec(memory_space=pltpu.VMEM),
+        out_shape=jax.ShapeDtypeStruct((4, 4, columns), F32),
+        compiler_params=PARAMS,
+        name="route",
+    )(where, doc_owner, *means, *parts)
+    sent, last_vals = lax.optimization_barrier((sent, near_vals[1]))
+    far_vals.append(onward(last_vals))
+    context = finish(0, acc[0], far_weights[0], far_vals[0], None)
+    sent, context = lax.optimization_barrier((sent, context))
+    got = lax.all_to_all(sent, "seq", split_axis=0, concat_axis=0, tiled=True)
+    pooled = pl.pallas_call(
+        pool_kernel,
+        in_specs=vmem(1),
+        out_specs=pl.BlockSpec(memory_space=pltpu.VMEM),
+        out_shape=jax.ShapeDtypeStruct((1, 4, 2, columns), BF16),
+        compiler_params=PARAMS,
+        name="pool",
+    )(got)
+    context = finish(1, acc[1], far_weights[1], far_vals[1], context)
+    return context, pooled
 
 
 def body(queries, keys, values, latent_keys, latent_values, pattern, doc_starts, doc_owner):
@@ -203,21 +462,13 @@
         ahead = lax.ppermute(near[1], "seq", [(s, s - 1) for s in range(1, shards - 1)])
         return [behind, ahead]
 
+    if shards == 4:
+        return four_shards(queries, keys, values, latent_keys, latent_values, pattern, doc_starts, doc_owner)
     near_keys = both_ways(keys, 1)
     near_vals = both_ways(values, 1)
     state_shapes = (shape(rows, columns),) * 3
-    *state, lat = pl.pallas_call(
-        own_kernel,
-        grid=(heads,),
-        in_specs=smem(2) + [spec(rows)] * 3 + [spec(latent_keys.shape[0])] * 2,
-        out_specs=[spec(rows)] * 3 + [spec(2 * PIECES)],
-        out_shape=state_shapes + (shape(2 * PIECES, columns),),
-        compiler_params=PARAMS,
-        cost_estimate=pl.CostEstimate(
-            flops=8 * rows * columns * rows, bytes_accessed=12 * rows * columns * 2, transcendentals=2 * heads * rows * rows
-        ),
-        name="own",
-    )(where, doc_starts, queries, keys, values, latent_keys, latent_values)
+    lat = latent_call(where, doc_starts, queries, latent_keys, latent_values)
+    state = own_call(queries, keys, values)
     near_keys, state = lax.optimization_barrier((near_keys, state))
 
     for level in levels[:-1]:

time: 112 us -> 111 us (level)
  waiting for transfers between devices: 50.4 us -> 22.1 us
  starting transfers between devices: 20 us -> 45 us
  Pallas kernels: 33 us -> 37.4 us
  local copies, waits for them, and re-layouts: 6.78 us -> 4.87 us
    ppermute x11 -> x17, waiting for transfers between devices: 50.4 us -> 20.6 us  [move(): return lax.ppermute(value, 'seq', pairs)]
    ppermute x11 -> x17, starting transfers between devices: 20 us -> 40.3 us  [move(): return lax.ppermute(value, 'seq', pairs)]
    all_to_all x0 -> x1, starting transfers between devices: none -> 4.73 us  [four_shards(): got = lax.all_to_all(sent, 'seq', split_axis=0, concat_axis=0, tiled=True)]
    pallas_call x4 -> x10, Pallas kernels: 33 us -> 37.4 us  [the longest x2 16.9 us: weigh(): pl.pallas_call(functools.partial(weigh_kernel, block, 4), grid=(heads //...]
    unnamed x16 -> x18, local copies, waits for them, and re-layouts: 6.78 us -> 2.48 us
    slice x0 -> x2, local copies, waits for them, and re-layouts: none -> 2.39 us  [part(): return array[block * BLK:(block + 1) * BLK]]
    all_to_all x0 -> x1, waiting for transfers between devices: none -> 1.48 us  [four_shards(): got = lax.all_to_all(sent, 'seq', split_axis=0, concat_axis=0, tiled=True)]
  transfers between devices with their start and end apart: 11 -> 18, of which waited for: 7 -> 6; matrix products, arithmetic and copies ran while one was open for 0% -> 0% of each run, Pallas kernels for 27% -> 33%
where the time goes in v3:
time: 111 us; the launch traced here: 110 us
  starting transfers between devices  45 us (41%)
  Pallas kernels  37.4 us (34%)
  waiting for transfers between devices  22.1 us (20%)
  local copies, waits for them, and re-layouts  4.87 us (4%)
    ppermute x17, starting transfers between devices, move(): return lax.ppermute(value, 'seq', pairs)  40.3 us
    ppermute x17, waiting for transfers between devices, move(): return lax.ppermute(value, 'seq', pairs)  20.6 us
    pallas_call x2, Pallas kernels, weigh(): pl.pallas_call(functools.partial(weigh_kernel, block, 4), grid=(heads //...  16.9 us
    pallas_call x2, Pallas kernels, mix(): pl.pallas_call(functools.partial(mix_kernel, block), grid=(heads // step,...  5.62 us
    pallas_call x1, Pallas kernels, latent_call(): pl.pallas_call(latent_kernel, grid=(columns // wide,), in_specs=smem(2) +...  5.38 us
    pallas_call x1, Pallas kernels, own_call(): pl.pallas_call(own_kernel, grid=(columns // wide,), in_specs=[spec(rows,...  5.27 us
    all_to_all x1, starting transfers between devices, four_shards(): got = lax.all_to_all(sent, 'seq', split_axis=0, concat_axis=0, tiled=True)  4.73 us
    unnamed x18, local copies, waits for them, and re-layouts  2.48 us
  transfers between devices with their start and end apart: 18, of which 6 were waited for; matrix products, arithmetic and copies ran while one was open for 0% of the time, Pallas kernels for 33%

profile of v3, /device:TPU:0, one launch (start us, length us, event | category | flops | bytes accessed | tf_op | source)
XLA Modules:
  0.0 110.4 jit_solution(10032222061952403281)
XLA Ops:
  0.6 2.3 %fusion = (bf16[256,1024]{1,0:T(8,128)(2,1)}, bf16[256,1024]{1,0:T(8,128)(2,1)}) fusion(bf16[512,1024]{1,0:T(8,128)(2,1)} %k_ref.1), kind=kLoop, calls=%fused_computation.1 | loop fusion | bytes 2097152 | tf_op jit(solution)/shard_map/slice | solution.py:345
  3.0 5.9 %collective-permute-start.4 = (bf16[256,1024]{1,0:T(8,128)(2,1)}, bf16[256,1024]{1,0:T(8,128)(2,1)}, u32[]{:S(2)}, u32[]{:S(2)}) collective-permute-start(bf16[256,1024]{1,0:T(8,128)(2,1)} %get-tuple-element.72), channel_id=1, source_target_pairs={{0,4},{4,8},{8,12},{1,5},{5,9},{9,13},{2,6},{6,10},{10,14},{3,7},{... | collective-permute-start | bytes 1572872 | tf_op jit(solution)/shard_map/ppermute | solution.py:336
  12.6 5.4 %latent.1.lat_ref = f32[8,1024]{1,0:T(8,128)S(1)} custom-call(s32[1]{0:T(128)} %bitcast.where, s32[32]{0:T(128)S(1)} %copy-done.3, bf16[512,1024]{1,0:T(8,128)(2,1)S(1)} %copy-done.1, bf16[512,1024]{1,0:T(8,128)(2,1)S(1)} %copy-done.6, bf16[512,1024]{1,0:T(8,128)(2,1)S(1)} %copy-done.7), custom_call_target="tpu_custom_call" | custom-call | flops 1073741824 | bytes 3145728 | tf_op jit(solution)/shard_map/latent/pallas_call | solution.py:310
  18.0 4.6 %collective-permute-start = (bf16[256,1024]{1,0:T(8,128)(2,1)S(1)}, bf16[256,1024]{1,0:T(8,128)(2,1)S(1)}, u32[]{:S(2)}, u32[]{:S(2)}) collective-permute-start(bf16[256,1024]{1,0:T(8,128)(2,1)S(1)} %copy-done.8), channel_id=1, source_target_pairs={{0,4},{4,8},{8,12},{1,5},{5,9},{9,13},{2,6},{6,10},{10,14},{3,7},{... | collective-permute-start | bytes 1572872 | tf_op jit(solution)/shard_map/ppermute | solution.py:336
  22.6 1.3 %collective-permute-start.1 = (bf16[256,1024]{1,0:T(8,128)(2,1)S(1)}, bf16[256,1024]{1,0:T(8,128)(2,1)S(1)}, u32[]{:S(2)}, u32[]{:S(2)}) collective-permute-start(bf16[256,1024]{1,0:T(8,128)(2,1)S(1)} %copy-done.8), channel_id=1, source_target_pairs={{4,0},{8,4},{12,8},{5,1},{9,5},{13,9},{6,2},{10,6},{14,10},{7,3},{... | collective-permute-start | bytes 1572872 | tf_op jit(solution)/shard_map/ppermute | solution.py:336
  23.9 5.3 %own.1 = (f32[512,1024]{1,0:T(8,128)S(1)}, f32[512,1024]{1,0:T(8,128)S(1)}, f32[512,1024]{1,0:T(8,128)S(1)}) custom-call(bf16[512,1024]{1,0:T(8,128)(2,1)S(1)} %copy-done.1, bf16[512,1024]{1,0:T(8,128)(2,1)S(1)} %copy-done.2, bf16[512,1024]{1,0:T(8,128)(2,1)S(1)} %copy-done), custom_call_target="tpu_custom_call" | custom-call | flops 1073741824 | bytes 9437184 | tf_op jit(solution)/shard_map/own/pallas_call | solution.py:291
  29.9 1.3 %collective-permute-start.9 = (bf16[256,1024]{1,0:T(8,128)(2,1)}, bf16[256,1024]{1,0:T(8,128)(2,1)S(1)}, u32[]{:S(2)}, u32[]{:S(2)}) collective-permute-start(bf16[256,1024]{1,0:T(8,128)(2,1)} %collective-permute-done.5.na_ref), channel_id=1, source_target_pairs={{4,0},{8,4},{5,1},{9,5},{6,2},{10,6},{7,3},{11,7},{20,16},{24,20},... | collective-permute-start | bytes 1572872 | tf_op jit(solution)/shard_map/ppermute | solution.py:336
  31.2 1.9 %collective-permute-done.nb_ref = bf16[256,1024]{1,0:T(8,128)(2,1)S(1)} collective-permute-done((bf16[256,1024]{1,0:T(8,128)(2,1)S(1)}, bf16[256,1024]{1,0:T(8,128)(2,1)S(1)}, u32[]{:S(2)}, u32[]{:S(2)}) %collective-permute-start) | collective-permute-done | bytes 524320 | tf_op jit(solution)/shard_map/ppermute | solution.py:336
  33.9 4.1 %collective-permute-done.1.na_ref = bf16[256,1024]{1,0:T(8,128)(2,1)S(1)} collective-permute-done((bf16[256,1024]{1,0:T(8,128)(2,1)S(1)}, bf16[256,1024]{1,0:T(8,128)(2,1)S(1)}, u32[]{:S(2)}, u32[]{:S(2)}) %collective-permute-start.1) | collective-permute-done | bytes 524320 | tf_op jit(solution)/shard_map/ppermute | solution.py:336
  39.4 5.4 %collective-permute-start.11 = (bf16[256,1024]{1,0:T(8,128)(2,1)S(1)}, bf16[256,1024]{1,0:T(8,128)(2,1)S(1)}, u32[]{:S(2)}, u32[]{:S(2)}) collective-permute-start(bf16[256,1024]{1,0:T(8,128)(2,1)S(1)} %get-tuple-element.60), channel_id=1, source_target_pairs={{0,4},{4,8},{8,12},{1,5},{5,9},{9,13},{2,6},{6,10},{10,14},{3,7},{... | collective-permute-start | bytes 1572872 | tf_op jit(solution)/shard_map/ppermute | solution.py:336
  44.8 1.3 %collective-permute-start.12 = (bf16[256,1024]{1,0:T(8,128)(2,1)S(1)}, bf16[256,1024]{1,0:T(8,128)(2,1)S(1)}, u32[]{:S(2)}, u32[]{:S(2)}) collective-permute-start(bf16[256,1024]{1,0:T(8,128)(2,1)S(1)} %get-tuple-element.60), channel_id=1, source_target_pairs={{4,0},{8,4},{12,8},{5,1},{9,5},{13,9},{6,2},{10,6},{14,10},{7,3},{... | collective-permute-start | bytes 1572872 | tf_op jit(solution)/shard_map/ppermute | solution.py:336
  46.1 3.8 %collective-permute-done.9.fa_ref = bf16[256,1024]{1,0:T(8,128)(2,1)S(1)} collective-permute-done((bf16[256,1024]{1,0:T(8,128)(2,1)}, bf16[256,1024]{1,0:T(8,128)(2,1)S(1)}, u32[]{:S(2)}, u32[]{:S(2)}) %collective-permute-start.9) | collective-permute-done | bytes 524320 | tf_op jit(solution)/shard_map/ppermute | solution.py:336
  49.8 4.7 %collective-permute-start.6 = (bf16[256,1024]{1,0:T(8,128)(2,1)S(1)}, bf16[256,1024]{1,0:T(8,128)(2,1)}, u32[]{:S(2)}, u32[]{:S(2)}) collective-permute-start(bf16[256,1024]{1,0:T(8,128)(2,1)S(1)} %get-tuple-element.49), channel_id=1, source_target_pairs={{0,4},{4,8},{8,12},{1,5},{5,9},{9,13},{2,6},{6,10},{10,14},{3,7},{... | collective-permute-start | bytes 1572872 | tf_op jit(solution)/shard_map/ppermute | solution.py:336
  55.9 8.6 %weigh.3 = (f32[256,1024]{1,0:T(8,128)S(1)}, bf16[256,2048]{1,0:T(8,128)(2,1)S(1)}, bf16[256,2048]{1,0:T(8,128)(2,1)S(1)}, bf16[256,2048]{1,0:T(8,128)(2,1)S(1)}, f32[4,2048]{1,0:T(4,128)S(1)}) custom-call(s32[1]{0:T(128)} %bitcast.where, s32[2,8]{1,0:T(2,128)S(1)} %copy-done.4, s32[32]{0:T(128)S(1)} %copy-done.3, bf16[512,1024]{1,0:T(8,128)(2,1)S(1)} %copy-done.1, ...), custom_call_target="tpu_custom_call" | custom-call | flops 402653184 | bytes 5767168 | tf_op jit(solution)/shard_map/weigh/pallas_call | solution.py:351
  64.5 8.3 %weigh.2 = (f32[256,1024]{1,0:T(8,128)S(1)}, bf16[256,2048]{1,0:T(8,128)(2,1)S(1)}, bf16[256,2048]{1,0:T(8,128)(2,1)S(1)}, bf16[256,2048]{1,0:T(8,128)(2,1)S(1)}, f32[4,2048]{1,0:T(4,128)S(1)}) custom-call(s32[1]{0:T(128)} %bitcast.where, s32[2,8]{1,0:T(2,128)S(1)} %copy-done.4, s32[32]{0:T(128)S(1)} %copy-done.3, bf16[512,1024]{1,0:T(8,128)(2,1)S(1)} %copy-done.1, ...), custom_call_target="tpu_custom_call" | custom-call | flops 402653184 | bytes 5767168 | tf_op jit(solution)/shard_map/weigh/pallas_call | solution.py:351
  72.8 6.7 %collective-permute-start.10 = (f32[8,2048]{1,0:T(8,128)S(1)}, f32[8,2048]{1,0:T(8,128)S(1)}, u32[]{:S(2)}, u32[]{:S(2)}) collective-permute-start(f32[8,2048]{1,0:T(8,128)S(1)} %pad_maximum_fusion), channel_id=1, source_target_pairs={{0,8},{4,12},{8,0},{12,4},{1,9},{5,13},{9,1},{13,5},{2,10},{6,14},... | collective-permute-start | bytes 196616 | tf_op jit(solution)/shard_map/ppermute | solution.py:336
  80.3 1.3 %collective-permute-start.16 = (bf16[256,1024]{1,0:T(8,128)(2,1)S(1)}, bf16[256,1024]{1,0:T(8,128)(2,1)S(1)}, u32[]{:S(2)}, u32[]{:S(2)}) collective-permute-start(bf16[256,1024]{1,0:T(8,128)(2,1)S(1)} %collective-permute-done.12.va_ref), channel_id=1, source_target_pairs={{4,0},{8,4},{5,1},{9,5},{6,2},{10,6},{7,3},{11,7},{20,16},{24,20},... | collective-permute-start | bytes 1572872 | tf_op jit(solution)/shard_map/ppermute | solution.py:336
  81.6 6.2 %collective-permute-done.10.sums_ref = f32[8,2048]{1,0:T(8,128)S(1)} collective-permute-done((f32[8,2048]{1,0:T(8,128)S(1)}, f32[8,2048]{1,0:T(8,128)S(1)}, u32[]{:S(2)}, u32[]{:S(2)}) %collective-permute-start.10) | collective-permute-done | bytes 65568 | tf_op jit(solution)/shard_map/ppermute | solution.py:336
  87.8 2.3 %mix.3 = (f32[256,1024]{1,0:T(8,128)S(1)}, f32[4,1024]{1,0:T(4,128)S(1)}, f32[4,1024]{1,0:T(4,128)S(1)}) custom-call(s32[1]{0:T(128)} %bitcast.where, s32[32]{0:T(128)S(1)} %copy-done.3, f32[256,1024]{1,0:T(8,128)S(1)} %get-tuple-element.57.acc_in, bf16[256,2048]{1,0:T(8,128)(2,1)S(1)} %get-tuple-element.58.wb_ref, ...), custom_call_target="tpu_custom_call" | custom-call | flops 335544320 | bytes 5767168 | tf_op jit(solution)/shard_map/mix/pallas_call | solution.py:365
  90.2 3.3 %mix.2 = (f32[256,1024]{1,0:T(8,128)S(1)}, f32[4,1024]{1,0:T(4,128)S(1)}, f32[4,1024]{1,0:T(4,128)S(1)}) custom-call(s32[1]{0:T(128)} %bitcast.where, s32[32]{0:T(128)S(1)} %copy-done.3, f32[256,1024]{1,0:T(8,128)S(1)} %get-tuple-element.46.acc_in, bf16[256,2048]{1,0:T(8,128)(2,1)S(1)} %get-tuple-element.47.wb_ref, ...), custom_call_target="tpu_custom_call" | custom-call | flops 335544320 | bytes 5767168 | tf_op jit(solution)/shard_map/mix/pallas_call | solution.py:365
  95.4 1.3 %collective-permute-start.14 = (bf16[256,1024]{1,0:T(8,128)(2,1)}, bf16[256,1024]{1,0:T(8,128)(2,1)S(1)}, u32[]{:S(2)}, u32[]{:S(2)}) collective-permute-start(bf16[256,1024]{1,0:T(8,128)(2,1)} %collective-permute-done.7.va_ref), channel_id=1, source_target_pairs={{4,0},{8,4},{5,1},{9,5},{6,2},{10,6},{7,3},{11,7},{20,16},{24,20},... | collective-permute-start | bytes 1572872 | tf_op jit(solution)/shard_map/ppermute | solution.py:336
  97.9 4.7 %all-to-all-start = ((f32[4,4,1024]{2,1,0:T(4,128)}), f32[4,4,1024]{2,1,0:T(4,128)S(1)}, u32[]{:S(2)}, u32[]{:S(2)}) async-start(f32[4,4,1024]{2,1,0:T(4,128)} %route.1), calls=%async_computation | async-start | bytes 131072 | tf_op jit(solution)/shard_map/all_to_all | solution.py:429
  102.6 4.5 %collective-permute-done.14.va_ref = bf16[256,1024]{1,0:T(8,128)(2,1)S(1)} collective-permute-done((bf16[256,1024]{1,0:T(8,128)(2,1)}, bf16[256,1024]{1,0:T(8,128)(2,1)S(1)}, u32[]{:S(2)}, u32[]{:S(2)}) %collective-permute-start.14) | collective-permute-done | bytes 524320 | tf_op jit(solution)/shard_map/ppermute | solution.py:336
  108.3 1.5 %all-to-all-done.got_ref = f32[4,4,1024]{2,1,0:T(4,128)S(1)} async-done(((f32[4,4,1024]{2,1,0:T(4,128)}), f32[4,4,1024]{2,1,0:T(4,128)S(1)}, u32[]{:S(2)}, u32[]{:S(2)}) %all-to-all-start) | async-done | bytes 65568 | tf_op jit(solution)/shard_map/all_to_all | solution.py:429
  (43 shorter events, 13.3 us)
Async XLA Ops:
  0.6 9.5 %copy-start.1 = (bf16[512,1024]{1,0:T(8,128)(2,1)S(1)}, bf16[512,1024]{1,0:T(8,128)(2,1)}, u32[]{:S(2)}) copy-start(bf16[512,1024]{1,0:T(8,128)(2,1)} %q_ref.7) | copy-start | bytes 3145732
  0.6 9.5 %copy-start.3 = (s32[32]{0:T(128)S(1)}, s32[32]{0:T(128)}, u32[]{:S(2)}) copy-start(s32[32]{0:T(128)} %starts.9) | copy-start | bytes 388
  3.0 20.9 %copy-start = (bf16[512,1024]{1,0:T(8,128)(2,1)S(1)}, bf16[512,1024]{1,0:T(8,128)(2,1)}, u32[]{:S(2)}) copy-start(bf16[512,1024]{1,0:T(8,128)(2,1)} %v_ref.5) | copy-start | bytes 3145732
  3.0 20.9 %copy-start.2 = (bf16[512,1024]{1,0:T(8,128)(2,1)S(1)}, bf16[512,1024]{1,0:T(8,128)(2,1)}, u32[]{:S(2)}) copy-start(bf16[512,1024]{1,0:T(8,128)(2,1)} %k_ref.1) | copy-start | bytes 3145732
  3.0 26.2 %collective-permute-start.4 = (bf16[256,1024]{1,0:T(8,128)(2,1)}, bf16[256,1024]{1,0:T(8,128)(2,1)}, u32[]{:S(2)}, u32[]{:S(2)}) collective-permute-start(bf16[256,1024]{1,0:T(8,128)(2,1)} %get-tuple-element.72), channel_id=1, source_target_pairs={{0,4},{4,8},{8,12},{1,5},{5,9},{9,13},{2,6},{6,10},{10,14},{3,7},{... | collective-permute-start | bytes 1572872 | tf_op jit(solution)/shard_map/ppermute | solution.py:336
  8.8 20.4 %collective-permute-start.5 = (bf16[256,1024]{1,0:T(8,128)(2,1)}, bf16[256,1024]{1,0:T(8,128)(2,1)}, u32[]{:S(2)}, u32[]{:S(2)}) collective-permute-start(bf16[256,1024]{1,0:T(8,128)(2,1)} %get-tuple-element.72), channel_id=1, source_target_pairs={{4,0},{8,4},{12,8},{5,1},{9,5},{13,9},{6,2},{10,6},{14,10},{7,3},{... | collective-permute-start | bytes 1572872 | tf_op jit(solution)/shard_map/ppermute | solution.py:336
  12.6 5.4 %copy-start.8 = (bf16[256,1024]{1,0:T(8,128)(2,1)S(1)}, bf16[256,1024]{1,0:T(8,128)(2,1)}, u32[]{:S(2)}) copy-start(bf16[256,1024]{1,0:T(8,128)(2,1)} %get-tuple-element.37) | copy-start | bytes 1572868
  18.0 37.8 %copy-start.4 = (s32[2,8]{1,0:T(2,128)S(1)}, s32[2,8]{1,0:T(2,128)}, u32[]{:S(2)}) copy-start(s32[2,8]{1,0:T(2,128)} %pattern.3) | copy-start | bytes 196
  18.0 15.2 %collective-permute-start = (bf16[256,1024]{1,0:T(8,128)(2,1)S(1)}, bf16[256,1024]{1,0:T(8,128)(2,1)S(1)}, u32[]{:S(2)}, u32[]{:S(2)}) collective-permute-start(bf16[256,1024]{1,0:T(8,128)(2,1)S(1)} %copy-done.8), channel_id=1, source_target_pairs={{0,4},{4,8},{8,12},{1,5},{5,9},{9,13},{2,6},{6,10},{10,14},{3,7},{... | collective-permute-start | bytes 1572872 | tf_op jit(solution)/shard_map/ppermute | solution.py:336
  22.6 15.4 %collective-permute-start.1 = (bf16[256,1024]{1,0:T(8,128)(2,1)S(1)}, bf16[256,1024]{1,0:T(8,128)(2,1)S(1)}, u32[]{:S(2)}, u32[]{:S(2)}) collective-permute-start(bf16[256,1024]{1,0:T(8,128)(2,1)S(1)} %copy-done.8), channel_id=1, source_target_pairs={{4,0},{8,4},{12,8},{5,1},{9,5},{13,9},{6,2},{10,6},{14,10},{7,3},{... | collective-permute-start | bytes 1572872 | tf_op jit(solution)/shard_map/ppermute | solution.py:336
  29.2 15.6 %collective-permute-start.8 = (bf16[256,1024]{1,0:T(8,128)(2,1)}, bf16[256,1024]{1,0:T(8,128)(2,1)S(1)}, u32[]{:S(2)}, u32[]{:S(2)}) collective-permute-start(bf16[256,1024]{1,0:T(8,128)(2,1)} %collective-permute-done.4.nb_ref), channel_id=1, source_target_pairs={{4,8},{8,12},{5,9},{9,13},{6,10},{10,14},{7,11},{11,15},{20,24},{2... | collective-permute-start | bytes 1572872 | tf_op jit(solution)/shard_map/ppermute | solution.py:336
  29.9 19.9 %collective-permute-start.9 = (bf16[256,1024]{1,0:T(8,128)(2,1)}, bf16[256,1024]{1,0:T(8,128)(2,1)S(1)}, u32[]{:S(2)}, u32[]{:S(2)}) collective-permute-start(bf16[256,1024]{1,0:T(8,128)(2,1)} %collective-permute-done.5.na_ref), channel_id=1, source_target_pairs={{4,0},{8,4},{5,1},{9,5},{6,2},{10,6},{7,3},{11,7},{20,16},{24,20},... | collective-permute-start | bytes 1572872 | tf_op jit(solution)/shard_map/ppermute | solution.py:336
  33.2 21.4 %collective-permute-start.2 = (bf16[256,1024]{1,0:T(8,128)(2,1)S(1)}, bf16[256,1024]{1,0:T(8,128)(2,1)S(1)}, u32[]{:S(2)}, u32[]{:S(2)}) collective-permute-start(bf16[256,1024]{1,0:T(8,128)(2,1)S(1)} %collective-permute-done.nb_ref), channel_id=1, source_target_pairs={{4,8},{8,12},{5,9},{9,13},{6,10},{10,14},{7,11},{11,15},{20,24},{2... | collective-permute-start | bytes 1572872 | tf_op jit(solution)/shard_map/ppermute | solution.py:336
  38.0 26.5 %collective-permute-start.3 = (bf16[256,1024]{1,0:T(8,128)(2,1)S(1)}, bf16[256,1024]{1,0:T(8,128)(2,1)S(1)}, u32[]{:S(2)}, u32[]{:S(2)}) collective-permute-start(bf16[256,1024]{1,0:T(8,128)(2,1)S(1)} %collective-permute-done.1.na_ref), channel_id=1, source_target_pairs={{4,0},{8,4},{5,1},{9,5},{6,2},{10,6},{7,3},{11,7},{20,16},{24,20},... | collective-permute-start | bytes 1572872 | tf_op jit(solution)/shard_map/ppermute | solution.py:336
  39.4 40.2 %collective-permute-start.11 = (bf16[256,1024]{1,0:T(8,128)(2,1)S(1)}, bf16[256,1024]{1,0:T(8,128)(2,1)S(1)}, u32[]{:S(2)}, u32[]{:S(2)}) collective-permute-start(bf16[256,1024]{1,0:T(8,128)(2,1)S(1)} %get-tuple-element.60), channel_id=1, source_target_pairs={{0,4},{4,8},{8,12},{1,5},{5,9},{9,13},{2,6},{6,10},{10,14},{3,7},{... | collective-permute-start | bytes 1572872 | tf_op jit(solution)/shard_map/ppermute | solution.py:336
  44.8 35.5 %collective-permute-start.12 = (bf16[256,1024]{1,0:T(8,128)(2,1)S(1)}, bf16[256,1024]{1,0:T(8,128)(2,1)S(1)}, u32[]{:S(2)}, u32[]{:S(2)}) collective-permute-start(bf16[256,1024]{1,0:T(8,128)(2,1)S(1)} %get-tuple-element.60), channel_id=1, source_target_pairs={{4,0},{8,4},{12,8},{5,1},{9,5},{13,9},{6,2},{10,6},{14,10},{7,3},{... | collective-permute-start | bytes 1572872 | tf_op jit(solution)/shard_map/ppermute | solution.py:336
  49.8 40.3 %collective-permute-start.6 = (bf16[256,1024]{1,0:T(8,128)(2,1)S(1)}, bf16[256,1024]{1,0:T(8,128)(2,1)}, u32[]{:S(2)}, u32[]{:S(2)}) collective-permute-start(bf16[256,1024]{1,0:T(8,128)(2,1)S(1)} %get-tuple-element.49), channel_id=1, source_target_pairs={{0,4},{4,8},{8,12},{1,5},{5,9},{9,13},{2,6},{6,10},{10,14},{3,7},{... | collective-permute-start | bytes 1572872 | tf_op jit(solution)/shard_map/ppermute | solution.py:336
  54.6 35.6 %collective-permute-start.7 = (bf16[256,1024]{1,0:T(8,128)(2,1)S(1)}, bf16[256,1024]{1,0:T(8,128)(2,1)}, u32[]{:S(2)}, u32[]{:S(2)}) collective-permute-start(bf16[256,1024]{1,0:T(8,128)(2,1)S(1)} %get-tuple-element.49), channel_id=1, source_target_pairs={{4,0},{8,4},{12,8},{5,1},{9,5},{13,9},{6,2},{10,6},{14,10},{7,3},{... | collective-permute-start | bytes 1572872 | tf_op jit(solution)/shard_map/ppermute | solution.py:336
  72.8 15.0 %collective-permute-start.10 = (f32[8,2048]{1,0:T(8,128)S(1)}, f32[8,2048]{1,0:T(8,128)S(1)}, u32[]{:S(2)}, u32[]{:S(2)}) collective-permute-start(f32[8,2048]{1,0:T(8,128)S(1)} %pad_maximum_fusion), channel_id=1, source_target_pairs={{0,8},{4,12},{8,0},{12,4},{1,9},{5,13},{9,1},{13,5},{2,10},{6,14},... | collective-permute-start | bytes 196616 | tf_op jit(solution)/shard_map/ppermute | solution.py:336
  79.6 17.1 %collective-permute-start.15 = (bf16[256,1024]{1,0:T(8,128)(2,1)S(1)}, bf16[256,1024]{1,0:T(8,128)(2,1)S(1)}, u32[]{:S(2)}, u32[]{:S(2)}) collective-permute-start(bf16[256,1024]{1,0:T(8,128)(2,1)S(1)} %collective-permute-done.11.vb_ref), channel_id=1, source_target_pairs={{4,8},{8,12},{5,9},{9,13},{6,10},{10,14},{7,11},{11,15},{20,24},{2... | collective-permute-start | bytes 1572872 | tf_op jit(solution)/shard_map/ppermute | solution.py:336
  80.3 16.4 %collective-permute-start.16 = (bf16[256,1024]{1,0:T(8,128)(2,1)S(1)}, bf16[256,1024]{1,0:T(8,128)(2,1)S(1)}, u32[]{:S(2)}, u32[]{:S(2)}) collective-permute-start(bf16[256,1024]{1,0:T(8,128)(2,1)S(1)} %collective-permute-done.12.va_ref), channel_id=1, source_target_pairs={{4,0},{8,4},{5,1},{9,5},{6,2},{10,6},{7,3},{11,7},{20,16},{24,20},... | collective-permute-start | bytes 1572872 | tf_op jit(solution)/shard_map/ppermute | solution.py:336
  94.7 7.9 %collective-permute-start.13 = (bf16[256,1024]{1,0:T(8,128)(2,1)}, bf16[256,1024]{1,0:T(8,128)(2,1)S(1)}, u32[]{:S(2)}, u32[]{:S(2)}) collective-permute-start(bf16[256,1024]{1,0:T(8,128)(2,1)} %collective-permute-done.6.vb_ref), channel_id=1, source_target_pairs={{4,8},{8,12},{5,9},{9,13},{6,10},{10,14},{7,11},{11,15},{20,24},{2... | collective-permute-start | bytes 1572872 | tf_op jit(solution)/shard_map/ppermute | solution.py:336
  95.4 11.7 %collective-permute-start.14 = (bf16[256,1024]{1,0:T(8,128)(2,1)}, bf16[256,1024]{1,0:T(8,128)(2,1)S(1)}, u32[]{:S(2)}, u32[]{:S(2)}) collective-permute-start(bf16[256,1024]{1,0:T(8,128)(2,1)} %collective-permute-done.7.va_ref), channel_id=1, source_target_pairs={{4,0},{8,4},{5,1},{9,5},{6,2},{10,6},{7,3},{11,7},{20,16},{24,20},... | collective-permute-start | bytes 1572872 | tf_op jit(solution)/shard_map/ppermute | solution.py:336
  97.9 11.9 %all-to-all-start = ((f32[4,4,1024]{2,1,0:T(4,128)}), f32[4,4,1024]{2,1,0:T(4,128)S(1)}, u32[]{:S(2)}, u32[]{:S(2)}) async-start(f32[4,4,1024]{2,1,0:T(4,128)} %route.1), calls=%async_computation | async-start | bytes 131072 | tf_op jit(solution)/shard_map/all_to_all | solution.py:429
  (3 other events, 5.8 us)

commit v4 on v3

--- a/solution.py
+++ b/solution.py
@@ -177,74 +177,92 @@
     far_live = [slot_live(where, pattern, shards, 1, side, block) for side in range(2)]
     live = [slot_live(where, pattern, shards, 0, side, block) for side in range(2)]
     live.append((behind & far_live[0]) | (jnp.logical_not(behind) & far_live[1]))
+    bias = [jnp.where(on, 0.0, -jnp.inf) for on in live]
     pieces = sums_ref.shape[0] // 2
     piece = BLK // pieces
+    place = lax.broadcasted_iota(jnp.int32, (piece, HD), 0)
+    firsts = [place < split_of(where, starts, block * pieces + p) for p in range(pieces)]
+    lanes = [slice(i * HD, (i + 1) * HD) for i in range(BLK // HD)]
     for h in range(q_ref.shape[1] // HD):
         head = slice(h * HD, (h + 1) * HD)
-        slots = slice(h * BLK, (h + 1) * BLK)
-        q = q_ref[:, head]
         keys = [nb_ref[:, head], na_ref[:, head], jnp.where(behind, fb_ref[:, head], fa_ref[:, head])]
-        scores = [live_scores(on, q, k) for on, k in zip(live, keys)]
-        old = top_in[:, h * HD : h * HD + 1]
-        top = jnp.max(jnp.maximum(jnp.maximum(scores[0], scores[1]), scores[2]), axis=1, keepdims=True)
-        top = jnp.maximum(top, old)
-        shrink = jnp.exp2(old - top)
-        exps = [jnp.exp2(s - top) for s in scores]
-        total = sum_in[:, h * HD : h * HD + 1] * shrink
-        total = total + jnp.sum(exps[0] + exps[1] + exps[2], axis=1, keepdims=True)
-        inverse = 1.0 / total
-        acc_ref[:, head] = acc_in[:, head] * (shrink * inverse)
-        wb_ref[:, slots] = (exps[0] * inverse).astype(BF16)
-        wa_ref[:, slots] = (exps[1] * inverse).astype(BF16)
-        far = exps[2] * inverse
-        wf_ref[:, slots] = far.astype(BF16)
         for p in range(pieces):
-            split = split_of(where, starts, block * pieces + p)
-            sums_ref[2 * p : 2 * p + 2, slots] = doc_rows(far[p * piece : (p + 1) * piece], split)
-
-
-def mix_kernel(block, where, starts, acc_in, wb_ref, wa_ref, vb_ref, va_ref, v_ref, sums_ref, lat_ref, *refs):
-    acc_ref, mean_ref, part_ref = refs
+            rows = slice(p * piece, (p + 1) * piece)
+            q = q_ref[rows, head]
+            scores = []
+            for k, low in zip(keys, bias):
+                s = dot_t(q, k)
+                scores += [s[:, part] * SCALE + low for part in lanes]
+            old = top_in[rows, head]
+            top = jnp.maximum(jnp.max(functools.reduce(jnp.maximum, scores), axis=1, keepdims=True), old)
+            shrink = jnp.exp2(old - top)
+            exps = [jnp.exp2(s - top) for s in scores]
+            added = jnp.sum(functools.reduce(jnp.add, exps), axis=1, keepdims=True)
+            inverse = 1.0 / (sum_in[rows, head] * shrink + added)
+            acc_ref[rows, head] = acc_in[rows, head] * (shrink * inverse)
+            for i, e in enumerate(exps):
+                out = (wb_ref, wa_ref, wf_ref)[i // len(lanes)]
+                first = h * BLK + i % len(lanes) * HD
+                w = e * inverse
+                out[rows, first : first + HD] = w.astype(BF16)
+                if out is wf_ref:
+                    sums = [jnp.sum(x, axis=0, keepdims=True) for x in (jnp.where(firsts[p], w, 0.0), jnp.where(firsts[p], 0.0, w))]
+                    sums_ref[2 * p : 2 * p + 2, first : first + HD] = jnp.concatenate(sums, axis=0)
+
+
+def doc_counts(split, piece, columns):
+    side = lax.broadcasted_iota(jnp.int32, (2, columns), 0)
+    return jnp.where(side == 0, split, piece - split).astype(F32)
+
+
+def mix_kernel(block, where, starts, acc_in, wb_ref, wa_ref, vb_ref, va_ref, lat_ref, acc_ref, mean_ref):
     pieces = mean_ref.shape[0] // 2
     piece = BLK // pieces
-    partner = lax.rem(where[0] + 2, 4)
-    side = lax.broadcasted_iota(jnp.int32, (2, HD), 0)
-
-    def counts(split):
-        return jnp.where(side == 0, split, piece - split).astype(F32)
-
     for h in range(acc_in.shape[1] // HD):
         head = slice(h * HD, (h + 1) * HD)
         slots = slice(h * BLK, (h + 1) * BLK)
         acc = acc_in[:, head] + dot(wb_ref[:, slots], vb_ref[:, head]) + dot(wa_ref[:, slots], va_ref[:, head])
         acc_ref[:, head] = acc
-        part = dot(sums_ref[:, slots].astype(BF16), v_ref[:, head])
         for p in range(pieces):
-            rows = slice(2 * p, 2 * p + 2)
             index = block * pieces + p
             split = split_of(where, starts, index)
-            found = doc_rows(acc[p * piece : (p + 1) * piece], split)
-            mean_ref[rows, head] = (found + lat_ref[2 * index : 2 * index + 2, head]) / counts(split)
-            part_ref[rows, head] = part[2 * index : 2 * index + 2] / counts(split_of(where, starts, index, partner))
-
-
-def route_kernel(where, owners, *refs):
-    halves, out_ref = refs[:-1], refs[-1]
-    means, parts = halves[: len(halves) // 2], halves[len(halves) // 2 :]
-    pieces = means[0].shape[0] // 2
+            found = doc_rows(acc[p * piece : (p + 1) * piece], split) + lat_ref[2 * index : 2 * index + 2, head]
+            mean_ref[2 * p : 2 * p + 2, head] = found / doc_counts(split, piece, HD)
+
+
+def part_kernel(where, starts, sums_ref, v_ref, part_ref):
+    piece = v_ref.shape[0] // PIECES
+    per_block = BLK // piece
+    partner = lax.rem(where[0] + 2, 4)
+    counts = [doc_counts(split_of(where, starts, p, partner), piece, HD) for p in range(PIECES)]
+    for h in range(v_ref.shape[1] // HD):
+        head = slice(h * HD, (h + 1) * HD)
+        sums = sums_ref[:, h * BLK : (h + 1) * BLK]
+        found = [dot(sums.astype(BF16), v_ref[block * BLK : (block + 1) * BLK, head]) for block in range(v_ref.shape[0] // BLK)]
+        for p in range(PIECES):
+            rows = slice(2 * p, 2 * p + 2)
+            part_ref[rows, head] = found[p // per_block][rows] / counts[p]
+
+
+def route_kernel(where, owners, part_ref, *refs):
+    mean_refs, out_ref = refs[:-1], refs[-1]
+    here, partner = where[0], lax.rem(where[0] + 2, 4)
+    means = jnp.concatenate([mean_ref[...] for mean_ref in mean_refs], axis=0)
+    parts = part_ref[...]
     for target in range(out_ref.shape[0]):
-        for first, group, shard in ((0, means, where[0]), (2, parts, lax.rem(where[0] + 2, 4))):
+        rows = []
+        for group, shard in ((means, here), (parts, partner)):
             chosen = jnp.zeros((2, out_ref.shape[2]), F32)
             for p in range(PIECES):
-                row = 2 * (p % pieces)
-                mine = owners[2 * (PIECES * shard + p)] == target
-                chosen = jnp.where(mine, group[p // pieces][row : row + 2, :], chosen)
-            out_ref[target, first : first + 2, :] = chosen
+                chosen = jnp.where(owners[2 * (PIECES * shard + p)] == target, group[2 * p : 2 * p + 2], chosen)
+            rows.append(chosen)
+        out_ref[target] = jnp.concatenate(rows, axis=0).astype(BF16)
 
 
 def pool_kernel(got_ref, out_ref):
+    got = [got_ref[s].astype(F32) for s in range(4)]
     for s in range(4):
-        out_ref[0, s] = (got_ref[s, :2, :] + got_ref[s ^ 2, 2:, :]).astype(BF16)
+        out_ref[0, s] = (got[s][:2] + got[s ^ 2][2:]).astype(BF16)
 
 
 def context_kernel(block, where, acc_ref, w_ref, vb_ref, va_ref, *refs):
@@ -284,19 +302,20 @@
     return 2 if heads % 2 == 0 else 1
 
 
-def own_call(queries, keys, values):
+def own_call(queries, keys, values, block=None):
     rows, columns = queries.shape
     heads = columns // HD
     wide = step_of(heads) * HD
+    here = rows if block is None else BLK
     return pl.pallas_call(
         own_kernel,
         grid=(columns // wide,),
-        in_specs=[spec(rows, wide)] * 3,
-        out_specs=[spec(rows, wide)] * 3,
-        out_shape=(shape(rows, columns),) * 3,
+        in_specs=[pl.BlockSpec((here, wide), lambda h: (block or 0, h))] + [spec(rows, wide)] * 2,
+        out_specs=[spec(here, wide)] * 3,
+        out_shape=(shape(here, columns),) * 3,
         compiler_params=PARAMS,
         cost_estimate=pl.CostEstimate(
-            flops=4 * rows * columns * rows, bytes_accessed=18 * rows * columns, transcendentals=heads * rows * rows
+            flops=4 * here * columns * rows, bytes_accessed=18 * here * columns, transcendentals=heads * here * rows
         ),
         name="own",
     )(queries, keys, values)
@@ -351,7 +370,7 @@
         return pl.pallas_call(
             functools.partial(weigh_kernel, block, 4),
             grid=(heads // step,),
-            in_specs=smem(3) + [row_spec(block)] + [row_spec(0)] * 4 + [row_spec(block)] * 3,
+            in_specs=smem(3) + [row_spec(block)] + [row_spec(0)] * 7,
             out_specs=[row_spec(0)] + [row_spec(0, step * BLK)] * 3 + [spec(docs, step * BLK)],
             out_shape=(shape(BLK, columns),) + (shape(BLK, slots, BF16),) * 3 + (shape(docs, slots),),
             compiler_params=PARAMS,
@@ -361,21 +380,17 @@
             name="weigh",
         )(where, pattern, doc_starts, queries, *near_keys, *far_keys, *state)
 
-    def mix(block, acc, weights, near_vals, sums, lat):
+    def mix(block, acc, weights, near_vals, lat):
         return pl.pallas_call(
             functools.partial(mix_kernel, block),
             grid=(heads // step,),
-            in_specs=smem(2)
-            + [row_spec(0)]
-            + [row_spec(0, step * BLK)] * 2
-            + [row_spec(0)] * 2
-            + [row_spec(block), spec(2 * PIECES, step * BLK), spec(2 * PIECES, wide)],
-            out_specs=[row_spec(0)] + [spec(docs, wide)] * 2,
-            out_shape=(shape(BLK, columns),) + (shape(docs, columns),) * 2,
+            in_specs=smem(2) + [row_spec(0)] + [row_spec(0, step * BLK)] * 2 + [row_spec(0)] * 2 + [spec(2 * PIECES, wide)],
+            out_specs=[row_spec(0), spec(docs, wide)],
+            out_shape=(shape(BLK, columns), shape(docs, columns)),
             compiler_params=PARAMS,
-            cost_estimate=pl.CostEstimate(flops=5 * BLK * columns * BLK, bytes_accessed=22 * BLK * columns, transcendentals=0),
+            cost_estimate=pl.CostEstimate(flops=4 * BLK * columns * BLK, bytes_accessed=20 * BLK * columns, transcendentals=0),
             name="mix",
-        )(where, doc_starts, acc, *weights, *near_vals, values, sums, lat)
+        )(where, doc_starts, acc, *weights, *near_vals, lat)
 
     def finish(block, acc, weights, far_vals, context):
         held = [] if context is None else [context]
@@ -393,37 +408,47 @@
 
     near_keys = [near(part(keys, 0))]
     lat = latent_call(where, doc_starts, queries, latent_keys, latent_values)
-    lat, late_keys = lax.optimization_barrier((lat, part(keys, 1)))
-    near_keys.append(near(late_keys))
-    state = own_call(queries, keys, values)
+    lat, late_keys, late_vals = lax.optimization_barrier((lat, keys, values))
+    near_keys.append(near(part(late_keys, 1)))
+    state = own_call(queries, keys, values, 0)
     near_keys[0], state = lax.optimization_barrier((near_keys[0], state))
+    near_keys[1], late_queries = lax.optimization_barrier((near_keys[1], queries))
     far_keys = [onward(pair) for pair in near_keys]
-    late_vals, near_keys[1] = lax.optimization_barrier(([part(values, block) for block in range(blocks)], near_keys[1]))
-    near_vals = [near(value) for value in late_vals]
-    acc, near_weights, far_weights, sums = [], [], [], []
-    for block in range(blocks):
-        out = weigh(block, near_keys[block], far_keys[block], state)
-        acc.append(out[0])
-        near_weights.append(out[1:3])
-        far_weights.append(out[3])
-        sums.append(out[4])
-    sums = move(jnp.concatenate(sums), [(s, s ^ 2) for s in range(4)])
+    late_state = own_call(late_queries, keys, values, 1)
+    late_vals, late_state = lax.optimization_barrier((late_vals, late_state))
+    near_vals = [near(part(late_vals, 0))]
+    out = [weigh(0, near_keys[0], far_keys[0], state)]
+    out[0], last_vals = lax.optimization_barrier((out[0], late_vals))
+    near_vals.append(near(part(last_vals, 1)))
+    out.append(weigh(1, near_keys[1], far_keys[1], late_state))
+    sums = jnp.concatenate([o[4] for o in out])
+    near_vals[0], out[1], sums = lax.optimization_barrier((near_vals[0], out[1], sums))
+    sums = move(sums, [(s, s ^ 2) for s in range(4)])
+    mixed = [mix(0, out[0][0], out[0][1:3], near_vals[0], lat)]
     far_vals = [onward(near_vals[0])]
-    means, parts = [], []
-    for block in range(blocks):
-        acc[block], mean, far_part = mix(block, acc[block], near_weights[block], near_vals[block], sums, lat)
-        means.append(mean)
-        parts.append(far_part)
+    parts = pl.pallas_call(
+        part_kernel,
+        grid=(heads // step,),
+        in_specs=smem(2) + [spec(2 * PIECES, step * BLK), spec(rows, wide)],
+        out_specs=spec(2 * PIECES, wide),
+        out_shape=shape(2 * PIECES, columns),
+        compiler_params=PARAMS,
+        cost_estimate=pl.CostEstimate(flops=32 * BLK * columns, bytes_accessed=3 * rows * columns, transcendentals=0),
+        name="part",
+    )(where, doc_starts, sums, values)
+    near_vals[1], parts = lax.optimization_barrier((near_vals[1], parts))
+    far_vals.append(onward(near_vals[1]))
+    mixed.append(mix(1, out[1][0], out[1][1:3], near_vals[1], lat))
+    acc = [m[0] for m in mixed]
+    far_weights = [o[3] for o in out]
     sent = pl.pallas_call(
         route_kernel,
-        in_specs=smem(2) + vmem(2 * blocks),
+        in_specs=smem(2) + vmem(3),
         out_specs=pl.BlockSpec(memory_space=pltpu.VMEM),
-        out_shape=jax.ShapeDtypeStruct((4, 4, columns), F32),
+        out_shape=jax.ShapeDtypeStruct((4, 4, columns), BF16),
         compiler_params=PARAMS,
         name="route",
-    )(where, doc_owner, *means, *parts)
-    sent, last_vals = lax.optimization_barrier((sent, near_vals[1]))
-    far_vals.append(onward(last_vals))
+    )(where, doc_owner, parts, *[m[1] for m in mixed])
     context = finish(0, acc[0], far_weights[0], far_vals[0], None)
     sent, context = lax.optimization_barrier((sent, context))
     got = lax.all_to_all(sent, "seq", split_axis=0, concat_axis=0, tiled=True)

time: 111 us -> 110 us (level)
  starting transfers between devices: 45 us -> 32.6 us
  blocking collectives: 0 us -> 10.9 us
  waiting for transfers between devices: 22.1 us -> 28.6 us
  Pallas kernels: 37.4 us -> 31.5 us
    all_to_all x0 -> x1, blocking collectives: none -> 10.9 us  [four_shards(): got = lax.all_to_all(sent, 'seq', split_axis=0, concat_axis=0, tiled=True)]
    ppermute x17, waiting for transfers between devices: 20.6 us -> 28.6 us  [move(): return lax.ppermute(value, 'seq', pairs)]
    ppermute x17, starting transfers between devices: 40.3 us -> 32.6 us  [move(): return lax.ppermute(value, 'seq', pairs)]
    pallas_call x2, Pallas kernels: 16.9 us -> 9.51 us  [weigh(): pl.pallas_call(functools.partial(weigh_kernel, block, 4), grid=(heads //...]
    all_to_all x1 -> x0, starting transfers between devices: 4.73 us -> none  [four_shards(): got = lax.all_to_all(sent, 'seq', split_axis=0, concat_axis=0, tiled=True)]
    pallas_call x2 -> x4, Pallas kernels: 6.49 us -> 9.25 us  [the longest x2 7.33 us: own_call(): pl.pallas_call(own_kernel, grid=(columns // wide,), in_specs=[pl.BlockSpe...]
    all_to_all x1 -> x0, waiting for transfers between devices: 1.48 us -> none  [four_shards(): got = lax.all_to_all(sent, 'seq', split_axis=0, concat_axis=0, tiled=True)]
    unnamed x18 -> x16, local copies, waits for them, and re-layouts: 2.48 us -> 3.76 us
  transfers between devices with their start and end apart: 18 -> 17, of which waited for: 6 -> 4; matrix products, arithmetic and copies ran while one was open for 0% -> 0% of each run, Pallas kernels for 33% -> 28%
where the time goes in v4:
time: 110 us
  starting transfers between devices  32.6 us (30%)
  Pallas kernels  31.5 us (29%)
  waiting for transfers between devices  28.6 us (26%)
  blocking collectives  10.9 us (10%)
  local copies, waits for them, and re-layouts  5.03 us (5%)
    ppermute x17, starting transfers between devices, move(): return lax.ppermute(value, 'seq', pairs)  32.6 us
    ppermute x17, waiting for transfers between devices, move(): return lax.ppermute(value, 'seq', pairs)  28.6 us
    all_to_all x1, blocking collectives, four_shards(): got = lax.all_to_all(sent, 'seq', split_axis=0, concat_axis=0, tiled=True)  10.9 us
    pallas_call x2, Pallas kernels, weigh(): pl.pallas_call(functools.partial(weigh_kernel, block, 4), grid=(heads //...  9.51 us
    pallas_call x2, Pallas kernels, own_call(): pl.pallas_call(own_kernel, grid=(columns // wide,), in_specs=[pl.BlockSpe...  7.33 us
    pallas_call x1, Pallas kernels, latent_call(): pl.pallas_call(latent_kernel, grid=(columns // wide,), in_specs=smem(2) +...  5.38 us
    pallas_call x2, Pallas kernels, mix(): pl.pallas_call(functools.partial(mix_kernel, block), grid=(heads // step,...  4.39 us
    unnamed x16, local copies, waits for them, and re-layouts  3.76 us
  transfers between devices with their start and end apart: 17, of which 4 were waited for; matrix products, arithmetic and copies ran while one was open for 0% of the time, Pallas kernels for 28%

profile of v4, /device:TPU:0, one launch (start us, length us, event | category | flops | bytes accessed | tf_op | source)
XLA Modules:
  0.0 109.8 jit_solution(5483148229984739251)
XLA Ops:
  1.8 5.0 %collective-permute-start.6 = (bf16[256,1024]{1,0:T(8,128)(2,1)S(1)}, bf16[256,1024]{1,0:T(8,128)(2,1)S(1)}, u32[]{:S(2)}, u32[]{:S(2)}) collective-permute-start(bf16[256,1024]{1,0:T(8,128)(2,1)S(1)} %slice.14), channel_id=1, source_target_pairs={{0,4},{4,8},{8,12},{1,5},{5,9},{9,13},{2,6},{6,10},{10,14},{3,7},{... | collective-permute-start | bytes 1572872 | tf_op jit(solution)/shard_map/ppermute | solution.py:355
  6.8 1.3 %collective-permute-start.7 = (bf16[256,1024]{1,0:T(8,128)(2,1)S(1)}, bf16[256,1024]{1,0:T(8,128)(2,1)S(1)}, u32[]{:S(2)}, u32[]{:S(2)}) collective-permute-start(bf16[256,1024]{1,0:T(8,128)(2,1)S(1)} %slice.14), channel_id=1, source_target_pairs={{4,0},{8,4},{12,8},{5,1},{9,5},{13,9},{6,2},{10,6},{14,10},{7,3},{... | collective-permute-start | bytes 1572872 | tf_op jit(solution)/shard_map/ppermute | solution.py:355
  11.2 5.4 %latent.1.lat_ref = f32[8,1024]{1,0:T(8,128)S(1)} custom-call(s32[1]{0:T(128)} %bitcast.where, s32[32]{0:T(128)S(1)} %copy-done.3, bf16[512,1024]{1,0:T(8,128)(2,1)S(1)} %copy-done.1, bf16[512,1024]{1,0:T(8,128)(2,1)S(1)} %copy-done.6, bf16[512,1024]{1,0:T(8,128)(2,1)S(1)} %copy-done.7), custom_call_target="tpu_custom_call" | custom-call | flops 1073741824 | bytes 3145728 | tf_op jit(solution)/shard_map/latent/pallas_call | solution.py:329
  16.6 4.7 %collective-permute-start = (bf16[256,1024]{1,0:T(8,128)(2,1)S(1)}, bf16[256,1024]{1,0:T(8,128)(2,1)S(1)}, u32[]{:S(2)}, u32[]{:S(2)}) collective-permute-start(bf16[256,1024]{1,0:T(8,128)(2,1)S(1)} %slice.12), channel_id=1, source_target_pairs={{0,4},{4,8},{8,12},{1,5},{5,9},{9,13},{2,6},{6,10},{10,14},{3,7},{... | collective-permute-start | bytes 1572872 | tf_op jit(solution)/shard_map/ppermute | solution.py:355
  21.4 1.3 %collective-permute-start.1 = (bf16[256,1024]{1,0:T(8,128)(2,1)S(1)}, bf16[256,1024]{1,0:T(8,128)(2,1)S(1)}, u32[]{:S(2)}, u32[]{:S(2)}) collective-permute-start(bf16[256,1024]{1,0:T(8,128)(2,1)S(1)} %slice.12), channel_id=1, source_target_pairs={{4,0},{8,4},{12,8},{5,1},{9,5},{13,9},{6,2},{10,6},{14,10},{7,3},{... | collective-permute-start | bytes 1572872 | tf_op jit(solution)/shard_map/ppermute | solution.py:355
  22.7 3.7 %own.3 = (f32[256,1024]{1,0:T(8,128)S(1)}, f32[256,1024]{1,0:T(8,128)S(1)}, f32[256,1024]{1,0:T(8,128)S(1)}) custom-call(bf16[512,1024]{1,0:T(8,128)(2,1)S(1)} %copy-done.1, bf16[512,1024]{1,0:T(8,128)(2,1)S(1)} %copy-done.2, bf16[512,1024]{1,0:T(8,128)(2,1)S(1)} %copy-done), custom_call_target="tpu_custom_call" | custom-call | flops 536870912 | bytes 4718592 | tf_op jit(solution)/shard_map/own/pallas_call | solution.py:310
  27.1 1.3 %collective-permute-start.9 = (bf16[256,1024]{1,0:T(8,128)(2,1)S(1)}, bf16[256,1024]{1,0:T(8,128)(2,1)S(1)}, u32[]{:S(2)}, u32[]{:S(2)}) collective-permute-start(bf16[256,1024]{1,0:T(8,128)(2,1)S(1)} %collective-permute-done.7.na_ref), channel_id=1, source_target_pairs={{4,0},{8,4},{5,1},{9,5},{6,2},{10,6},{7,3},{11,7},{20,16},{24,20},... | collective-permute-start | bytes 1572872 | tf_op jit(solution)/shard_map/ppermute | solution.py:355
  28.4 3.6 %collective-permute-done.nb_ref = bf16[256,1024]{1,0:T(8,128)(2,1)S(1)} collective-permute-done((bf16[256,1024]{1,0:T(8,128)(2,1)S(1)}, bf16[256,1024]{1,0:T(8,128)(2,1)S(1)}, u32[]{:S(2)}, u32[]{:S(2)}) %collective-permute-start) | collective-permute-done | bytes 524320 | tf_op jit(solution)/shard_map/ppermute | solution.py:355
  31.9 6.2 %collective-permute-done.1.na_ref = bf16[256,1024]{1,0:T(8,128)(2,1)S(1)} collective-permute-done((bf16[256,1024]{1,0:T(8,128)(2,1)S(1)}, bf16[256,1024]{1,0:T(8,128)(2,1)S(1)}, u32[]{:S(2)}, u32[]{:S(2)}) %collective-permute-start.1) | collective-permute-done | bytes 524320 | tf_op jit(solution)/shard_map/ppermute | solution.py:355
  38.8 1.3 %collective-permute-start.5 = (bf16[256,1024]{1,0:T(8,128)(2,1)S(1)}, bf16[256,1024]{1,0:T(8,128)(2,1)S(1)}, u32[]{:S(2)}, u32[]{:S(2)}) collective-permute-start(bf16[256,1024]{1,0:T(8,128)(2,1)S(1)} %collective-permute-done.1.na_ref), channel_id=1, source_target_pairs={{4,0},{8,4},{5,1},{9,5},{6,2},{10,6},{7,3},{11,7},{20,16},{24,20},... | collective-permute-start | bytes 1572872 | tf_op jit(solution)/shard_map/ppermute | solution.py:355
  40.1 3.7 %own.2 = (f32[256,1024]{1,0:T(8,128)S(1)}, f32[256,1024]{1,0:T(8,128)S(1)}, f32[256,1024]{1,0:T(8,128)S(1)}) custom-call(bf16[512,1024]{1,0:T(8,128)(2,1)S(1)} %copy-done.1, bf16[512,1024]{1,0:T(8,128)(2,1)S(1)} %copy-done.2, bf16[512,1024]{1,0:T(8,128)(2,1)S(1)} %copy-done), custom_call_target="tpu_custom_call" | custom-call | flops 536870912 | bytes 4718592 | tf_op jit(solution)/shard_map/own/pallas_call | solution.py:310
  43.8 4.9 %collective-permute-start.2 = (bf16[256,1024]{1,0:T(8,128)(2,1)S(1)}, bf16[256,1024]{1,0:T(8,128)(2,1)S(1)}, u32[]{:S(2)}, u32[]{:S(2)}) collective-permute-start(bf16[256,1024]{1,0:T(8,128)(2,1)S(1)} %slice.13), channel_id=1, source_target_pairs={{0,4},{4,8},{8,12},{1,5},{5,9},{9,13},{2,6},{6,10},{10,14},{3,7},{... | collective-permute-start | bytes 1572872 | tf_op jit(solution)/shard_map/ppermute | solution.py:355
  48.8 1.3 %collective-permute-start.3 = (bf16[256,1024]{1,0:T(8,128)(2,1)S(1)}, bf16[256,1024]{1,0:T(8,128)(2,1)S(1)}, u32[]{:S(2)}, u32[]{:S(2)}) collective-permute-start(bf16[256,1024]{1,0:T(8,128)(2,1)S(1)} %slice.13), channel_id=1, source_target_pairs={{4,0},{8,4},{12,8},{5,1},{9,5},{13,9},{6,2},{10,6},{14,10},{7,3},{... | collective-permute-start | bytes 1572872 | tf_op jit(solution)/shard_map/ppermute | solution.py:355
  50.1 4.8 %weigh.3 = (f32[256,1024]{1,0:T(8,128)S(1)}, bf16[256,2048]{1,0:T(8,128)(2,1)S(1)}, bf16[256,2048]{1,0:T(8,128)(2,1)S(1)}, bf16[256,2048]{1,0:T(8,128)(2,1)S(1)}, f32[4,2048]{1,0:T(4,128)S(1)}) custom-call(s32[1]{0:T(128)} %bitcast.where, s32[2,8]{1,0:T(2,128)S(1)} %copy-done.4, s32[32]{0:T(128)S(1)} %copy-done.3, bf16[512,1024]{1,0:T(8,128)(2,1)S(1)} %copy-done.1, ...), custom_call_target="tpu_custom_call" | custom-call | flops 402653184 | bytes 5767168 | tf_op jit(solution)/shard_map/weigh/pallas_call | solution.py:370
  54.9 4.6 %collective-permute-start.10 = (bf16[256,1024]{1,0:T(8,128)(2,1)S(1)}, bf16[256,1024]{1,0:T(8,128)(2,1)S(1)}, u32[]{:S(2)}, u32[]{:S(2)}) collective-permute-start(bf16[256,1024]{1,0:T(8,128)(2,1)S(1)} %slice.15), channel_id=1, source_target_pairs={{0,4},{4,8},{8,12},{1,5},{5,9},{9,13},{2,6},{6,10},{10,14},{3,7},{... | collective-permute-start | bytes 1572872 | tf_op jit(solution)/shard_map/ppermute | solution.py:355
  59.5 1.3 %collective-permute-start.11 = (bf16[256,1024]{1,0:T(8,128)(2,1)S(1)}, bf16[256,1024]{1,0:T(8,128)(2,1)S(1)}, u32[]{:S(2)}, u32[]{:S(2)}) collective-permute-start(bf16[256,1024]{1,0:T(8,128)(2,1)S(1)} %slice.15), channel_id=1, source_target_pairs={{4,0},{8,4},{12,8},{5,1},{9,5},{13,9},{6,2},{10,6},{14,10},{7,3},{... | collective-permute-start | bytes 1572872 | tf_op jit(solution)/shard_map/ppermute | solution.py:355
  60.8 4.8 %weigh.2 = (f32[256,1024]{1,0:T(8,128)S(1)}, bf16[256,2048]{1,0:T(8,128)(2,1)S(1)}, bf16[256,2048]{1,0:T(8,128)(2,1)S(1)}, bf16[256,2048]{1,0:T(8,128)(2,1)S(1)}, f32[4,2048]{1,0:T(4,128)S(1)}) custom-call(s32[1]{0:T(128)} %bitcast.where, s32[2,8]{1,0:T(2,128)S(1)} %copy-done.4, s32[32]{0:T(128)S(1)} %copy-done.3, bf16[512,1024]{1,0:T(8,128)(2,1)S(1)} %copy-done.1, ...), custom_call_target="tpu_custom_call" | custom-call | flops 402653184 | bytes 5767168 | tf_op jit(solution)/shard_map/weigh/pallas_call | solution.py:370
  65.6 6.2 %collective-permute-done.3.va_ref = bf16[256,1024]{1,0:T(8,128)(2,1)S(1)} collective-permute-done((bf16[256,1024]{1,0:T(8,128)(2,1)S(1)}, bf16[256,1024]{1,0:T(8,128)(2,1)S(1)}, u32[]{:S(2)}, u32[]{:S(2)}) %collective-permute-start.3) | collective-permute-done | bytes 524320 | tf_op jit(solution)/shard_map/ppermute | solution.py:355
  72.9 1.3 %collective-permute-start.16 = (bf16[256,1024]{1,0:T(8,128)(2,1)S(1)}, bf16[256,1024]{1,0:T(8,128)(2,1)S(1)}, u32[]{:S(2)}, u32[]{:S(2)}) collective-permute-start(bf16[256,1024]{1,0:T(8,128)(2,1)S(1)} %collective-permute-done.3.va_ref), channel_id=1, source_target_pairs={{4,0},{8,4},{5,1},{9,5},{6,2},{10,6},{7,3},{11,7},{20,16},{24,20},... | collective-permute-start | bytes 1572872 | tf_op jit(solution)/shard_map/ppermute | solution.py:355
  74.2 12.6 %collective-permute-done.12.sums_ref = f32[8,2048]{1,0:T(8,128)S(1)} collective-permute-done((f32[8,2048]{1,0:T(8,128)S(1)}, f32[8,2048]{1,0:T(8,128)S(1)}, u32[]{:S(2)}, u32[]{:S(2)}) %collective-permute-start.12) | collective-permute-done | bytes 65568 | tf_op jit(solution)/shard_map/ppermute | solution.py:355
  88.8 1.3 %collective-permute-start.14 = (bf16[256,1024]{1,0:T(8,128)(2,1)S(1)}, bf16[256,1024]{1,0:T(8,128)(2,1)S(1)}, u32[]{:S(2)}, u32[]{:S(2)}) collective-permute-start(bf16[256,1024]{1,0:T(8,128)(2,1)S(1)} %collective-permute-done.11.va_ref), channel_id=1, source_target_pairs={{4,0},{8,4},{5,1},{9,5},{6,2},{10,6},{7,3},{11,7},{20,16},{24,20},... | collective-permute-start | bytes 1572872 | tf_op jit(solution)/shard_map/ppermute | solution.py:355
  90.1 2.2 %mix.3 = (f32[256,1024]{1,0:T(8,128)S(1)}, f32[4,1024]{1,0:T(4,128)S(1)}) custom-call(s32[1]{0:T(128)} %bitcast.where, s32[32]{0:T(128)S(1)} %copy-done.3, f32[256,1024]{1,0:T(8,128)S(1)} %get-tuple-element.97.acc_in, bf16[256,2048]{1,0:T(8,128)(2,1)S(1)} %get-tuple-element.98.wb_ref, bf16[256,2048]{1,0:T(8,128)(2,1)S(1)} %get-tuple-element.99.wa_ref, ...), custom_call_target="tpu_custom_call" | custom-call | flops 268435456 | bytes 5242880 | tf_op jit(solution)/shard_map/mix/pallas_call | solution.py:384
  92.3 2.2 %mix.2 = (f32[256,1024]{1,0:T(8,128)S(1)}, f32[4,1024]{1,0:T(4,128)S(1)}) custom-call(s32[1]{0:T(128)} %bitcast.where, s32[32]{0:T(128)S(1)} %copy-done.3, f32[256,1024]{1,0:T(8,128)S(1)} %get-tuple-element.86.acc_in, bf16[256,2048]{1,0:T(8,128)(2,1)S(1)} %get-tuple-element.87.wb_ref, bf16[256,2048]{1,0:T(8,128)(2,1)S(1)} %get-tuple-element.88.wa_ref, ...), custom_call_target="tpu_custom_call" | custom-call | flops 268435456 | bytes 5242880 | tf_op jit(solution)/shard_map/mix/pallas_call | solution.py:384
  97.0 10.9 %all_to_all.5.got_ref = bf16[4,4,1024]{2,1,0:T(4,128)(2,1)S(1)} all-to-all(bf16[4,4,1024]{2,1,0:T(4,128)(2,1)S(1)} %route.1), channel_id=1, replica_groups=mesh['groups'=2,'seq'=4,'head'=2,'sub'=2] {'seq'}, dimensions={0} | all-to-all | bytes 65536 | tf_op jit(solution)/shard_map/all_to_all | solution.py:454
  (44 shorter events, 13.1 us)
Async XLA Ops:
  0.6 7.5 %copy-start.1 = (bf16[512,1024]{1,0:T(8,128)(2,1)S(1)}, bf16[512,1024]{1,0:T(8,128)(2,1)}, u32[]{:S(2)}) copy-start(bf16[512,1024]{1,0:T(8,128)(2,1)} %q_ref.8) | copy-start | bytes 3145732
  1.8 24.5 %collective-permute-start.6 = (bf16[256,1024]{1,0:T(8,128)(2,1)S(1)}, bf16[256,1024]{1,0:T(8,128)(2,1)S(1)}, u32[]{:S(2)}, u32[]{:S(2)}) collective-permute-start(bf16[256,1024]{1,0:T(8,128)(2,1)S(1)} %slice.14), channel_id=1, source_target_pairs={{0,4},{4,8},{8,12},{1,5},{5,9},{9,13},{2,6},{6,10},{10,14},{3,7},{... | collective-permute-start | bytes 1572872 | tf_op jit(solution)/shard_map/ppermute | solution.py:355
  6.8 19.6 %collective-permute-start.7 = (bf16[256,1024]{1,0:T(8,128)(2,1)S(1)}, bf16[256,1024]{1,0:T(8,128)(2,1)S(1)}, u32[]{:S(2)}, u32[]{:S(2)}) collective-permute-start(bf16[256,1024]{1,0:T(8,128)(2,1)S(1)} %slice.14), channel_id=1, source_target_pairs={{4,0},{8,4},{12,8},{5,1},{9,5},{13,9},{6,2},{10,6},{14,10},{7,3},{... | collective-permute-start | bytes 1572872 | tf_op jit(solution)/shard_map/ppermute | solution.py:355
  8.1 0.7 copy-start.3
  8.7 1.2 %copy-start.6 = (bf16[512,1024]{1,0:T(8,128)(2,1)S(1)}, bf16[512,1024]{1,0:T(8,128)(2,1)}, u32[]{:S(2)}) copy-start(bf16[512,1024]{1,0:T(8,128)(2,1)} %lk_ref.1) | copy-start | bytes 3145732
  10.0 1.2 %copy-start.7 = (bf16[512,1024]{1,0:T(8,128)(2,1)S(1)}, bf16[512,1024]{1,0:T(8,128)(2,1)}, u32[]{:S(2)}) copy-start(bf16[512,1024]{1,0:T(8,128)(2,1)} %lv_ref.1) | copy-start | bytes 3145732
  11.2 5.4 %copy-start.2 = (bf16[512,1024]{1,0:T(8,128)(2,1)S(1)}, bf16[512,1024]{1,0:T(8,128)(2,1)}, u32[]{:S(2)}) copy-start(bf16[512,1024]{1,0:T(8,128)(2,1)} %k_ref.3) | copy-start | bytes 3145732
  16.6 6.1 %copy-start = (bf16[512,1024]{1,0:T(8,128)(2,1)S(1)}, bf16[512,1024]{1,0:T(8,128)(2,1)}, u32[]{:S(2)}) copy-start(bf16[512,1024]{1,0:T(8,128)(2,1)} %v_ref.5) | copy-start | bytes 3145732
  16.6 15.3 %collective-permute-start = (bf16[256,1024]{1,0:T(8,128)(2,1)S(1)}, bf16[256,1024]{1,0:T(8,128)(2,1)S(1)}, u32[]{:S(2)}, u32[]{:S(2)}) collective-permute-start(bf16[256,1024]{1,0:T(8,128)(2,1)S(1)} %slice.12), channel_id=1, source_target_pairs={{0,4},{4,8},{8,12},{1,5},{5,9},{9,13},{2,6},{6,10},{10,14},{3,7},{... | collective-permute-start | bytes 1572872 | tf_op jit(solution)/shard_map/ppermute | solution.py:355
  21.4 16.8 %collective-permute-start.1 = (bf16[256,1024]{1,0:T(8,128)(2,1)S(1)}, bf16[256,1024]{1,0:T(8,128)(2,1)S(1)}, u32[]{:S(2)}, u32[]{:S(2)}) collective-permute-start(bf16[256,1024]{1,0:T(8,128)(2,1)S(1)} %slice.12), channel_id=1, source_target_pairs={{4,0},{8,4},{12,8},{5,1},{9,5},{13,9},{6,2},{10,6},{14,10},{7,3},{... | collective-permute-start | bytes 1572872 | tf_op jit(solution)/shard_map/ppermute | solution.py:355
  26.4 22.4 %collective-permute-start.8 = (bf16[256,1024]{1,0:T(8,128)(2,1)S(1)}, bf16[256,1024]{1,0:T(8,128)(2,1)S(1)}, u32[]{:S(2)}, u32[]{:S(2)}) collective-permute-start(bf16[256,1024]{1,0:T(8,128)(2,1)S(1)} %collective-permute-done.6.nb_ref), channel_id=1, source_target_pairs={{4,8},{8,12},{5,9},{9,13},{6,10},{10,14},{7,11},{11,15},{20,24},{2... | collective-permute-start | bytes 1572872 | tf_op jit(solution)/shard_map/ppermute | solution.py:355
  27.1 23.0 %collective-permute-start.9 = (bf16[256,1024]{1,0:T(8,128)(2,1)S(1)}, bf16[256,1024]{1,0:T(8,128)(2,1)S(1)}, u32[]{:S(2)}, u32[]{:S(2)}) collective-permute-start(bf16[256,1024]{1,0:T(8,128)(2,1)S(1)} %collective-permute-done.7.na_ref), channel_id=1, source_target_pairs={{4,0},{8,4},{5,1},{9,5},{6,2},{10,6},{7,3},{11,7},{20,16},{24,20},... | collective-permute-start | bytes 1572872 | tf_op jit(solution)/shard_map/ppermute | solution.py:355
  38.1 21.3 %collective-permute-start.4 = (bf16[256,1024]{1,0:T(8,128)(2,1)S(1)}, bf16[256,1024]{1,0:T(8,128)(2,1)S(1)}, u32[]{:S(2)}, u32[]{:S(2)}) collective-permute-start(bf16[256,1024]{1,0:T(8,128)(2,1)S(1)} %collective-permute-done.nb_ref), channel_id=1, source_target_pairs={{4,8},{8,12},{5,9},{9,13},{6,10},{10,14},{7,11},{11,15},{20,24},{2... | collective-permute-start | bytes 1572872 | tf_op jit(solution)/shard_map/ppermute | solution.py:355
  38.8 22.0 %collective-permute-start.5 = (bf16[256,1024]{1,0:T(8,128)(2,1)S(1)}, bf16[256,1024]{1,0:T(8,128)(2,1)S(1)}, u32[]{:S(2)}, u32[]{:S(2)}) collective-permute-start(bf16[256,1024]{1,0:T(8,128)(2,1)S(1)} %collective-permute-done.1.na_ref), channel_id=1, source_target_pairs={{4,0},{8,4},{5,1},{9,5},{6,2},{10,6},{7,3},{11,7},{20,16},{24,20},... | collective-permute-start | bytes 1572872 | tf_op jit(solution)/shard_map/ppermute | solution.py:355
  43.8 6.3 %copy-start.4 = (s32[2,8]{1,0:T(2,128)S(1)}, s32[2,8]{1,0:T(2,128)}, u32[]{:S(2)}) copy-start(s32[2,8]{1,0:T(2,128)} %pattern.3) | copy-start | bytes 196
  43.8 21.7 %collective-permute-start.2 = (bf16[256,1024]{1,0:T(8,128)(2,1)S(1)}, bf16[256,1024]{1,0:T(8,128)(2,1)S(1)}, u32[]{:S(2)}, u32[]{:S(2)}) collective-permute-start(bf16[256,1024]{1,0:T(8,128)(2,1)S(1)} %slice.13), channel_id=1, source_target_pairs={{0,4},{4,8},{8,12},{1,5},{5,9},{9,13},{2,6},{6,10},{10,14},{3,7},{... | collective-permute-start | bytes 1572872 | tf_op jit(solution)/shard_map/ppermute | solution.py:355
  48.8 23.1 %collective-permute-start.3 = (bf16[256,1024]{1,0:T(8,128)(2,1)S(1)}, bf16[256,1024]{1,0:T(8,128)(2,1)S(1)}, u32[]{:S(2)}, u32[]{:S(2)}) collective-permute-start(bf16[256,1024]{1,0:T(8,128)(2,1)S(1)} %slice.13), channel_id=1, source_target_pairs={{4,0},{8,4},{12,8},{5,1},{9,5},{13,9},{6,2},{10,6},{14,10},{7,3},{... | collective-permute-start | bytes 1572872 | tf_op jit(solution)/shard_map/ppermute | solution.py:355
  54.9 33.2 %collective-permute-start.10 = (bf16[256,1024]{1,0:T(8,128)(2,1)S(1)}, bf16[256,1024]{1,0:T(8,128)(2,1)S(1)}, u32[]{:S(2)}, u32[]{:S(2)}) collective-permute-start(bf16[256,1024]{1,0:T(8,128)(2,1)S(1)} %slice.15), channel_id=1, source_target_pairs={{0,4},{4,8},{8,12},{1,5},{5,9},{9,13},{2,6},{6,10},{10,14},{3,7},{... | collective-permute-start | bytes 1572872 | tf_op jit(solution)/shard_map/ppermute | solution.py:355
  59.5 28.6 %collective-permute-start.11 = (bf16[256,1024]{1,0:T(8,128)(2,1)S(1)}, bf16[256,1024]{1,0:T(8,128)(2,1)S(1)}, u32[]{:S(2)}, u32[]{:S(2)}) collective-permute-start(bf16[256,1024]{1,0:T(8,128)(2,1)S(1)} %slice.15), channel_id=1, source_target_pairs={{4,0},{8,4},{12,8},{5,1},{9,5},{13,9},{6,2},{10,6},{14,10},{7,3},{... | collective-permute-start | bytes 1572872 | tf_op jit(solution)/shard_map/ppermute | solution.py:355
  71.8 15.0 %collective-permute-start.12 = (f32[8,2048]{1,0:T(8,128)S(1)}, f32[8,2048]{1,0:T(8,128)S(1)}, u32[]{:S(2)}, u32[]{:S(2)}) collective-permute-start(f32[8,2048]{1,0:T(8,128)S(1)} %pad_maximum_fusion), channel_id=1, source_target_pairs={{0,8},{4,12},{8,0},{12,4},{1,9},{5,13},{9,1},{13,5},{2,10},{6,14},... | collective-permute-start | bytes 196616 | tf_op jit(solution)/shard_map/ppermute | solution.py:355
  72.2 23.6 %collective-permute-start.15 = (bf16[256,1024]{1,0:T(8,128)(2,1)S(1)}, bf16[256,1024]{1,0:T(8,128)(2,1)S(1)}, u32[]{:S(2)}, u32[]{:S(2)}) collective-permute-start(bf16[256,1024]{1,0:T(8,128)(2,1)S(1)} %collective-permute-done.2.vb_ref), channel_id=1, source_target_pairs={{4,8},{8,12},{5,9},{9,13},{6,10},{10,14},{7,11},{11,15},{20,24},{2... | collective-permute-start | bytes 1572872 | tf_op jit(solution)/shard_map/ppermute | solution.py:355
  72.9 22.9 %collective-permute-start.16 = (bf16[256,1024]{1,0:T(8,128)(2,1)S(1)}, bf16[256,1024]{1,0:T(8,128)(2,1)S(1)}, u32[]{:S(2)}, u32[]{:S(2)}) collective-permute-start(bf16[256,1024]{1,0:T(8,128)(2,1)S(1)} %collective-permute-done.3.va_ref), channel_id=1, source_target_pairs={{4,0},{8,4},{5,1},{9,5},{6,2},{10,6},{7,3},{11,7},{20,16},{24,20},... | collective-permute-start | bytes 1572872 | tf_op jit(solution)/shard_map/ppermute | solution.py:355
  88.1 20.5 %collective-permute-start.13 = (bf16[256,1024]{1,0:T(8,128)(2,1)S(1)}, bf16[256,1024]{1,0:T(8,128)(2,1)S(1)}, u32[]{:S(2)}, u32[]{:S(2)}) collective-permute-start(bf16[256,1024]{1,0:T(8,128)(2,1)S(1)} %collective-permute-done.10.vb_ref), channel_id=1, source_target_pairs={{4,8},{8,12},{5,9},{9,13},{6,10},{10,14},{7,11},{11,15},{20,24},{2... | collective-permute-start | bytes 1572872 | tf_op jit(solution)/shard_map/ppermute | solution.py:355
  88.8 19.8 %collective-permute-start.14 = (bf16[256,1024]{1,0:T(8,128)(2,1)S(1)}, bf16[256,1024]{1,0:T(8,128)(2,1)S(1)}, u32[]{:S(2)}, u32[]{:S(2)}) collective-permute-start(bf16[256,1024]{1,0:T(8,128)(2,1)S(1)} %collective-permute-done.11.va_ref), channel_id=1, source_target_pairs={{4,0},{8,4},{5,1},{9,5},{6,2},{10,6},{7,3},{11,7},{20,16},{24,20},... | collective-permute-start | bytes 1572872 | tf_op jit(solution)/shard_map/ppermute | solution.py:355
  (1 other events, 0.7 us)

commit v5 on v4

--- a/solution.py
+++ b/solution.py
@@ -171,26 +171,32 @@
             outs[r][...] = chosen.astype(BF16)
 
 
-def weigh_kernel(block, shards, where, pattern, starts, q_ref, nb_ref, na_ref, fb_ref, fa_ref, *refs):
+def weigh_kernel(shards, where, pattern, starts, q_ref, nb_ref, na_ref, fb_ref, fa_ref, *refs):
     acc_in, top_in, sum_in, acc_ref, wb_ref, wa_ref, wf_ref, sums_ref = refs
     behind = where[0] >= 2
-    far_live = [slot_live(where, pattern, shards, 1, side, block) for side in range(2)]
-    live = [slot_live(where, pattern, shards, 0, side, block) for side in range(2)]
-    live.append((behind & far_live[0]) | (jnp.logical_not(behind) & far_live[1]))
-    bias = [jnp.where(on, 0.0, -jnp.inf) for on in live]
-    pieces = sums_ref.shape[0] // 2
-    piece = BLK // pieces
+    blocks = q_ref.shape[0] // BLK
+    bias = []
+    for block in range(blocks):
+        far_live = [slot_live(where, pattern, shards, 1, side, block) for side in range(2)]
+        live = [slot_live(where, pattern, shards, 0, side, block) for side in range(2)]
+        live.append((behind & far_live[0]) | (jnp.logical_not(behind) & far_live[1]))
+        bias.append([jnp.where(on, 0.0, -jnp.inf) for on in live])
+    piece = q_ref.shape[0] // PIECES
     place = lax.broadcasted_iota(jnp.int32, (piece, HD), 0)
-    firsts = [place < split_of(where, starts, block * pieces + p) for p in range(pieces)]
+    firsts = [place < split_of(where, starts, p) for p in range(PIECES)]
     lanes = [slice(i * HD, (i + 1) * HD) for i in range(BLK // HD)]
     for h in range(q_ref.shape[1] // HD):
         head = slice(h * HD, (h + 1) * HD)
-        keys = [nb_ref[:, head], na_ref[:, head], jnp.where(behind, fb_ref[:, head], fa_ref[:, head])]
-        for p in range(pieces):
+        for p in range(PIECES):
             rows = slice(p * piece, (p + 1) * piece)
+            block = p * piece // BLK
+            if p * piece % BLK == 0:
+                held = slice(block * BLK, (block + 1) * BLK)
+                far = jnp.where(behind, fb_ref[held, head], fa_ref[held, head])
+                keys = [nb_ref[held, head], na_ref[held, head], far]
             q = q_ref[rows, head]
             scores = []
-            for k, low in zip(keys, bias):
+            for k, low in zip(keys, bias[block]):
                 s = dot_t(q, k)
                 scores += [s[:, part] * SCALE + low for part in lanes]
             old = top_in[rows, head]
@@ -259,25 +265,27 @@
         out_ref[target] = jnp.concatenate(rows, axis=0).astype(BF16)
 
 
-def pool_kernel(got_ref, out_ref):
-    got = [got_ref[s].astype(F32) for s in range(4)]
-    for s in range(4):
-        out_ref[0, s] = (got[s][:2] + got[s ^ 2][2:]).astype(BF16)
-
-
 def context_kernel(block, where, acc_ref, w_ref, vb_ref, va_ref, *refs):
-    out_ref, stage, sem = refs[-3:]
+    stage, sem = refs[-2:]
+    if len(refs) == 3:
+        out_ref = refs[0]
+    else:
+        got_ref, _, out_ref, pooled_ref = refs[:4]
     behind = where[0] >= 2
     copies = []
     for h in range(acc_ref.shape[1] // HD):
         head = pl.ds(h * HD, HD)
         v = jnp.where(behind, vb_ref[:, head], va_ref[:, head])
-        stage[:, head] = (acc_ref[:, head] + dot(w_ref[:, pl.ds(h * BLK, BLK)], v)).astype(BF16)
+        stage[:, head] = (acc_ref[:, head] + dot(w_ref[pl.ds(block * BLK, BLK), pl.ds(h * BLK, BLK)], v)).astype(BF16)
         if h % 2:
             pair = pl.ds((h - 1) * HD, 2 * HD)
             copy = pltpu.make_async_copy(stage.at[:, pair], out_ref.at[pl.ds(block * BLK, BLK), pair], sem.at[h // 2])
             copy.start()
             copies.append(copy)
+    if len(refs) > 3:
+        got = [got_ref[s].astype(F32) for s in range(4)]
+        for s in range(4):
+            pooled_ref[0, s] = (got[s][:2] + got[s ^ 2][2:]).astype(BF16)
     for copy in copies:
         copy.wait()
 
@@ -302,39 +310,40 @@
     return 2 if heads % 2 == 0 else 1
 
 
-def own_call(queries, keys, values, block=None):
+def own_call(queries, keys, values):
     rows, columns = queries.shape
     heads = columns // HD
     wide = step_of(heads) * HD
-    here = rows if block is None else BLK
     return pl.pallas_call(
         own_kernel,
         grid=(columns // wide,),
-        in_specs=[pl.BlockSpec((here, wide), lambda h: (block or 0, h))] + [spec(rows, wide)] * 2,
-        out_specs=[spec(here, wide)] * 3,
-        out_shape=(shape(here, columns),) * 3,
+        in_specs=[spec(rows, wide)] * 3,
+        out_specs=[spec(rows, wide)] * 3,
+        out_shape=(shape(rows, columns),) * 3,
         compiler_params=PARAMS,
         cost_estimate=pl.CostEstimate(
-            flops=4 * here * columns * rows, bytes_accessed=18 * here * columns, transcendentals=heads * here * rows
+            flops=4 * rows * columns * rows, bytes_accessed=18 * rows * columns, transcendentals=heads * rows * rows
         ),
         name="own",
     )(queries, keys, values)
 
 
-def latent_call(where, doc_starts, queries, latent_keys, latent_values):
+def latent_call(where, doc_starts, queries, latent_keys, latent_values, first=0, last=None):
     rows, columns = queries.shape
     latents = latent_keys.shape[0]
-    heads = columns // HD
-    wide = step_of(heads) * HD
+    wide = step_of(columns // HD) * HD
+    steps = (last or columns // wide) - first
     return pl.pallas_call(
         latent_kernel,
-        grid=(columns // wide,),
-        in_specs=smem(2) + [spec(rows, wide)] + [spec(latents, wide)] * 2,
+        grid=(steps,),
+        in_specs=smem(2) + [pl.BlockSpec((size, wide), lambda h: (0, h + first)) for size in (rows, latents, latents)],
         out_specs=spec(2 * PIECES, wide),
-        out_shape=shape(2 * PIECES, columns),
+        out_shape=shape(2 * PIECES, steps * wide),
         compiler_params=PARAMS,
         cost_estimate=pl.CostEstimate(
-            flops=4 * rows * columns * latents, bytes_accessed=6 * rows * columns, transcendentals=heads * rows * latents
+            flops=4 * rows * steps * wide * latents * (1 if first == 0 else 10),
+            bytes_accessed=6 * rows * steps * wide,
+            transcendentals=steps * wide // HD * rows * latents,
         ),
         name="latent",
     )(where, doc_starts, queries, latent_keys, latent_values)
@@ -366,16 +375,16 @@
     def row_spec(block, width=wide):
         return pl.BlockSpec((BLK, width), lambda h: (block, h))
 
-    def weigh(block, near_keys, far_keys, state):
+    def weigh(near_keys, far_keys, state):
         return pl.pallas_call(
-            functools.partial(weigh_kernel, block, 4),
+            functools.partial(weigh_kernel, 4),
             grid=(heads // step,),
-            in_specs=smem(3) + [row_spec(block)] + [row_spec(0)] * 7,
-            out_specs=[row_spec(0)] + [row_spec(0, step * BLK)] * 3 + [spec(docs, step * BLK)],
-            out_shape=(shape(BLK, columns),) + (shape(BLK, slots, BF16),) * 3 + (shape(docs, slots),),
+            in_specs=smem(3) + [spec(rows, wide)] * 8,
+            out_specs=[spec(rows, wide)] + [spec(rows, step * BLK)] * 3 + [spec(2 * PIECES, step * BLK)],
+            out_shape=(shape(rows, columns),) + (shape(rows, slots, BF16),) * 3 + (shape(2 * PIECES, slots),),
             compiler_params=PARAMS,
             cost_estimate=pl.CostEstimate(
-                flops=6 * BLK * columns * BLK, bytes_accessed=22 * BLK * columns, transcendentals=3 * heads * BLK * BLK
+                flops=6 * rows * columns * BLK, bytes_accessed=22 * rows * columns, transcendentals=3 * heads * rows * BLK
             ),
             name="weigh",
         )(where, pattern, doc_starts, queries, *near_keys, *far_keys, *state)
@@ -384,7 +393,11 @@
         return pl.pallas_call(
             functools.partial(mix_kernel, block),
             grid=(heads // step,),
-            in_specs=smem(2) + [row_spec(0)] + [row_spec(0, step * BLK)] * 2 + [row_spec(0)] * 2 + [spec(2 * PIECES, wide)],
+            in_specs=smem(2)
+            + [row_spec(block)]
+            + [row_spec(block, step * BLK)] * 2
+            + [row_spec(0)] * 2
+            + [spec(2 * PIECES, wide)],
             out_specs=[row_spec(0), spec(docs, wide)],
             out_shape=(shape(BLK, columns), shape(docs, columns)),
             compiler_params=PARAMS,
@@ -392,40 +405,43 @@
             name="mix",
         )(where, doc_starts, acc, *weights, *near_vals, lat)
 
-    def finish(block, acc, weights, far_vals, context):
-        held = [] if context is None else [context]
+    def finish(block, acc, weights, far_vals, held):
+        context = shape(rows, columns, BF16)
+        pooled = jax.ShapeDtypeStruct((1, 4, 2, columns), BF16)
+        anywhere = pl.BlockSpec(memory_space=pl.ANY)
+        whole = pl.BlockSpec(memory_space=pltpu.VMEM)
         return pl.pallas_call(
             functools.partial(context_kernel, block),
-            in_specs=smem(1) + vmem(4) + [pl.BlockSpec(memory_space=pl.ANY)] * len(held),
-            out_specs=pl.BlockSpec(memory_space=pl.ANY),
-            out_shape=shape(rows, columns, BF16),
+            in_specs=smem(1) + vmem(4) + ([whole, anywhere] if held else []),
+            out_specs=[anywhere, whole] if held else anywhere,
+            out_shape=(context, pooled) if held else context,
             scratch_shapes=[pltpu.VMEM((BLK, columns), BF16), pltpu.SemaphoreType.DMA((heads // 2,))],
-            input_output_aliases={5: 0} if held else {},
+            input_output_aliases={6: 0} if held else {},
             compiler_params=PARAMS,
             cost_estimate=pl.CostEstimate(flops=2 * BLK * columns * BLK, bytes_accessed=14 * BLK * columns, transcendentals=0),
             name="finish",
         )(where, acc, weights, *far_vals, *held)
 
-    near_keys = [near(part(keys, 0))]
-    lat = latent_call(where, doc_starts, queries, latent_keys, latent_values)
-    lat, late_keys, late_vals = lax.optimization_barrier((lat, keys, values))
-    near_keys.append(near(part(late_keys, 1)))
-    state = own_call(queries, keys, values, 0)
-    near_keys[0], state = lax.optimization_barrier((near_keys[0], state))
-    near_keys[1], late_queries = lax.optimization_barrier((near_keys[1], queries))
-    far_keys = [onward(pair) for pair in near_keys]
-    late_state = own_call(late_queries, keys, values, 1)
-    late_vals, late_state = lax.optimization_barrier((late_vals, late_state))
+    near_keys = near(keys)
+    lats = [latent_call(where, doc_starts, queries, latent_keys, latent_values, 0, 1)]
+    lats, late_vals, late_queries = lax.optimization_barrier((lats, values, queries))
     near_vals = [near(part(late_vals, 0))]
-    out = [weigh(0, near_keys[0], far_keys[0], state)]
-    out[0], last_vals = lax.optimization_barrier((out[0], late_vals))
-    near_vals.append(near(part(last_vals, 1)))
-    out.append(weigh(1, near_keys[1], far_keys[1], late_state))
-    sums = jnp.concatenate([o[4] for o in out])
-    near_vals[0], out[1], sums = lax.optimization_barrier((near_vals[0], out[1], sums))
+    state = own_call(late_queries, keys, values)
+    near_keys, state = lax.optimization_barrier((near_keys, state))
+    far_keys = onward(near_keys)
+    near_vals[0], late_vals, late_queries = lax.optimization_barrier((near_vals[0], late_vals, late_queries))
+    lats.append(latent_call(where, doc_starts, late_queries, latent_keys, latent_values, 1))
+    lat = jnp.concatenate(lats, axis=1)
+    near_vals.append(near(part(late_vals, 1)))
+    far_keys, lat = lax.optimization_barrier((far_keys, lat))
+    weighed = weigh(near_keys, far_keys, state)
+    near_vals[1], weighed = lax.optimization_barrier((near_vals[1], weighed))
+    acc, *near_weights, far_weights, sums = weighed
     sums = move(sums, [(s, s ^ 2) for s in range(4)])
-    mixed = [mix(0, out[0][0], out[0][1:3], near_vals[0], lat)]
     far_vals = [onward(near_vals[0])]
+    mixed = [mix(0, acc, near_weights, near_vals[0], lat)]
+    near_vals[1], mixed[0] = lax.optimization_barrier((near_vals[1], mixed[0]))
+    far_vals.append(onward(near_vals[1]))
     parts = pl.pallas_call(
         part_kernel,
         grid=(heads // step,),
@@ -433,14 +449,11 @@
         out_specs=spec(2 * PIECES, wide),
         out_shape=shape(2 * PIECES, columns),
         compiler_params=PARAMS,
-        cost_estimate=pl.CostEstimate(flops=32 * BLK * columns, bytes_accessed=3 * rows * columns, transcendentals=0),
+        cost_estimate=pl.CostEstimate(flops=64 * rows * columns * 128, bytes_accessed=3 * rows * columns, transcendentals=0),
         name="part",
     )(where, doc_starts, sums, values)
-    near_vals[1], parts = lax.optimization_barrier((near_vals[1], parts))
-    far_vals.append(onward(near_vals[1]))
-    mixed.append(mix(1, out[1][0], out[1][1:3], near_vals[1], lat))
-    acc = [m[0] for m in mixed]
-    far_weights = [o[3] for o in out]
+    acc, parts = lax.optimization_barrier((acc, parts))
+    mixed.append(mix(1, acc, near_weights, near_vals[1], lat))
     sent = pl.pallas_call(
         route_kernel,
         in_specs=smem(2) + vmem(3),
@@ -449,19 +462,11 @@
         compiler_params=PARAMS,
         name="route",
     )(where, doc_owner, parts, *[m[1] for m in mixed])
-    context = finish(0, acc[0], far_weights[0], far_vals[0], None)
+    mixed[0], parts = lax.optimization_barrier((mixed[0], parts))
+    context = finish(0, mixed[0][0], far_weights, far_vals[0], [])
     sent, context = lax.optimization_barrier((sent, context))
     got = lax.all_to_all(sent, "seq", split_axis=0, concat_axis=0, tiled=True)
-    pooled = pl.pallas_call(
-        pool_kernel,
-        in_specs=vmem(1),
-        out_specs=pl.BlockSpec(memory_space=pltpu.VMEM),
-        out_shape=jax.ShapeDtypeStruct((1, 4, 2, columns), BF16),
-        compiler_params=PARAMS,
-        name="pool",
-    )(got)
-    context = finish(1, acc[1], far_weights[1], far_vals[1], context)
-    return context, pooled
+    return finish(1, mixed[1][0], far_weights, far_vals[1], [got, context])
 
 
 def body(queries, keys, values, latent_keys, latent_values, pattern, doc_starts, doc_owner):

time: 110 us -> 109 us (level)
  waiting for transfers between devices: 28.6 us -> 43.5 us
  starting transfers between devices: 32.6 us -> 23.5 us
  Pallas kernels: 31.5 us -> 28.5 us
  blocking collectives: 10.9 us -> 8.01 us
    ppermute x17 -> x13, waiting for transfers between devices: 28.6 us -> 43.5 us  [move(): return lax.ppermute(value, 'seq', pairs)]
    ppermute x17 -> x13, starting transfers between devices: 32.6 us -> 23.5 us  [move(): return lax.ppermute(value, 'seq', pairs)]
    pallas_call x6 -> x4, Pallas kernels: 22.8 us -> 19.2 us  [the longest x1 8.14 us: weigh(): pl.pallas_call(functools.partial(weigh_kernel, 4), grid=(heads // step,),...]
    all_to_all x1, blocking collectives: 10.9 us -> 8.01 us  [four_shards(): got = lax.all_to_all(sent, 'seq', split_axis=0, concat_axis=0, tiled=True)]
    slice x4 -> x2, local copies, waits for them, and re-layouts: 1.27 us -> 0.07 us  [part(): return array[block * BLK:(block + 1) * BLK]]
    unnamed x16 -> x22, local copies, waits for them, and re-layouts: 3.76 us -> 4.36 us
  transfers between devices with their start and end apart: 17 -> 13, of which waited for: 4 -> 7; matrix products, arithmetic and copies ran while one was open for 0% -> 0% of each run, Pallas kernels for 28% -> 24%
where the time goes in v5:
time: 109 us
  waiting for transfers between devices  43.5 us (40%)
  Pallas kernels  28.5 us (26%)
  starting transfers between devices  23.5 us (22%)
  blocking collectives  8.01 us (7%)
  local copies, waits for them, and re-layouts  4.43 us (4%)
    ppermute x13, waiting for transfers between devices, move(): return lax.ppermute(value, 'seq', pairs)  43.5 us
    ppermute x13, starting transfers between devices, move(): return lax.ppermute(value, 'seq', pairs)  23.5 us
    pallas_call x1, Pallas kernels, weigh(): pl.pallas_call(functools.partial(weigh_kernel, 4), grid=(heads // step,),...  8.14 us
    all_to_all x1, blocking collectives, four_shards(): got = lax.all_to_all(sent, 'seq', split_axis=0, concat_axis=0, tiled=True)  8.01 us
    pallas_call x2, Pallas kernels, latent_call(): pl.pallas_call(latent_kernel, grid=(steps,), in_specs=smem(2) + [pl.Block...  5.81 us
    pallas_call x1, Pallas kernels, own_call(): pl.pallas_call(own_kernel, grid=(columns // wide,), in_specs=[spec(rows,...  5.27 us
    pallas_call x2, Pallas kernels, mix(): pl.pallas_call(functools.partial(mix_kernel, block), grid=(heads // step,...  4.38 us
    unnamed x22, local copies, waits for them, and re-layouts  4.36 us
  transfers between devices with their start and end apart: 13, of which 7 were waited for; matrix products, arithmetic and copies ran while one was open for 0% of the time, Pallas kernels for 24%

profile of v5, /device:TPU:0, one launch (start us, length us, event | category | flops | bytes accessed | tf_op | source)
XLA Modules:
  0.0 108.9 jit_solution(11345740394870518062)
XLA Ops:
  0.6 5.0 %collective-permute-start.4 = (bf16[512,1024]{1,0:T(8,128)(2,1)}, bf16[512,1024]{1,0:T(8,128)(2,1)S(1)}, u32[]{:S(2)}, u32[]{:S(2)}) collective-permute-start(bf16[512,1024]{1,0:T(8,128)(2,1)} %k_ref.1), channel_id=1, source_target_pairs={{0,4},{4,8},{8,12},{1,5},{5,9},{9,13},{2,6},{6,10},{10,14},{3,7},{... | collective-permute-start | bytes 3145736 | tf_op jit(solution)/shard_map/ppermute | solution.py:364
  5.6 1.3 %collective-permute-start.5 = (bf16[512,1024]{1,0:T(8,128)(2,1)}, bf16[512,1024]{1,0:T(8,128)(2,1)S(1)}, u32[]{:S(2)}, u32[]{:S(2)}) collective-permute-start(bf16[512,1024]{1,0:T(8,128)(2,1)} %k_ref.1), channel_id=1, source_target_pairs={{4,0},{8,4},{12,8},{5,1},{9,5},{13,9},{6,2},{10,6},{14,10},{7,3},{... | collective-permute-start | bytes 3145736 | tf_op jit(solution)/shard_map/ppermute | solution.py:364
  11.3 1.6 %latent.2 = f32[8,256]{1,0:T(8,128)S(1)} custom-call(s32[1]{0:T(128)} %bitcast.where, s32[32]{0:T(128)S(1)} %copy-done.6, bf16[512,1024]{1,0:T(8,128)(2,1)S(1)} %copy-done, bf16[512,1024]{1,0:T(8,128)(2,1)S(1)} %copy-done.1, bf16[512,1024]{1,0:T(8,128)(2,1)S(1)} %copy-done.3), custom_call_target="tpu_custom_call" | custom-call | flops 268435456 | bytes 786432 | tf_op jit(solution)/shard_map/latent/pallas_call | solution.py:336
  13.0 4.7 %collective-permute-start = (bf16[256,1024]{1,0:T(8,128)(2,1)S(1)}, bf16[256,1024]{1,0:T(8,128)(2,1)S(1)}, u32[]{:S(2)}, u32[]{:S(2)}) collective-permute-start(bf16[256,1024]{1,0:T(8,128)(2,1)S(1)} %slice.6), channel_id=1, source_target_pairs={{0,4},{4,8},{8,12},{1,5},{5,9},{9,13},{2,6},{6,10},{10,14},{3,7},{... | collective-permute-start | bytes 1572872 | tf_op jit(solution)/shard_map/ppermute | solution.py:364
  17.7 1.3 %collective-permute-start.1 = (bf16[256,1024]{1,0:T(8,128)(2,1)S(1)}, bf16[256,1024]{1,0:T(8,128)(2,1)S(1)}, u32[]{:S(2)}, u32[]{:S(2)}) collective-permute-start(bf16[256,1024]{1,0:T(8,128)(2,1)S(1)} %slice.6), channel_id=1, source_target_pairs={{4,0},{8,4},{12,8},{5,1},{9,5},{13,9},{6,2},{10,6},{14,10},{7,3},{... | collective-permute-start | bytes 1572872 | tf_op jit(solution)/shard_map/ppermute | solution.py:364
  19.0 5.3 %own.1 = (f32[512,1024]{1,0:T(8,128)S(1)}, f32[512,1024]{1,0:T(8,128)S(1)}, f32[512,1024]{1,0:T(8,128)S(1)}) custom-call(bf16[512,1024]{1,0:T(8,128)(2,1)S(1)} %copy-done, bf16[512,1024]{1,0:T(8,128)(2,1)S(1)} %copy-done.10, bf16[512,1024]{1,0:T(8,128)(2,1)S(1)} %copy-done.5), custom_call_target="tpu_custom_call" | custom-call | flops 1073741824 | bytes 9437184 | tf_op jit(solution)/shard_map/own/pallas_call | solution.py:317
  24.3 5.1 %collective-permute-done.4.nb_ref = bf16[512,1024]{1,0:T(8,128)(2,1)S(1)} collective-permute-done((bf16[512,1024]{1,0:T(8,128)(2,1)}, bf16[512,1024]{1,0:T(8,128)(2,1)S(1)}, u32[]{:S(2)}, u32[]{:S(2)}) %collective-permute-start.4) | collective-permute-done | bytes 1048608 | tf_op jit(solution)/shard_map/ppermute | solution.py:364
  29.4 4.4 %collective-permute-done.5.na_ref = bf16[512,1024]{1,0:T(8,128)(2,1)S(1)} collective-permute-done((bf16[512,1024]{1,0:T(8,128)(2,1)}, bf16[512,1024]{1,0:T(8,128)(2,1)S(1)}, u32[]{:S(2)}, u32[]{:S(2)}) %collective-permute-start.5) | collective-permute-done | bytes 1048608 | tf_op jit(solution)/shard_map/ppermute | solution.py:364
  34.5 1.3 %collective-permute-start.7 = (bf16[512,1024]{1,0:T(8,128)(2,1)S(1)}, bf16[512,1024]{1,0:T(8,128)(2,1)S(1)}, u32[]{:S(2)}, u32[]{:S(2)}) collective-permute-start(bf16[512,1024]{1,0:T(8,128)(2,1)S(1)} %collective-permute-done.5.na_ref), channel_id=1, source_target_pairs={{4,0},{8,4},{5,1},{9,5},{6,2},{10,6},{7,3},{11,7},{20,16},{24,20},... | collective-permute-start | bytes 3145736 | tf_op jit(solution)/shard_map/ppermute | solution.py:364
  35.8 3.6 %collective-permute-done.vb_ref = bf16[256,1024]{1,0:T(8,128)(2,1)S(1)} collective-permute-done((bf16[256,1024]{1,0:T(8,128)(2,1)S(1)}, bf16[256,1024]{1,0:T(8,128)(2,1)S(1)}, u32[]{:S(2)}, u32[]{:S(2)}) %collective-permute-start) | collective-permute-done | bytes 524320 | tf_op jit(solution)/shard_map/ppermute | solution.py:364
  39.4 5.6 %collective-permute-done.1.va_ref = bf16[256,1024]{1,0:T(8,128)(2,1)S(1)} collective-permute-done((bf16[256,1024]{1,0:T(8,128)(2,1)S(1)}, bf16[256,1024]{1,0:T(8,128)(2,1)S(1)}, u32[]{:S(2)}, u32[]{:S(2)}) %collective-permute-start.1) | collective-permute-done | bytes 524320 | tf_op jit(solution)/shard_map/ppermute | solution.py:364
  45.1 3.5 %collective-permute-start.2 = (bf16[256,1024]{1,0:T(8,128)(2,1)S(1)}, bf16[256,1024]{1,0:T(8,128)(2,1)S(1)}, u32[]{:S(2)}, u32[]{:S(2)}) collective-permute-start(bf16[256,1024]{1,0:T(8,128)(2,1)S(1)} %slice.7), channel_id=1, source_target_pairs={{0,4},{4,8},{8,12},{1,5},{5,9},{9,13},{2,6},{6,10},{10,14},{3,7},{... | collective-permute-start | bytes 1572872 | tf_op jit(solution)/shard_map/ppermute | solution.py:364
  48.6 1.3 %collective-permute-start.3 = (bf16[256,1024]{1,0:T(8,128)(2,1)S(1)}, bf16[256,1024]{1,0:T(8,128)(2,1)S(1)}, u32[]{:S(2)}, u32[]{:S(2)}) collective-permute-start(bf16[256,1024]{1,0:T(8,128)(2,1)S(1)} %slice.7), channel_id=1, source_target_pairs={{4,0},{8,4},{12,8},{5,1},{9,5},{13,9},{6,2},{10,6},{14,10},{7,3},{... | collective-permute-start | bytes 1572872 | tf_op jit(solution)/shard_map/ppermute | solution.py:364
  49.9 4.2 %latent.3 = f32[8,768]{1,0:T(8,128)S(1)} custom-call(s32[1]{0:T(128)} %bitcast.where, s32[32]{0:T(128)S(1)} %copy-done.7, bf16[512,1024]{1,0:T(8,128)(2,1)S(1)} %copy-done, bf16[512,1024]{1,0:T(8,128)(2,1)S(1)} %copy-done.2, bf16[512,1024]{1,0:T(8,128)(2,1)S(1)} %copy-done.4), custom_call_target="tpu_custom_call" | custom-call | flops 8053063680 | bytes 2359296 | tf_op jit(solution)/shard_map/latent/pallas_call | solution.py:336
  54.8 1.3 %collective-permute-start.12 = (bf16[256,1024]{1,0:T(8,128)(2,1)S(1)}, bf16[256,1024]{1,0:T(8,128)(2,1)S(1)}, u32[]{:S(2)}, u32[]{:S(2)}) collective-permute-start(bf16[256,1024]{1,0:T(8,128)(2,1)S(1)} %collective-permute-done.1.va_ref), channel_id=1, source_target_pairs={{4,0},{8,4},{5,1},{9,5},{6,2},{10,6},{7,3},{11,7},{20,16},{24,20},... | collective-permute-start | bytes 1572872 | tf_op jit(solution)/shard_map/ppermute | solution.py:364
  56.1 11.4 %collective-permute-done.7.fa_ref = bf16[512,1024]{1,0:T(8,128)(2,1)S(1)} collective-permute-done((bf16[512,1024]{1,0:T(8,128)(2,1)S(1)}, bf16[512,1024]{1,0:T(8,128)(2,1)S(1)}, u32[]{:S(2)}, u32[]{:S(2)}) %collective-permute-start.7) | collective-permute-done | bytes 1048608 | tf_op jit(solution)/shard_map/ppermute | solution.py:364
  67.5 8.1 %weigh.1 = (f32[512,1024]{1,0:T(8,128)S(1)}, bf16[512,2048]{1,0:T(8,128)(2,1)S(1)}, bf16[512,2048]{1,0:T(8,128)(2,1)S(1)}, bf16[512,2048]{1,0:T(8,128)(2,1)S(1)}, f32[8,2048]{1,0:T(8,128)S(1)}) custom-call(s32[1]{0:T(128)} %bitcast.where, s32[2,8]{1,0:T(2,128)S(1)} %copy-done.8, s32[32]{0:T(128)S(1)} %copy-done.7, bf16[512,1024]{1,0:T(8,128)(2,1)S(1)} %copy-done, ...), custom_call_target="tpu_custom_call" | custom-call | flops 805306368 | bytes 11534336 | tf_op jit(solution)/shard_map/weigh/pallas_call | solution.py:379
  75.7 3.1 %collective-permute-done.3.va_ref = bf16[256,1024]{1,0:T(8,128)(2,1)S(1)} collective-permute-done((bf16[256,1024]{1,0:T(8,128)(2,1)S(1)}, bf16[256,1024]{1,0:T(8,128)(2,1)S(1)}, u32[]{:S(2)}, u32[]{:S(2)}) %collective-permute-start.3) | collective-permute-done | bytes 524320 | tf_op jit(solution)/shard_map/ppermute | solution.py:364
  79.3 2.2 %mix.2 = (f32[256,1024]{1,0:T(8,128)S(1)}, f32[4,1024]{1,0:T(4,128)S(1)}) custom-call(s32[1]{0:T(128)} %bitcast.where, s32[32]{0:T(128)S(1)} %copy-done.7, f32[512,1024]{1,0:T(8,128)S(1)} %get-tuple-element.67.acc_in, bf16[512,2048]{1,0:T(8,128)(2,1)S(1)} %get-tuple-element.68.wb_ref, bf16[512,2048]{1,0:T(8,128)(2,1)S(1)} %get-tuple-element.69.wa_ref, ...), custom_call_target="tpu_custom_call" | custom-call | flops 268435456 | bytes 5242880 | tf_op jit(solution)/shard_map/mix/pallas_call | solution.py:393
  81.4 1.3 %collective-permute-start.10 = (bf16[256,1024]{1,0:T(8,128)(2,1)S(1)}, bf16[256,1024]{1,0:T(8,128)(2,1)S(1)}, u32[]{:S(2)}, u32[]{:S(2)}) collective-permute-start(bf16[256,1024]{1,0:T(8,128)(2,1)S(1)} %collective-permute-done.3.va_ref), channel_id=1, source_target_pairs={{4,0},{8,4},{5,1},{9,5},{6,2},{10,6},{7,3},{11,7},{20,16},{24,20},... | collective-permute-start | bytes 1572872 | tf_op jit(solution)/shard_map/ppermute | solution.py:364
  83.5 10.3 %collective-permute-done.8.sums_ref = f32[8,2048]{1,0:T(8,128)S(1)} collective-permute-done((f32[8,2048]{1,0:T(8,128)S(1)}, f32[8,2048]{1,0:T(8,128)S(1)}, u32[]{:S(2)}, u32[]{:S(2)}) %collective-permute-start.8) | collective-permute-done | bytes 65568 | tf_op jit(solution)/shard_map/ppermute | solution.py:364
  95.0 2.2 %mix.3 = (f32[256,1024]{1,0:T(8,128)S(1)}, f32[4,1024]{1,0:T(4,128)S(1)}) custom-call(s32[1]{0:T(128)} %bitcast.where, s32[32]{0:T(128)S(1)} %copy-done.7, f32[512,1024]{1,0:T(8,128)S(1)} %get-tuple-element.67.acc_in, bf16[512,2048]{1,0:T(8,128)(2,1)S(1)} %get-tuple-element.68.wb_ref, bf16[512,2048]{1,0:T(8,128)(2,1)S(1)} %get-tuple-element.69.wa_ref, ...), custom_call_target="tpu_custom_call" | custom-call | flops 268435456 | bytes 5242880 | tf_op jit(solution)/shard_map/mix/pallas_call | solution.py:393
  99.1 8.0 %all_to_all.5.refs_0_ = bf16[4,4,1024]{2,1,0:T(4,128)(2,1)S(1)} all-to-all(bf16[4,4,1024]{2,1,0:T(4,128)(2,1)S(1)} %route.1), channel_id=1, replica_groups=mesh['groups'=2,'seq'=4,'head'=2,'sub'=2] {'seq'}, dimensions={0} | all-to-all | bytes 65536 | tf_op jit(solution)/shard_map/all_to_all | solution.py:468
  107.1 1.8 %finish.3 = (bf16[512,1024]{1,0:T(8,128)(2,1)}, bf16[1,4,2,1024]{3,2,1,0:T(2,128)(2,1)}) custom-call(s32[1]{0:T(128)} %bitcast.where, f32[256,1024]{1,0:T(8,128)S(1)} %get-tuple-element.79.acc_ref, bf16[512,2048]{1,0:T(8,128)(2,1)S(1)} %get-tuple-element.80.w_ref, ...), custom_call_target="tpu_custom_call", output_to_operand_aliasing={{0}: (6, {})} | custom-call | flops 134217728 | bytes 3670016 | tf_op jit(solution)/shard_map/finish/pallas_call | solution.py:413
  (38 shorter events, 10.1 us)
Async XLA Ops:
  0.6 28.8 %collective-permute-start.4 = (bf16[512,1024]{1,0:T(8,128)(2,1)}, bf16[512,1024]{1,0:T(8,128)(2,1)S(1)}, u32[]{:S(2)}, u32[]{:S(2)}) collective-permute-start(bf16[512,1024]{1,0:T(8,128)(2,1)} %k_ref.1), channel_id=1, source_target_pairs={{0,4},{4,8},{8,12},{1,5},{5,9},{9,13},{2,6},{6,10},{10,14},{3,7},{... | collective-permute-start | bytes 3145736 | tf_op jit(solution)/shard_map/ppermute | solution.py:364
  5.6 28.2 %collective-permute-start.5 = (bf16[512,1024]{1,0:T(8,128)(2,1)}, bf16[512,1024]{1,0:T(8,128)(2,1)S(1)}, u32[]{:S(2)}, u32[]{:S(2)}) collective-permute-start(bf16[512,1024]{1,0:T(8,128)(2,1)} %k_ref.1), channel_id=1, source_target_pairs={{4,0},{8,4},{12,8},{5,1},{9,5},{13,9},{6,2},{10,6},{14,10},{7,3},{... | collective-permute-start | bytes 3145736 | tf_op jit(solution)/shard_map/ppermute | solution.py:364
  6.9 1.2 %copy-start = (bf16[512,1024]{1,0:T(8,128)(2,1)S(1)}, bf16[512,1024]{1,0:T(8,128)(2,1)}, u32[]{:S(2)}) copy-start(bf16[512,1024]{1,0:T(8,128)(2,1)} %q_ref.5) | copy-start | bytes 3145732
  8.2 1.2 %copy-start.1 = (bf16[512,1024]{1,0:T(8,128)(2,1)S(1)}, bf16[512,1024]{1,0:T(8,128)(2,1)}, u32[]{:S(2)}) copy-start(bf16[512,1024]{1,0:T(8,128)(2,1)} %lk_ref.3) | copy-start | bytes 3145732
  9.4 1.2 %copy-start.3 = (bf16[512,1024]{1,0:T(8,128)(2,1)S(1)}, bf16[512,1024]{1,0:T(8,128)(2,1)}, u32[]{:S(2)}) copy-start(bf16[512,1024]{1,0:T(8,128)(2,1)} %lv_ref.3) | copy-start | bytes 3145732
  10.6 0.7 copy-start.6
  11.3 1.7 %copy-start.5 = (bf16[512,1024]{1,0:T(8,128)(2,1)S(1)}, bf16[512,1024]{1,0:T(8,128)(2,1)}, u32[]{:S(2)}) copy-start(bf16[512,1024]{1,0:T(8,128)(2,1)} %v_ref.3) | copy-start | bytes 3145732
  11.3 7.8 %copy-start.10 = (bf16[512,1024]{1,0:T(8,128)(2,1)S(1)}, bf16[512,1024]{1,0:T(8,128)(2,1)}, u32[]{:S(2)}) copy-start(bf16[512,1024]{1,0:T(8,128)(2,1)} %k_ref.1) | copy-start | bytes 3145732
  13.0 36.9 %copy-start.2 = (bf16[512,1024]{1,0:T(8,128)(2,1)S(1)}, bf16[512,1024]{1,0:T(8,128)(2,1)}, u32[]{:S(2)}) copy-start(bf16[512,1024]{1,0:T(8,128)(2,1)} %lk_ref.3) | copy-start | bytes 3145732
  13.0 36.9 %copy-start.4 = (bf16[512,1024]{1,0:T(8,128)(2,1)S(1)}, bf16[512,1024]{1,0:T(8,128)(2,1)}, u32[]{:S(2)}) copy-start(bf16[512,1024]{1,0:T(8,128)(2,1)} %lv_ref.3) | copy-start | bytes 3145732
  13.0 36.9 %copy-start.7 = (s32[32]{0:T(128)S(1)}, s32[32]{0:T(128)}, u32[]{:S(2)}) copy-start(s32[32]{0:T(128)} %starts.11) | copy-start | bytes 388
  13.0 26.4 %collective-permute-start = (bf16[256,1024]{1,0:T(8,128)(2,1)S(1)}, bf16[256,1024]{1,0:T(8,128)(2,1)S(1)}, u32[]{:S(2)}, u32[]{:S(2)}) collective-permute-start(bf16[256,1024]{1,0:T(8,128)(2,1)S(1)} %slice.6), channel_id=1, source_target_pairs={{0,4},{4,8},{8,12},{1,5},{5,9},{9,13},{2,6},{6,10},{10,14},{3,7},{... | collective-permute-start | bytes 1572872 | tf_op jit(solution)/shard_map/ppermute | solution.py:364
  17.7 27.3 %collective-permute-start.1 = (bf16[256,1024]{1,0:T(8,128)(2,1)S(1)}, bf16[256,1024]{1,0:T(8,128)(2,1)S(1)}, u32[]{:S(2)}, u32[]{:S(2)}) collective-permute-start(bf16[256,1024]{1,0:T(8,128)(2,1)S(1)} %slice.6), channel_id=1, source_target_pairs={{4,0},{8,4},{12,8},{5,1},{9,5},{13,9},{6,2},{10,6},{14,10},{7,3},{... | collective-permute-start | bytes 1572872 | tf_op jit(solution)/shard_map/ppermute | solution.py:364
  33.8 21.0 %collective-permute-start.6 = (bf16[512,1024]{1,0:T(8,128)(2,1)S(1)}, bf16[512,1024]{1,0:T(8,128)(2,1)S(1)}, u32[]{:S(2)}, u32[]{:S(2)}) collective-permute-start(bf16[512,1024]{1,0:T(8,128)(2,1)S(1)} %collective-permute-done.4.nb_ref), channel_id=1, source_target_pairs={{4,8},{8,12},{5,9},{9,13},{6,10},{10,14},{7,11},{11,15},{20,24},{2... | collective-permute-start | bytes 3145736 | tf_op jit(solution)/shard_map/ppermute | solution.py:364
  34.5 33.0 %collective-permute-start.7 = (bf16[512,1024]{1,0:T(8,128)(2,1)S(1)}, bf16[512,1024]{1,0:T(8,128)(2,1)S(1)}, u32[]{:S(2)}, u32[]{:S(2)}) collective-permute-start(bf16[512,1024]{1,0:T(8,128)(2,1)S(1)} %collective-permute-done.5.na_ref), channel_id=1, source_target_pairs={{4,0},{8,4},{5,1},{9,5},{6,2},{10,6},{7,3},{11,7},{20,16},{24,20},... | collective-permute-start | bytes 3145736 | tf_op jit(solution)/shard_map/ppermute | solution.py:364
  45.1 22.4 %copy-start.8 = (s32[2,8]{1,0:T(2,128)S(1)}, s32[2,8]{1,0:T(2,128)}, u32[]{:S(2)}) copy-start(s32[2,8]{1,0:T(2,128)} %pattern.1) | copy-start | bytes 196
  45.1 30.6 %collective-permute-start.2 = (bf16[256,1024]{1,0:T(8,128)(2,1)S(1)}, bf16[256,1024]{1,0:T(8,128)(2,1)S(1)}, u32[]{:S(2)}, u32[]{:S(2)}) collective-permute-start(bf16[256,1024]{1,0:T(8,128)(2,1)S(1)} %slice.7), channel_id=1, source_target_pairs={{0,4},{4,8},{8,12},{1,5},{5,9},{9,13},{2,6},{6,10},{10,14},{3,7},{... | collective-permute-start | bytes 1572872 | tf_op jit(solution)/shard_map/ppermute | solution.py:364
  48.6 30.2 %collective-permute-start.3 = (bf16[256,1024]{1,0:T(8,128)(2,1)S(1)}, bf16[256,1024]{1,0:T(8,128)(2,1)S(1)}, u32[]{:S(2)}, u32[]{:S(2)}) collective-permute-start(bf16[256,1024]{1,0:T(8,128)(2,1)S(1)} %slice.7), channel_id=1, source_target_pairs={{4,0},{8,4},{12,8},{5,1},{9,5},{13,9},{6,2},{10,6},{14,10},{7,3},{... | collective-permute-start | bytes 1572872 | tf_op jit(solution)/shard_map/ppermute | solution.py:364
  54.1 43.8 %collective-permute-start.11 = (bf16[256,1024]{1,0:T(8,128)(2,1)S(1)}, bf16[256,1024]{1,0:T(8,128)(2,1)S(1)}, u32[]{:S(2)}, u32[]{:S(2)}) collective-permute-start(bf16[256,1024]{1,0:T(8,128)(2,1)S(1)} %collective-permute-done.vb_ref), channel_id=1, source_target_pairs={{4,8},{8,12},{5,9},{9,13},{6,10},{10,14},{7,11},{11,15},{20,24},{2... | collective-permute-start | bytes 1572872 | tf_op jit(solution)/shard_map/ppermute | solution.py:364
  54.8 43.1 %collective-permute-start.12 = (bf16[256,1024]{1,0:T(8,128)(2,1)S(1)}, bf16[256,1024]{1,0:T(8,128)(2,1)S(1)}, u32[]{:S(2)}, u32[]{:S(2)}) collective-permute-start(bf16[256,1024]{1,0:T(8,128)(2,1)S(1)} %collective-permute-done.1.va_ref), channel_id=1, source_target_pairs={{4,0},{8,4},{5,1},{9,5},{6,2},{10,6},{7,3},{11,7},{20,16},{24,20},... | collective-permute-start | bytes 1572872 | tf_op jit(solution)/shard_map/ppermute | solution.py:364
  78.8 15.0 %collective-permute-start.8 = (f32[8,2048]{1,0:T(8,128)S(1)}, f32[8,2048]{1,0:T(8,128)S(1)}, u32[]{:S(2)}, u32[]{:S(2)}) collective-permute-start(f32[8,2048]{1,0:T(8,128)S(1)} %get-tuple-element.66), channel_id=1, source_target_pairs={{0,8},{4,12},{8,0},{12,4},{1,9},{5,13},{9,1},{13,5},{2,10},{6,14},... | collective-permute-start | bytes 196616 | tf_op jit(solution)/shard_map/ppermute | solution.py:364
  81.4 25.7 %collective-permute-start.10 = (bf16[256,1024]{1,0:T(8,128)(2,1)S(1)}, bf16[256,1024]{1,0:T(8,128)(2,1)S(1)}, u32[]{:S(2)}, u32[]{:S(2)}) collective-permute-start(bf16[256,1024]{1,0:T(8,128)(2,1)S(1)} %collective-permute-done.3.va_ref), channel_id=1, source_target_pairs={{4,0},{8,4},{5,1},{9,5},{6,2},{10,6},{7,3},{11,7},{20,16},{24,20},... | collective-permute-start | bytes 1572872 | tf_op jit(solution)/shard_map/ppermute | solution.py:364
  82.7 24.4 %collective-permute-start.9 = (bf16[256,1024]{1,0:T(8,128)(2,1)S(1)}, bf16[256,1024]{1,0:T(8,128)(2,1)S(1)}, u32[]{:S(2)}, u32[]{:S(2)}) collective-permute-start(bf16[256,1024]{1,0:T(8,128)(2,1)S(1)} %collective-permute-done.2.vb_ref), channel_id=1, source_target_pairs={{4,8},{8,12},{5,9},{9,13},{6,10},{10,14},{7,11},{11,15},{20,24},{2... | collective-permute-start | bytes 1572872 | tf_op jit(solution)/shard_map/ppermute | solution.py:364
  95.0 2.2 %copy-start.9 = (s32[32]{0:T(128)S(1)}, s32[32]{0:T(128)}, u32[]{:S(2)}) copy-start(s32[32]{0:T(128)} %owners.1) | copy-start | bytes 388

commit v6 on v5

--- a/solution.py
+++ b/solution.py
@@ -13,7 +13,7 @@
 BLK = 256
 PIECES = 4
 SCALE = math.log2(math.e) / math.sqrt(HD)
-PARAMS = pltpu.CompilerParams(vmem_limit_bytes=24 * 1024 * 1024)
+PARAMS = pltpu.CompilerParams(vmem_limit_bytes=16 * 1024 * 1024)
 F32 = jnp.float32
 BF16 = jnp.bfloat16
 
@@ -187,6 +187,7 @@
     lanes = [slice(i * HD, (i + 1) * HD) for i in range(BLK // HD)]
     for h in range(q_ref.shape[1] // HD):
         head = slice(h * HD, (h + 1) * HD)
+        sums = [[] for _ in lanes]
         for p in range(PIECES):
             rows = slice(p * piece, (p + 1) * piece)
             block = p * piece // BLK
@@ -212,8 +213,13 @@
                 w = e * inverse
                 out[rows, first : first + HD] = w.astype(BF16)
                 if out is wf_ref:
-                    sums = [jnp.sum(x, axis=0, keepdims=True) for x in (jnp.where(firsts[p], w, 0.0), jnp.where(firsts[p], 0.0, w))]
-                    sums_ref[2 * p : 2 * p + 2, first : first + HD] = jnp.concatenate(sums, axis=0)
+                    sums[i % len(lanes)] += [
+                        jnp.sum(jnp.where(firsts[p], w, 0.0), axis=0, keepdims=True),
+                        jnp.sum(jnp.where(firsts[p], 0.0, w), axis=0, keepdims=True),
+                    ]
+        for i, found in enumerate(sums):
+            first = h * BLK + i * HD
+            sums_ref[:, first : first + HD] = jnp.concatenate(found, axis=0).astype(sums_ref.dtype)
 
 
 def doc_counts(split, piece, columns):
@@ -265,12 +271,14 @@
         out_ref[target] = jnp.concatenate(rows, axis=0).astype(BF16)
 
 
+def pool_kernel(got_ref, out_ref):
+    got = [got_ref[s].astype(F32) for s in range(4)]
+    for s in range(4):
+        out_ref[0, s] = (got[s][:2] + got[s ^ 2][2:]).astype(BF16)
+
+
 def context_kernel(block, where, acc_ref, w_ref, vb_ref, va_ref, *refs):
-    stage, sem = refs[-2:]
-    if len(refs) == 3:
-        out_ref = refs[0]
-    else:
-        got_ref, _, out_ref, pooled_ref = refs[:4]
+    out_ref, stage, sem = refs[-3:]
     behind = where[0] >= 2
     copies = []
     for h in range(acc_ref.shape[1] // HD):
@@ -282,10 +290,6 @@
             copy = pltpu.make_async_copy(stage.at[:, pair], out_ref.at[pl.ds(block * BLK, BLK), pair], sem.at[h // 2])
             copy.start()
             copies.append(copy)
-    if len(refs) > 3:
-        got = [got_ref[s].astype(F32) for s in range(4)]
-        for s in range(4):
-            pooled_ref[0, s] = (got[s][:2] + got[s ^ 2][2:]).astype(BF16)
     for copy in copies:
         copy.wait()
 
@@ -381,7 +385,7 @@
             grid=(heads // step,),
             in_specs=smem(3) + [spec(rows, wide)] * 8,
             out_specs=[spec(rows, wide)] + [spec(rows, step * BLK)] * 3 + [spec(2 * PIECES, step * BLK)],
-            out_shape=(shape(rows, columns),) + (shape(rows, slots, BF16),) * 3 + (shape(2 * PIECES, slots),),
+            out_shape=(shape(rows, columns),) + (shape(rows, slots, BF16),) * 3 + (shape(2 * PIECES, slots, BF16),),
             compiler_params=PARAMS,
             cost_estimate=pl.CostEstimate(
                 flops=6 * rows * columns * BLK, bytes_accessed=22 * rows * columns, transcendentals=3 * heads * rows * BLK
@@ -405,18 +409,16 @@
             name="mix",
         )(where, doc_starts, acc, *weights, *near_vals, lat)
 
-    def finish(block, acc, weights, far_vals, held):
-        context = shape(rows, columns, BF16)
-        pooled = jax.ShapeDtypeStruct((1, 4, 2, columns), BF16)
+    def finish(block, acc, weights, far_vals, context):
+        held = [] if context is None else [context]
         anywhere = pl.BlockSpec(memory_space=pl.ANY)
-        whole = pl.BlockSpec(memory_space=pltpu.VMEM)
         return pl.pallas_call(
             functools.partial(context_kernel, block),
-            in_specs=smem(1) + vmem(4) + ([whole, anywhere] if held else []),
-            out_specs=[anywhere, whole] if held else anywhere,
-            out_shape=(context, pooled) if held else context,
+            in_specs=smem(1) + vmem(4) + [anywhere] * len(held),
+            out_specs=anywhere,
+            out_shape=shape(rows, columns, BF16),
             scratch_shapes=[pltpu.VMEM((BLK, columns), BF16), pltpu.SemaphoreType.DMA((heads // 2,))],
-            input_output_aliases={6: 0} if held else {},
+            input_output_aliases={5: 0} if held else {},
             compiler_params=PARAMS,
             cost_estimate=pl.CostEstimate(flops=2 * BLK * columns * BLK, bytes_accessed=14 * BLK * columns, transcendentals=0),
             name="finish",
@@ -449,7 +451,7 @@
         out_specs=spec(2 * PIECES, wide),
         out_shape=shape(2 * PIECES, columns),
         compiler_params=PARAMS,
-        cost_estimate=pl.CostEstimate(flops=64 * rows * columns * 128, bytes_accessed=3 * rows * columns, transcendentals=0),
+        cost_estimate=pl.CostEstimate(flops=64 * rows * columns * 144, bytes_accessed=3 * rows * columns, transcendentals=0),
         name="part",
     )(where, doc_starts, sums, values)
     acc, parts = lax.optimization_barrier((acc, parts))
@@ -463,10 +465,20 @@
         name="route",
     )(where, doc_owner, parts, *[m[1] for m in mixed])
     mixed[0], parts = lax.optimization_barrier((mixed[0], parts))
-    context = finish(0, mixed[0][0], far_weights, far_vals[0], [])
+    context = finish(0, mixed[0][0], far_weights, far_vals[0], None)
     sent, context = lax.optimization_barrier((sent, context))
     got = lax.all_to_all(sent, "seq", split_axis=0, concat_axis=0, tiled=True)
-    return finish(1, mixed[1][0], far_weights, far_vals[1], [got, context])
+    context = finish(1, mixed[1][0], far_weights, far_vals[1], context)
+    got, context = lax.optimization_barrier((got, context))
+    pooled = pl.pallas_call(
+        pool_kernel,
+        in_specs=vmem(1),
+        out_specs=pl.BlockSpec(memory_space=pltpu.VMEM),
+        out_shape=jax.ShapeDtypeStruct((1, 4, 2, columns), BF16),
+        compiler_params=PARAMS,
+        name="pool",
+    )(got)
+    return context, pooled
 
 
 def body(queries, keys, values, latent_keys, latent_values, pattern, doc_starts, doc_owner):

time: 109 us -> 109 us (level)
  blocking collectives: 8.01 us -> 0 us
  starting transfers between devices: 23.5 us -> 28.4 us
  Pallas kernels: 28.5 us -> 31.2 us
  local copies, waits for them, and re-layouts: 4.43 us -> 5.66 us
    all_to_all x1 -> x0, blocking collectives: 8.01 us -> none  [four_shards(): got = lax.all_to_all(sent, 'seq', split_axis=0, concat_axis=0, tiled=True)]
    ppermute x13, waiting for transfers between devices: 43.5 us -> 39.3 us  [move(): return lax.ppermute(value, 'seq', pairs)]
    all_to_all x0 -> x1, starting transfers between devices: none -> 3.27 us  [four_shards(): got = lax.all_to_all(sent, 'seq', split_axis=0, concat_axis=0, tiled=True)]
    all_to_all x0 -> x1, waiting for transfers between devices: none -> 3.25 us  [four_shards(): got = lax.all_to_all(sent, 'seq', split_axis=0, concat_axis=0, tiled=True)]
    ppermute x13, starting transfers between devices: 23.5 us -> 25.2 us  [move(): return lax.ppermute(value, 'seq', pairs)]
    unnamed x22 -> x26, local copies, waits for them, and re-layouts: 4.36 us -> 5.59 us
  transfers between devices with their start and end apart: 13 -> 14, of which waited for: 7 -> 8; matrix products, arithmetic and copies ran while one was open for 0% -> 0% of each run, Pallas kernels for 24% -> 28%
where the time goes in v6:
time: 109 us
  waiting for transfers between devices  42.5 us (39%)
  Pallas kernels  31.2 us (29%)
  starting transfers between devices  28.4 us (26%)
  local copies, waits for them, and re-layouts  5.66 us (5%)
    ppermute x13, waiting for transfers between devices, move(): return lax.ppermute(value, 'seq', pairs)  39.3 us
    ppermute x13, starting transfers between devices, move(): return lax.ppermute(value, 'seq', pairs)  25.2 us
    pallas_call x1, Pallas kernels, weigh(): pl.pallas_call(functools.partial(weigh_kernel, 4), grid=(heads // step,),...  8.11 us
    pallas_call x2, Pallas kernels, latent_call(): pl.pallas_call(latent_kernel, grid=(steps,), in_specs=smem(2) + [pl.Block...  5.81 us
    unnamed x26, local copies, waits for them, and re-layouts  5.59 us
    pallas_call x2, Pallas kernels, mix(): pl.pallas_call(functools.partial(mix_kernel, block), grid=(heads // step,...  5.34 us
    pallas_call x1, Pallas kernels, own_call(): pl.pallas_call(own_kernel, grid=(columns // wide,), in_specs=[spec(rows,...  5.27 us
    pallas_call x2, Pallas kernels, finish(): pl.pallas_call(functools.partial(context_kernel, block), in_specs=smem(1)...  3.51 us
  transfers between devices with their start and end apart: 14, of which 8 were waited for; matrix products, arithmetic and copies ran while one was open for 0% of the time, Pallas kernels for 28%

profile of v6, /device:TPU:0, one launch (start us, length us, event | category | flops | bytes accessed | tf_op | source)
XLA Modules:
  0.0 108.8 jit_solution(17231472855982831874)
XLA Ops:
  0.6 5.0 %collective-permute-start.4 = (bf16[512,1024]{1,0:T(8,128)(2,1)}, bf16[512,1024]{1,0:T(8,128)(2,1)S(1)}, u32[]{:S(2)}, u32[]{:S(2)}) collective-permute-start(bf16[512,1024]{1,0:T(8,128)(2,1)} %k_ref.1), channel_id=1, source_target_pairs={{0,4},{4,8},{8,12},{1,5},{5,9},{9,13},{2,6},{6,10},{10,14},{3,7},{... | collective-permute-start | bytes 3145736 | tf_op jit(solution)/shard_map/ppermute | solution.py:368
  5.6 1.3 %collective-permute-start.5 = (bf16[512,1024]{1,0:T(8,128)(2,1)}, bf16[512,1024]{1,0:T(8,128)(2,1)S(1)}, u32[]{:S(2)}, u32[]{:S(2)}) collective-permute-start(bf16[512,1024]{1,0:T(8,128)(2,1)} %k_ref.1), channel_id=1, source_target_pairs={{4,0},{8,4},{12,8},{5,1},{9,5},{13,9},{6,2},{10,6},{14,10},{7,3},{... | collective-permute-start | bytes 3145736 | tf_op jit(solution)/shard_map/ppermute | solution.py:368
  11.3 1.6 %latent.2 = f32[8,256]{1,0:T(8,128)S(1)} custom-call(s32[1]{0:T(128)} %bitcast.where, s32[32]{0:T(128)S(1)} %copy-done.8, bf16[512,1024]{1,0:T(8,128)(2,1)S(1)} %copy-done, bf16[512,1024]{1,0:T(8,128)(2,1)S(1)} %copy-done.3, bf16[512,1024]{1,0:T(8,128)(2,1)S(1)} %copy-done.5), custom_call_target="tpu_custom_call" | custom-call | flops 268435456 | bytes 786432 | tf_op jit(solution)/shard_map/latent/pallas_call | solution.py:340
  13.0 4.7 %collective-permute-start = (bf16[256,1024]{1,0:T(8,128)(2,1)S(1)}, bf16[256,1024]{1,0:T(8,128)(2,1)S(1)}, u32[]{:S(2)}, u32[]{:S(2)}) collective-permute-start(bf16[256,1024]{1,0:T(8,128)(2,1)S(1)} %slice.6), channel_id=1, source_target_pairs={{0,4},{4,8},{8,12},{1,5},{5,9},{9,13},{2,6},{6,10},{10,14},{3,7},{... | collective-permute-start | bytes 1572872 | tf_op jit(solution)/shard_map/ppermute | solution.py:368
  17.7 1.3 %collective-permute-start.1 = (bf16[256,1024]{1,0:T(8,128)(2,1)S(1)}, bf16[256,1024]{1,0:T(8,128)(2,1)S(1)}, u32[]{:S(2)}, u32[]{:S(2)}) collective-permute-start(bf16[256,1024]{1,0:T(8,128)(2,1)S(1)} %slice.6), channel_id=1, source_target_pairs={{4,0},{8,4},{12,8},{5,1},{9,5},{13,9},{6,2},{10,6},{14,10},{7,3},{... | collective-permute-start | bytes 1572872 | tf_op jit(solution)/shard_map/ppermute | solution.py:368
  19.0 5.3 %own.1 = (f32[512,1024]{1,0:T(8,128)S(1)}, f32[512,1024]{1,0:T(8,128)S(1)}, f32[512,1024]{1,0:T(8,128)S(1)}) custom-call(bf16[512,1024]{1,0:T(8,128)(2,1)S(1)} %copy-done, bf16[512,1024]{1,0:T(8,128)(2,1)S(1)} %copy-done.12, bf16[512,1024]{1,0:T(8,128)(2,1)S(1)} %copy-done.7), custom_call_target="tpu_custom_call" | custom-call | flops 1073741824 | bytes 9437184 | tf_op jit(solution)/shard_map/own/pallas_call | solution.py:321
  24.3 5.1 %collective-permute-done.4.nb_ref = bf16[512,1024]{1,0:T(8,128)(2,1)S(1)} collective-permute-done((bf16[512,1024]{1,0:T(8,128)(2,1)}, bf16[512,1024]{1,0:T(8,128)(2,1)S(1)}, u32[]{:S(2)}, u32[]{:S(2)}) %collective-permute-start.4) | collective-permute-done | bytes 1048608 | tf_op jit(solution)/shard_map/ppermute | solution.py:368
  29.4 4.4 %collective-permute-done.5.na_ref = bf16[512,1024]{1,0:T(8,128)(2,1)S(1)} collective-permute-done((bf16[512,1024]{1,0:T(8,128)(2,1)}, bf16[512,1024]{1,0:T(8,128)(2,1)S(1)}, u32[]{:S(2)}, u32[]{:S(2)}) %collective-permute-start.5) | collective-permute-done | bytes 1048608 | tf_op jit(solution)/shard_map/ppermute | solution.py:368
  34.5 1.3 %collective-permute-start.7 = (bf16[512,1024]{1,0:T(8,128)(2,1)S(1)}, bf16[512,1024]{1,0:T(8,128)(2,1)S(1)}, u32[]{:S(2)}, u32[]{:S(2)}) collective-permute-start(bf16[512,1024]{1,0:T(8,128)(2,1)S(1)} %collective-permute-done.5.na_ref), channel_id=1, source_target_pairs={{4,0},{8,4},{5,1},{9,5},{6,2},{10,6},{7,3},{11,7},{20,16},{24,20},... | collective-permute-start | bytes 3145736 | tf_op jit(solution)/shard_map/ppermute | solution.py:368
  35.8 3.6 %collective-permute-done.vb_ref = bf16[256,1024]{1,0:T(8,128)(2,1)S(1)} collective-permute-done((bf16[256,1024]{1,0:T(8,128)(2,1)S(1)}, bf16[256,1024]{1,0:T(8,128)(2,1)S(1)}, u32[]{:S(2)}, u32[]{:S(2)}) %collective-permute-start) | collective-permute-done | bytes 524320 | tf_op jit(solution)/shard_map/ppermute | solution.py:368
  39.4 5.6 %collective-permute-done.1.va_ref = bf16[256,1024]{1,0:T(8,128)(2,1)S(1)} collective-permute-done((bf16[256,1024]{1,0:T(8,128)(2,1)S(1)}, bf16[256,1024]{1,0:T(8,128)(2,1)S(1)}, u32[]{:S(2)}, u32[]{:S(2)}) %collective-permute-start.1) | collective-permute-done | bytes 524320 | tf_op jit(solution)/shard_map/ppermute | solution.py:368
  45.1 4.2 %collective-permute-start.2 = (bf16[256,1024]{1,0:T(8,128)(2,1)S(1)}, bf16[256,1024]{1,0:T(8,128)(2,1)}, u32[]{:S(2)}, u32[]{:S(2)}) collective-permute-start(bf16[256,1024]{1,0:T(8,128)(2,1)S(1)} %slice.7), channel_id=1, source_target_pairs={{0,4},{4,8},{8,12},{1,5},{5,9},{9,13},{2,6},{6,10},{10,14},{3,7},{... | collective-permute-start | bytes 1572872 | tf_op jit(solution)/shard_map/ppermute | solution.py:368
  50.7 4.2 %latent.3 = f32[8,768]{1,0:T(8,128)S(1)} custom-call(s32[1]{0:T(128)} %bitcast.where, s32[32]{0:T(128)S(1)} %copy-done.9, bf16[512,1024]{1,0:T(8,128)(2,1)S(1)} %copy-done, bf16[512,1024]{1,0:T(8,128)(2,1)S(1)} %copy-done.4, bf16[512,1024]{1,0:T(8,128)(2,1)S(1)} %copy-done.6), custom_call_target="tpu_custom_call" | custom-call | flops 8053063680 | bytes 2359296 | tf_op jit(solution)/shard_map/latent/pallas_call | solution.py:340
  54.8 1.3 %collective-permute-start.10 = (bf16[256,1024]{1,0:T(8,128)(2,1)S(1)}, bf16[256,1024]{1,0:T(8,128)(2,1)S(1)}, u32[]{:S(2)}, u32[]{:S(2)}) collective-permute-start(bf16[256,1024]{1,0:T(8,128)(2,1)S(1)} %collective-permute-done.1.va_ref), channel_id=1, source_target_pairs={{4,0},{8,4},{5,1},{9,5},{6,2},{10,6},{7,3},{11,7},{20,16},{24,20},... | collective-permute-start | bytes 1572872 | tf_op jit(solution)/shard_map/ppermute | solution.py:368
  56.9 10.7 %collective-permute-done.7.fa_ref = bf16[512,1024]{1,0:T(8,128)(2,1)S(1)} collective-permute-done((bf16[512,1024]{1,0:T(8,128)(2,1)S(1)}, bf16[512,1024]{1,0:T(8,128)(2,1)S(1)}, u32[]{:S(2)}, u32[]{:S(2)}) %collective-permute-start.7) | collective-permute-done | bytes 1048608 | tf_op jit(solution)/shard_map/ppermute | solution.py:368
  68.8 8.1 %weigh.1 = (f32[512,1024]{1,0:T(8,128)S(1)}, bf16[512,2048]{1,0:T(8,128)(2,1)S(1)}, bf16[512,2048]{1,0:T(8,128)(2,1)S(1)}, bf16[512,2048]{1,0:T(8,128)(2,1)S(1)}, bf16[8,2048]{1,0:T(8,128)(2,1)S(1)}) custom-call(s32[1]{0:T(128)} %bitcast.where, s32[2,8]{1,0:T(2,128)S(1)} %copy-done.10, s32[32]{0:T(128)S(1)} %copy-done.9, bf16[512,1024]{1,0:T(8,128)(2,1)S(1)} %copy-done, ...), custom_call_target="tpu_custom_call" | custom-call | flops 805306368 | bytes 11534336 | tf_op jit(solution)/shard_map/weigh/pallas_call | solution.py:383
  76.9 2.0 %collective-permute-done.3.va_ref = bf16[256,1024]{1,0:T(8,128)(2,1)} collective-permute-done((bf16[256,1024]{1,0:T(8,128)(2,1)S(1)}, bf16[256,1024]{1,0:T(8,128)(2,1)}, u32[]{:S(2)}, u32[]{:S(2)}) %collective-permute-start.3) | collective-permute-done | bytes 524320 | tf_op jit(solution)/shard_map/ppermute | solution.py:368
  79.5 2.2 %mix.2 = (f32[256,1024]{1,0:T(8,128)S(1)}, f32[4,1024]{1,0:T(4,128)S(1)}) custom-call(s32[1]{0:T(128)} %bitcast.where, s32[32]{0:T(128)S(1)} %copy-done.9, f32[512,1024]{1,0:T(8,128)S(1)} %get-tuple-element.80.acc_in, bf16[512,2048]{1,0:T(8,128)(2,1)S(1)} %get-tuple-element.72.wb_ref, bf16[512,2048]{1,0:T(8,128)(2,1)S(1)} %get-tuple-element.73.wa_ref, ...), custom_call_target="tpu_custom_call" | custom-call | flops 268435456 | bytes 5242880 | tf_op jit(solution)/shard_map/mix/pallas_call | solution.py:397
  81.7 1.5 %collective-permute-start.11 = (bf16[256,1024]{1,0:T(8,128)(2,1)}, bf16[256,1024]{1,0:T(8,128)(2,1)}, u32[]{:S(2)}, u32[]{:S(2)}) collective-permute-start(bf16[256,1024]{1,0:T(8,128)(2,1)} %collective-permute-done.2.vb_ref), channel_id=1, source_target_pairs={{4,8},{8,12},{5,9},{9,13},{6,10},{10,14},{7,11},{11,15},{20,24},{2... | collective-permute-start | bytes 1572872 | tf_op jit(solution)/shard_map/ppermute | solution.py:368
  84.4 7.9 %collective-permute-done.8.sums_ref = bf16[8,2048]{1,0:T(8,128)(2,1)S(1)} collective-permute-done((bf16[8,2048]{1,0:T(8,128)(2,1)S(1)}, bf16[8,2048]{1,0:T(8,128)(2,1)S(1)}, u32[]{:S(2)}, u32[]{:S(2)}) %collective-permute-start.8) | collective-permute-done | bytes 32800 | tf_op jit(solution)/shard_map/ppermute | solution.py:368
  93.6 3.2 %mix.3 = (f32[256,1024]{1,0:T(8,128)S(1)}, f32[4,1024]{1,0:T(4,128)S(1)}) custom-call(s32[1]{0:T(128)} %bitcast.where, s32[32]{0:T(128)S(1)} %copy-done.9, f32[512,1024]{1,0:T(8,128)S(1)} %get-tuple-element.80.acc_in, bf16[512,2048]{1,0:T(8,128)(2,1)S(1)} %get-tuple-element.72.wb_ref, bf16[512,2048]{1,0:T(8,128)(2,1)S(1)} %get-tuple-element.73.wa_ref, ...), custom_call_target="tpu_custom_call" | custom-call | flops 268435456 | bytes 5242880 | tf_op jit(solution)/shard_map/mix/pallas_call | solution.py:397
  99.2 3.3 %all-to-all-start = ((bf16[4,4,1024]{2,1,0:T(4,128)(2,1)}), bf16[4,4,1024]{2,1,0:T(4,128)(2,1)S(1)}, u32[]{:S(2)}, u32[]{:S(2)}) async-start(bf16[4,4,1024]{2,1,0:T(4,128)(2,1)} %route.1), calls=%async_computation | async-start | bytes 65536 | tf_op jit(solution)/shard_map/all_to_all | solution.py:470
  102.5 2.3 %finish.3 = bf16[512,1024]{1,0:T(8,128)(2,1)} custom-call(s32[1]{0:T(128)} %bitcast.where, f32[256,1024]{1,0:T(8,128)S(1)} %get-tuple-element.88.acc_ref, bf16[512,2048]{1,0:T(8,128)(2,1)S(1)} %get-tuple-element.86.w_ref, bf16[256,1024]{1,0:T(8,128)(2,1)} %collective-permute-done.11.vb_ref, ...), custom_call_target="tpu_custom_call", output_to_operand_aliasing={{}: (5, {})} | custom-call | flops 134217728 | bytes 3670016 | tf_op jit(solution)/shard_map/finish/pallas_call | solution.py:415
  104.9 3.2 %all-to-all-done.got_ref = bf16[4,4,1024]{2,1,0:T(4,128)(2,1)S(1)} async-done(((bf16[4,4,1024]{2,1,0:T(4,128)(2,1)}), bf16[4,4,1024]{2,1,0:T(4,128)(2,1)S(1)}, u32[]{:S(2)}, u32[]{:S(2)}) %all-to-all-start) | async-done | bytes 32800 | tf_op jit(solution)/shard_map/all_to_all | solution.py:470
  (44 shorter events, 14.5 us)
Async XLA Ops:
  0.6 28.8 %collective-permute-start.4 = (bf16[512,1024]{1,0:T(8,128)(2,1)}, bf16[512,1024]{1,0:T(8,128)(2,1)S(1)}, u32[]{:S(2)}, u32[]{:S(2)}) collective-permute-start(bf16[512,1024]{1,0:T(8,128)(2,1)} %k_ref.1), channel_id=1, source_target_pairs={{0,4},{4,8},{8,12},{1,5},{5,9},{9,13},{2,6},{6,10},{10,14},{3,7},{... | collective-permute-start | bytes 3145736 | tf_op jit(solution)/shard_map/ppermute | solution.py:368
  5.6 28.2 %collective-permute-start.5 = (bf16[512,1024]{1,0:T(8,128)(2,1)}, bf16[512,1024]{1,0:T(8,128)(2,1)S(1)}, u32[]{:S(2)}, u32[]{:S(2)}) collective-permute-start(bf16[512,1024]{1,0:T(8,128)(2,1)} %k_ref.1), channel_id=1, source_target_pairs={{4,0},{8,4},{12,8},{5,1},{9,5},{13,9},{6,2},{10,6},{14,10},{7,3},{... | collective-permute-start | bytes 3145736 | tf_op jit(solution)/shard_map/ppermute | solution.py:368
  6.9 1.2 %copy-start = (bf16[512,1024]{1,0:T(8,128)(2,1)S(1)}, bf16[512,1024]{1,0:T(8,128)(2,1)}, u32[]{:S(2)}) copy-start(bf16[512,1024]{1,0:T(8,128)(2,1)} %q_ref.5) | copy-start | bytes 3145732
  11.3 1.7 %copy-start.7 = (bf16[512,1024]{1,0:T(8,128)(2,1)S(1)}, bf16[512,1024]{1,0:T(8,128)(2,1)}, u32[]{:S(2)}) copy-start(bf16[512,1024]{1,0:T(8,128)(2,1)} %v_ref.3) | copy-start | bytes 3145732
  11.3 7.8 %copy-start.12 = (bf16[512,1024]{1,0:T(8,128)(2,1)S(1)}, bf16[512,1024]{1,0:T(8,128)(2,1)}, u32[]{:S(2)}) copy-start(bf16[512,1024]{1,0:T(8,128)(2,1)} %k_ref.1) | copy-start | bytes 3145732
  13.0 37.7 %copy-start.4 = (bf16[512,1024]{1,0:T(8,128)(2,1)S(1)}, bf16[512,1024]{1,0:T(8,128)(2,1)}, u32[]{:S(2)}) copy-start(bf16[512,1024]{1,0:T(8,128)(2,1)} %lk_ref.3) | copy-start | bytes 3145732
  13.0 37.7 %copy-start.6 = (bf16[512,1024]{1,0:T(8,128)(2,1)S(1)}, bf16[512,1024]{1,0:T(8,128)(2,1)}, u32[]{:S(2)}) copy-start(bf16[512,1024]{1,0:T(8,128)(2,1)} %lv_ref.3) | copy-start | bytes 3145732
  13.0 37.7 %copy-start.9 = (s32[32]{0:T(128)S(1)}, s32[32]{0:T(128)}, u32[]{:S(2)}) copy-start(s32[32]{0:T(128)} %starts.11) | copy-start | bytes 388
  13.0 26.4 %collective-permute-start = (bf16[256,1024]{1,0:T(8,128)(2,1)S(1)}, bf16[256,1024]{1,0:T(8,128)(2,1)S(1)}, u32[]{:S(2)}, u32[]{:S(2)}) collective-permute-start(bf16[256,1024]{1,0:T(8,128)(2,1)S(1)} %slice.6), channel_id=1, source_target_pairs={{0,4},{4,8},{8,12},{1,5},{5,9},{9,13},{2,6},{6,10},{10,14},{3,7},{... | collective-permute-start | bytes 1572872 | tf_op jit(solution)/shard_map/ppermute | solution.py:368
  17.7 27.3 %collective-permute-start.1 = (bf16[256,1024]{1,0:T(8,128)(2,1)S(1)}, bf16[256,1024]{1,0:T(8,128)(2,1)S(1)}, u32[]{:S(2)}, u32[]{:S(2)}) collective-permute-start(bf16[256,1024]{1,0:T(8,128)(2,1)S(1)} %slice.6), channel_id=1, source_target_pairs={{4,0},{8,4},{12,8},{5,1},{9,5},{13,9},{6,2},{10,6},{14,10},{7,3},{... | collective-permute-start | bytes 1572872 | tf_op jit(solution)/shard_map/ppermute | solution.py:368
  33.8 21.0 %copy-start.1 = (bf16[512,1024]{1,0:T(8,128)(2,1)}, bf16[512,1024]{1,0:T(8,128)(2,1)S(1)}, u32[]{:S(2)}) copy-start(bf16[512,1024]{1,0:T(8,128)(2,1)S(1)} %collective-permute-done.5.na_ref) | copy-start | bytes 3145732
  33.8 22.3 %collective-permute-start.6 = (bf16[512,1024]{1,0:T(8,128)(2,1)S(1)}, bf16[512,1024]{1,0:T(8,128)(2,1)S(1)}, u32[]{:S(2)}, u32[]{:S(2)}) collective-permute-start(bf16[512,1024]{1,0:T(8,128)(2,1)S(1)} %collective-permute-done.4.nb_ref), channel_id=1, source_target_pairs={{4,8},{8,12},{5,9},{9,13},{6,10},{10,14},{7,11},{11,15},{20,24},{2... | collective-permute-start | bytes 3145736 | tf_op jit(solution)/shard_map/ppermute | solution.py:368
  34.5 33.0 %collective-permute-start.7 = (bf16[512,1024]{1,0:T(8,128)(2,1)S(1)}, bf16[512,1024]{1,0:T(8,128)(2,1)S(1)}, u32[]{:S(2)}, u32[]{:S(2)}) collective-permute-start(bf16[512,1024]{1,0:T(8,128)(2,1)S(1)} %collective-permute-done.5.na_ref), channel_id=1, source_target_pairs={{4,0},{8,4},{5,1},{9,5},{6,2},{10,6},{7,3},{11,7},{20,16},{24,20},... | collective-permute-start | bytes 3145736 | tf_op jit(solution)/shard_map/ppermute | solution.py:368
  45.1 22.4 %copy-start.10 = (s32[2,8]{1,0:T(2,128)S(1)}, s32[2,8]{1,0:T(2,128)}, u32[]{:S(2)}) copy-start(s32[2,8]{1,0:T(2,128)} %pattern.1) | copy-start | bytes 196
  45.1 31.8 %collective-permute-start.2 = (bf16[256,1024]{1,0:T(8,128)(2,1)S(1)}, bf16[256,1024]{1,0:T(8,128)(2,1)}, u32[]{:S(2)}, u32[]{:S(2)}) collective-permute-start(bf16[256,1024]{1,0:T(8,128)(2,1)S(1)} %slice.7), channel_id=1, source_target_pairs={{0,4},{4,8},{8,12},{1,5},{5,9},{9,13},{2,6},{6,10},{10,14},{3,7},{... | collective-permute-start | bytes 1572872 | tf_op jit(solution)/shard_map/ppermute | solution.py:368
  49.3 29.5 %collective-permute-start.3 = (bf16[256,1024]{1,0:T(8,128)(2,1)S(1)}, bf16[256,1024]{1,0:T(8,128)(2,1)}, u32[]{:S(2)}, u32[]{:S(2)}) collective-permute-start(bf16[256,1024]{1,0:T(8,128)(2,1)S(1)} %slice.7), channel_id=1, source_target_pairs={{4,0},{8,4},{12,8},{5,1},{9,5},{13,9},{6,2},{10,6},{14,10},{7,3},{... | collective-permute-start | bytes 1572872 | tf_op jit(solution)/shard_map/ppermute | solution.py:368
  54.8 43.2 %collective-permute-start.10 = (bf16[256,1024]{1,0:T(8,128)(2,1)S(1)}, bf16[256,1024]{1,0:T(8,128)(2,1)S(1)}, u32[]{:S(2)}, u32[]{:S(2)}) collective-permute-start(bf16[256,1024]{1,0:T(8,128)(2,1)S(1)} %collective-permute-done.1.va_ref), channel_id=1, source_target_pairs={{4,0},{8,4},{5,1},{9,5},{6,2},{10,6},{7,3},{11,7},{20,16},{24,20},... | collective-permute-start | bytes 1572872 | tf_op jit(solution)/shard_map/ppermute | solution.py:368
  56.2 41.9 %collective-permute-start.9 = (bf16[256,1024]{1,0:T(8,128)(2,1)S(1)}, bf16[256,1024]{1,0:T(8,128)(2,1)S(1)}, u32[]{:S(2)}, u32[]{:S(2)}) collective-permute-start(bf16[256,1024]{1,0:T(8,128)(2,1)S(1)} %collective-permute-done.vb_ref), channel_id=1, source_target_pairs={{4,8},{8,12},{5,9},{9,13},{6,10},{10,14},{7,11},{11,15},{20,24},{2... | collective-permute-start | bytes 1572872 | tf_op jit(solution)/shard_map/ppermute | solution.py:368
  67.5 1.2 %copy-start.2 = (bf16[512,1024]{1,0:T(8,128)(2,1)S(1)}, bf16[512,1024]{1,0:T(8,128)(2,1)}, u32[]{:S(2)}) copy-start(bf16[512,1024]{1,0:T(8,128)(2,1)} %copy-done.1) | copy-start | bytes 3145732
  78.9 13.5 %collective-permute-start.8 = (bf16[8,2048]{1,0:T(8,128)(2,1)S(1)}, bf16[8,2048]{1,0:T(8,128)(2,1)S(1)}, u32[]{:S(2)}, u32[]{:S(2)}) collective-permute-start(bf16[8,2048]{1,0:T(8,128)(2,1)S(1)} %get-tuple-element.68), channel_id=1, source_target_pairs={{0,8},{4,12},{8,0},{12,4},{1,9},{5,13},{9,1},{13,5},{2,10},{6,14},... | collective-permute-start | bytes 98312 | tf_op jit(solution)/shard_map/ppermute | solution.py:368
  81.7 20.9 %collective-permute-start.11 = (bf16[256,1024]{1,0:T(8,128)(2,1)}, bf16[256,1024]{1,0:T(8,128)(2,1)}, u32[]{:S(2)}, u32[]{:S(2)}) collective-permute-start(bf16[256,1024]{1,0:T(8,128)(2,1)} %collective-permute-done.2.vb_ref), channel_id=1, source_target_pairs={{4,8},{8,12},{5,9},{9,13},{6,10},{10,14},{7,11},{11,15},{20,24},{2... | collective-permute-start | bytes 1572872 | tf_op jit(solution)/shard_map/ppermute | solution.py:368
  83.1 19.4 %collective-permute-start.12 = (bf16[256,1024]{1,0:T(8,128)(2,1)}, bf16[256,1024]{1,0:T(8,128)(2,1)}, u32[]{:S(2)}, u32[]{:S(2)}) collective-permute-start(bf16[256,1024]{1,0:T(8,128)(2,1)} %collective-permute-done.3.va_ref), channel_id=1, source_target_pairs={{4,0},{8,4},{5,1},{9,5},{6,2},{10,6},{7,3},{11,7},{20,16},{24,20},... | collective-permute-start | bytes 1572872 | tf_op jit(solution)/shard_map/ppermute | solution.py:368
  93.6 3.2 %copy-start.11 = (s32[32]{0:T(128)S(1)}, s32[32]{0:T(128)}, u32[]{:S(2)}) copy-start(s32[32]{0:T(128)} %owners.1) | copy-start | bytes 388
  99.2 8.9 %all-to-all-start = ((bf16[4,4,1024]{2,1,0:T(4,128)(2,1)}), bf16[4,4,1024]{2,1,0:T(4,128)(2,1)S(1)}, u32[]{:S(2)}, u32[]{:S(2)}) async-start(bf16[4,4,1024]{2,1,0:T(4,128)(2,1)} %route.1), calls=%async_computation | async-start | bytes 65536 | tf_op jit(solution)/shard_map/all_to_all | solution.py:470
  (3 other events, 3.1 us)

commit v7 on v5

--- a/solution.py
+++ b/solution.py
@@ -171,49 +171,77 @@
             outs[r][...] = chosen.astype(BF16)
 
 
-def weigh_kernel(shards, where, pattern, starts, q_ref, nb_ref, na_ref, fb_ref, fa_ref, *refs):
-    acc_in, top_in, sum_in, acc_ref, wb_ref, wa_ref, wf_ref, sums_ref = refs
-    behind = where[0] >= 2
-    blocks = q_ref.shape[0] // BLK
-    bias = []
-    for block in range(blocks):
-        far_live = [slot_live(where, pattern, shards, 1, side, block) for side in range(2)]
-        live = [slot_live(where, pattern, shards, 0, side, block) for side in range(2)]
-        live.append((behind & far_live[0]) | (jnp.logical_not(behind) & far_live[1]))
-        bias.append([jnp.where(on, 0.0, -jnp.inf) for on in live])
+def live_bias(where, pattern, shards, level, side, block):
+    return jnp.where(slot_live(where, pattern, shards, level, side, block), 0.0, -jnp.inf)
+
+
+def halves(s, bias):
+    return [s[:, i : i + HD] * SCALE + bias for i in range(0, BLK, HD)]
+
+
+def near_weigh_kernel(shards, where, pattern, q_ref, nb_ref, na_ref, acc_in, top_in, sum_in, *refs):
+    acc_ref, top_ref, sum_ref, wb_ref, wa_ref = refs
+    biases = [[live_bias(where, pattern, shards, 0, side, block) for side in range(2)] for block in range(q_ref.shape[0] // BLK)]
     piece = q_ref.shape[0] // PIECES
-    place = lax.broadcasted_iota(jnp.int32, (piece, HD), 0)
-    firsts = [place < split_of(where, starts, p) for p in range(PIECES)]
-    lanes = [slice(i * HD, (i + 1) * HD) for i in range(BLK // HD)]
     for h in range(q_ref.shape[1] // HD):
         head = slice(h * HD, (h + 1) * HD)
         for p in range(PIECES):
             rows = slice(p * piece, (p + 1) * piece)
             block = p * piece // BLK
-            if p * piece % BLK == 0:
-                held = slice(block * BLK, (block + 1) * BLK)
-                far = jnp.where(behind, fb_ref[held, head], fa_ref[held, head])
-                keys = [nb_ref[held, head], na_ref[held, head], far]
+            held = slice(block * BLK, (block + 1) * BLK)
             q = q_ref[rows, head]
-            scores = []
-            for k, low in zip(keys, bias[block]):
-                s = dot_t(q, k)
-                scores += [s[:, part] * SCALE + low for part in lanes]
+            scores = [halves(dot_t(q, k_ref[held, head]), bias) for k_ref, bias in zip((nb_ref, na_ref), biases[block])]
+            old = top_in[rows, head]
+            top = jnp.max(functools.reduce(jnp.maximum, scores[0] + scores[1]), axis=1, keepdims=True)
+            top = jnp.maximum(top, old)
+            shrink = jnp.exp2(old - top)
+            exps = [[jnp.exp2(x - top) for x in pair] for pair in scores]
+            added = jnp.sum(functools.reduce(jnp.add, exps[0] + exps[1]), axis=1, keepdims=True)
+            top_ref[rows, head] = top
+            sum_ref[rows, head] = sum_in[rows, head] * shrink + added
+            acc_ref[rows, head] = acc_in[rows, head] * shrink
+            for pair, out in zip(exps, (wb_ref, wa_ref)):
+                for i, e in enumerate(pair):
+                    first = h * BLK + i * HD
+                    out[rows, first : first + HD] = e.astype(BF16)
+
+
+def far_weigh_kernel(shards, where, pattern, starts, q_ref, fb_ref, fa_ref, top_in, sum_in, scale_ref, wf_ref, sums_ref):
+    behind = where[0] >= 2
+    biases = []
+    for block in range(q_ref.shape[0] // BLK):
+        pair = [live_bias(where, pattern, shards, 1, side, block) for side in range(2)]
+        biases.append(jnp.where(behind, pair[0], pair[1]))
+    piece = q_ref.shape[0] // PIECES
+    place = lax.broadcasted_iota(jnp.int32, (piece, HD), 0)
+    firsts = [place < split_of(where, starts, p) for p in range(PIECES)]
+    for h in range(q_ref.shape[1] // HD):
+        head = slice(h * HD, (h + 1) * HD)
+        sums = [[] for _ in range(BLK // HD)]
+        for p in range(PIECES):
+            rows = slice(p * piece, (p + 1) * piece)
+            block = p * piece // BLK
+            held = slice(block * BLK, (block + 1) * BLK)
+            keys = jnp.where(behind, fb_ref[held, head], fa_ref[held, head])
+            scores = halves(dot_t(q_ref[rows, head], keys), biases[block])
             old = top_in[rows, head]
             top = jnp.maximum(jnp.max(functools.reduce(jnp.maximum, scores), axis=1, keepdims=True), old)
             shrink = jnp.exp2(old - top)
-            exps = [jnp.exp2(s - top) for s in scores]
+            exps = [jnp.exp2(x - top) for x in scores]
             added = jnp.sum(functools.reduce(jnp.add, exps), axis=1, keepdims=True)
             inverse = 1.0 / (sum_in[rows, head] * shrink + added)
-            acc_ref[rows, head] = acc_in[rows, head] * (shrink * inverse)
+            scale_ref[rows, head] = shrink * inverse
             for i, e in enumerate(exps):
-                out = (wb_ref, wa_ref, wf_ref)[i // len(lanes)]
-                first = h * BLK + i % len(lanes) * HD
+                first = h * BLK + i * HD
                 w = e * inverse
-                out[rows, first : first + HD] = w.astype(BF16)
-                if out is wf_ref:
-                    sums = [jnp.sum(x, axis=0, keepdims=True) for x in (jnp.where(firsts[p], w, 0.0), jnp.where(firsts[p], 0.0, w))]
-                    sums_ref[2 * p : 2 * p + 2, first : first + HD] = jnp.concatenate(sums, axis=0)
+                wf_ref[rows, first : first + HD] = w.astype(BF16)
+                sums[i] += [
+                    jnp.sum(jnp.where(firsts[p], w, 0.0), axis=0, keepdims=True),
+                    jnp.sum(jnp.where(firsts[p], 0.0, w), axis=0, keepdims=True),
+                ]
+        for i, found in enumerate(sums):
+            first = h * BLK + i * HD
+            sums_ref[:, first : first + HD] = jnp.concatenate(found, axis=0).astype(sums_ref.dtype)
 
 
 def doc_counts(split, piece, columns):
@@ -221,13 +249,14 @@
     return jnp.where(side == 0, split, piece - split).astype(F32)
 
 
-def mix_kernel(block, where, starts, acc_in, wb_ref, wa_ref, vb_ref, va_ref, lat_ref, acc_ref, mean_ref):
+def mix_kernel(block, where, starts, acc_in, scale_in, wb_ref, wa_ref, vb_ref, va_ref, lat_ref, acc_ref, mean_ref):
     pieces = mean_ref.shape[0] // 2
     piece = BLK // pieces
     for h in range(acc_in.shape[1] // HD):
         head = slice(h * HD, (h + 1) * HD)
         slots = slice(h * BLK, (h + 1) * BLK)
         acc = acc_in[:, head] + dot(wb_ref[:, slots], vb_ref[:, head]) + dot(wa_ref[:, slots], va_ref[:, head])
+        acc = acc * scale_in[:, head]
         acc_ref[:, head] = acc
         for p in range(pieces):
             index = block * pieces + p
@@ -375,26 +404,41 @@
     def row_spec(block, width=wide):
         return pl.BlockSpec((BLK, width), lambda h: (block, h))
 
-    def weigh(near_keys, far_keys, state):
+    def weigh_near(near_keys, state):
         return pl.pallas_call(
-            functools.partial(weigh_kernel, 4),
+            functools.partial(near_weigh_kernel, 4),
             grid=(heads // step,),
-            in_specs=smem(3) + [spec(rows, wide)] * 8,
-            out_specs=[spec(rows, wide)] + [spec(rows, step * BLK)] * 3 + [spec(2 * PIECES, step * BLK)],
-            out_shape=(shape(rows, columns),) + (shape(rows, slots, BF16),) * 3 + (shape(2 * PIECES, slots),),
+            in_specs=smem(2) + [spec(rows, wide)] * 6,
+            out_specs=[spec(rows, wide)] * 3 + [spec(rows, step * BLK)] * 2,
+            out_shape=(shape(rows, columns),) * 3 + (shape(rows, slots, BF16),) * 2,
+            input_output_aliases={5: 0, 6: 1, 7: 2},
             compiler_params=PARAMS,
             cost_estimate=pl.CostEstimate(
-                flops=6 * rows * columns * BLK, bytes_accessed=22 * rows * columns, transcendentals=3 * heads * rows * BLK
+                flops=4 * rows * columns * BLK, bytes_accessed=20 * rows * columns, transcendentals=2 * heads * rows * BLK
             ),
-            name="weigh",
-        )(where, pattern, doc_starts, queries, *near_keys, *far_keys, *state)
-
-    def mix(block, acc, weights, near_vals, lat):
+            name="weigh_near",
+        )(where, pattern, queries, *near_keys, *state)
+
+    def weigh_far(far_keys, top, total):
+        return pl.pallas_call(
+            functools.partial(far_weigh_kernel, 4),
+            grid=(heads // step,),
+            in_specs=smem(3) + [spec(rows, wide)] * 5,
+            out_specs=[spec(rows, wide), spec(rows, step * BLK), spec(2 * PIECES, step * BLK)],
+            out_shape=(shape(rows, columns), shape(rows, slots, BF16), shape(2 * PIECES, slots, BF16)),
+            compiler_params=PARAMS,
+            cost_estimate=pl.CostEstimate(
+                flops=2 * rows * columns * BLK, bytes_accessed=22 * rows * columns, transcendentals=heads * rows * BLK
+            ),
+            name="weigh_far",
+        )(where, pattern, doc_starts, queries, *far_keys, top, total)
+
+    def mix(block, acc, scale, weights, near_vals, lat):
         return pl.pallas_call(
             functools.partial(mix_kernel, block),
             grid=(heads // step,),
             in_specs=smem(2)
-            + [row_spec(block)]
+            + [row_spec(block)] * 2
             + [row_spec(block, step * BLK)] * 2
             + [row_spec(0)] * 2
             + [spec(2 * PIECES, wide)],
@@ -403,7 +447,7 @@
             compiler_params=PARAMS,
             cost_estimate=pl.CostEstimate(flops=4 * BLK * columns * BLK, bytes_accessed=20 * BLK * columns, transcendentals=0),
             name="mix",
-        )(where, doc_starts, acc, *weights, *near_vals, lat)
+        )(where, doc_starts, acc, scale, *weights, *near_vals, lat)
 
     def finish(block, acc, weights, far_vals, held):
         context = shape(rows, columns, BF16)
@@ -433,15 +477,13 @@
     lats.append(latent_call(where, doc_starts, late_queries, latent_keys, latent_values, 1))
     lat = jnp.concatenate(lats, axis=1)
     near_vals.append(near(part(late_vals, 1)))
-    far_keys, lat = lax.optimization_barrier((far_keys, lat))
-    weighed = weigh(near_keys, far_keys, state)
-    near_vals[1], weighed = lax.optimization_barrier((near_vals[1], weighed))
-    acc, *near_weights, far_weights, sums = weighed
+    acc, top, total, *near_weights = weigh_near(near_keys, state)
+    far_keys, lat, top = lax.optimization_barrier((far_keys, lat, top))
+    weighed = weigh_far(far_keys, top, total)
+    near_vals[0], weighed = lax.optimization_barrier((near_vals[0], weighed))
+    scale, far_weights, sums = weighed
     sums = move(sums, [(s, s ^ 2) for s in range(4)])
     far_vals = [onward(near_vals[0])]
-    mixed = [mix(0, acc, near_weights, near_vals[0], lat)]
-    near_vals[1], mixed[0] = lax.optimization_barrier((near_vals[1], mixed[0]))
-    far_vals.append(onward(near_vals[1]))
     parts = pl.pallas_call(
         part_kernel,
         grid=(heads // step,),
@@ -449,11 +491,14 @@
         out_specs=spec(2 * PIECES, wide),
         out_shape=shape(2 * PIECES, columns),
         compiler_params=PARAMS,
-        cost_estimate=pl.CostEstimate(flops=64 * rows * columns * 128, bytes_accessed=3 * rows * columns, transcendentals=0),
+        cost_estimate=pl.CostEstimate(flops=64 * rows * columns * 32, bytes_accessed=3 * rows * columns, transcendentals=0),
         name="part",
     )(where, doc_starts, sums, values)
-    acc, parts = lax.optimization_barrier((acc, parts))
-    mixed.append(mix(1, acc, near_weights, near_vals[1], lat))
+    mixed = [mix(0, acc, scale, near_weights, near_vals[0], lat)]
+    near_vals[1], parts, mixed[0] = lax.optimization_barrier((near_vals[1], parts, mixed[0]))
+    far_vals.append(onward(near_vals[1]))
+    mixed.append(mix(1, acc, scale, near_weights, near_vals[1], lat))
+    context = finish(0, mixed[0][0], far_weights, far_vals[0], [])
     sent = pl.pallas_call(
         route_kernel,
         in_specs=smem(2) + vmem(3),
@@ -462,8 +507,6 @@
         compiler_params=PARAMS,
         name="route",
     )(where, doc_owner, parts, *[m[1] for m in mixed])
-    mixed[0], parts = lax.optimization_barrier((mixed[0], parts))
-    context = finish(0, mixed[0][0], far_weights, far_vals[0], [])
     sent, context = lax.optimization_barrier((sent, context))
     got = lax.all_to_all(sent, "seq", split_axis=0, concat_axis=0, tiled=True)
     return finish(1, mixed[1][0], far_weights, far_vals[1], [got, context])

time: 109 us -> 107 us (0.982)
  blocking collectives: 8.01 us -> 0 us
  starting transfers between devices: 23.5 us -> 29.2 us
  waiting for transfers between devices: 43.5 us -> 38.5 us
  Pallas kernels: 28.5 us -> 33.3 us
    all_to_all x1 -> x0, blocking collectives: 8.01 us -> none  [four_shards(): got = lax.all_to_all(sent, 'seq', split_axis=0, concat_axis=0, tiled=True)]
    ppermute x13, waiting for transfers between devices: 43.5 us -> 36 us  [move(): return lax.ppermute(value, 'seq', pairs)]
    all_to_all x0 -> x1, starting transfers between devices: none -> 4.01 us  [four_shards(): got = lax.all_to_all(sent, 'seq', split_axis=0, concat_axis=0, tiled=True)]
    all_to_all x0 -> x1, waiting for transfers between devices: none -> 2.44 us  [four_shards(): got = lax.all_to_all(sent, 'seq', split_axis=0, concat_axis=0, tiled=True)]
    pallas_call x1 -> x2, Pallas kernels: 8.14 us -> 10.1 us  [the longest x1 5.41 us: weigh_near(): pl.pallas_call(functools.partial(near_weigh_kernel, 4), grid=(heads // st...]
    ppermute x13, starting transfers between devices: 23.5 us -> 25.1 us  [move(): return lax.ppermute(value, 'seq', pairs)]
    pallas_call x2, Pallas kernels: 2.95 us -> 4.12 us  [finish(): pl.pallas_call(functools.partial(context_kernel, block), in_specs=smem(1)...]
  transfers between devices with their start and end apart: 13 -> 14, of which waited for: 7 -> 9; matrix products, arithmetic and copies ran while one was open for 0% -> 0% of each run, Pallas kernels for 24% -> 29%
where the time goes in v7:
time: 107 us; the launch traced here: 106 us
  waiting for transfers between devices  38.5 us (36%)
  Pallas kernels  33.3 us (31%)
  starting transfers between devices  29.2 us (27%)
  local copies, waits for them, and re-layouts  4.43 us (4%)
    ppermute x13, waiting for transfers between devices, move(): return lax.ppermute(value, 'seq', pairs)  36 us
    ppermute x13, starting transfers between devices, move(): return lax.ppermute(value, 'seq', pairs)  25.1 us
    pallas_call x2, Pallas kernels, latent_call(): pl.pallas_call(latent_kernel, grid=(steps,), in_specs=smem(2) + [pl.Block...  5.81 us
    pallas_call x2, Pallas kernels, mix(): pl.pallas_call(functools.partial(mix_kernel, block), grid=(heads // step,...  5.46 us
    pallas_call x1, Pallas kernels, weigh_near(): pl.pallas_call(functools.partial(near_weigh_kernel, 4), grid=(heads // st...  5.41 us
    pallas_call x1, Pallas kernels, own_call(): pl.pallas_call(own_kernel, grid=(columns // wide,), in_specs=[spec(rows,...  5.27 us
    pallas_call x1, Pallas kernels, weigh_far(): pl.pallas_call(functools.partial(far_weigh_kernel, 4), grid=(heads // ste...  4.68 us
    unnamed x22, local copies, waits for them, and re-layouts  4.36 us
  transfers between devices with their start and end apart: 14, of which 9 were waited for; matrix products, arithmetic and copies ran while one was open for 0% of the time, Pallas kernels for 29%

profile of v7, /device:TPU:0, one launch (start us, length us, event | category | flops | bytes accessed | tf_op | source)
XLA Modules:
  0.0 106.2 jit_solution(7295631766247604451)
XLA Ops:
  0.6 5.0 %collective-permute-start = (bf16[512,1024]{1,0:T(8,128)(2,1)}, bf16[512,1024]{1,0:T(8,128)(2,1)S(1)}, u32[]{:S(2)}, u32[]{:S(2)}) collective-permute-start(bf16[512,1024]{1,0:T(8,128)(2,1)} %k_ref.1), channel_id=1, source_target_pairs={{0,4},{4,8},{8,12},{1,5},{5,9},{9,13},{2,6},{6,10},{10,14},{3,7},{... | collective-permute-start | bytes 3145736 | tf_op jit(solution)/shard_map/ppermute | solution.py:393
  11.3 1.6 %latent.2 = f32[8,256]{1,0:T(8,128)S(1)} custom-call(s32[1]{0:T(128)} %bitcast.where, s32[32]{0:T(128)S(1)} %copy-done.6, bf16[512,1024]{1,0:T(8,128)(2,1)S(1)} %copy-done, bf16[512,1024]{1,0:T(8,128)(2,1)S(1)} %copy-done.1, bf16[512,1024]{1,0:T(8,128)(2,1)S(1)} %copy-done.3), custom_call_target="tpu_custom_call" | custom-call | flops 268435456 | bytes 786432 | tf_op jit(solution)/shard_map/latent/pallas_call | solution.py:365
  13.0 4.7 %collective-permute-start.2 = (bf16[256,1024]{1,0:T(8,128)(2,1)S(1)}, bf16[256,1024]{1,0:T(8,128)(2,1)S(1)}, u32[]{:S(2)}, u32[]{:S(2)}) collective-permute-start(bf16[256,1024]{1,0:T(8,128)(2,1)S(1)} %slice.6), channel_id=1, source_target_pairs={{0,4},{4,8},{8,12},{1,5},{5,9},{9,13},{2,6},{6,10},{10,14},{3,7},{... | collective-permute-start | bytes 1572872 | tf_op jit(solution)/shard_map/ppermute | solution.py:393
  17.7 1.3 %collective-permute-start.3 = (bf16[256,1024]{1,0:T(8,128)(2,1)S(1)}, bf16[256,1024]{1,0:T(8,128)(2,1)S(1)}, u32[]{:S(2)}, u32[]{:S(2)}) collective-permute-start(bf16[256,1024]{1,0:T(8,128)(2,1)S(1)} %slice.6), channel_id=1, source_target_pairs={{4,0},{8,4},{12,8},{5,1},{9,5},{13,9},{6,2},{10,6},{14,10},{7,3},{... | collective-permute-start | bytes 1572872 | tf_op jit(solution)/shard_map/ppermute | solution.py:393
  19.0 5.3 %own.1 = (f32[512,1024]{1,0:T(8,128)S(1)}, f32[512,1024]{1,0:T(8,128)S(1)}, f32[512,1024]{1,0:T(8,128)S(1)}) custom-call(bf16[512,1024]{1,0:T(8,128)(2,1)S(1)} %copy-done, bf16[512,1024]{1,0:T(8,128)(2,1)S(1)} %copy-done.10, bf16[512,1024]{1,0:T(8,128)(2,1)S(1)} %copy-done.5), custom_call_target="tpu_custom_call" | custom-call | flops 1073741824 | bytes 9437184 | tf_op jit(solution)/shard_map/own/pallas_call | solution.py:346
  24.3 5.1 %collective-permute-done.nb_ref = bf16[512,1024]{1,0:T(8,128)(2,1)S(1)} collective-permute-done((bf16[512,1024]{1,0:T(8,128)(2,1)}, bf16[512,1024]{1,0:T(8,128)(2,1)S(1)}, u32[]{:S(2)}, u32[]{:S(2)}) %collective-permute-start) | collective-permute-done | bytes 1048608 | tf_op jit(solution)/shard_map/ppermute | solution.py:393
  29.4 4.4 %collective-permute-done.1.na_ref = bf16[512,1024]{1,0:T(8,128)(2,1)S(1)} collective-permute-done((bf16[512,1024]{1,0:T(8,128)(2,1)}, bf16[512,1024]{1,0:T(8,128)(2,1)S(1)}, u32[]{:S(2)}, u32[]{:S(2)}) %collective-permute-start.1) | collective-permute-done | bytes 1048608 | tf_op jit(solution)/shard_map/ppermute | solution.py:393
  35.8 3.6 %collective-permute-done.2.vb_ref = bf16[256,1024]{1,0:T(8,128)(2,1)S(1)} collective-permute-done((bf16[256,1024]{1,0:T(8,128)(2,1)S(1)}, bf16[256,1024]{1,0:T(8,128)(2,1)S(1)}, u32[]{:S(2)}, u32[]{:S(2)}) %collective-permute-start.2) | collective-permute-done | bytes 524320 | tf_op jit(solution)/shard_map/ppermute | solution.py:393
  39.4 5.6 %collective-permute-done.3.va_ref = bf16[256,1024]{1,0:T(8,128)(2,1)S(1)} collective-permute-done((bf16[256,1024]{1,0:T(8,128)(2,1)S(1)}, bf16[256,1024]{1,0:T(8,128)(2,1)S(1)}, u32[]{:S(2)}, u32[]{:S(2)}) %collective-permute-start.3) | collective-permute-done | bytes 524320 | tf_op jit(solution)/shard_map/ppermute | solution.py:393
  45.1 4.2 %collective-permute-start.6 = (bf16[256,1024]{1,0:T(8,128)(2,1)S(1)}, bf16[256,1024]{1,0:T(8,128)(2,1)}, u32[]{:S(2)}, u32[]{:S(2)}) collective-permute-start(bf16[256,1024]{1,0:T(8,128)(2,1)S(1)} %slice.7), channel_id=1, source_target_pairs={{0,4},{4,8},{8,12},{1,5},{5,9},{9,13},{2,6},{6,10},{10,14},{3,7},{... | collective-permute-start | bytes 1572872 | tf_op jit(solution)/shard_map/ppermute | solution.py:393
  50.7 4.2 %latent.3 = f32[8,768]{1,0:T(8,128)S(1)} custom-call(s32[1]{0:T(128)} %bitcast.where, s32[32]{0:T(128)S(1)} %copy-done.7, bf16[512,1024]{1,0:T(8,128)(2,1)S(1)} %copy-done, bf16[512,1024]{1,0:T(8,128)(2,1)S(1)} %copy-done.2, bf16[512,1024]{1,0:T(8,128)(2,1)S(1)} %copy-done.4), custom_call_target="tpu_custom_call" | custom-call | flops 8053063680 | bytes 2359296 | tf_op jit(solution)/shard_map/latent/pallas_call | solution.py:365
  54.9 5.4 %weigh_near.1 = (f32[512,1024]{1,0:T(8,128)S(1)}, f32[512,1024]{1,0:T(8,128)S(1)}, f32[512,1024]{1,0:T(8,128)S(1)}, bf16[512,2048]{1,0:T(8,128)(2,1)S(1)}, bf16[512,2048]{1,0:T(8,128)(2,1)S(1)}) custom-call(s32[1]{0:T(128)} %bitcast.where, s32[2,8]{1,0:T(2,128)S(1)} %copy-done.8, ...), custom_call_target="tpu_custom_call", output_to_operand_aliasing={{0}: (5, {}), {1}: (6, {}), {2}: (7, {})} | custom-call | flops 536870912 | bytes 10485760 | tf_op jit(solution)/shard_map/weigh_near/pallas_call | solution.py:408
  60.3 7.2 %collective-permute-done.5.fa_ref = bf16[512,1024]{1,0:T(8,128)(2,1)S(1)} collective-permute-done((bf16[512,1024]{1,0:T(8,128)(2,1)S(1)}, bf16[512,1024]{1,0:T(8,128)(2,1)S(1)}, u32[]{:S(2)}, u32[]{:S(2)}) %collective-permute-start.5) | collective-permute-done | bytes 1048608 | tf_op jit(solution)/shard_map/ppermute | solution.py:393
  67.5 4.7 %weigh_far.1 = (f32[512,1024]{1,0:T(8,128)S(1)}, bf16[512,2048]{1,0:T(8,128)(2,1)S(1)}, bf16[8,2048]{1,0:T(8,128)(2,1)S(1)}) custom-call(s32[1]{0:T(128)} %bitcast.where, s32[2,8]{1,0:T(2,128)S(1)} %copy-done.8, s32[32]{0:T(128)S(1)} %copy-done.7, bf16[512,1024]{1,0:T(8,128)(2,1)S(1)} %copy-done, bf16[512,1024]{1,0:T(8,128)(2,1)S(1)} %collective-permute-done.4.fb_ref, ...), custom_call_target="tpu_custom_call" | custom-call | flops 268435456 | bytes 11534336 | tf_op jit(solution)/shard_map/weigh_far/pallas_call | solution.py:423
  73.5 1.3 %collective-permute-start.12 = (bf16[256,1024]{1,0:T(8,128)(2,1)S(1)}, bf16[256,1024]{1,0:T(8,128)(2,1)S(1)}, u32[]{:S(2)}, u32[]{:S(2)}) collective-permute-start(bf16[256,1024]{1,0:T(8,128)(2,1)S(1)} %collective-permute-done.3.va_ref), channel_id=1, source_target_pairs={{4,0},{8,4},{5,1},{9,5},{6,2},{10,6},{7,3},{11,7},{20,16},{24,20},... | collective-permute-start | bytes 1572872 | tf_op jit(solution)/shard_map/ppermute | solution.py:393
  74.8 2.3 %mix.2 = (f32[256,1024]{1,0:T(8,128)S(1)}, f32[4,1024]{1,0:T(4,128)S(1)}) custom-call(s32[1]{0:T(128)} %bitcast.where, s32[32]{0:T(128)S(1)} %copy-done.7, f32[512,1024]{1,0:T(8,128)S(1)} %get-tuple-element.54.acc_in, f32[512,1024]{1,0:T(8,128)S(1)} %get-tuple-element.68.scale_in, bf16[512,2048]{1,0:T(8,128)(2,1)S(1)} %get-tuple-element.69.wb_ref, ...), custom_call_target="tpu_custom_call" | custom-call | flops 268435456 | bytes 5242880 | tf_op jit(solution)/shard_map/mix/pallas_call | solution.py:437
  77.0 3.9 %collective-permute-done.8.sums_ref = bf16[8,2048]{1,0:T(8,128)(2,1)S(1)} collective-permute-done((bf16[8,2048]{1,0:T(8,128)(2,1)S(1)}, bf16[8,2048]{1,0:T(8,128)(2,1)S(1)}, u32[]{:S(2)}, u32[]{:S(2)}) %collective-permute-start.8) | collective-permute-done | bytes 32800 | tf_op jit(solution)/shard_map/ppermute | solution.py:393
  83.6 1.5 %collective-permute-start.9 = (bf16[256,1024]{1,0:T(8,128)(2,1)}, bf16[256,1024]{1,0:T(8,128)(2,1)}, u32[]{:S(2)}, u32[]{:S(2)}) collective-permute-start(bf16[256,1024]{1,0:T(8,128)(2,1)} %collective-permute-done.6.vb_ref), channel_id=1, source_target_pairs={{4,8},{8,12},{5,9},{9,13},{6,10},{10,14},{7,11},{11,15},{20,24},{2... | collective-permute-start | bytes 1572872 | tf_op jit(solution)/shard_map/ppermute | solution.py:393
  85.1 3.2 %mix.3 = (f32[256,1024]{1,0:T(8,128)S(1)}, f32[4,1024]{1,0:T(4,128)S(1)}) custom-call(s32[1]{0:T(128)} %bitcast.where, s32[32]{0:T(128)S(1)} %copy-done.7, f32[512,1024]{1,0:T(8,128)S(1)} %get-tuple-element.54.acc_in, f32[512,1024]{1,0:T(8,128)S(1)} %get-tuple-element.68.scale_in, bf16[512,2048]{1,0:T(8,128)(2,1)S(1)} %get-tuple-element.69.wb_ref, ...), custom_call_target="tpu_custom_call" | custom-call | flops 268435456 | bytes 5242880 | tf_op jit(solution)/shard_map/mix/pallas_call | solution.py:437
  89.5 2.9 %collective-permute-done.12.va_ref = bf16[256,1024]{1,0:T(8,128)(2,1)S(1)} collective-permute-done((bf16[256,1024]{1,0:T(8,128)(2,1)S(1)}, bf16[256,1024]{1,0:T(8,128)(2,1)S(1)}, u32[]{:S(2)}, u32[]{:S(2)}) %collective-permute-start.12) | collective-permute-done | bytes 524320 | tf_op jit(solution)/shard_map/ppermute | solution.py:393
  93.6 4.0 %all-to-all-start = ((bf16[4,4,1024]{2,1,0:T(4,128)(2,1)}), bf16[4,4,1024]{2,1,0:T(4,128)(2,1)S(1)}, u32[]{:S(2)}, u32[]{:S(2)}) async-start(bf16[4,4,1024]{2,1,0:T(4,128)(2,1)} %route.1), calls=%async_computation | async-start | bytes 65536 | tf_op jit(solution)/shard_map/all_to_all | solution.py:511
  97.6 3.2 %collective-permute-done.10.va_ref = bf16[256,1024]{1,0:T(8,128)(2,1)} collective-permute-done((bf16[256,1024]{1,0:T(8,128)(2,1)}, bf16[256,1024]{1,0:T(8,128)(2,1)}, u32[]{:S(2)}, u32[]{:S(2)}) %collective-permute-start.10) | collective-permute-done | bytes 524320 | tf_op jit(solution)/shard_map/ppermute | solution.py:393
  100.8 2.4 %all-to-all-done.refs_0_ = bf16[4,4,1024]{2,1,0:T(4,128)(2,1)S(1)} async-done(((bf16[4,4,1024]{2,1,0:T(4,128)(2,1)}), bf16[4,4,1024]{2,1,0:T(4,128)(2,1)S(1)}, u32[]{:S(2)}, u32[]{:S(2)}) %all-to-all-start) | async-done | bytes 32800 | tf_op jit(solution)/shard_map/all_to_all | solution.py:511
  103.3 3.0 %finish.3 = (bf16[512,1024]{1,0:T(8,128)(2,1)}, bf16[1,4,2,1024]{3,2,1,0:T(2,128)(2,1)}) custom-call(s32[1]{0:T(128)} %bitcast.where, f32[256,1024]{1,0:T(8,128)S(1)} %get-tuple-element.80.acc_ref, bf16[512,2048]{1,0:T(8,128)(2,1)S(1)} %get-tuple-element.81.w_ref, bf16[256,1024]{1,0:T(8,128)(2,1)} %collective-permute-done.9.vb_ref, ...), custom_call_target="tpu_custom_call", output_to_operand_aliasing={{0}: (6, {})} | custom-call | flops 134217728 | bytes 3670016 | tf_op jit(solution)/shard_map/finish/pallas_call | solution.py:457
  (40 shorter events, 15.2 us)
Async XLA Ops:
  0.6 28.8 %collective-permute-start = (bf16[512,1024]{1,0:T(8,128)(2,1)}, bf16[512,1024]{1,0:T(8,128)(2,1)S(1)}, u32[]{:S(2)}, u32[]{:S(2)}) collective-permute-start(bf16[512,1024]{1,0:T(8,128)(2,1)} %k_ref.1), channel_id=1, source_target_pairs={{0,4},{4,8},{8,12},{1,5},{5,9},{9,13},{2,6},{6,10},{10,14},{3,7},{... | collective-permute-start | bytes 3145736 | tf_op jit(solution)/shard_map/ppermute | solution.py:393
  5.6 28.2 %collective-permute-start.1 = (bf16[512,1024]{1,0:T(8,128)(2,1)}, bf16[512,1024]{1,0:T(8,128)(2,1)S(1)}, u32[]{:S(2)}, u32[]{:S(2)}) collective-permute-start(bf16[512,1024]{1,0:T(8,128)(2,1)} %k_ref.1), channel_id=1, source_target_pairs={{4,0},{8,4},{12,8},{5,1},{9,5},{13,9},{6,2},{10,6},{14,10},{7,3},{... | collective-permute-start | bytes 3145736 | tf_op jit(solution)/shard_map/ppermute | solution.py:393
  6.9 1.2 %copy-start = (bf16[512,1024]{1,0:T(8,128)(2,1)S(1)}, bf16[512,1024]{1,0:T(8,128)(2,1)}, u32[]{:S(2)}) copy-start(bf16[512,1024]{1,0:T(8,128)(2,1)} %q_ref.7) | copy-start | bytes 3145732
  8.2 1.2 %copy-start.1 = (bf16[512,1024]{1,0:T(8,128)(2,1)S(1)}, bf16[512,1024]{1,0:T(8,128)(2,1)}, u32[]{:S(2)}) copy-start(bf16[512,1024]{1,0:T(8,128)(2,1)} %lk_ref.3) | copy-start | bytes 3145732
  9.4 1.2 %copy-start.3 = (bf16[512,1024]{1,0:T(8,128)(2,1)S(1)}, bf16[512,1024]{1,0:T(8,128)(2,1)}, u32[]{:S(2)}) copy-start(bf16[512,1024]{1,0:T(8,128)(2,1)} %lv_ref.3) | copy-start | bytes 3145732
  11.3 1.7 %copy-start.5 = (bf16[512,1024]{1,0:T(8,128)(2,1)S(1)}, bf16[512,1024]{1,0:T(8,128)(2,1)}, u32[]{:S(2)}) copy-start(bf16[512,1024]{1,0:T(8,128)(2,1)} %v_ref.3) | copy-start | bytes 3145732
  11.3 7.8 %copy-start.10 = (bf16[512,1024]{1,0:T(8,128)(2,1)S(1)}, bf16[512,1024]{1,0:T(8,128)(2,1)}, u32[]{:S(2)}) copy-start(bf16[512,1024]{1,0:T(8,128)(2,1)} %k_ref.1) | copy-start | bytes 3145732
  13.0 37.7 %copy-start.2 = (bf16[512,1024]{1,0:T(8,128)(2,1)S(1)}, bf16[512,1024]{1,0:T(8,128)(2,1)}, u32[]{:S(2)}) copy-start(bf16[512,1024]{1,0:T(8,128)(2,1)} %lk_ref.3) | copy-start | bytes 3145732
  13.0 37.7 %copy-start.4 = (bf16[512,1024]{1,0:T(8,128)(2,1)S(1)}, bf16[512,1024]{1,0:T(8,128)(2,1)}, u32[]{:S(2)}) copy-start(bf16[512,1024]{1,0:T(8,128)(2,1)} %lv_ref.3) | copy-start | bytes 3145732
  13.0 37.7 %copy-start.7 = (s32[32]{0:T(128)S(1)}, s32[32]{0:T(128)}, u32[]{:S(2)}) copy-start(s32[32]{0:T(128)} %starts.11) | copy-start | bytes 388
  13.0 26.4 %collective-permute-start.2 = (bf16[256,1024]{1,0:T(8,128)(2,1)S(1)}, bf16[256,1024]{1,0:T(8,128)(2,1)S(1)}, u32[]{:S(2)}, u32[]{:S(2)}) collective-permute-start(bf16[256,1024]{1,0:T(8,128)(2,1)S(1)} %slice.6), channel_id=1, source_target_pairs={{0,4},{4,8},{8,12},{1,5},{5,9},{9,13},{2,6},{6,10},{10,14},{3,7},{... | collective-permute-start | bytes 1572872 | tf_op jit(solution)/shard_map/ppermute | solution.py:393
  17.7 27.3 %collective-permute-start.3 = (bf16[256,1024]{1,0:T(8,128)(2,1)S(1)}, bf16[256,1024]{1,0:T(8,128)(2,1)S(1)}, u32[]{:S(2)}, u32[]{:S(2)}) collective-permute-start(bf16[256,1024]{1,0:T(8,128)(2,1)S(1)} %slice.6), channel_id=1, source_target_pairs={{4,0},{8,4},{12,8},{5,1},{9,5},{13,9},{6,2},{10,6},{14,10},{7,3},{... | collective-permute-start | bytes 1572872 | tf_op jit(solution)/shard_map/ppermute | solution.py:393
  33.8 26.5 %collective-permute-start.4 = (bf16[512,1024]{1,0:T(8,128)(2,1)S(1)}, bf16[512,1024]{1,0:T(8,128)(2,1)S(1)}, u32[]{:S(2)}, u32[]{:S(2)}) collective-permute-start(bf16[512,1024]{1,0:T(8,128)(2,1)S(1)} %collective-permute-done.nb_ref), channel_id=1, source_target_pairs={{4,8},{8,12},{5,9},{9,13},{6,10},{10,14},{7,11},{11,15},{20,24},{2... | collective-permute-start | bytes 3145736 | tf_op jit(solution)/shard_map/ppermute | solution.py:393
  34.5 33.0 %collective-permute-start.5 = (bf16[512,1024]{1,0:T(8,128)(2,1)S(1)}, bf16[512,1024]{1,0:T(8,128)(2,1)S(1)}, u32[]{:S(2)}, u32[]{:S(2)}) collective-permute-start(bf16[512,1024]{1,0:T(8,128)(2,1)S(1)} %collective-permute-done.1.na_ref), channel_id=1, source_target_pairs={{4,0},{8,4},{5,1},{9,5},{6,2},{10,6},{7,3},{11,7},{20,16},{24,20},... | collective-permute-start | bytes 3145736 | tf_op jit(solution)/shard_map/ppermute | solution.py:393
  45.1 9.8 %copy-start.8 = (s32[2,8]{1,0:T(2,128)S(1)}, s32[2,8]{1,0:T(2,128)}, u32[]{:S(2)}) copy-start(s32[2,8]{1,0:T(2,128)} %pattern.3) | copy-start | bytes 196
  45.1 37.1 %collective-permute-start.6 = (bf16[256,1024]{1,0:T(8,128)(2,1)S(1)}, bf16[256,1024]{1,0:T(8,128)(2,1)}, u32[]{:S(2)}, u32[]{:S(2)}) collective-permute-start(bf16[256,1024]{1,0:T(8,128)(2,1)S(1)} %slice.7), channel_id=1, source_target_pairs={{0,4},{4,8},{8,12},{1,5},{5,9},{9,13},{2,6},{6,10},{10,14},{3,7},{... | collective-permute-start | bytes 1572872 | tf_op jit(solution)/shard_map/ppermute | solution.py:393
  49.4 32.9 %collective-permute-start.7 = (bf16[256,1024]{1,0:T(8,128)(2,1)S(1)}, bf16[256,1024]{1,0:T(8,128)(2,1)}, u32[]{:S(2)}, u32[]{:S(2)}) collective-permute-start(bf16[256,1024]{1,0:T(8,128)(2,1)S(1)} %slice.7), channel_id=1, source_target_pairs={{4,0},{8,4},{12,8},{5,1},{9,5},{13,9},{6,2},{10,6},{14,10},{7,3},{... | collective-permute-start | bytes 1572872 | tf_op jit(solution)/shard_map/ppermute | solution.py:393
  72.2 8.7 %collective-permute-start.8 = (bf16[8,2048]{1,0:T(8,128)(2,1)S(1)}, bf16[8,2048]{1,0:T(8,128)(2,1)S(1)}, u32[]{:S(2)}, u32[]{:S(2)}) collective-permute-start(bf16[8,2048]{1,0:T(8,128)(2,1)S(1)} %get-tuple-element.72), channel_id=1, source_target_pairs={{0,8},{4,12},{8,0},{12,4},{1,9},{5,13},{9,1},{13,5},{2,10},{6,14},... | collective-permute-start | bytes 98312 | tf_op jit(solution)/shard_map/ppermute | solution.py:393
  72.8 16.8 %collective-permute-start.11 = (bf16[256,1024]{1,0:T(8,128)(2,1)S(1)}, bf16[256,1024]{1,0:T(8,128)(2,1)S(1)}, u32[]{:S(2)}, u32[]{:S(2)}) collective-permute-start(bf16[256,1024]{1,0:T(8,128)(2,1)S(1)} %collective-permute-done.2.vb_ref), channel_id=1, source_target_pairs={{4,8},{8,12},{5,9},{9,13},{6,10},{10,14},{7,11},{11,15},{20,24},{2... | collective-permute-start | bytes 1572872 | tf_op jit(solution)/shard_map/ppermute | solution.py:393
  73.5 19.0 %collective-permute-start.12 = (bf16[256,1024]{1,0:T(8,128)(2,1)S(1)}, bf16[256,1024]{1,0:T(8,128)(2,1)S(1)}, u32[]{:S(2)}, u32[]{:S(2)}) collective-permute-start(bf16[256,1024]{1,0:T(8,128)(2,1)S(1)} %collective-permute-done.3.va_ref), channel_id=1, source_target_pairs={{4,0},{8,4},{5,1},{9,5},{6,2},{10,6},{7,3},{11,7},{20,16},{24,20},... | collective-permute-start | bytes 1572872 | tf_op jit(solution)/shard_map/ppermute | solution.py:393
  82.2 6.0 %copy-start.9 = (s32[32]{0:T(128)S(1)}, s32[32]{0:T(128)}, u32[]{:S(2)}) copy-start(s32[32]{0:T(128)} %owners.1) | copy-start | bytes 388
  82.3 18.6 %collective-permute-start.10 = (bf16[256,1024]{1,0:T(8,128)(2,1)}, bf16[256,1024]{1,0:T(8,128)(2,1)}, u32[]{:S(2)}, u32[]{:S(2)}) collective-permute-start(bf16[256,1024]{1,0:T(8,128)(2,1)} %collective-permute-done.7.va_ref), channel_id=1, source_target_pairs={{4,0},{8,4},{5,1},{9,5},{6,2},{10,6},{7,3},{11,7},{20,16},{24,20},... | collective-permute-start | bytes 1572872 | tf_op jit(solution)/shard_map/ppermute | solution.py:393
  83.6 17.3 %collective-permute-start.9 = (bf16[256,1024]{1,0:T(8,128)(2,1)}, bf16[256,1024]{1,0:T(8,128)(2,1)}, u32[]{:S(2)}, u32[]{:S(2)}) collective-permute-start(bf16[256,1024]{1,0:T(8,128)(2,1)} %collective-permute-done.6.vb_ref), channel_id=1, source_target_pairs={{4,8},{8,12},{5,9},{9,13},{6,10},{10,14},{7,11},{11,15},{20,24},{2... | collective-permute-start | bytes 1572872 | tf_op jit(solution)/shard_map/ppermute | solution.py:393
  93.6 9.7 %all-to-all-start = ((bf16[4,4,1024]{2,1,0:T(4,128)(2,1)}), bf16[4,4,1024]{2,1,0:T(4,128)(2,1)S(1)}, u32[]{:S(2)}, u32[]{:S(2)}) async-start(bf16[4,4,1024]{2,1,0:T(4,128)(2,1)} %route.1), calls=%async_computation | async-start | bytes 65536 | tf_op jit(solution)/shard_map/all_to_all | solution.py:511
  (1 other events, 0.7 us)

commit v8 on v7

--- a/solution.py
+++ b/solution.py
@@ -294,27 +294,41 @@
         out_ref[target] = jnp.concatenate(rows, axis=0).astype(BF16)
 
 
+def pool_kernel(got_ref, out_ref):
+    got = [got_ref[s].astype(F32) for s in range(4)]
+    for s in range(4):
+        out_ref[0, s] = (got[s][:2] + got[s ^ 2][2:]).astype(BF16)
+
+
 def context_kernel(block, where, acc_ref, w_ref, vb_ref, va_ref, *refs):
-    stage, sem = refs[-2:]
-    if len(refs) == 3:
-        out_ref = refs[0]
-    else:
-        got_ref, _, out_ref, pooled_ref = refs[:4]
+    out_ref, vals, stage, in_sems, out_sems = refs[-5:]
     behind = where[0] >= 2
+    width = 2 * HD
+    pairs = [pl.ds(first, width) for first in range(0, acc_ref.shape[1], width)]
+
+    def fetch(source, i):
+        return pltpu.make_async_copy(source.at[:, pairs[i]], vals.at[:, pairs[i]], in_sems.at[i])
+
+    @pl.when(behind)
+    def _():
+        for i in range(len(pairs)):
+            fetch(vb_ref, i).start()
+
+    @pl.when(jnp.logical_not(behind))
+    def _():
+        for i in range(len(pairs)):
+            fetch(va_ref, i).start()
+
     copies = []
-    for h in range(acc_ref.shape[1] // HD):
-        head = pl.ds(h * HD, HD)
-        v = jnp.where(behind, vb_ref[:, head], va_ref[:, head])
-        stage[:, head] = (acc_ref[:, head] + dot(w_ref[pl.ds(block * BLK, BLK), pl.ds(h * BLK, BLK)], v)).astype(BF16)
-        if h % 2:
-            pair = pl.ds((h - 1) * HD, 2 * HD)
-            copy = pltpu.make_async_copy(stage.at[:, pair], out_ref.at[pl.ds(block * BLK, BLK), pair], sem.at[h // 2])
-            copy.start()
-            copies.append(copy)
-    if len(refs) > 3:
-        got = [got_ref[s].astype(F32) for s in range(4)]
-        for s in range(4):
-            pooled_ref[0, s] = (got[s][:2] + got[s ^ 2][2:]).astype(BF16)
+    for i, pair in enumerate(pairs):
+        fetch(vb_ref, i).wait()
+        for h in range(2 * i, 2 * i + 2):
+            head = pl.ds(h * HD, HD)
+            found = dot(w_ref[pl.ds(block * BLK, BLK), pl.ds(h * BLK, BLK)], vals[:, head])
+            stage[:, head] = (acc_ref[:, head] + found).astype(BF16)
+        copy = pltpu.make_async_copy(stage.at[:, pair], out_ref.at[pl.ds(block * BLK, BLK), pair], out_sems.at[i])
+        copy.start()
+        copies.append(copy)
     for copy in copies:
         copy.wait()
 
@@ -449,18 +463,16 @@
             name="mix",
         )(where, doc_starts, acc, scale, *weights, *near_vals, lat)
 
-    def finish(block, acc, weights, far_vals, held):
-        context = shape(rows, columns, BF16)
-        pooled = jax.ShapeDtypeStruct((1, 4, 2, columns), BF16)
+    def finish(block, acc, weights, far_vals, context):
+        held = [] if context is None else [context]
         anywhere = pl.BlockSpec(memory_space=pl.ANY)
-        whole = pl.BlockSpec(memory_space=pltpu.VMEM)
         return pl.pallas_call(
             functools.partial(context_kernel, block),
-            in_specs=smem(1) + vmem(4) + ([whole, anywhere] if held else []),
-            out_specs=[anywhere, whole] if held else anywhere,
-            out_shape=(context, pooled) if held else context,
-            scratch_shapes=[pltpu.VMEM((BLK, columns), BF16), pltpu.SemaphoreType.DMA((heads // 2,))],
-            input_output_aliases={6: 0} if held else {},
+            in_specs=smem(1) + vmem(2) + [anywhere] * (2 + len(held)),
+            out_specs=anywhere,
+            out_shape=shape(rows, columns, BF16),
+            scratch_shapes=[pltpu.VMEM((BLK, columns), BF16)] * 2 + [pltpu.SemaphoreType.DMA((heads // 2,))] * 2,
+            input_output_aliases={5: 0} if held else {},
             compiler_params=PARAMS,
             cost_estimate=pl.CostEstimate(flops=2 * BLK * columns * BLK, bytes_accessed=14 * BLK * columns, transcendentals=0),
             name="finish",
@@ -498,7 +510,7 @@
     near_vals[1], parts, mixed[0] = lax.optimization_barrier((near_vals[1], parts, mixed[0]))
     far_vals.append(onward(near_vals[1]))
     mixed.append(mix(1, acc, scale, near_weights, near_vals[1], lat))
-    context = finish(0, mixed[0][0], far_weights, far_vals[0], [])
+    context = finish(0, mixed[0][0], far_weights, far_vals[0], None)
     sent = pl.pallas_call(
         route_kernel,
         in_specs=smem(2) + vmem(3),
@@ -509,7 +521,17 @@
     )(where, doc_owner, parts, *[m[1] for m in mixed])
     sent, context = lax.optimization_barrier((sent, context))
     got = lax.all_to_all(sent, "seq", split_axis=0, concat_axis=0, tiled=True)
-    return finish(1, mixed[1][0], far_weights, far_vals[1], [got, context])
+    context = finish(1, mixed[1][0], far_weights, far_vals[1], context)
+    got, context = lax.optimization_barrier((got, context))
+    pooled = pl.pallas_call(
+        pool_kernel,
+        in_specs=vmem(1),
+        out_specs=pl.BlockSpec(memory_space=pltpu.VMEM),
+        out_shape=jax.ShapeDtypeStruct((1, 4, 2, columns), BF16),
+        compiler_params=PARAMS,
+        name="pool",
+    )(got)
+    return context, pooled
 
 
 def body(queries, keys, values, latent_keys, latent_values, pattern, doc_starts, doc_owner):

time: 107 us -> 105 us (0.981)
  waiting for transfers between devices: 38.5 us -> 34.2 us
  starting transfers between devices: 29.2 us -> 30.6 us
    all_to_all x1, waiting for transfers between devices: 2.44 us -> 0.26 us  [four_shards(): got = lax.all_to_all(sent, 'seq', split_axis=0, concat_axis=0, tiled=True)]
    ppermute x13, waiting for transfers between devices: 36 us -> 33.9 us  [move(): return lax.ppermute(value, 'seq', pairs)]
    all_to_all x1, starting transfers between devices: 4.01 us -> 5.48 us  [four_shards(): got = lax.all_to_all(sent, 'seq', split_axis=0, concat_axis=0, tiled=True)]
  transfers between devices with their start and end apart: 14 -> 14, of which waited for: 9 -> 9; matrix products, arithmetic and copies ran while one was open for 0% -> 0% of each run, Pallas kernels for 29% -> 32%
where the time goes in v8:
time: 105 us; the launch traced here: 104 us
  waiting for transfers between devices  34.2 us (33%)
  Pallas kernels  34 us (32%)
  starting transfers between devices  30.6 us (29%)
  local copies, waits for them, and re-layouts  4.43 us (4%)
    ppermute x13, waiting for transfers between devices, move(): return lax.ppermute(value, 'seq', pairs)  33.9 us
    ppermute x13, starting transfers between devices, move(): return lax.ppermute(value, 'seq', pairs)  25.1 us
    pallas_call x2, Pallas kernels, latent_call(): pl.pallas_call(latent_kernel, grid=(steps,), in_specs=smem(2) + [pl.Block...  5.81 us
    pallas_call x2, Pallas kernels, mix(): pl.pallas_call(functools.partial(mix_kernel, block), grid=(heads // step,...  5.49 us
    all_to_all x1, starting transfers between devices, four_shards(): got = lax.all_to_all(sent, 'seq', split_axis=0, concat_axis=0, tiled=True)  5.48 us
    pallas_call x1, Pallas kernels, weigh_near(): pl.pallas_call(functools.partial(near_weigh_kernel, 4), grid=(heads // st...  5.41 us
    pallas_call x1, Pallas kernels, own_call(): pl.pallas_call(own_kernel, grid=(columns // wide,), in_specs=[spec(rows,...  5.27 us
    pallas_call x1, Pallas kernels, weigh_far(): pl.pallas_call(functools.partial(far_weigh_kernel, 4), grid=(heads // ste...  4.68 us
  transfers between devices with their start and end apart: 14, of which 9 were waited for; matrix products, arithmetic and copies ran while one was open for 0% of the time, Pallas kernels for 32%

profile of v8, /device:TPU:0, one launch (start us, length us, event | category | flops | bytes accessed | tf_op | source)
XLA Modules:
  0.0 104.1 jit_solution(12184099494367296240)
XLA Ops:
  0.6 5.0 %collective-permute-start.4 = (bf16[512,1024]{1,0:T(8,128)(2,1)}, bf16[512,1024]{1,0:T(8,128)(2,1)S(1)}, u32[]{:S(2)}, u32[]{:S(2)}) collective-permute-start(bf16[512,1024]{1,0:T(8,128)(2,1)} %k_ref.1), channel_id=1, source_target_pairs={{0,4},{4,8},{8,12},{1,5},{5,9},{9,13},{2,6},{6,10},{10,14},{3,7},{... | collective-permute-start | bytes 3145736 | tf_op jit(solution)/shard_map/ppermute | solution.py:407
  5.6 1.3 %collective-permute-start.5 = (bf16[512,1024]{1,0:T(8,128)(2,1)}, bf16[512,1024]{1,0:T(8,128)(2,1)S(1)}, u32[]{:S(2)}, u32[]{:S(2)}) collective-permute-start(bf16[512,1024]{1,0:T(8,128)(2,1)} %k_ref.1), channel_id=1, source_target_pairs={{4,0},{8,4},{12,8},{5,1},{9,5},{13,9},{6,2},{10,6},{14,10},{7,3},{... | collective-permute-start | bytes 3145736 | tf_op jit(solution)/shard_map/ppermute | solution.py:407
  11.3 1.6 %latent.2 = f32[8,256]{1,0:T(8,128)S(1)} custom-call(s32[1]{0:T(128)} %bitcast.where, s32[32]{0:T(128)S(1)} %copy-done.6, bf16[512,1024]{1,0:T(8,128)(2,1)S(1)} %copy-done, bf16[512,1024]{1,0:T(8,128)(2,1)S(1)} %copy-done.1, bf16[512,1024]{1,0:T(8,128)(2,1)S(1)} %copy-done.3), custom_call_target="tpu_custom_call" | custom-call | flops 268435456 | bytes 786432 | tf_op jit(solution)/shard_map/latent/pallas_call | solution.py:379
  13.0 4.7 %collective-permute-start = (bf16[256,1024]{1,0:T(8,128)(2,1)S(1)}, bf16[256,1024]{1,0:T(8,128)(2,1)S(1)}, u32[]{:S(2)}, u32[]{:S(2)}) collective-permute-start(bf16[256,1024]{1,0:T(8,128)(2,1)S(1)} %slice.6), channel_id=1, source_target_pairs={{0,4},{4,8},{8,12},{1,5},{5,9},{9,13},{2,6},{6,10},{10,14},{3,7},{... | collective-permute-start | bytes 1572872 | tf_op jit(solution)/shard_map/ppermute | solution.py:407
  17.7 1.3 %collective-permute-start.1 = (bf16[256,1024]{1,0:T(8,128)(2,1)S(1)}, bf16[256,1024]{1,0:T(8,128)(2,1)S(1)}, u32[]{:S(2)}, u32[]{:S(2)}) collective-permute-start(bf16[256,1024]{1,0:T(8,128)(2,1)S(1)} %slice.6), channel_id=1, source_target_pairs={{4,0},{8,4},{12,8},{5,1},{9,5},{13,9},{6,2},{10,6},{14,10},{7,3},{... | collective-permute-start | bytes 1572872 | tf_op jit(solution)/shard_map/ppermute | solution.py:407
  19.0 5.3 %own.1 = (f32[512,1024]{1,0:T(8,128)S(1)}, f32[512,1024]{1,0:T(8,128)S(1)}, f32[512,1024]{1,0:T(8,128)S(1)}) custom-call(bf16[512,1024]{1,0:T(8,128)(2,1)S(1)} %copy-done, bf16[512,1024]{1,0:T(8,128)(2,1)S(1)} %copy-done.10, bf16[512,1024]{1,0:T(8,128)(2,1)S(1)} %copy-done.5), custom_call_target="tpu_custom_call" | custom-call | flops 1073741824 | bytes 9437184 | tf_op jit(solution)/shard_map/own/pallas_call | solution.py:360
  24.3 5.1 %collective-permute-done.4.nb_ref = bf16[512,1024]{1,0:T(8,128)(2,1)S(1)} collective-permute-done((bf16[512,1024]{1,0:T(8,128)(2,1)}, bf16[512,1024]{1,0:T(8,128)(2,1)S(1)}, u32[]{:S(2)}, u32[]{:S(2)}) %collective-permute-start.4) | collective-permute-done | bytes 1048608 | tf_op jit(solution)/shard_map/ppermute | solution.py:407
  29.4 4.4 %collective-permute-done.5.na_ref = bf16[512,1024]{1,0:T(8,128)(2,1)S(1)} collective-permute-done((bf16[512,1024]{1,0:T(8,128)(2,1)}, bf16[512,1024]{1,0:T(8,128)(2,1)S(1)}, u32[]{:S(2)}, u32[]{:S(2)}) %collective-permute-start.5) | collective-permute-done | bytes 1048608 | tf_op jit(solution)/shard_map/ppermute | solution.py:407
  34.5 1.3 %collective-permute-start.7 = (bf16[512,1024]{1,0:T(8,128)(2,1)S(1)}, bf16[512,1024]{1,0:T(8,128)(2,1)S(1)}, u32[]{:S(2)}, u32[]{:S(2)}) collective-permute-start(bf16[512,1024]{1,0:T(8,128)(2,1)S(1)} %collective-permute-done.5.na_ref), channel_id=1, source_target_pairs={{4,0},{8,4},{5,1},{9,5},{6,2},{10,6},{7,3},{11,7},{20,16},{24,20},... | collective-permute-start | bytes 3145736 | tf_op jit(solution)/shard_map/ppermute | solution.py:407
  35.8 3.6 %collective-permute-done.vb_ref = bf16[256,1024]{1,0:T(8,128)(2,1)S(1)} collective-permute-done((bf16[256,1024]{1,0:T(8,128)(2,1)S(1)}, bf16[256,1024]{1,0:T(8,128)(2,1)S(1)}, u32[]{:S(2)}, u32[]{:S(2)}) %collective-permute-start) | collective-permute-done | bytes 524320 | tf_op jit(solution)/shard_map/ppermute | solution.py:407
  39.4 5.6 %collective-permute-done.1.va_ref = bf16[256,1024]{1,0:T(8,128)(2,1)S(1)} collective-permute-done((bf16[256,1024]{1,0:T(8,128)(2,1)S(1)}, bf16[256,1024]{1,0:T(8,128)(2,1)S(1)}, u32[]{:S(2)}, u32[]{:S(2)}) %collective-permute-start.1) | collective-permute-done | bytes 524320 | tf_op jit(solution)/shard_map/ppermute | solution.py:407
  45.1 4.3 %collective-permute-start.2 = (bf16[256,1024]{1,0:T(8,128)(2,1)S(1)}, bf16[256,1024]{1,0:T(8,128)(2,1)}, u32[]{:S(2)}, u32[]{:S(2)}) collective-permute-start(bf16[256,1024]{1,0:T(8,128)(2,1)S(1)} %slice.7), channel_id=1, source_target_pairs={{0,4},{4,8},{8,12},{1,5},{5,9},{9,13},{2,6},{6,10},{10,14},{3,7},{... | collective-permute-start | bytes 1572872 | tf_op jit(solution)/shard_map/ppermute | solution.py:407
  50.7 4.2 %latent.3 = f32[8,768]{1,0:T(8,128)S(1)} custom-call(s32[1]{0:T(128)} %bitcast.where, s32[32]{0:T(128)S(1)} %copy-done.7, bf16[512,1024]{1,0:T(8,128)(2,1)S(1)} %copy-done, bf16[512,1024]{1,0:T(8,128)(2,1)S(1)} %copy-done.2, bf16[512,1024]{1,0:T(8,128)(2,1)S(1)} %copy-done.4), custom_call_target="tpu_custom_call" | custom-call | flops 8053063680 | bytes 2359296 | tf_op jit(solution)/shard_map/latent/pallas_call | solution.py:379
  54.9 5.4 %weigh_near.1 = (f32[512,1024]{1,0:T(8,128)S(1)}, f32[512,1024]{1,0:T(8,128)S(1)}, f32[512,1024]{1,0:T(8,128)S(1)}, bf16[512,2048]{1,0:T(8,128)(2,1)S(1)}, bf16[512,2048]{1,0:T(8,128)(2,1)S(1)}) custom-call(s32[1]{0:T(128)} %bitcast.where, s32[2,8]{1,0:T(2,128)S(1)} %copy-done.8, ...), custom_call_target="tpu_custom_call", output_to_operand_aliasing={{0}: (5, {}), {1}: (6, {}), {2}: (7, {})} | custom-call | flops 536870912 | bytes 10485760 | tf_op jit(solution)/shard_map/weigh_near/pallas_call | solution.py:422
  60.3 7.2 %collective-permute-done.7.fa_ref = bf16[512,1024]{1,0:T(8,128)(2,1)S(1)} collective-permute-done((bf16[512,1024]{1,0:T(8,128)(2,1)S(1)}, bf16[512,1024]{1,0:T(8,128)(2,1)S(1)}, u32[]{:S(2)}, u32[]{:S(2)}) %collective-permute-start.7) | collective-permute-done | bytes 1048608 | tf_op jit(solution)/shard_map/ppermute | solution.py:407
  67.5 4.7 %weigh_far.1 = (f32[512,1024]{1,0:T(8,128)S(1)}, bf16[512,2048]{1,0:T(8,128)(2,1)S(1)}, bf16[8,2048]{1,0:T(8,128)(2,1)S(1)}) custom-call(s32[1]{0:T(128)} %bitcast.where, s32[2,8]{1,0:T(2,128)S(1)} %copy-done.8, s32[32]{0:T(128)S(1)} %copy-done.7, bf16[512,1024]{1,0:T(8,128)(2,1)S(1)} %copy-done, bf16[512,1024]{1,0:T(8,128)(2,1)S(1)} %collective-permute-done.6.fb_ref, ...), custom_call_target="tpu_custom_call" | custom-call | flops 268435456 | bytes 11534336 | tf_op jit(solution)/shard_map/weigh_far/pallas_call | solution.py:437
  74.8 2.3 %mix.2 = (f32[256,1024]{1,0:T(8,128)S(1)}, f32[4,1024]{1,0:T(4,128)S(1)}) custom-call(s32[1]{0:T(128)} %bitcast.where, s32[32]{0:T(128)S(1)} %copy-done.7, f32[512,1024]{1,0:T(8,128)S(1)} %get-tuple-element.71.acc_in, f32[512,1024]{1,0:T(8,128)S(1)} %get-tuple-element.72.scale_in, bf16[512,2048]{1,0:T(8,128)(2,1)S(1)} %get-tuple-element.73.wb_ref, ...), custom_call_target="tpu_custom_call" | custom-call | flops 268435456 | bytes 5242880 | tf_op jit(solution)/shard_map/mix/pallas_call | solution.py:451
  77.0 4.1 %collective-permute-done.8.sums_ref = bf16[8,2048]{1,0:T(8,128)(2,1)S(1)} collective-permute-done((bf16[8,2048]{1,0:T(8,128)(2,1)S(1)}, bf16[8,2048]{1,0:T(8,128)(2,1)S(1)}, u32[]{:S(2)}, u32[]{:S(2)}) %collective-permute-start.8) | collective-permute-done | bytes 32800 | tf_op jit(solution)/shard_map/ppermute | solution.py:407
  82.4 1.5 %collective-permute-start.11 = (bf16[256,1024]{1,0:T(8,128)(2,1)}, bf16[256,1024]{1,0:T(8,128)(2,1)}, u32[]{:S(2)}, u32[]{:S(2)}) collective-permute-start(bf16[256,1024]{1,0:T(8,128)(2,1)} %collective-permute-done.2.vb_ref), channel_id=1, source_target_pairs={{4,8},{8,12},{5,9},{9,13},{6,10},{10,14},{7,11},{11,15},{20,24},{2... | collective-permute-start | bytes 1572872 | tf_op jit(solution)/shard_map/ppermute | solution.py:407
  85.2 3.2 %mix.3 = (f32[256,1024]{1,0:T(8,128)S(1)}, f32[4,1024]{1,0:T(4,128)S(1)}) custom-call(s32[1]{0:T(128)} %bitcast.where, s32[32]{0:T(128)S(1)} %copy-done.7, f32[512,1024]{1,0:T(8,128)S(1)} %get-tuple-element.71.acc_in, f32[512,1024]{1,0:T(8,128)S(1)} %get-tuple-element.72.scale_in, bf16[512,2048]{1,0:T(8,128)(2,1)S(1)} %get-tuple-element.73.wb_ref, ...), custom_call_target="tpu_custom_call" | custom-call | flops 268435456 | bytes 5242880 | tf_op jit(solution)/shard_map/mix/pallas_call | solution.py:451
  90.7 1.7 %finish.2.refs_0_ = bf16[512,1024]{1,0:T(8,128)(2,1)} custom-call(s32[1]{0:T(128)} %bitcast.where, f32[256,1024]{1,0:T(8,128)S(1)} %get-tuple-element.85.acc_ref, bf16[512,2048]{1,0:T(8,128)(2,1)S(1)} %get-tuple-element.86.w_ref, bf16[256,1024]{1,0:T(8,128)(2,1)S(1)} %collective-permute-done.9.vb_ref, bf16[256,1024]{1,0:T(8,128)(2,1)S(1)} %collective-permute-done.10.va_ref), custom_call_target="tpu_custom_call" | custom-call | flops 134217728 | bytes 3670016 | tf_op jit(solution)/shard_map/finish/pallas_call | solution.py:469
  92.4 5.5 %all-to-all-start = ((bf16[4,4,1024]{2,1,0:T(4,128)(2,1)}), bf16[4,4,1024]{2,1,0:T(4,128)(2,1)S(1)}, u32[]{:S(2)}, u32[]{:S(2)}) async-start(bf16[4,4,1024]{2,1,0:T(4,128)(2,1)} %route.1), calls=%async_computation | async-start | bytes 65536 | tf_op jit(solution)/shard_map/all_to_all | solution.py:523
  97.9 2.9 %collective-permute-done.12.va_ref = bf16[256,1024]{1,0:T(8,128)(2,1)} collective-permute-done((bf16[256,1024]{1,0:T(8,128)(2,1)}, bf16[256,1024]{1,0:T(8,128)(2,1)}, u32[]{:S(2)}, u32[]{:S(2)}) %collective-permute-start.12) | collective-permute-done | bytes 524320 | tf_op jit(solution)/shard_map/ppermute | solution.py:407
  100.7 2.5 %finish.3 = bf16[512,1024]{1,0:T(8,128)(2,1)} custom-call(s32[1]{0:T(128)} %bitcast.where, f32[256,1024]{1,0:T(8,128)S(1)} %get-tuple-element.88.acc_ref, bf16[512,2048]{1,0:T(8,128)(2,1)S(1)} %get-tuple-element.86.w_ref, bf16[256,1024]{1,0:T(8,128)(2,1)} %collective-permute-done.11.vb_ref, ...), custom_call_target="tpu_custom_call", output_to_operand_aliasing={{}: (5, {})} | custom-call | flops 134217728 | bytes 3670016 | tf_op jit(solution)/shard_map/finish/pallas_call | solution.py:469
  (41 shorter events, 14.7 us)
Async XLA Ops:
  0.6 28.8 %collective-permute-start.4 = (bf16[512,1024]{1,0:T(8,128)(2,1)}, bf16[512,1024]{1,0:T(8,128)(2,1)S(1)}, u32[]{:S(2)}, u32[]{:S(2)}) collective-permute-start(bf16[512,1024]{1,0:T(8,128)(2,1)} %k_ref.1), channel_id=1, source_target_pairs={{0,4},{4,8},{8,12},{1,5},{5,9},{9,13},{2,6},{6,10},{10,14},{3,7},{... | collective-permute-start | bytes 3145736 | tf_op jit(solution)/shard_map/ppermute | solution.py:407
  5.6 28.2 %collective-permute-start.5 = (bf16[512,1024]{1,0:T(8,128)(2,1)}, bf16[512,1024]{1,0:T(8,128)(2,1)S(1)}, u32[]{:S(2)}, u32[]{:S(2)}) collective-permute-start(bf16[512,1024]{1,0:T(8,128)(2,1)} %k_ref.1), channel_id=1, source_target_pairs={{4,0},{8,4},{12,8},{5,1},{9,5},{13,9},{6,2},{10,6},{14,10},{7,3},{... | collective-permute-start | bytes 3145736 | tf_op jit(solution)/shard_map/ppermute | solution.py:407
  6.9 1.2 %copy-start = (bf16[512,1024]{1,0:T(8,128)(2,1)S(1)}, bf16[512,1024]{1,0:T(8,128)(2,1)}, u32[]{:S(2)}) copy-start(bf16[512,1024]{1,0:T(8,128)(2,1)} %q_ref.7) | copy-start | bytes 3145732
  8.2 1.2 %copy-start.1 = (bf16[512,1024]{1,0:T(8,128)(2,1)S(1)}, bf16[512,1024]{1,0:T(8,128)(2,1)}, u32[]{:S(2)}) copy-start(bf16[512,1024]{1,0:T(8,128)(2,1)} %lk_ref.3) | copy-start | bytes 3145732
  9.4 1.2 %copy-start.3 = (bf16[512,1024]{1,0:T(8,128)(2,1)S(1)}, bf16[512,1024]{1,0:T(8,128)(2,1)}, u32[]{:S(2)}) copy-start(bf16[512,1024]{1,0:T(8,128)(2,1)} %lv_ref.3) | copy-start | bytes 3145732
  11.3 1.7 %copy-start.5 = (bf16[512,1024]{1,0:T(8,128)(2,1)S(1)}, bf16[512,1024]{1,0:T(8,128)(2,1)}, u32[]{:S(2)}) copy-start(bf16[512,1024]{1,0:T(8,128)(2,1)} %v_ref.3) | copy-start | bytes 3145732
  11.3 7.8 %copy-start.10 = (bf16[512,1024]{1,0:T(8,128)(2,1)S(1)}, bf16[512,1024]{1,0:T(8,128)(2,1)}, u32[]{:S(2)}) copy-start(bf16[512,1024]{1,0:T(8,128)(2,1)} %k_ref.1) | copy-start | bytes 3145732
  13.0 37.7 %copy-start.2 = (bf16[512,1024]{1,0:T(8,128)(2,1)S(1)}, bf16[512,1024]{1,0:T(8,128)(2,1)}, u32[]{:S(2)}) copy-start(bf16[512,1024]{1,0:T(8,128)(2,1)} %lk_ref.3) | copy-start | bytes 3145732
  13.0 37.7 %copy-start.4 = (bf16[512,1024]{1,0:T(8,128)(2,1)S(1)}, bf16[512,1024]{1,0:T(8,128)(2,1)}, u32[]{:S(2)}) copy-start(bf16[512,1024]{1,0:T(8,128)(2,1)} %lv_ref.3) | copy-start | bytes 3145732
  13.0 37.7 %copy-start.7 = (s32[32]{0:T(128)S(1)}, s32[32]{0:T(128)}, u32[]{:S(2)}) copy-start(s32[32]{0:T(128)} %starts.11) | copy-start | bytes 388
  13.0 26.4 %collective-permute-start = (bf16[256,1024]{1,0:T(8,128)(2,1)S(1)}, bf16[256,1024]{1,0:T(8,128)(2,1)S(1)}, u32[]{:S(2)}, u32[]{:S(2)}) collective-permute-start(bf16[256,1024]{1,0:T(8,128)(2,1)S(1)} %slice.6), channel_id=1, source_target_pairs={{0,4},{4,8},{8,12},{1,5},{5,9},{9,13},{2,6},{6,10},{10,14},{3,7},{... | collective-permute-start | bytes 1572872 | tf_op jit(solution)/shard_map/ppermute | solution.py:407
  17.7 27.3 %collective-permute-start.1 = (bf16[256,1024]{1,0:T(8,128)(2,1)S(1)}, bf16[256,1024]{1,0:T(8,128)(2,1)S(1)}, u32[]{:S(2)}, u32[]{:S(2)}) collective-permute-start(bf16[256,1024]{1,0:T(8,128)(2,1)S(1)} %slice.6), channel_id=1, source_target_pairs={{4,0},{8,4},{12,8},{5,1},{9,5},{13,9},{6,2},{10,6},{14,10},{7,3},{... | collective-permute-start | bytes 1572872 | tf_op jit(solution)/shard_map/ppermute | solution.py:407
  33.8 26.5 %collective-permute-start.6 = (bf16[512,1024]{1,0:T(8,128)(2,1)S(1)}, bf16[512,1024]{1,0:T(8,128)(2,1)S(1)}, u32[]{:S(2)}, u32[]{:S(2)}) collective-permute-start(bf16[512,1024]{1,0:T(8,128)(2,1)S(1)} %collective-permute-done.4.nb_ref), channel_id=1, source_target_pairs={{4,8},{8,12},{5,9},{9,13},{6,10},{10,14},{7,11},{11,15},{20,24},{2... | collective-permute-start | bytes 3145736 | tf_op jit(solution)/shard_map/ppermute | solution.py:407
  34.5 33.0 %collective-permute-start.7 = (bf16[512,1024]{1,0:T(8,128)(2,1)S(1)}, bf16[512,1024]{1,0:T(8,128)(2,1)S(1)}, u32[]{:S(2)}, u32[]{:S(2)}) collective-permute-start(bf16[512,1024]{1,0:T(8,128)(2,1)S(1)} %collective-permute-done.5.na_ref), channel_id=1, source_target_pairs={{4,0},{8,4},{5,1},{9,5},{6,2},{10,6},{7,3},{11,7},{20,16},{24,20},... | collective-permute-start | bytes 3145736 | tf_op jit(solution)/shard_map/ppermute | solution.py:407
  45.1 9.8 %copy-start.8 = (s32[2,8]{1,0:T(2,128)S(1)}, s32[2,8]{1,0:T(2,128)}, u32[]{:S(2)}) copy-start(s32[2,8]{1,0:T(2,128)} %pattern.3) | copy-start | bytes 196
  45.1 37.3 %collective-permute-start.2 = (bf16[256,1024]{1,0:T(8,128)(2,1)S(1)}, bf16[256,1024]{1,0:T(8,128)(2,1)}, u32[]{:S(2)}, u32[]{:S(2)}) collective-permute-start(bf16[256,1024]{1,0:T(8,128)(2,1)S(1)} %slice.7), channel_id=1, source_target_pairs={{0,4},{4,8},{8,12},{1,5},{5,9},{9,13},{2,6},{6,10},{10,14},{3,7},{... | collective-permute-start | bytes 1572872 | tf_op jit(solution)/shard_map/ppermute | solution.py:407
  49.4 33.0 %collective-permute-start.3 = (bf16[256,1024]{1,0:T(8,128)(2,1)S(1)}, bf16[256,1024]{1,0:T(8,128)(2,1)}, u32[]{:S(2)}, u32[]{:S(2)}) collective-permute-start(bf16[256,1024]{1,0:T(8,128)(2,1)S(1)} %slice.7), channel_id=1, source_target_pairs={{4,0},{8,4},{12,8},{5,1},{9,5},{13,9},{6,2},{10,6},{14,10},{7,3},{... | collective-permute-start | bytes 1572872 | tf_op jit(solution)/shard_map/ppermute | solution.py:407
  72.2 8.9 %collective-permute-start.8 = (bf16[8,2048]{1,0:T(8,128)(2,1)S(1)}, bf16[8,2048]{1,0:T(8,128)(2,1)S(1)}, u32[]{:S(2)}, u32[]{:S(2)}) collective-permute-start(bf16[8,2048]{1,0:T(8,128)(2,1)S(1)} %get-tuple-element.70), channel_id=1, source_target_pairs={{0,8},{4,12},{8,0},{12,4},{1,9},{5,13},{9,1},{13,5},{2,10},{6,14},... | collective-permute-start | bytes 98312 | tf_op jit(solution)/shard_map/ppermute | solution.py:407
  72.8 17.9 %collective-permute-start.10 = (bf16[256,1024]{1,0:T(8,128)(2,1)S(1)}, bf16[256,1024]{1,0:T(8,128)(2,1)S(1)}, u32[]{:S(2)}, u32[]{:S(2)}) collective-permute-start(bf16[256,1024]{1,0:T(8,128)(2,1)S(1)} %collective-permute-done.1.va_ref), channel_id=1, source_target_pairs={{4,0},{8,4},{5,1},{9,5},{6,2},{10,6},{7,3},{11,7},{20,16},{24,20},... | collective-permute-start | bytes 1572872 | tf_op jit(solution)/shard_map/ppermute | solution.py:407
  74.0 16.7 %collective-permute-start.9 = (bf16[256,1024]{1,0:T(8,128)(2,1)S(1)}, bf16[256,1024]{1,0:T(8,128)(2,1)S(1)}, u32[]{:S(2)}, u32[]{:S(2)}) collective-permute-start(bf16[256,1024]{1,0:T(8,128)(2,1)S(1)} %collective-permute-done.vb_ref), channel_id=1, source_target_pairs={{4,8},{8,12},{5,9},{9,13},{6,10},{10,14},{7,11},{11,15},{20,24},{2... | collective-permute-start | bytes 1572872 | tf_op jit(solution)/shard_map/ppermute | solution.py:407
  82.4 6.0 %copy-start.9 = (s32[32]{0:T(128)S(1)}, s32[32]{0:T(128)}, u32[]{:S(2)}) copy-start(s32[32]{0:T(128)} %owners.1) | copy-start | bytes 388
  82.4 15.4 %collective-permute-start.11 = (bf16[256,1024]{1,0:T(8,128)(2,1)}, bf16[256,1024]{1,0:T(8,128)(2,1)}, u32[]{:S(2)}, u32[]{:S(2)}) collective-permute-start(bf16[256,1024]{1,0:T(8,128)(2,1)} %collective-permute-done.2.vb_ref), channel_id=1, source_target_pairs={{4,8},{8,12},{5,9},{9,13},{6,10},{10,14},{7,11},{11,15},{20,24},{2... | collective-permute-start | bytes 1572872 | tf_op jit(solution)/shard_map/ppermute | solution.py:407
  83.9 16.8 %collective-permute-start.12 = (bf16[256,1024]{1,0:T(8,128)(2,1)}, bf16[256,1024]{1,0:T(8,128)(2,1)}, u32[]{:S(2)}, u32[]{:S(2)}) collective-permute-start(bf16[256,1024]{1,0:T(8,128)(2,1)} %collective-permute-done.3.va_ref), channel_id=1, source_target_pairs={{4,0},{8,4},{5,1},{9,5},{6,2},{10,6},{7,3},{11,7},{20,16},{24,20},... | collective-permute-start | bytes 1572872 | tf_op jit(solution)/shard_map/ppermute | solution.py:407
  92.4 11.1 %all-to-all-start = ((bf16[4,4,1024]{2,1,0:T(4,128)(2,1)}), bf16[4,4,1024]{2,1,0:T(4,128)(2,1)S(1)}, u32[]{:S(2)}, u32[]{:S(2)}) async-start(bf16[4,4,1024]{2,1,0:T(4,128)(2,1)} %route.1), calls=%async_computation | async-start | bytes 65536 | tf_op jit(solution)/shard_map/all_to_all | solution.py:523
  (1 other events, 0.7 us)

commit v9 on v7

--- a/solution.py
+++ b/solution.py
@@ -280,26 +280,36 @@
 
 
 def route_kernel(where, owners, part_ref, *refs):
-    mean_refs, out_ref = refs[:-1], refs[-1]
+    mean_refs, out_refs = refs[:-4], refs[-4:]
     here, partner = where[0], lax.rem(where[0] + 2, 4)
     means = jnp.concatenate([mean_ref[...] for mean_ref in mean_refs], axis=0)
     parts = part_ref[...]
-    for target in range(out_ref.shape[0]):
+    for r, out_ref in enumerate(out_refs):
+        target = lax.rem(here + r, 4)
         rows = []
         for group, shard in ((means, here), (parts, partner)):
-            chosen = jnp.zeros((2, out_ref.shape[2]), F32)
+            chosen = jnp.zeros((2, out_ref.shape[1]), F32)
             for p in range(PIECES):
                 chosen = jnp.where(owners[2 * (PIECES * shard + p)] == target, group[2 * p : 2 * p + 2], chosen)
             rows.append(chosen)
-        out_ref[target] = jnp.concatenate(rows, axis=0).astype(BF16)
+        out_ref[...] = jnp.concatenate(rows, axis=0)
+
+
+def pool_kernel(where, *refs):
+    got, out_ref = refs[:4], refs[4]
+    for s in range(4):
+        rows = []
+        for first, shard in ((0, s), (2, s ^ 2)):
+            back = lax.rem(where[0] - shard + 4, 4)
+            found = got[0][first : first + 2, :]
+            for r in range(1, 4):
+                found = jnp.where(back == r, got[r][first : first + 2, :], found)
+            rows.append(found)
+        out_ref[0, s] = (rows[0] + rows[1]).astype(BF16)
 
 
 def context_kernel(block, where, acc_ref, w_ref, vb_ref, va_ref, *refs):
-    stage, sem = refs[-2:]
-    if len(refs) == 3:
-        out_ref = refs[0]
-    else:
-        got_ref, _, out_ref, pooled_ref = refs[:4]
+    out_ref, stage, sem = refs[-3:]
     behind = where[0] >= 2
     copies = []
     for h in range(acc_ref.shape[1] // HD):
@@ -311,10 +321,6 @@
             copy = pltpu.make_async_copy(stage.at[:, pair], out_ref.at[pl.ds(block * BLK, BLK), pair], sem.at[h // 2])
             copy.start()
             copies.append(copy)
-    if len(refs) > 3:
-        got = [got_ref[s].astype(F32) for s in range(4)]
-        for s in range(4):
-            pooled_ref[0, s] = (got[s][:2] + got[s ^ 2][2:]).astype(BF16)
     for copy in copies:
         copy.wait()
 
@@ -449,18 +455,16 @@
             name="mix",
         )(where, doc_starts, acc, scale, *weights, *near_vals, lat)
 
-    def finish(block, acc, weights, far_vals, held):
-        context = shape(rows, columns, BF16)
-        pooled = jax.ShapeDtypeStruct((1, 4, 2, columns), BF16)
+    def finish(block, acc, weights, far_vals, context):
+        held = [] if context is None else [context]
         anywhere = pl.BlockSpec(memory_space=pl.ANY)
-        whole = pl.BlockSpec(memory_space=pltpu.VMEM)
         return pl.pallas_call(
             functools.partial(context_kernel, block),
-            in_specs=smem(1) + vmem(4) + ([whole, anywhere] if held else []),
-            out_specs=[anywhere, whole] if held else anywhere,
-            out_shape=(context, pooled) if held else context,
+            in_specs=smem(1) + vmem(4) + [anywhere] * len(held),
+            out_specs=anywhere,
+            out_shape=shape(rows, columns, BF16),
             scratch_shapes=[pltpu.VMEM((BLK, columns), BF16), pltpu.SemaphoreType.DMA((heads // 2,))],
-            input_output_aliases={6: 0} if held else {},
+            input_output_aliases={5: 0} if held else {},
             compiler_params=PARAMS,
             cost_estimate=pl.CostEstimate(flops=2 * BLK * columns * BLK, bytes_accessed=14 * BLK * columns, transcendentals=0),
             name="finish",
@@ -498,18 +502,28 @@
     near_vals[1], parts, mixed[0] = lax.optimization_barrier((near_vals[1], parts, mixed[0]))
     far_vals.append(onward(near_vals[1]))
     mixed.append(mix(1, acc, scale, near_weights, near_vals[1], lat))
-    context = finish(0, mixed[0][0], far_weights, far_vals[0], [])
+    context = finish(0, mixed[0][0], far_weights, far_vals[0], None)
     sent = pl.pallas_call(
         route_kernel,
         in_specs=smem(2) + vmem(3),
-        out_specs=pl.BlockSpec(memory_space=pltpu.VMEM),
-        out_shape=jax.ShapeDtypeStruct((4, 4, columns), BF16),
+        out_specs=vmem(4),
+        out_shape=(shape(4, columns),) * 4,
         compiler_params=PARAMS,
         name="route",
     )(where, doc_owner, parts, *[m[1] for m in mixed])
     sent, context = lax.optimization_barrier((sent, context))
-    got = lax.all_to_all(sent, "seq", split_axis=0, concat_axis=0, tiled=True)
-    return finish(1, mixed[1][0], far_weights, far_vals[1], [got, context])
+    got = [sent[0]] + [move(sent[r], [(s, (s + r) % 4) for s in range(4)]) for r in range(1, 4)]
+    context = finish(1, mixed[1][0], far_weights, far_vals[1], context)
+    got, context = lax.optimization_barrier((got, context))
+    pooled = pl.pallas_call(
+        pool_kernel,
+        in_specs=smem(1) + vmem(4),
+        out_specs=pl.BlockSpec(memory_space=pltpu.VMEM),
+        out_shape=jax.ShapeDtypeStruct((1, 4, 2, columns), BF16),
+        compiler_params=PARAMS,
+        name="pool",
+    )(where, *got)
+    return context, pooled
 
 
 def body(queries, keys, values, latent_keys, latent_values, pattern, doc_starts, doc_owner):

time: 107 us -> 105 us (0.981)
  Pallas kernels: 33.3 us -> 30.6 us
    ppermute x13 -> x16, starting transfers between devices: 25.1 us -> 29.8 us  [move(): return lax.ppermute(value, 'seq', pairs)]
    all_to_all x1 -> x0, starting transfers between devices: 4.01 us -> none  [four_shards(): got = lax.all_to_all(sent, 'seq', split_axis=0, concat_axis=0, tiled=True)]
    all_to_all x1 -> x0, waiting for transfers between devices: 2.44 us -> none  [four_shards(): got = lax.all_to_all(sent, 'seq', split_axis=0, concat_axis=0, tiled=True)]
    ppermute x13 -> x16, waiting for transfers between devices: 36 us -> 38.2 us  [move(): return lax.ppermute(value, 'seq', pairs)]
    pallas_call x2, Pallas kernels: 4.12 us -> 2.32 us  [finish(): pl.pallas_call(functools.partial(context_kernel, block), in_specs=smem(1)...]
  transfers between devices with their start and end apart: 14 -> 16, of which waited for: 9 -> 9; matrix products, arithmetic and copies ran while one was open for 0% -> 0% of each run, Pallas kernels for 29% -> 29%
where the time goes in v9:
time: 105 us; the launch traced here: 104 us
  waiting for transfers between devices  38.2 us (36%)
  Pallas kernels  30.6 us (29%)
  starting transfers between devices  29.8 us (28%)
  local copies, waits for them, and re-layouts  4.43 us (4%)
    ppermute x16, waiting for transfers between devices, move(): return lax.ppermute(value, 'seq', pairs)  38.2 us
    ppermute x16, starting transfers between devices, move(): return lax.ppermute(value, 'seq', pairs)  29.8 us
    pallas_call x2, Pallas kernels, latent_call(): pl.pallas_call(latent_kernel, grid=(steps,), in_specs=smem(2) + [pl.Block...  5.81 us
    pallas_call x1, Pallas kernels, weigh_near(): pl.pallas_call(functools.partial(near_weigh_kernel, 4), grid=(heads // st...  5.41 us
    pallas_call x1, Pallas kernels, own_call(): pl.pallas_call(own_kernel, grid=(columns // wide,), in_specs=[spec(rows,...  5.27 us
    pallas_call x1, Pallas kernels, weigh_far(): pl.pallas_call(functools.partial(far_weigh_kernel, 4), grid=(heads // ste...  4.67 us
    pallas_call x2, Pallas kernels, mix(): pl.pallas_call(functools.partial(mix_kernel, block), grid=(heads // step,...  4.52 us
    unnamed x22, local copies, waits for them, and re-layouts  4.36 us
  transfers between devices with their start and end apart: 16, of which 9 were waited for; matrix products, arithmetic and copies ran while one was open for 0% of the time, Pallas kernels for 29%

profile of v9, /device:TPU:0, one launch (start us, length us, event | category | flops | bytes accessed | tf_op | source)
XLA Modules:
  0.0 104.0 jit_solution(13866897252225996879)
XLA Ops:
  0.6 5.0 %collective-permute-start.4 = (bf16[512,1024]{1,0:T(8,128)(2,1)}, bf16[512,1024]{1,0:T(8,128)(2,1)S(1)}, u32[]{:S(2)}, u32[]{:S(2)}) collective-permute-start(bf16[512,1024]{1,0:T(8,128)(2,1)} %k_ref.1), channel_id=1, source_target_pairs={{0,4},{4,8},{8,12},{1,5},{5,9},{9,13},{2,6},{6,10},{10,14},{3,7},{... | collective-permute-start | bytes 3145736 | tf_op jit(solution)/shard_map/ppermute | solution.py:399
  5.6 1.3 %collective-permute-start.5 = (bf16[512,1024]{1,0:T(8,128)(2,1)}, bf16[512,1024]{1,0:T(8,128)(2,1)S(1)}, u32[]{:S(2)}, u32[]{:S(2)}) collective-permute-start(bf16[512,1024]{1,0:T(8,128)(2,1)} %k_ref.1), channel_id=1, source_target_pairs={{4,0},{8,4},{12,8},{5,1},{9,5},{13,9},{6,2},{10,6},{14,10},{7,3},{... | collective-permute-start | bytes 3145736 | tf_op jit(solution)/shard_map/ppermute | solution.py:399
  11.3 1.6 %latent.2 = f32[8,256]{1,0:T(8,128)S(1)} custom-call(s32[1]{0:T(128)} %bitcast.where, s32[32]{0:T(128)S(1)} %copy-done.6, bf16[512,1024]{1,0:T(8,128)(2,1)S(1)} %copy-done, bf16[512,1024]{1,0:T(8,128)(2,1)S(1)} %copy-done.1, bf16[512,1024]{1,0:T(8,128)(2,1)S(1)} %copy-done.3), custom_call_target="tpu_custom_call" | custom-call | flops 268435456 | bytes 786432 | tf_op jit(solution)/shard_map/latent/pallas_call | solution.py:371
  13.0 4.7 %collective-permute-start = (bf16[256,1024]{1,0:T(8,128)(2,1)S(1)}, bf16[256,1024]{1,0:T(8,128)(2,1)S(1)}, u32[]{:S(2)}, u32[]{:S(2)}) collective-permute-start(bf16[256,1024]{1,0:T(8,128)(2,1)S(1)} %slice.6), channel_id=1, source_target_pairs={{0,4},{4,8},{8,12},{1,5},{5,9},{9,13},{2,6},{6,10},{10,14},{3,7},{... | collective-permute-start | bytes 1572872 | tf_op jit(solution)/shard_map/ppermute | solution.py:399
  17.7 1.3 %collective-permute-start.1 = (bf16[256,1024]{1,0:T(8,128)(2,1)S(1)}, bf16[256,1024]{1,0:T(8,128)(2,1)S(1)}, u32[]{:S(2)}, u32[]{:S(2)}) collective-permute-start(bf16[256,1024]{1,0:T(8,128)(2,1)S(1)} %slice.6), channel_id=1, source_target_pairs={{4,0},{8,4},{12,8},{5,1},{9,5},{13,9},{6,2},{10,6},{14,10},{7,3},{... | collective-permute-start | bytes 1572872 | tf_op jit(solution)/shard_map/ppermute | solution.py:399
  19.0 5.3 %own.1 = (f32[512,1024]{1,0:T(8,128)S(1)}, f32[512,1024]{1,0:T(8,128)S(1)}, f32[512,1024]{1,0:T(8,128)S(1)}) custom-call(bf16[512,1024]{1,0:T(8,128)(2,1)S(1)} %copy-done, bf16[512,1024]{1,0:T(8,128)(2,1)S(1)} %copy-done.10, bf16[512,1024]{1,0:T(8,128)(2,1)S(1)} %copy-done.5), custom_call_target="tpu_custom_call" | custom-call | flops 1073741824 | bytes 9437184 | tf_op jit(solution)/shard_map/own/pallas_call | solution.py:352
  24.3 5.1 %collective-permute-done.4.nb_ref = bf16[512,1024]{1,0:T(8,128)(2,1)S(1)} collective-permute-done((bf16[512,1024]{1,0:T(8,128)(2,1)}, bf16[512,1024]{1,0:T(8,128)(2,1)S(1)}, u32[]{:S(2)}, u32[]{:S(2)}) %collective-permute-start.4) | collective-permute-done | bytes 1048608 | tf_op jit(solution)/shard_map/ppermute | solution.py:399
  29.4 4.4 %collective-permute-done.5.na_ref = bf16[512,1024]{1,0:T(8,128)(2,1)S(1)} collective-permute-done((bf16[512,1024]{1,0:T(8,128)(2,1)}, bf16[512,1024]{1,0:T(8,128)(2,1)S(1)}, u32[]{:S(2)}, u32[]{:S(2)}) %collective-permute-start.5) | collective-permute-done | bytes 1048608 | tf_op jit(solution)/shard_map/ppermute | solution.py:399
  34.5 1.3 %collective-permute-start.7 = (bf16[512,1024]{1,0:T(8,128)(2,1)S(1)}, bf16[512,1024]{1,0:T(8,128)(2,1)S(1)}, u32[]{:S(2)}, u32[]{:S(2)}) collective-permute-start(bf16[512,1024]{1,0:T(8,128)(2,1)S(1)} %collective-permute-done.5.na_ref), channel_id=1, source_target_pairs={{4,0},{8,4},{5,1},{9,5},{6,2},{10,6},{7,3},{11,7},{20,16},{24,20},... | collective-permute-start | bytes 3145736 | tf_op jit(solution)/shard_map/ppermute | solution.py:399
  35.8 3.6 %collective-permute-done.vb_ref = bf16[256,1024]{1,0:T(8,128)(2,1)S(1)} collective-permute-done((bf16[256,1024]{1,0:T(8,128)(2,1)S(1)}, bf16[256,1024]{1,0:T(8,128)(2,1)S(1)}, u32[]{:S(2)}, u32[]{:S(2)}) %collective-permute-start) | collective-permute-done | bytes 524320 | tf_op jit(solution)/shard_map/ppermute | solution.py:399
  39.4 5.6 %collective-permute-done.1.va_ref = bf16[256,1024]{1,0:T(8,128)(2,1)S(1)} collective-permute-done((bf16[256,1024]{1,0:T(8,128)(2,1)S(1)}, bf16[256,1024]{1,0:T(8,128)(2,1)S(1)}, u32[]{:S(2)}, u32[]{:S(2)}) %collective-permute-start.1) | collective-permute-done | bytes 524320 | tf_op jit(solution)/shard_map/ppermute | solution.py:399
  45.1 3.5 %collective-permute-start.2 = (bf16[256,1024]{1,0:T(8,128)(2,1)S(1)}, bf16[256,1024]{1,0:T(8,128)(2,1)S(1)}, u32[]{:S(2)}, u32[]{:S(2)}) collective-permute-start(bf16[256,1024]{1,0:T(8,128)(2,1)S(1)} %slice.7), channel_id=1, source_target_pairs={{0,4},{4,8},{8,12},{1,5},{5,9},{9,13},{2,6},{6,10},{10,14},{3,7},{... | collective-permute-start | bytes 1572872 | tf_op jit(solution)/shard_map/ppermute | solution.py:399
  48.6 1.3 %collective-permute-start.3 = (bf16[256,1024]{1,0:T(8,128)(2,1)S(1)}, bf16[256,1024]{1,0:T(8,128)(2,1)S(1)}, u32[]{:S(2)}, u32[]{:S(2)}) collective-permute-start(bf16[256,1024]{1,0:T(8,128)(2,1)S(1)} %slice.7), channel_id=1, source_target_pairs={{4,0},{8,4},{12,8},{5,1},{9,5},{13,9},{6,2},{10,6},{14,10},{7,3},{... | collective-permute-start | bytes 1572872 | tf_op jit(solution)/shard_map/ppermute | solution.py:399
  49.9 4.2 %latent.3 = f32[8,768]{1,0:T(8,128)S(1)} custom-call(s32[1]{0:T(128)} %bitcast.where, s32[32]{0:T(128)S(1)} %copy-done.7, bf16[512,1024]{1,0:T(8,128)(2,1)S(1)} %copy-done, bf16[512,1024]{1,0:T(8,128)(2,1)S(1)} %copy-done.2, bf16[512,1024]{1,0:T(8,128)(2,1)S(1)} %copy-done.4), custom_call_target="tpu_custom_call" | custom-call | flops 8053063680 | bytes 2359296 | tf_op jit(solution)/shard_map/latent/pallas_call | solution.py:371
  54.1 5.4 %weigh_near.1 = (f32[512,1024]{1,0:T(8,128)S(1)}, f32[512,1024]{1,0:T(8,128)S(1)}, f32[512,1024]{1,0:T(8,128)S(1)}, bf16[512,2048]{1,0:T(8,128)(2,1)S(1)}, bf16[512,2048]{1,0:T(8,128)(2,1)S(1)}) custom-call(s32[1]{0:T(128)} %bitcast.where, s32[2,8]{1,0:T(2,128)S(1)} %copy-done.8, ...), custom_call_target="tpu_custom_call", output_to_operand_aliasing={{0}: (5, {}), {1}: (6, {}), {2}: (7, {})} | custom-call | flops 536870912 | bytes 10485760 | tf_op jit(solution)/shard_map/weigh_near/pallas_call | solution.py:414
  59.5 8.0 %collective-permute-done.7.fa_ref = bf16[512,1024]{1,0:T(8,128)(2,1)S(1)} collective-permute-done((bf16[512,1024]{1,0:T(8,128)(2,1)S(1)}, bf16[512,1024]{1,0:T(8,128)(2,1)S(1)}, u32[]{:S(2)}, u32[]{:S(2)}) %collective-permute-start.7) | collective-permute-done | bytes 1048608 | tf_op jit(solution)/shard_map/ppermute | solution.py:399
  67.5 4.7 %weigh_far.1 = (f32[512,1024]{1,0:T(8,128)S(1)}, bf16[512,2048]{1,0:T(8,128)(2,1)S(1)}, bf16[8,2048]{1,0:T(8,128)(2,1)S(1)}) custom-call(s32[1]{0:T(128)} %bitcast.where, s32[2,8]{1,0:T(2,128)S(1)} %copy-done.8, s32[32]{0:T(128)S(1)} %copy-done.7, bf16[512,1024]{1,0:T(8,128)(2,1)S(1)} %copy-done, bf16[512,1024]{1,0:T(8,128)(2,1)S(1)} %collective-permute-done.6.fb_ref, ...), custom_call_target="tpu_custom_call" | custom-call | flops 268435456 | bytes 11534336 | tf_op jit(solution)/shard_map/weigh_far/pallas_call | solution.py:429
  74.8 2.3 %mix.2 = (f32[256,1024]{1,0:T(8,128)S(1)}, f32[4,1024]{1,0:T(4,128)S(1)}) custom-call(s32[1]{0:T(128)} %bitcast.where, s32[32]{0:T(128)S(1)} %copy-done.7, f32[512,1024]{1,0:T(8,128)S(1)} %get-tuple-element.81.acc_in, f32[512,1024]{1,0:T(8,128)S(1)} %get-tuple-element.82.scale_in, bf16[512,2048]{1,0:T(8,128)(2,1)S(1)} %get-tuple-element.83.wb_ref, ...), custom_call_target="tpu_custom_call" | custom-call | flops 268435456 | bytes 5242880 | tf_op jit(solution)/shard_map/mix/pallas_call | solution.py:443
  77.0 4.1 %collective-permute-done.8.sums_ref = bf16[8,2048]{1,0:T(8,128)(2,1)S(1)} collective-permute-done((bf16[8,2048]{1,0:T(8,128)(2,1)S(1)}, bf16[8,2048]{1,0:T(8,128)(2,1)S(1)}, u32[]{:S(2)}, u32[]{:S(2)}) %collective-permute-start.8) | collective-permute-done | bytes 32800 | tf_op jit(solution)/shard_map/ppermute | solution.py:399
  84.4 2.3 %mix.3 = (f32[256,1024]{1,0:T(8,128)S(1)}, f32[4,1024]{1,0:T(4,128)S(1)}) custom-call(s32[1]{0:T(128)} %bitcast.where, s32[32]{0:T(128)S(1)} %copy-done.7, f32[512,1024]{1,0:T(8,128)S(1)} %get-tuple-element.81.acc_in, f32[512,1024]{1,0:T(8,128)S(1)} %get-tuple-element.82.scale_in, bf16[512,2048]{1,0:T(8,128)(2,1)S(1)} %get-tuple-element.83.wb_ref, ...), custom_call_target="tpu_custom_call" | custom-call | flops 268435456 | bytes 5242880 | tf_op jit(solution)/shard_map/mix/pallas_call | solution.py:443
  87.4 3.3 %collective-permute-done.10.va_ref = bf16[256,1024]{1,0:T(8,128)(2,1)S(1)} collective-permute-done((bf16[256,1024]{1,0:T(8,128)(2,1)S(1)}, bf16[256,1024]{1,0:T(8,128)(2,1)S(1)}, u32[]{:S(2)}, u32[]{:S(2)}) %collective-permute-start.10) | collective-permute-done | bytes 524320 | tf_op jit(solution)/shard_map/ppermute | solution.py:399
  91.9 2.3 %collective-permute-start.11 = (f32[4,1024]{1,0:T(4,128)S(1)}, f32[4,1024]{1,0:T(4,128)S(1)}, u32[]{:S(2)}, u32[]{:S(2)}) collective-permute-start(f32[4,1024]{1,0:T(4,128)S(1)} %get-tuple-element.102), channel_id=1, source_target_pairs={{0,4},{4,8},{8,12},{12,0},{1,5},{5,9},{9,13},{13,1},{2,6},{6,10},{... | collective-permute-start | bytes 49160 | tf_op jit(solution)/shard_map/ppermute | solution.py:399
  95.4 2.7 %collective-permute-start.13 = (f32[4,1024]{1,0:T(4,128)S(1)}, f32[4,1024]{1,0:T(4,128)S(1)}, u32[]{:S(2)}, u32[]{:S(2)}) collective-permute-start(f32[4,1024]{1,0:T(4,128)S(1)} %get-tuple-element.104), channel_id=1, source_target_pairs={{0,12},{4,0},{8,4},{12,8},{1,13},{5,1},{9,5},{13,9},{2,14},{6,2},{... | collective-permute-start | bytes 49160 | tf_op jit(solution)/shard_map/ppermute | solution.py:399
  98.1 2.9 %collective-permute-done.15.va_ref = bf16[256,1024]{1,0:T(8,128)(2,1)S(1)} collective-permute-done((bf16[256,1024]{1,0:T(8,128)(2,1)S(1)}, bf16[256,1024]{1,0:T(8,128)(2,1)S(1)}, u32[]{:S(2)}, u32[]{:S(2)}) %collective-permute-start.15) | collective-permute-done | bytes 524320 | tf_op jit(solution)/shard_map/ppermute | solution.py:399
  (45 shorter events, 17.0 us)
Async XLA Ops:
  0.6 28.8 %collective-permute-start.4 = (bf16[512,1024]{1,0:T(8,128)(2,1)}, bf16[512,1024]{1,0:T(8,128)(2,1)S(1)}, u32[]{:S(2)}, u32[]{:S(2)}) collective-permute-start(bf16[512,1024]{1,0:T(8,128)(2,1)} %k_ref.1), channel_id=1, source_target_pairs={{0,4},{4,8},{8,12},{1,5},{5,9},{9,13},{2,6},{6,10},{10,14},{3,7},{... | collective-permute-start | bytes 3145736 | tf_op jit(solution)/shard_map/ppermute | solution.py:399
  5.6 28.2 %collective-permute-start.5 = (bf16[512,1024]{1,0:T(8,128)(2,1)}, bf16[512,1024]{1,0:T(8,128)(2,1)S(1)}, u32[]{:S(2)}, u32[]{:S(2)}) collective-permute-start(bf16[512,1024]{1,0:T(8,128)(2,1)} %k_ref.1), channel_id=1, source_target_pairs={{4,0},{8,4},{12,8},{5,1},{9,5},{13,9},{6,2},{10,6},{14,10},{7,3},{... | collective-permute-start | bytes 3145736 | tf_op jit(solution)/shard_map/ppermute | solution.py:399
  6.9 1.2 %copy-start = (bf16[512,1024]{1,0:T(8,128)(2,1)S(1)}, bf16[512,1024]{1,0:T(8,128)(2,1)}, u32[]{:S(2)}) copy-start(bf16[512,1024]{1,0:T(8,128)(2,1)} %q_ref.7) | copy-start | bytes 3145732
  11.3 1.7 %copy-start.5 = (bf16[512,1024]{1,0:T(8,128)(2,1)S(1)}, bf16[512,1024]{1,0:T(8,128)(2,1)}, u32[]{:S(2)}) copy-start(bf16[512,1024]{1,0:T(8,128)(2,1)} %v_ref.3) | copy-start | bytes 3145732
  11.3 7.8 %copy-start.10 = (bf16[512,1024]{1,0:T(8,128)(2,1)S(1)}, bf16[512,1024]{1,0:T(8,128)(2,1)}, u32[]{:S(2)}) copy-start(bf16[512,1024]{1,0:T(8,128)(2,1)} %k_ref.1) | copy-start | bytes 3145732
  13.0 36.9 %copy-start.2 = (bf16[512,1024]{1,0:T(8,128)(2,1)S(1)}, bf16[512,1024]{1,0:T(8,128)(2,1)}, u32[]{:S(2)}) copy-start(bf16[512,1024]{1,0:T(8,128)(2,1)} %lk_ref.3) | copy-start | bytes 3145732
  13.0 36.9 %copy-start.4 = (bf16[512,1024]{1,0:T(8,128)(2,1)S(1)}, bf16[512,1024]{1,0:T(8,128)(2,1)}, u32[]{:S(2)}) copy-start(bf16[512,1024]{1,0:T(8,128)(2,1)} %lv_ref.3) | copy-start | bytes 3145732
  13.0 36.9 %copy-start.7 = (s32[32]{0:T(128)S(1)}, s32[32]{0:T(128)}, u32[]{:S(2)}) copy-start(s32[32]{0:T(128)} %starts.11) | copy-start | bytes 388
  13.0 26.4 %collective-permute-start = (bf16[256,1024]{1,0:T(8,128)(2,1)S(1)}, bf16[256,1024]{1,0:T(8,128)(2,1)S(1)}, u32[]{:S(2)}, u32[]{:S(2)}) collective-permute-start(bf16[256,1024]{1,0:T(8,128)(2,1)S(1)} %slice.6), channel_id=1, source_target_pairs={{0,4},{4,8},{8,12},{1,5},{5,9},{9,13},{2,6},{6,10},{10,14},{3,7},{... | collective-permute-start | bytes 1572872 | tf_op jit(solution)/shard_map/ppermute | solution.py:399
  17.7 27.3 %collective-permute-start.1 = (bf16[256,1024]{1,0:T(8,128)(2,1)S(1)}, bf16[256,1024]{1,0:T(8,128)(2,1)S(1)}, u32[]{:S(2)}, u32[]{:S(2)}) collective-permute-start(bf16[256,1024]{1,0:T(8,128)(2,1)S(1)} %slice.6), channel_id=1, source_target_pairs={{4,0},{8,4},{12,8},{5,1},{9,5},{13,9},{6,2},{10,6},{14,10},{7,3},{... | collective-permute-start | bytes 1572872 | tf_op jit(solution)/shard_map/ppermute | solution.py:399
  33.8 25.7 %collective-permute-start.6 = (bf16[512,1024]{1,0:T(8,128)(2,1)S(1)}, bf16[512,1024]{1,0:T(8,128)(2,1)S(1)}, u32[]{:S(2)}, u32[]{:S(2)}) collective-permute-start(bf16[512,1024]{1,0:T(8,128)(2,1)S(1)} %collective-permute-done.4.nb_ref), channel_id=1, source_target_pairs={{4,8},{8,12},{5,9},{9,13},{6,10},{10,14},{7,11},{11,15},{20,24},{2... | collective-permute-start | bytes 3145736 | tf_op jit(solution)/shard_map/ppermute | solution.py:399
  34.5 33.0 %collective-permute-start.7 = (bf16[512,1024]{1,0:T(8,128)(2,1)S(1)}, bf16[512,1024]{1,0:T(8,128)(2,1)S(1)}, u32[]{:S(2)}, u32[]{:S(2)}) collective-permute-start(bf16[512,1024]{1,0:T(8,128)(2,1)S(1)} %collective-permute-done.5.na_ref), channel_id=1, source_target_pairs={{4,0},{8,4},{5,1},{9,5},{6,2},{10,6},{7,3},{11,7},{20,16},{24,20},... | collective-permute-start | bytes 3145736 | tf_op jit(solution)/shard_map/ppermute | solution.py:399
  45.1 9.0 %copy-start.8 = (s32[2,8]{1,0:T(2,128)S(1)}, s32[2,8]{1,0:T(2,128)}, u32[]{:S(2)}) copy-start(s32[2,8]{1,0:T(2,128)} %pattern.3) | copy-start | bytes 196
  45.1 37.3 %collective-permute-start.2 = (bf16[256,1024]{1,0:T(8,128)(2,1)S(1)}, bf16[256,1024]{1,0:T(8,128)(2,1)S(1)}, u32[]{:S(2)}, u32[]{:S(2)}) collective-permute-start(bf16[256,1024]{1,0:T(8,128)(2,1)S(1)} %slice.7), channel_id=1, source_target_pairs={{0,4},{4,8},{8,12},{1,5},{5,9},{9,13},{2,6},{6,10},{10,14},{3,7},{... | collective-permute-start | bytes 1572872 | tf_op jit(solution)/shard_map/ppermute | solution.py:399
  48.6 33.8 %collective-permute-start.3 = (bf16[256,1024]{1,0:T(8,128)(2,1)S(1)}, bf16[256,1024]{1,0:T(8,128)(2,1)S(1)}, u32[]{:S(2)}, u32[]{:S(2)}) collective-permute-start(bf16[256,1024]{1,0:T(8,128)(2,1)S(1)} %slice.7), channel_id=1, source_target_pairs={{4,0},{8,4},{12,8},{5,1},{9,5},{13,9},{6,2},{10,6},{14,10},{7,3},{... | collective-permute-start | bytes 1572872 | tf_op jit(solution)/shard_map/ppermute | solution.py:399
  72.2 8.9 %collective-permute-start.8 = (bf16[8,2048]{1,0:T(8,128)(2,1)S(1)}, bf16[8,2048]{1,0:T(8,128)(2,1)S(1)}, u32[]{:S(2)}, u32[]{:S(2)}) collective-permute-start(bf16[8,2048]{1,0:T(8,128)(2,1)S(1)} %get-tuple-element.80), channel_id=1, source_target_pairs={{0,8},{4,12},{8,0},{12,4},{1,9},{5,13},{9,1},{13,5},{2,10},{6,14},... | collective-permute-start | bytes 98312 | tf_op jit(solution)/shard_map/ppermute | solution.py:399
  72.8 17.9 %collective-permute-start.10 = (bf16[256,1024]{1,0:T(8,128)(2,1)S(1)}, bf16[256,1024]{1,0:T(8,128)(2,1)S(1)}, u32[]{:S(2)}, u32[]{:S(2)}) collective-permute-start(bf16[256,1024]{1,0:T(8,128)(2,1)S(1)} %collective-permute-done.1.va_ref), channel_id=1, source_target_pairs={{4,0},{8,4},{5,1},{9,5},{6,2},{10,6},{7,3},{11,7},{20,16},{24,20},... | collective-permute-start | bytes 1572872 | tf_op jit(solution)/shard_map/ppermute | solution.py:399
  74.1 16.6 %collective-permute-start.9 = (bf16[256,1024]{1,0:T(8,128)(2,1)S(1)}, bf16[256,1024]{1,0:T(8,128)(2,1)S(1)}, u32[]{:S(2)}, u32[]{:S(2)}) collective-permute-start(bf16[256,1024]{1,0:T(8,128)(2,1)S(1)} %collective-permute-done.vb_ref), channel_id=1, source_target_pairs={{4,8},{8,12},{5,9},{9,13},{6,10},{10,14},{7,11},{11,15},{20,24},{2... | collective-permute-start | bytes 1572872 | tf_op jit(solution)/shard_map/ppermute | solution.py:399
  82.4 4.3 %copy-start.9 = (s32[32]{0:T(128)S(1)}, s32[32]{0:T(128)}, u32[]{:S(2)}) copy-start(s32[32]{0:T(128)} %owners.1) | copy-start | bytes 388
  82.4 15.7 %collective-permute-start.14 = (bf16[256,1024]{1,0:T(8,128)(2,1)S(1)}, bf16[256,1024]{1,0:T(8,128)(2,1)S(1)}, u32[]{:S(2)}, u32[]{:S(2)}) collective-permute-start(bf16[256,1024]{1,0:T(8,128)(2,1)S(1)} %collective-permute-done.2.vb_ref), channel_id=1, source_target_pairs={{4,8},{8,12},{5,9},{9,13},{6,10},{10,14},{7,11},{11,15},{20,24},{2... | collective-permute-start | bytes 1572872 | tf_op jit(solution)/shard_map/ppermute | solution.py:399
  83.1 17.9 %collective-permute-start.15 = (bf16[256,1024]{1,0:T(8,128)(2,1)S(1)}, bf16[256,1024]{1,0:T(8,128)(2,1)S(1)}, u32[]{:S(2)}, u32[]{:S(2)}) collective-permute-start(bf16[256,1024]{1,0:T(8,128)(2,1)S(1)} %collective-permute-done.3.va_ref), channel_id=1, source_target_pairs={{4,0},{8,4},{5,1},{9,5},{6,2},{10,6},{7,3},{11,7},{20,16},{24,20},... | collective-permute-start | bytes 1572872 | tf_op jit(solution)/shard_map/ppermute | solution.py:399
  91.9 10.3 %collective-permute-start.11 = (f32[4,1024]{1,0:T(4,128)S(1)}, f32[4,1024]{1,0:T(4,128)S(1)}, u32[]{:S(2)}, u32[]{:S(2)}) collective-permute-start(f32[4,1024]{1,0:T(4,128)S(1)} %get-tuple-element.102), channel_id=1, source_target_pairs={{0,4},{4,8},{8,12},{12,0},{1,5},{5,9},{9,13},{13,1},{2,6},{6,10},{... | collective-permute-start | bytes 49160 | tf_op jit(solution)/shard_map/ppermute | solution.py:399
  94.1 9.2 %collective-permute-start.12 = (f32[4,1024]{1,0:T(4,128)S(1)}, f32[4,1024]{1,0:T(4,128)S(1)}, u32[]{:S(2)}, u32[]{:S(2)}) collective-permute-start(f32[4,1024]{1,0:T(4,128)S(1)} %get-tuple-element.103), channel_id=1, source_target_pairs={{0,8},{4,12},{8,0},{12,4},{1,9},{5,13},{9,1},{13,5},{2,10},{6,14},... | collective-permute-start | bytes 49160 | tf_op jit(solution)/shard_map/ppermute | solution.py:399
  95.4 8.0 %collective-permute-start.13 = (f32[4,1024]{1,0:T(4,128)S(1)}, f32[4,1024]{1,0:T(4,128)S(1)}, u32[]{:S(2)}, u32[]{:S(2)}) collective-permute-start(f32[4,1024]{1,0:T(4,128)S(1)} %get-tuple-element.104), channel_id=1, source_target_pairs={{0,12},{4,0},{8,4},{12,8},{1,13},{5,1},{9,5},{13,9},{2,14},{6,2},{... | collective-permute-start | bytes 49160 | tf_op jit(solution)/shard_map/ppermute | solution.py:399
  (3 other events, 3.1 us)

commit v10 on v9

--- a/solution.py
+++ b/solution.py
@@ -292,18 +292,18 @@
             for p in range(PIECES):
                 chosen = jnp.where(owners[2 * (PIECES * shard + p)] == target, group[2 * p : 2 * p + 2], chosen)
             rows.append(chosen)
-        out_ref[...] = jnp.concatenate(rows, axis=0)
+        out_ref[...] = jnp.concatenate(rows, axis=0).astype(BF16)
 
 
 def pool_kernel(where, *refs):
-    got, out_ref = refs[:4], refs[4]
+    got, out_ref = [ref[...].astype(F32) for ref in refs[:4]], refs[4]
     for s in range(4):
         rows = []
         for first, shard in ((0, s), (2, s ^ 2)):
             back = lax.rem(where[0] - shard + 4, 4)
-            found = got[0][first : first + 2, :]
+            found = got[0][first : first + 2]
             for r in range(1, 4):
-                found = jnp.where(back == r, got[r][first : first + 2, :], found)
+                found = jnp.where(back == r, got[r][first : first + 2], found)
             rows.append(found)
         out_ref[0, s] = (rows[0] + rows[1]).astype(BF16)
 
@@ -507,7 +507,7 @@
         route_kernel,
         in_specs=smem(2) + vmem(3),
         out_specs=vmem(4),
-        out_shape=(shape(4, columns),) * 4,
+        out_shape=(shape(4, columns, BF16),) * 4,
         compiler_params=PARAMS,
         name="route",
     )(where, doc_owner, parts, *[m[1] for m in mixed])

time: 105 us -> 104 us (level)
  no operation moved by 1% of the time
where the time goes in v10:
time: 104 us; the launch traced here: 103 us
  waiting for transfers between devices  37.6 us (36%)
  Pallas kernels  30.6 us (29%)
  starting transfers between devices  29.8 us (29%)
  local copies, waits for them, and re-layouts  4.43 us (4%)
    ppermute x16, waiting for transfers between devices, move(): return lax.ppermute(value, 'seq', pairs)  37.6 us
    ppermute x16, starting transfers between devices, move(): return lax.ppermute(value, 'seq', pairs)  29.8 us
    pallas_call x2, Pallas kernels, latent_call(): pl.pallas_call(latent_kernel, grid=(steps,), in_specs=smem(2) + [pl.Block...  5.81 us
    pallas_call x1, Pallas kernels, weigh_near(): pl.pallas_call(functools.partial(near_weigh_kernel, 4), grid=(heads // st...  5.41 us
    pallas_call x1, Pallas kernels, own_call(): pl.pallas_call(own_kernel, grid=(columns // wide,), in_specs=[spec(rows,...  5.27 us
    pallas_call x1, Pallas kernels, weigh_far(): pl.pallas_call(functools.partial(far_weigh_kernel, 4), grid=(heads // ste...  4.67 us
    pallas_call x2, Pallas kernels, mix(): pl.pallas_call(functools.partial(mix_kernel, block), grid=(heads // step,...  4.52 us
    unnamed x22, local copies, waits for them, and re-layouts  4.36 us
  transfers between devices with their start and end apart: 16, of which 9 were waited for; matrix products, arithmetic and copies ran while one was open for 0% of the time, Pallas kernels for 29%

profile of v10, /device:TPU:0, one launch (start us, length us, event | category | flops | bytes accessed | tf_op | source)
XLA Modules:
  0.0 103.4 jit_solution(2665854613790712828)
XLA Ops:
  0.6 5.0 %collective-permute-start.4 = (bf16[512,1024]{1,0:T(8,128)(2,1)}, bf16[512,1024]{1,0:T(8,128)(2,1)S(1)}, u32[]{:S(2)}, u32[]{:S(2)}) collective-permute-start(bf16[512,1024]{1,0:T(8,128)(2,1)} %k_ref.1), channel_id=1, source_target_pairs={{0,4},{4,8},{8,12},{1,5},{5,9},{9,13},{2,6},{6,10},{10,14},{3,7},{... | collective-permute-start | bytes 3145736 | tf_op jit(solution)/shard_map/ppermute | solution.py:399
  5.6 1.3 %collective-permute-start.5 = (bf16[512,1024]{1,0:T(8,128)(2,1)}, bf16[512,1024]{1,0:T(8,128)(2,1)S(1)}, u32[]{:S(2)}, u32[]{:S(2)}) collective-permute-start(bf16[512,1024]{1,0:T(8,128)(2,1)} %k_ref.1), channel_id=1, source_target_pairs={{4,0},{8,4},{12,8},{5,1},{9,5},{13,9},{6,2},{10,6},{14,10},{7,3},{... | collective-permute-start | bytes 3145736 | tf_op jit(solution)/shard_map/ppermute | solution.py:399
  11.3 1.6 %latent.2 = f32[8,256]{1,0:T(8,128)S(1)} custom-call(s32[1]{0:T(128)} %bitcast.where, s32[32]{0:T(128)S(1)} %copy-done.6, bf16[512,1024]{1,0:T(8,128)(2,1)S(1)} %copy-done, bf16[512,1024]{1,0:T(8,128)(2,1)S(1)} %copy-done.1, bf16[512,1024]{1,0:T(8,128)(2,1)S(1)} %copy-done.3), custom_call_target="tpu_custom_call" | custom-call | flops 268435456 | bytes 786432 | tf_op jit(solution)/shard_map/latent/pallas_call | solution.py:371
  13.0 4.7 %collective-permute-start = (bf16[256,1024]{1,0:T(8,128)(2,1)S(1)}, bf16[256,1024]{1,0:T(8,128)(2,1)S(1)}, u32[]{:S(2)}, u32[]{:S(2)}) collective-permute-start(bf16[256,1024]{1,0:T(8,128)(2,1)S(1)} %slice.6), channel_id=1, source_target_pairs={{0,4},{4,8},{8,12},{1,5},{5,9},{9,13},{2,6},{6,10},{10,14},{3,7},{... | collective-permute-start | bytes 1572872 | tf_op jit(solution)/shard_map/ppermute | solution.py:399
  17.7 1.3 %collective-permute-start.1 = (bf16[256,1024]{1,0:T(8,128)(2,1)S(1)}, bf16[256,1024]{1,0:T(8,128)(2,1)S(1)}, u32[]{:S(2)}, u32[]{:S(2)}) collective-permute-start(bf16[256,1024]{1,0:T(8,128)(2,1)S(1)} %slice.6), channel_id=1, source_target_pairs={{4,0},{8,4},{12,8},{5,1},{9,5},{13,9},{6,2},{10,6},{14,10},{7,3},{... | collective-permute-start | bytes 1572872 | tf_op jit(solution)/shard_map/ppermute | solution.py:399
  19.0 5.3 %own.1 = (f32[512,1024]{1,0:T(8,128)S(1)}, f32[512,1024]{1,0:T(8,128)S(1)}, f32[512,1024]{1,0:T(8,128)S(1)}) custom-call(bf16[512,1024]{1,0:T(8,128)(2,1)S(1)} %copy-done, bf16[512,1024]{1,0:T(8,128)(2,1)S(1)} %copy-done.10, bf16[512,1024]{1,0:T(8,128)(2,1)S(1)} %copy-done.5), custom_call_target="tpu_custom_call" | custom-call | flops 1073741824 | bytes 9437184 | tf_op jit(solution)/shard_map/own/pallas_call | solution.py:352
  24.3 5.1 %collective-permute-done.4.nb_ref = bf16[512,1024]{1,0:T(8,128)(2,1)S(1)} collective-permute-done((bf16[512,1024]{1,0:T(8,128)(2,1)}, bf16[512,1024]{1,0:T(8,128)(2,1)S(1)}, u32[]{:S(2)}, u32[]{:S(2)}) %collective-permute-start.4) | collective-permute-done | bytes 1048608 | tf_op jit(solution)/shard_map/ppermute | solution.py:399
  29.4 4.4 %collective-permute-done.5.na_ref = bf16[512,1024]{1,0:T(8,128)(2,1)S(1)} collective-permute-done((bf16[512,1024]{1,0:T(8,128)(2,1)}, bf16[512,1024]{1,0:T(8,128)(2,1)S(1)}, u32[]{:S(2)}, u32[]{:S(2)}) %collective-permute-start.5) | collective-permute-done | bytes 1048608 | tf_op jit(solution)/shard_map/ppermute | solution.py:399
  34.5 1.3 %collective-permute-start.7 = (bf16[512,1024]{1,0:T(8,128)(2,1)S(1)}, bf16[512,1024]{1,0:T(8,128)(2,1)S(1)}, u32[]{:S(2)}, u32[]{:S(2)}) collective-permute-start(bf16[512,1024]{1,0:T(8,128)(2,1)S(1)} %collective-permute-done.5.na_ref), channel_id=1, source_target_pairs={{4,0},{8,4},{5,1},{9,5},{6,2},{10,6},{7,3},{11,7},{20,16},{24,20},... | collective-permute-start | bytes 3145736 | tf_op jit(solution)/shard_map/ppermute | solution.py:399
  35.8 3.6 %collective-permute-done.vb_ref = bf16[256,1024]{1,0:T(8,128)(2,1)S(1)} collective-permute-done((bf16[256,1024]{1,0:T(8,128)(2,1)S(1)}, bf16[256,1024]{1,0:T(8,128)(2,1)S(1)}, u32[]{:S(2)}, u32[]{:S(2)}) %collective-permute-start) | collective-permute-done | bytes 524320 | tf_op jit(solution)/shard_map/ppermute | solution.py:399
  39.4 5.6 %collective-permute-done.1.va_ref = bf16[256,1024]{1,0:T(8,128)(2,1)S(1)} collective-permute-done((bf16[256,1024]{1,0:T(8,128)(2,1)S(1)}, bf16[256,1024]{1,0:T(8,128)(2,1)S(1)}, u32[]{:S(2)}, u32[]{:S(2)}) %collective-permute-start.1) | collective-permute-done | bytes 524320 | tf_op jit(solution)/shard_map/ppermute | solution.py:399
  45.1 3.5 %collective-permute-start.2 = (bf16[256,1024]{1,0:T(8,128)(2,1)S(1)}, bf16[256,1024]{1,0:T(8,128)(2,1)S(1)}, u32[]{:S(2)}, u32[]{:S(2)}) collective-permute-start(bf16[256,1024]{1,0:T(8,128)(2,1)S(1)} %slice.7), channel_id=1, source_target_pairs={{0,4},{4,8},{8,12},{1,5},{5,9},{9,13},{2,6},{6,10},{10,14},{3,7},{... | collective-permute-start | bytes 1572872 | tf_op jit(solution)/shard_map/ppermute | solution.py:399
  48.6 1.3 %collective-permute-start.3 = (bf16[256,1024]{1,0:T(8,128)(2,1)S(1)}, bf16[256,1024]{1,0:T(8,128)(2,1)S(1)}, u32[]{:S(2)}, u32[]{:S(2)}) collective-permute-start(bf16[256,1024]{1,0:T(8,128)(2,1)S(1)} %slice.7), channel_id=1, source_target_pairs={{4,0},{8,4},{12,8},{5,1},{9,5},{13,9},{6,2},{10,6},{14,10},{7,3},{... | collective-permute-start | bytes 1572872 | tf_op jit(solution)/shard_map/ppermute | solution.py:399
  49.9 4.2 %latent.3 = f32[8,768]{1,0:T(8,128)S(1)} custom-call(s32[1]{0:T(128)} %bitcast.where, s32[32]{0:T(128)S(1)} %copy-done.7, bf16[512,1024]{1,0:T(8,128)(2,1)S(1)} %copy-done, bf16[512,1024]{1,0:T(8,128)(2,1)S(1)} %copy-done.2, bf16[512,1024]{1,0:T(8,128)(2,1)S(1)} %copy-done.4), custom_call_target="tpu_custom_call" | custom-call | flops 8053063680 | bytes 2359296 | tf_op jit(solution)/shard_map/latent/pallas_call | solution.py:371
  54.1 5.4 %weigh_near.1 = (f32[512,1024]{1,0:T(8,128)S(1)}, f32[512,1024]{1,0:T(8,128)S(1)}, f32[512,1024]{1,0:T(8,128)S(1)}, bf16[512,2048]{1,0:T(8,128)(2,1)S(1)}, bf16[512,2048]{1,0:T(8,128)(2,1)S(1)}) custom-call(s32[1]{0:T(128)} %bitcast.where, s32[2,8]{1,0:T(2,128)S(1)} %copy-done.8, ...), custom_call_target="tpu_custom_call", output_to_operand_aliasing={{0}: (5, {}), {1}: (6, {}), {2}: (7, {})} | custom-call | flops 536870912 | bytes 10485760 | tf_op jit(solution)/shard_map/weigh_near/pallas_call | solution.py:414
  59.5 8.0 %collective-permute-done.7.fa_ref = bf16[512,1024]{1,0:T(8,128)(2,1)S(1)} collective-permute-done((bf16[512,1024]{1,0:T(8,128)(2,1)S(1)}, bf16[512,1024]{1,0:T(8,128)(2,1)S(1)}, u32[]{:S(2)}, u32[]{:S(2)}) %collective-permute-start.7) | collective-permute-done | bytes 1048608 | tf_op jit(solution)/shard_map/ppermute | solution.py:399
  67.5 4.7 %weigh_far.1 = (f32[512,1024]{1,0:T(8,128)S(1)}, bf16[512,2048]{1,0:T(8,128)(2,1)S(1)}, bf16[8,2048]{1,0:T(8,128)(2,1)S(1)}) custom-call(s32[1]{0:T(128)} %bitcast.where, s32[2,8]{1,0:T(2,128)S(1)} %copy-done.8, s32[32]{0:T(128)S(1)} %copy-done.7, bf16[512,1024]{1,0:T(8,128)(2,1)S(1)} %copy-done, bf16[512,1024]{1,0:T(8,128)(2,1)S(1)} %collective-permute-done.6.fb_ref, ...), custom_call_target="tpu_custom_call" | custom-call | flops 268435456 | bytes 11534336 | tf_op jit(solution)/shard_map/weigh_far/pallas_call | solution.py:429
  74.8 2.3 %mix.2 = (f32[256,1024]{1,0:T(8,128)S(1)}, f32[4,1024]{1,0:T(4,128)S(1)}) custom-call(s32[1]{0:T(128)} %bitcast.where, s32[32]{0:T(128)S(1)} %copy-done.7, f32[512,1024]{1,0:T(8,128)S(1)} %get-tuple-element.81.acc_in, f32[512,1024]{1,0:T(8,128)S(1)} %get-tuple-element.82.scale_in, bf16[512,2048]{1,0:T(8,128)(2,1)S(1)} %get-tuple-element.83.wb_ref, ...), custom_call_target="tpu_custom_call" | custom-call | flops 268435456 | bytes 5242880 | tf_op jit(solution)/shard_map/mix/pallas_call | solution.py:443
  77.0 4.1 %collective-permute-done.8.sums_ref = bf16[8,2048]{1,0:T(8,128)(2,1)S(1)} collective-permute-done((bf16[8,2048]{1,0:T(8,128)(2,1)S(1)}, bf16[8,2048]{1,0:T(8,128)(2,1)S(1)}, u32[]{:S(2)}, u32[]{:S(2)}) %collective-permute-start.8) | collective-permute-done | bytes 32800 | tf_op jit(solution)/shard_map/ppermute | solution.py:399
  84.4 2.3 %mix.3 = (f32[256,1024]{1,0:T(8,128)S(1)}, f32[4,1024]{1,0:T(4,128)S(1)}) custom-call(s32[1]{0:T(128)} %bitcast.where, s32[32]{0:T(128)S(1)} %copy-done.7, f32[512,1024]{1,0:T(8,128)S(1)} %get-tuple-element.81.acc_in, f32[512,1024]{1,0:T(8,128)S(1)} %get-tuple-element.82.scale_in, bf16[512,2048]{1,0:T(8,128)(2,1)S(1)} %get-tuple-element.83.wb_ref, ...), custom_call_target="tpu_custom_call" | custom-call | flops 268435456 | bytes 5242880 | tf_op jit(solution)/shard_map/mix/pallas_call | solution.py:443
  87.4 3.3 %collective-permute-done.10.va_ref = bf16[256,1024]{1,0:T(8,128)(2,1)S(1)} collective-permute-done((bf16[256,1024]{1,0:T(8,128)(2,1)S(1)}, bf16[256,1024]{1,0:T(8,128)(2,1)S(1)}, u32[]{:S(2)}, u32[]{:S(2)}) %collective-permute-start.10) | collective-permute-done | bytes 524320 | tf_op jit(solution)/shard_map/ppermute | solution.py:399
  91.9 2.3 %collective-permute-start.11 = (bf16[4,1024]{1,0:T(4,128)(2,1)S(1)}, bf16[4,1024]{1,0:T(4,128)(2,1)S(1)}, u32[]{:S(2)}, u32[]{:S(2)}) collective-permute-start(bf16[4,1024]{1,0:T(4,128)(2,1)S(1)} %get-tuple-element.102), channel_id=1, source_target_pairs={{0,4},{4,8},{8,12},{12,0},{1,5},{5,9},{9,13},{13,1},{2,6},{6,10},{... | collective-permute-start | bytes 24584 | tf_op jit(solution)/shard_map/ppermute | solution.py:399
  95.4 2.7 %collective-permute-start.13 = (bf16[4,1024]{1,0:T(4,128)(2,1)S(1)}, bf16[4,1024]{1,0:T(4,128)(2,1)S(1)}, u32[]{:S(2)}, u32[]{:S(2)}) collective-permute-start(bf16[4,1024]{1,0:T(4,128)(2,1)S(1)} %get-tuple-element.104), channel_id=1, source_target_pairs={{0,12},{4,0},{8,4},{12,8},{1,13},{5,1},{9,5},{13,9},{2,14},{6,2},{... | collective-permute-start | bytes 24584 | tf_op jit(solution)/shard_map/ppermute | solution.py:399
  98.1 2.6 %collective-permute-done.15.va_ref = bf16[256,1024]{1,0:T(8,128)(2,1)S(1)} collective-permute-done((bf16[256,1024]{1,0:T(8,128)(2,1)S(1)}, bf16[256,1024]{1,0:T(8,128)(2,1)S(1)}, u32[]{:S(2)}, u32[]{:S(2)}) %collective-permute-start.15) | collective-permute-done | bytes 524320 | tf_op jit(solution)/shard_map/ppermute | solution.py:399
  (45 shorter events, 16.7 us)
Async XLA Ops:
  0.6 28.8 %collective-permute-start.4 = (bf16[512,1024]{1,0:T(8,128)(2,1)}, bf16[512,1024]{1,0:T(8,128)(2,1)S(1)}, u32[]{:S(2)}, u32[]{:S(2)}) collective-permute-start(bf16[512,1024]{1,0:T(8,128)(2,1)} %k_ref.1), channel_id=1, source_target_pairs={{0,4},{4,8},{8,12},{1,5},{5,9},{9,13},{2,6},{6,10},{10,14},{3,7},{... | collective-permute-start | bytes 3145736 | tf_op jit(solution)/shard_map/ppermute | solution.py:399
  5.6 28.2 %collective-permute-start.5 = (bf16[512,1024]{1,0:T(8,128)(2,1)}, bf16[512,1024]{1,0:T(8,128)(2,1)S(1)}, u32[]{:S(2)}, u32[]{:S(2)}) collective-permute-start(bf16[512,1024]{1,0:T(8,128)(2,1)} %k_ref.1), channel_id=1, source_target_pairs={{4,0},{8,4},{12,8},{5,1},{9,5},{13,9},{6,2},{10,6},{14,10},{7,3},{... | collective-permute-start | bytes 3145736 | tf_op jit(solution)/shard_map/ppermute | solution.py:399
  6.9 1.2 %copy-start = (bf16[512,1024]{1,0:T(8,128)(2,1)S(1)}, bf16[512,1024]{1,0:T(8,128)(2,1)}, u32[]{:S(2)}) copy-start(bf16[512,1024]{1,0:T(8,128)(2,1)} %q_ref.7) | copy-start | bytes 3145732
  11.3 1.7 %copy-start.5 = (bf16[512,1024]{1,0:T(8,128)(2,1)S(1)}, bf16[512,1024]{1,0:T(8,128)(2,1)}, u32[]{:S(2)}) copy-start(bf16[512,1024]{1,0:T(8,128)(2,1)} %v_ref.3) | copy-start | bytes 3145732
  11.3 7.8 %copy-start.10 = (bf16[512,1024]{1,0:T(8,128)(2,1)S(1)}, bf16[512,1024]{1,0:T(8,128)(2,1)}, u32[]{:S(2)}) copy-start(bf16[512,1024]{1,0:T(8,128)(2,1)} %k_ref.1) | copy-start | bytes 3145732
  13.0 36.9 %copy-start.2 = (bf16[512,1024]{1,0:T(8,128)(2,1)S(1)}, bf16[512,1024]{1,0:T(8,128)(2,1)}, u32[]{:S(2)}) copy-start(bf16[512,1024]{1,0:T(8,128)(2,1)} %lk_ref.3) | copy-start | bytes 3145732
  13.0 36.9 %copy-start.4 = (bf16[512,1024]{1,0:T(8,128)(2,1)S(1)}, bf16[512,1024]{1,0:T(8,128)(2,1)}, u32[]{:S(2)}) copy-start(bf16[512,1024]{1,0:T(8,128)(2,1)} %lv_ref.3) | copy-start | bytes 3145732
  13.0 36.9 %copy-start.7 = (s32[32]{0:T(128)S(1)}, s32[32]{0:T(128)}, u32[]{:S(2)}) copy-start(s32[32]{0:T(128)} %starts.11) | copy-start | bytes 388
  13.0 26.4 %collective-permute-start = (bf16[256,1024]{1,0:T(8,128)(2,1)S(1)}, bf16[256,1024]{1,0:T(8,128)(2,1)S(1)}, u32[]{:S(2)}, u32[]{:S(2)}) collective-permute-start(bf16[256,1024]{1,0:T(8,128)(2,1)S(1)} %slice.6), channel_id=1, source_target_pairs={{0,4},{4,8},{8,12},{1,5},{5,9},{9,13},{2,6},{6,10},{10,14},{3,7},{... | collective-permute-start | bytes 1572872 | tf_op jit(solution)/shard_map/ppermute | solution.py:399
  17.7 27.3 %collective-permute-start.1 = (bf16[256,1024]{1,0:T(8,128)(2,1)S(1)}, bf16[256,1024]{1,0:T(8,128)(2,1)S(1)}, u32[]{:S(2)}, u32[]{:S(2)}) collective-permute-start(bf16[256,1024]{1,0:T(8,128)(2,1)S(1)} %slice.6), channel_id=1, source_target_pairs={{4,0},{8,4},{12,8},{5,1},{9,5},{13,9},{6,2},{10,6},{14,10},{7,3},{... | collective-permute-start | bytes 1572872 | tf_op jit(solution)/shard_map/ppermute | solution.py:399
  33.8 25.7 %collective-permute-start.6 = (bf16[512,1024]{1,0:T(8,128)(2,1)S(1)}, bf16[512,1024]{1,0:T(8,128)(2,1)S(1)}, u32[]{:S(2)}, u32[]{:S(2)}) collective-permute-start(bf16[512,1024]{1,0:T(8,128)(2,1)S(1)} %collective-permute-done.4.nb_ref), channel_id=1, source_target_pairs={{4,8},{8,12},{5,9},{9,13},{6,10},{10,14},{7,11},{11,15},{20,24},{2... | collective-permute-start | bytes 3145736 | tf_op jit(solution)/shard_map/ppermute | solution.py:399
  34.5 33.0 %collective-permute-start.7 = (bf16[512,1024]{1,0:T(8,128)(2,1)S(1)}, bf16[512,1024]{1,0:T(8,128)(2,1)S(1)}, u32[]{:S(2)}, u32[]{:S(2)}) collective-permute-start(bf16[512,1024]{1,0:T(8,128)(2,1)S(1)} %collective-permute-done.5.na_ref), channel_id=1, source_target_pairs={{4,0},{8,4},{5,1},{9,5},{6,2},{10,6},{7,3},{11,7},{20,16},{24,20},... | collective-permute-start | bytes 3145736 | tf_op jit(solution)/shard_map/ppermute | solution.py:399
  45.1 9.0 %copy-start.8 = (s32[2,8]{1,0:T(2,128)S(1)}, s32[2,8]{1,0:T(2,128)}, u32[]{:S(2)}) copy-start(s32[2,8]{1,0:T(2,128)} %pattern.3) | copy-start | bytes 196
  45.1 37.3 %collective-permute-start.2 = (bf16[256,1024]{1,0:T(8,128)(2,1)S(1)}, bf16[256,1024]{1,0:T(8,128)(2,1)S(1)}, u32[]{:S(2)}, u32[]{:S(2)}) collective-permute-start(bf16[256,1024]{1,0:T(8,128)(2,1)S(1)} %slice.7), channel_id=1, source_target_pairs={{0,4},{4,8},{8,12},{1,5},{5,9},{9,13},{2,6},{6,10},{10,14},{3,7},{... | collective-permute-start | bytes 1572872 | tf_op jit(solution)/shard_map/ppermute | solution.py:399
  48.6 33.8 %collective-permute-start.3 = (bf16[256,1024]{1,0:T(8,128)(2,1)S(1)}, bf16[256,1024]{1,0:T(8,128)(2,1)S(1)}, u32[]{:S(2)}, u32[]{:S(2)}) collective-permute-start(bf16[256,1024]{1,0:T(8,128)(2,1)S(1)} %slice.7), channel_id=1, source_target_pairs={{4,0},{8,4},{12,8},{5,1},{9,5},{13,9},{6,2},{10,6},{14,10},{7,3},{... | collective-permute-start | bytes 1572872 | tf_op jit(solution)/shard_map/ppermute | solution.py:399
  72.2 8.9 %collective-permute-start.8 = (bf16[8,2048]{1,0:T(8,128)(2,1)S(1)}, bf16[8,2048]{1,0:T(8,128)(2,1)S(1)}, u32[]{:S(2)}, u32[]{:S(2)}) collective-permute-start(bf16[8,2048]{1,0:T(8,128)(2,1)S(1)} %get-tuple-element.80), channel_id=1, source_target_pairs={{0,8},{4,12},{8,0},{12,4},{1,9},{5,13},{9,1},{13,5},{2,10},{6,14},... | collective-permute-start | bytes 98312 | tf_op jit(solution)/shard_map/ppermute | solution.py:399
  72.8 17.9 %collective-permute-start.10 = (bf16[256,1024]{1,0:T(8,128)(2,1)S(1)}, bf16[256,1024]{1,0:T(8,128)(2,1)S(1)}, u32[]{:S(2)}, u32[]{:S(2)}) collective-permute-start(bf16[256,1024]{1,0:T(8,128)(2,1)S(1)} %collective-permute-done.1.va_ref), channel_id=1, source_target_pairs={{4,0},{8,4},{5,1},{9,5},{6,2},{10,6},{7,3},{11,7},{20,16},{24,20},... | collective-permute-start | bytes 1572872 | tf_op jit(solution)/shard_map/ppermute | solution.py:399
  74.1 16.6 %collective-permute-start.9 = (bf16[256,1024]{1,0:T(8,128)(2,1)S(1)}, bf16[256,1024]{1,0:T(8,128)(2,1)S(1)}, u32[]{:S(2)}, u32[]{:S(2)}) collective-permute-start(bf16[256,1024]{1,0:T(8,128)(2,1)S(1)} %collective-permute-done.vb_ref), channel_id=1, source_target_pairs={{4,8},{8,12},{5,9},{9,13},{6,10},{10,14},{7,11},{11,15},{20,24},{2... | collective-permute-start | bytes 1572872 | tf_op jit(solution)/shard_map/ppermute | solution.py:399
  82.4 4.3 %copy-start.9 = (s32[32]{0:T(128)S(1)}, s32[32]{0:T(128)}, u32[]{:S(2)}) copy-start(s32[32]{0:T(128)} %owners.1) | copy-start | bytes 388
  82.4 15.7 %collective-permute-start.14 = (bf16[256,1024]{1,0:T(8,128)(2,1)S(1)}, bf16[256,1024]{1,0:T(8,128)(2,1)S(1)}, u32[]{:S(2)}, u32[]{:S(2)}) collective-permute-start(bf16[256,1024]{1,0:T(8,128)(2,1)S(1)} %collective-permute-done.2.vb_ref), channel_id=1, source_target_pairs={{4,8},{8,12},{5,9},{9,13},{6,10},{10,14},{7,11},{11,15},{20,24},{2... | collective-permute-start | bytes 1572872 | tf_op jit(solution)/shard_map/ppermute | solution.py:399
  83.1 17.6 %collective-permute-start.15 = (bf16[256,1024]{1,0:T(8,128)(2,1)S(1)}, bf16[256,1024]{1,0:T(8,128)(2,1)S(1)}, u32[]{:S(2)}, u32[]{:S(2)}) collective-permute-start(bf16[256,1024]{1,0:T(8,128)(2,1)S(1)} %collective-permute-done.3.va_ref), channel_id=1, source_target_pairs={{4,0},{8,4},{5,1},{9,5},{6,2},{10,6},{7,3},{11,7},{20,16},{24,20},... | collective-permute-start | bytes 1572872 | tf_op jit(solution)/shard_map/ppermute | solution.py:399
  91.9 10.0 %collective-permute-start.11 = (bf16[4,1024]{1,0:T(4,128)(2,1)S(1)}, bf16[4,1024]{1,0:T(4,128)(2,1)S(1)}, u32[]{:S(2)}, u32[]{:S(2)}) collective-permute-start(bf16[4,1024]{1,0:T(4,128)(2,1)S(1)} %get-tuple-element.102), channel_id=1, source_target_pairs={{0,4},{4,8},{8,12},{12,0},{1,5},{5,9},{9,13},{13,1},{2,6},{6,10},{... | collective-permute-start | bytes 24584 | tf_op jit(solution)/shard_map/ppermute | solution.py:399
  94.1 8.6 %collective-permute-start.12 = (bf16[4,1024]{1,0:T(4,128)(2,1)S(1)}, bf16[4,1024]{1,0:T(4,128)(2,1)S(1)}, u32[]{:S(2)}, u32[]{:S(2)}) collective-permute-start(bf16[4,1024]{1,0:T(4,128)(2,1)S(1)} %get-tuple-element.103), channel_id=1, source_target_pairs={{0,8},{4,12},{8,0},{12,4},{1,9},{5,13},{9,1},{13,5},{2,10},{6,14},... | collective-permute-start | bytes 24584 | tf_op jit(solution)/shard_map/ppermute | solution.py:399
  95.4 7.3 %collective-permute-start.13 = (bf16[4,1024]{1,0:T(4,128)(2,1)S(1)}, bf16[4,1024]{1,0:T(4,128)(2,1)S(1)}, u32[]{:S(2)}, u32[]{:S(2)}) collective-permute-start(bf16[4,1024]{1,0:T(4,128)(2,1)S(1)} %get-tuple-element.104), channel_id=1, source_target_pairs={{0,12},{4,0},{8,4},{12,8},{1,13},{5,1},{9,5},{13,9},{2,14},{6,2},{... | collective-permute-start | bytes 24584 | tf_op jit(solution)/shard_map/ppermute | solution.py:399
  (3 other events, 3.1 us)

commit v11 on v10

--- a/solution.py
+++ b/solution.py
@@ -266,17 +266,17 @@
 
 
 def part_kernel(where, starts, sums_ref, v_ref, part_ref):
-    piece = v_ref.shape[0] // PIECES
-    per_block = BLK // piece
+    rows_here = v_ref.shape[0]
+    piece = rows_here // PIECES
+    pieces = part_ref.shape[0] // 2
     partner = lax.rem(where[0] + 2, 4)
-    counts = [doc_counts(split_of(where, starts, p, partner), piece, HD) for p in range(PIECES)]
+    counts = [doc_counts(split_of(where, starts, PIECES - pieces + p, partner), piece, HD) for p in range(pieces)]
     for h in range(v_ref.shape[1] // HD):
         head = slice(h * HD, (h + 1) * HD)
-        sums = sums_ref[:, h * BLK : (h + 1) * BLK]
-        found = [dot(sums.astype(BF16), v_ref[block * BLK : (block + 1) * BLK, head]) for block in range(v_ref.shape[0] // BLK)]
-        for p in range(PIECES):
+        found = dot(sums_ref[:, h * BLK : (h + 1) * BLK], v_ref[rows_here - BLK :, head])
+        for p in range(pieces):
             rows = slice(2 * p, 2 * p + 2)
-            part_ref[rows, head] = found[p // per_block][rows] / counts[p]
+            part_ref[rows, head] = found[rows] / counts[p]
 
 
 def route_kernel(where, owners, part_ref, *refs):
@@ -289,8 +289,10 @@
         rows = []
         for group, shard in ((means, here), (parts, partner)):
             chosen = jnp.zeros((2, out_ref.shape[1]), F32)
-            for p in range(PIECES):
-                chosen = jnp.where(owners[2 * (PIECES * shard + p)] == target, group[2 * p : 2 * p + 2], chosen)
+            count = group.shape[0] // 2
+            for p in range(count):
+                mine = owners[2 * (PIECES * shard + PIECES - count + p)] == target
+                chosen = jnp.where(mine, group[2 * p : 2 * p + 2], chosen)
             rows.append(chosen)
         out_ref[...] = jnp.concatenate(rows, axis=0).astype(BF16)
 
@@ -308,14 +310,25 @@
         out_ref[0, s] = (rows[0] + rows[1]).astype(BF16)
 
 
-def context_kernel(block, where, acc_ref, w_ref, vb_ref, va_ref, *refs):
-    out_ref, stage, sem = refs[-3:]
+def context_kernel(block, where, starts, acc_ref, w_ref, vb_ref, va_ref, *refs):
+    if block == 0:
+        mean_in, out_ref, mean_ref, stage, sem = refs
+    else:
+        _, out_ref, stage, sem = refs
     behind = where[0] >= 2
     copies = []
     for h in range(acc_ref.shape[1] // HD):
         head = pl.ds(h * HD, HD)
         v = jnp.where(behind, vb_ref[:, head], va_ref[:, head])
-        stage[:, head] = (acc_ref[:, head] + dot(w_ref[pl.ds(block * BLK, BLK), pl.ds(h * BLK, BLK)], v)).astype(BF16)
+        found = dot(w_ref[pl.ds(block * BLK, BLK), pl.ds(h * BLK, BLK)], v)
+        stage[:, head] = (acc_ref[:, head] + found).astype(BF16)
+        if block == 0:
+            pieces = mean_ref.shape[0] // 2
+            piece = BLK // pieces
+            for p in range(pieces):
+                split = split_of(where, starts, p)
+                far = doc_rows(found[p * piece : (p + 1) * piece], split) / doc_counts(split, piece, HD)
+                mean_ref[2 * p : 2 * p + 2, head] = mean_in[2 * p : 2 * p + 2, head] + far
         if h % 2:
             pair = pl.ds((h - 1) * HD, 2 * HD)
             copy = pltpu.make_async_copy(stage.at[:, pair], out_ref.at[pl.ds(block * BLK, BLK), pair], sem.at[h // 2])
@@ -455,20 +468,21 @@
             name="mix",
         )(where, doc_starts, acc, scale, *weights, *near_vals, lat)
 
-    def finish(block, acc, weights, far_vals, context):
-        held = [] if context is None else [context]
+    def finish(block, acc, weights, far_vals, held):
+        first = block == 0
         anywhere = pl.BlockSpec(memory_space=pl.ANY)
+        context = shape(rows, columns, BF16)
         return pl.pallas_call(
             functools.partial(context_kernel, block),
-            in_specs=smem(1) + vmem(4) + [anywhere] * len(held),
-            out_specs=anywhere,
-            out_shape=shape(rows, columns, BF16),
+            in_specs=smem(2) + vmem(4) + (vmem(1) if first else [anywhere]),
+            out_specs=[anywhere] + vmem(1) if first else anywhere,
+            out_shape=(context, shape(docs, columns)) if first else context,
             scratch_shapes=[pltpu.VMEM((BLK, columns), BF16), pltpu.SemaphoreType.DMA((heads // 2,))],
-            input_output_aliases={5: 0} if held else {},
+            input_output_aliases={} if first else {6: 0},
             compiler_params=PARAMS,
             cost_estimate=pl.CostEstimate(flops=2 * BLK * columns * BLK, bytes_accessed=14 * BLK * columns, transcendentals=0),
             name="finish",
-        )(where, acc, weights, *far_vals, *held)
+        )(where, doc_starts, acc, weights, *far_vals, held)
 
     near_keys = near(keys)
     lats = [latent_call(where, doc_starts, queries, latent_keys, latent_values, 0, 1)]
@@ -486,14 +500,14 @@
     weighed = weigh_far(far_keys, top, total)
     near_vals[0], weighed = lax.optimization_barrier((near_vals[0], weighed))
     scale, far_weights, sums = weighed
-    sums = move(sums, [(s, s ^ 2) for s in range(4)])
+    sums = move(sums[docs:], [(s, s ^ 2) for s in range(4)])
     far_vals = [onward(near_vals[0])]
     parts = pl.pallas_call(
         part_kernel,
         grid=(heads // step,),
-        in_specs=smem(2) + [spec(2 * PIECES, step * BLK), spec(rows, wide)],
-        out_specs=spec(2 * PIECES, wide),
-        out_shape=shape(2 * PIECES, columns),
+        in_specs=smem(2) + [spec(docs, step * BLK), spec(rows, wide)],
+        out_specs=spec(docs, wide),
+        out_shape=shape(docs, columns),
         compiler_params=PARAMS,
         cost_estimate=pl.CostEstimate(flops=64 * rows * columns * 32, bytes_accessed=3 * rows * columns, transcendentals=0),
         name="part",
@@ -502,7 +516,7 @@
     near_vals[1], parts, mixed[0] = lax.optimization_barrier((near_vals[1], parts, mixed[0]))
     far_vals.append(onward(near_vals[1]))
     mixed.append(mix(1, acc, scale, near_weights, near_vals[1], lat))
-    context = finish(0, mixed[0][0], far_weights, far_vals[0], None)
+    context, mean = finish(0, mixed[0][0], far_weights, far_vals[0], mixed[0][1])
     sent = pl.pallas_call(
         route_kernel,
         in_specs=smem(2) + vmem(3),
@@ -510,7 +524,7 @@
         out_shape=(shape(4, columns, BF16),) * 4,
         compiler_params=PARAMS,
         name="route",
-    )(where, doc_owner, parts, *[m[1] for m in mixed])
+    )(where, doc_owner, parts, mean, mixed[1][1])
     sent, context = lax.optimization_barrier((sent, context))
     got = [sent[0]] + [move(sent[r], [(s, (s + r) % 4) for s in range(4)]) for r in range(1, 4)]
     context = finish(1, mixed[1][0], far_weights, far_vals[1], context)

time: 104 us -> 103 us (level)
  waiting for transfers between devices: 37.6 us -> 35.6 us
    ppermute x16, waiting for transfers between devices: 37.6 us -> 35.6 us  [move(): return lax.ppermute(value, 'seq', pairs)]
    pallas_call x2, Pallas kernels: 2.32 us -> 3.5 us  [finish(): pl.pallas_call(functools.partial(context_kernel, block), in_specs=smem(2)...]
  transfers between devices with their start and end apart: 16 -> 16, of which waited for: 9 -> 8; matrix products, arithmetic and copies ran while one was open for 0% -> 0% of each run, Pallas kernels for 29% -> 30%
where the time goes in v11:
time: 103 us
  waiting for transfers between devices  35.6 us (35%)
  Pallas kernels  31.6 us (31%)
  starting transfers between devices  30.2 us (29%)
  local copies, waits for them, and re-layouts  4.44 us (4%)
    ppermute x16, waiting for transfers between devices, move(): return lax.ppermute(value, 'seq', pairs)  35.6 us
    ppermute x16, starting transfers between devices, move(): return lax.ppermute(value, 'seq', pairs)  30.2 us
    pallas_call x2, Pallas kernels, latent_call(): pl.pallas_call(latent_kernel, grid=(steps,), in_specs=smem(2) + [pl.Block...  5.81 us
    pallas_call x1, Pallas kernels, weigh_near(): pl.pallas_call(functools.partial(near_weigh_kernel, 4), grid=(heads // st...  5.41 us
    pallas_call x1, Pallas kernels, own_call(): pl.pallas_call(own_kernel, grid=(columns // wide,), in_specs=[spec(rows,...  5.27 us
    pallas_call x1, Pallas kernels, weigh_far(): pl.pallas_call(functools.partial(far_weigh_kernel, 4), grid=(heads // ste...  4.68 us
    pallas_call x2, Pallas kernels, mix(): pl.pallas_call(functools.partial(mix_kernel, block), grid=(heads // step,...  4.52 us
    unnamed x22, local copies, waits for them, and re-layouts  4.36 us
  transfers between devices with their start and end apart: 16, of which 8 were waited for; matrix products, arithmetic and copies ran while one was open for 0% of the time, Pallas kernels for 30%

profile of v11, /device:TPU:0, one launch (start us, length us, event | category | flops | bytes accessed | tf_op | source)
XLA Modules:
  0.0 102.9 jit_solution(7817312363314991127)
XLA Ops:
  0.6 5.0 %collective-permute-start.4 = (bf16[512,1024]{1,0:T(8,128)(2,1)}, bf16[512,1024]{1,0:T(8,128)(2,1)S(1)}, u32[]{:S(2)}, u32[]{:S(2)}) collective-permute-start(bf16[512,1024]{1,0:T(8,128)(2,1)} %k_ref.1), channel_id=1, source_target_pairs={{0,4},{4,8},{8,12},{1,5},{5,9},{9,13},{2,6},{6,10},{10,14},{3,7},{... | collective-permute-start | bytes 3145736 | tf_op jit(solution)/shard_map/ppermute | solution.py:412
  5.6 1.3 %collective-permute-start.5 = (bf16[512,1024]{1,0:T(8,128)(2,1)}, bf16[512,1024]{1,0:T(8,128)(2,1)S(1)}, u32[]{:S(2)}, u32[]{:S(2)}) collective-permute-start(bf16[512,1024]{1,0:T(8,128)(2,1)} %k_ref.1), channel_id=1, source_target_pairs={{4,0},{8,4},{12,8},{5,1},{9,5},{13,9},{6,2},{10,6},{14,10},{7,3},{... | collective-permute-start | bytes 3145736 | tf_op jit(solution)/shard_map/ppermute | solution.py:412
  11.3 1.6 %latent.2 = f32[8,256]{1,0:T(8,128)S(1)} custom-call(s32[1]{0:T(128)} %bitcast.where, s32[32]{0:T(128)S(1)} %copy-done.6, bf16[512,1024]{1,0:T(8,128)(2,1)S(1)} %copy-done, bf16[512,1024]{1,0:T(8,128)(2,1)S(1)} %copy-done.1, bf16[512,1024]{1,0:T(8,128)(2,1)S(1)} %copy-done.3), custom_call_target="tpu_custom_call" | custom-call | flops 268435456 | bytes 786432 | tf_op jit(solution)/shard_map/latent/pallas_call | solution.py:384
  13.0 4.7 %collective-permute-start = (bf16[256,1024]{1,0:T(8,128)(2,1)S(1)}, bf16[256,1024]{1,0:T(8,128)(2,1)S(1)}, u32[]{:S(2)}, u32[]{:S(2)}) collective-permute-start(bf16[256,1024]{1,0:T(8,128)(2,1)S(1)} %slice.9), channel_id=1, source_target_pairs={{0,4},{4,8},{8,12},{1,5},{5,9},{9,13},{2,6},{6,10},{10,14},{3,7},{... | collective-permute-start | bytes 1572872 | tf_op jit(solution)/shard_map/ppermute | solution.py:412
  17.7 1.3 %collective-permute-start.1 = (bf16[256,1024]{1,0:T(8,128)(2,1)S(1)}, bf16[256,1024]{1,0:T(8,128)(2,1)S(1)}, u32[]{:S(2)}, u32[]{:S(2)}) collective-permute-start(bf16[256,1024]{1,0:T(8,128)(2,1)S(1)} %slice.9), channel_id=1, source_target_pairs={{4,0},{8,4},{12,8},{5,1},{9,5},{13,9},{6,2},{10,6},{14,10},{7,3},{... | collective-permute-start | bytes 1572872 | tf_op jit(solution)/shard_map/ppermute | solution.py:412
  19.0 5.3 %own.1 = (f32[512,1024]{1,0:T(8,128)S(1)}, f32[512,1024]{1,0:T(8,128)S(1)}, f32[512,1024]{1,0:T(8,128)S(1)}) custom-call(bf16[512,1024]{1,0:T(8,128)(2,1)S(1)} %copy-done, bf16[512,1024]{1,0:T(8,128)(2,1)S(1)} %copy-done.10, bf16[512,1024]{1,0:T(8,128)(2,1)S(1)} %copy-done.5), custom_call_target="tpu_custom_call" | custom-call | flops 1073741824 | bytes 9437184 | tf_op jit(solution)/shard_map/own/pallas_call | solution.py:365
  24.3 5.1 %collective-permute-done.4.nb_ref = bf16[512,1024]{1,0:T(8,128)(2,1)S(1)} collective-permute-done((bf16[512,1024]{1,0:T(8,128)(2,1)}, bf16[512,1024]{1,0:T(8,128)(2,1)S(1)}, u32[]{:S(2)}, u32[]{:S(2)}) %collective-permute-start.4) | collective-permute-done | bytes 1048608 | tf_op jit(solution)/shard_map/ppermute | solution.py:412
  29.4 4.4 %collective-permute-done.5.na_ref = bf16[512,1024]{1,0:T(8,128)(2,1)S(1)} collective-permute-done((bf16[512,1024]{1,0:T(8,128)(2,1)}, bf16[512,1024]{1,0:T(8,128)(2,1)S(1)}, u32[]{:S(2)}, u32[]{:S(2)}) %collective-permute-start.5) | collective-permute-done | bytes 1048608 | tf_op jit(solution)/shard_map/ppermute | solution.py:412
  35.8 3.6 %collective-permute-done.vb_ref = bf16[256,1024]{1,0:T(8,128)(2,1)S(1)} collective-permute-done((bf16[256,1024]{1,0:T(8,128)(2,1)S(1)}, bf16[256,1024]{1,0:T(8,128)(2,1)S(1)}, u32[]{:S(2)}, u32[]{:S(2)}) %collective-permute-start) | collective-permute-done | bytes 524320 | tf_op jit(solution)/shard_map/ppermute | solution.py:412
  39.4 5.6 %collective-permute-done.1.va_ref = bf16[256,1024]{1,0:T(8,128)(2,1)S(1)} collective-permute-done((bf16[256,1024]{1,0:T(8,128)(2,1)S(1)}, bf16[256,1024]{1,0:T(8,128)(2,1)S(1)}, u32[]{:S(2)}, u32[]{:S(2)}) %collective-permute-start.1) | collective-permute-done | bytes 524320 | tf_op jit(solution)/shard_map/ppermute | solution.py:412
  45.1 3.5 %collective-permute-start.2 = (bf16[256,1024]{1,0:T(8,128)(2,1)S(1)}, bf16[256,1024]{1,0:T(8,128)(2,1)S(1)}, u32[]{:S(2)}, u32[]{:S(2)}) collective-permute-start(bf16[256,1024]{1,0:T(8,128)(2,1)S(1)} %slice.10), channel_id=1, source_target_pairs={{0,4},{4,8},{8,12},{1,5},{5,9},{9,13},{2,6},{6,10},{10,14},{3,7},{... | collective-permute-start | bytes 1572872 | tf_op jit(solution)/shard_map/ppermute | solution.py:412
  49.9 4.2 %latent.3 = f32[8,768]{1,0:T(8,128)S(1)} custom-call(s32[1]{0:T(128)} %bitcast.where, s32[32]{0:T(128)S(1)} %copy-done.7, bf16[512,1024]{1,0:T(8,128)(2,1)S(1)} %copy-done, bf16[512,1024]{1,0:T(8,128)(2,1)S(1)} %copy-done.2, bf16[512,1024]{1,0:T(8,128)(2,1)S(1)} %copy-done.4), custom_call_target="tpu_custom_call" | custom-call | flops 8053063680 | bytes 2359296 | tf_op jit(solution)/shard_map/latent/pallas_call | solution.py:384
  54.1 5.4 %weigh_near.1 = (f32[512,1024]{1,0:T(8,128)S(1)}, f32[512,1024]{1,0:T(8,128)S(1)}, f32[512,1024]{1,0:T(8,128)S(1)}, bf16[512,2048]{1,0:T(8,128)(2,1)S(1)}, bf16[512,2048]{1,0:T(8,128)(2,1)S(1)}) custom-call(s32[1]{0:T(128)} %bitcast.where, s32[2,8]{1,0:T(2,128)S(1)} %copy-done.8, ...), custom_call_target="tpu_custom_call", output_to_operand_aliasing={{0}: (5, {}), {1}: (6, {}), {2}: (7, {})} | custom-call | flops 536870912 | bytes 10485760 | tf_op jit(solution)/shard_map/weigh_near/pallas_call | solution.py:427
  59.5 8.0 %collective-permute-done.7.fa_ref = bf16[512,1024]{1,0:T(8,128)(2,1)S(1)} collective-permute-done((bf16[512,1024]{1,0:T(8,128)(2,1)S(1)}, bf16[512,1024]{1,0:T(8,128)(2,1)S(1)}, u32[]{:S(2)}, u32[]{:S(2)}) %collective-permute-start.7) | collective-permute-done | bytes 1048608 | tf_op jit(solution)/shard_map/ppermute | solution.py:412
  67.5 4.7 %weigh_far.1 = (f32[512,1024]{1,0:T(8,128)S(1)}, bf16[512,2048]{1,0:T(8,128)(2,1)S(1)}, bf16[8,2048]{1,0:T(8,128)(2,1)S(1)}) custom-call(s32[1]{0:T(128)} %bitcast.where, s32[2,8]{1,0:T(2,128)S(1)} %copy-done.8, s32[32]{0:T(128)S(1)} %copy-done.7, bf16[512,1024]{1,0:T(8,128)(2,1)S(1)} %copy-done, bf16[512,1024]{1,0:T(8,128)(2,1)S(1)} %collective-permute-done.6.fb_ref, ...), custom_call_target="tpu_custom_call" | custom-call | flops 268435456 | bytes 11534336 | tf_op jit(solution)/shard_map/weigh_far/pallas_call | solution.py:442
  74.8 2.3 %mix.2 = (f32[256,1024]{1,0:T(8,128)S(1)}, f32[4,1024]{1,0:T(4,128)S(1)}) custom-call(s32[1]{0:T(128)} %bitcast.where, s32[32]{0:T(128)S(1)} %copy-done.7, f32[512,1024]{1,0:T(8,128)S(1)} %get-tuple-element.83.acc_in, f32[512,1024]{1,0:T(8,128)S(1)} %get-tuple-element.84.scale_in, bf16[512,2048]{1,0:T(8,128)(2,1)S(1)} %get-tuple-element.85.wb_ref, ...), custom_call_target="tpu_custom_call" | custom-call | flops 268435456 | bytes 5242880 | tf_op jit(solution)/shard_map/mix/pallas_call | solution.py:456
  77.0 3.4 %collective-permute-done.8.sums_ref = bf16[4,2048]{1,0:T(4,128)(2,1)S(1)} collective-permute-done((bf16[4,2048]{1,0:T(4,128)(2,1)S(1)}, bf16[4,2048]{1,0:T(4,128)(2,1)S(1)}, u32[]{:S(2)}, u32[]{:S(2)}) %collective-permute-start.8) | collective-permute-done | bytes 16416 | tf_op jit(solution)/shard_map/ppermute | solution.py:412
  83.6 2.3 %mix.3 = (f32[256,1024]{1,0:T(8,128)S(1)}, f32[4,1024]{1,0:T(4,128)S(1)}) custom-call(s32[1]{0:T(128)} %bitcast.where, s32[32]{0:T(128)S(1)} %copy-done.7, f32[512,1024]{1,0:T(8,128)S(1)} %get-tuple-element.83.acc_in, f32[512,1024]{1,0:T(8,128)S(1)} %get-tuple-element.84.scale_in, bf16[512,2048]{1,0:T(8,128)(2,1)S(1)} %get-tuple-element.85.wb_ref, ...), custom_call_target="tpu_custom_call" | custom-call | flops 268435456 | bytes 5242880 | tf_op jit(solution)/shard_map/mix/pallas_call | solution.py:456
  85.9 4.4 %collective-permute-done.10.va_ref = bf16[256,1024]{1,0:T(8,128)(2,1)S(1)} collective-permute-done((bf16[256,1024]{1,0:T(8,128)(2,1)S(1)}, bf16[256,1024]{1,0:T(8,128)(2,1)S(1)}, u32[]{:S(2)}, u32[]{:S(2)}) %collective-permute-start.10) | collective-permute-done | bytes 524320 | tf_op jit(solution)/shard_map/ppermute | solution.py:412
  90.3 1.8 %finish.2 = (bf16[512,1024]{1,0:T(8,128)(2,1)}, f32[4,1024]{1,0:T(4,128)S(1)}) custom-call(s32[1]{0:T(128)} %bitcast.where, s32[32]{0:T(128)S(1)} %copy-done.7, f32[256,1024]{1,0:T(8,128)S(1)} %get-tuple-element.93.acc_ref, bf16[512,2048]{1,0:T(8,128)(2,1)S(1)} %get-tuple-element.94.w_ref, bf16[256,1024]{1,0:T(8,128)(2,1)S(1)} %collective-permute-done.9.vb_ref, ...), custom_call_target="tpu_custom_call" | custom-call | flops 134217728 | bytes 3670016 | tf_op jit(solution)/shard_map/finish/pallas_call | solution.py:475
  92.8 1.9 %collective-permute-start.11 = (bf16[4,1024]{1,0:T(4,128)(2,1)S(1)}, bf16[4,1024]{1,0:T(4,128)(2,1)S(1)}, u32[]{:S(2)}, u32[]{:S(2)}) collective-permute-start(bf16[4,1024]{1,0:T(4,128)(2,1)S(1)} %get-tuple-element.106), channel_id=1, source_target_pairs={{0,4},{4,8},{8,12},{12,0},{1,5},{5,9},{9,13},{13,1},{2,6},{6,10},{... | collective-permute-start | bytes 24584 | tf_op jit(solution)/shard_map/ppermute | solution.py:412
  94.7 2.0 %collective-permute-start.12 = (bf16[4,1024]{1,0:T(4,128)(2,1)S(1)}, bf16[4,1024]{1,0:T(4,128)(2,1)S(1)}, u32[]{:S(2)}, u32[]{:S(2)}) collective-permute-start(bf16[4,1024]{1,0:T(4,128)(2,1)S(1)} %get-tuple-element.107), channel_id=1, source_target_pairs={{0,8},{4,12},{8,0},{12,4},{1,9},{5,13},{9,1},{13,5},{2,10},{6,14},... | collective-permute-start | bytes 24584 | tf_op jit(solution)/shard_map/ppermute | solution.py:412
  96.7 2.7 %collective-permute-start.13 = (bf16[4,1024]{1,0:T(4,128)(2,1)S(1)}, bf16[4,1024]{1,0:T(4,128)(2,1)S(1)}, u32[]{:S(2)}, u32[]{:S(2)}) collective-permute-start(bf16[4,1024]{1,0:T(4,128)(2,1)S(1)} %get-tuple-element.108), channel_id=1, source_target_pairs={{0,12},{4,0},{8,4},{12,8},{1,13},{5,1},{9,5},{13,9},{2,14},{6,2},{... | collective-permute-start | bytes 24584 | tf_op jit(solution)/shard_map/ppermute | solution.py:412
  100.5 1.7 %finish.3 = bf16[512,1024]{1,0:T(8,128)(2,1)} custom-call(s32[1]{0:T(128)} %bitcast.where, s32[32]{0:T(128)S(1)} %copy-done.7, f32[256,1024]{1,0:T(8,128)S(1)} %get-tuple-element.109.acc_ref, bf16[512,2048]{1,0:T(8,128)(2,1)S(1)} %get-tuple-element.94.w_ref, bf16[256,1024]{1,0:T(8,128)(2,1)S(1)} %collective-permute-done.14.vb_ref, ...), custom_call_target="tpu_custom_call", output_to_operand_aliasing={{}: (6, {})} | custom-call | flops 134217728 | bytes 3670016 | tf_op jit(solution)/shard_map/finish/pallas_call | solution.py:475
  (46 shorter events, 15.8 us)
Async XLA Ops:
  0.6 28.8 %collective-permute-start.4 = (bf16[512,1024]{1,0:T(8,128)(2,1)}, bf16[512,1024]{1,0:T(8,128)(2,1)S(1)}, u32[]{:S(2)}, u32[]{:S(2)}) collective-permute-start(bf16[512,1024]{1,0:T(8,128)(2,1)} %k_ref.1), channel_id=1, source_target_pairs={{0,4},{4,8},{8,12},{1,5},{5,9},{9,13},{2,6},{6,10},{10,14},{3,7},{... | collective-permute-start | bytes 3145736 | tf_op jit(solution)/shard_map/ppermute | solution.py:412
  5.6 28.2 %collective-permute-start.5 = (bf16[512,1024]{1,0:T(8,128)(2,1)}, bf16[512,1024]{1,0:T(8,128)(2,1)S(1)}, u32[]{:S(2)}, u32[]{:S(2)}) collective-permute-start(bf16[512,1024]{1,0:T(8,128)(2,1)} %k_ref.1), channel_id=1, source_target_pairs={{4,0},{8,4},{12,8},{5,1},{9,5},{13,9},{6,2},{10,6},{14,10},{7,3},{... | collective-permute-start | bytes 3145736 | tf_op jit(solution)/shard_map/ppermute | solution.py:412
  6.9 1.2 %copy-start = (bf16[512,1024]{1,0:T(8,128)(2,1)S(1)}, bf16[512,1024]{1,0:T(8,128)(2,1)}, u32[]{:S(2)}) copy-start(bf16[512,1024]{1,0:T(8,128)(2,1)} %q_ref.7) | copy-start | bytes 3145732
  11.3 1.7 %copy-start.5 = (bf16[512,1024]{1,0:T(8,128)(2,1)S(1)}, bf16[512,1024]{1,0:T(8,128)(2,1)}, u32[]{:S(2)}) copy-start(bf16[512,1024]{1,0:T(8,128)(2,1)} %v_ref.3) | copy-start | bytes 3145732
  11.3 7.8 %copy-start.10 = (bf16[512,1024]{1,0:T(8,128)(2,1)S(1)}, bf16[512,1024]{1,0:T(8,128)(2,1)}, u32[]{:S(2)}) copy-start(bf16[512,1024]{1,0:T(8,128)(2,1)} %k_ref.1) | copy-start | bytes 3145732
  13.0 36.9 %copy-start.2 = (bf16[512,1024]{1,0:T(8,128)(2,1)S(1)}, bf16[512,1024]{1,0:T(8,128)(2,1)}, u32[]{:S(2)}) copy-start(bf16[512,1024]{1,0:T(8,128)(2,1)} %lk_ref.3) | copy-start | bytes 3145732
  13.0 36.9 %copy-start.4 = (bf16[512,1024]{1,0:T(8,128)(2,1)S(1)}, bf16[512,1024]{1,0:T(8,128)(2,1)}, u32[]{:S(2)}) copy-start(bf16[512,1024]{1,0:T(8,128)(2,1)} %lv_ref.3) | copy-start | bytes 3145732
  13.0 36.9 %copy-start.7 = (s32[32]{0:T(128)S(1)}, s32[32]{0:T(128)}, u32[]{:S(2)}) copy-start(s32[32]{0:T(128)} %starts.15) | copy-start | bytes 388
  13.0 26.4 %collective-permute-start = (bf16[256,1024]{1,0:T(8,128)(2,1)S(1)}, bf16[256,1024]{1,0:T(8,128)(2,1)S(1)}, u32[]{:S(2)}, u32[]{:S(2)}) collective-permute-start(bf16[256,1024]{1,0:T(8,128)(2,1)S(1)} %slice.9), channel_id=1, source_target_pairs={{0,4},{4,8},{8,12},{1,5},{5,9},{9,13},{2,6},{6,10},{10,14},{3,7},{... | collective-permute-start | bytes 1572872 | tf_op jit(solution)/shard_map/ppermute | solution.py:412
  17.7 27.3 %collective-permute-start.1 = (bf16[256,1024]{1,0:T(8,128)(2,1)S(1)}, bf16[256,1024]{1,0:T(8,128)(2,1)S(1)}, u32[]{:S(2)}, u32[]{:S(2)}) collective-permute-start(bf16[256,1024]{1,0:T(8,128)(2,1)S(1)} %slice.9), channel_id=1, source_target_pairs={{4,0},{8,4},{12,8},{5,1},{9,5},{13,9},{6,2},{10,6},{14,10},{7,3},{... | collective-permute-start | bytes 1572872 | tf_op jit(solution)/shard_map/ppermute | solution.py:412
  33.8 25.7 %collective-permute-start.6 = (bf16[512,1024]{1,0:T(8,128)(2,1)S(1)}, bf16[512,1024]{1,0:T(8,128)(2,1)S(1)}, u32[]{:S(2)}, u32[]{:S(2)}) collective-permute-start(bf16[512,1024]{1,0:T(8,128)(2,1)S(1)} %collective-permute-done.4.nb_ref), channel_id=1, source_target_pairs={{4,8},{8,12},{5,9},{9,13},{6,10},{10,14},{7,11},{11,15},{20,24},{2... | collective-permute-start | bytes 3145736 | tf_op jit(solution)/shard_map/ppermute | solution.py:412
  34.5 33.0 %collective-permute-start.7 = (bf16[512,1024]{1,0:T(8,128)(2,1)S(1)}, bf16[512,1024]{1,0:T(8,128)(2,1)S(1)}, u32[]{:S(2)}, u32[]{:S(2)}) collective-permute-start(bf16[512,1024]{1,0:T(8,128)(2,1)S(1)} %collective-permute-done.5.na_ref), channel_id=1, source_target_pairs={{4,0},{8,4},{5,1},{9,5},{6,2},{10,6},{7,3},{11,7},{20,16},{24,20},... | collective-permute-start | bytes 3145736 | tf_op jit(solution)/shard_map/ppermute | solution.py:412
  45.1 9.0 %copy-start.8 = (s32[2,8]{1,0:T(2,128)S(1)}, s32[2,8]{1,0:T(2,128)}, u32[]{:S(2)}) copy-start(s32[2,8]{1,0:T(2,128)} %pattern.3) | copy-start | bytes 196
  45.1 36.5 %collective-permute-start.2 = (bf16[256,1024]{1,0:T(8,128)(2,1)S(1)}, bf16[256,1024]{1,0:T(8,128)(2,1)S(1)}, u32[]{:S(2)}, u32[]{:S(2)}) collective-permute-start(bf16[256,1024]{1,0:T(8,128)(2,1)S(1)} %slice.10), channel_id=1, source_target_pairs={{0,4},{4,8},{8,12},{1,5},{5,9},{9,13},{2,6},{6,10},{10,14},{3,7},{... | collective-permute-start | bytes 1572872 | tf_op jit(solution)/shard_map/ppermute | solution.py:412
  48.6 33.1 %collective-permute-start.3 = (bf16[256,1024]{1,0:T(8,128)(2,1)S(1)}, bf16[256,1024]{1,0:T(8,128)(2,1)S(1)}, u32[]{:S(2)}, u32[]{:S(2)}) collective-permute-start(bf16[256,1024]{1,0:T(8,128)(2,1)S(1)} %slice.10), channel_id=1, source_target_pairs={{4,0},{8,4},{12,8},{5,1},{9,5},{13,9},{6,2},{10,6},{14,10},{7,3},{... | collective-permute-start | bytes 1572872 | tf_op jit(solution)/shard_map/ppermute | solution.py:412
  72.2 8.2 %collective-permute-start.8 = (bf16[4,2048]{1,0:T(4,128)(2,1)S(1)}, bf16[4,2048]{1,0:T(4,128)(2,1)S(1)}, u32[]{:S(2)}, u32[]{:S(2)}) collective-permute-start(bf16[4,2048]{1,0:T(4,128)(2,1)S(1)} %slice.11), channel_id=1, source_target_pairs={{0,8},{4,12},{8,0},{12,4},{1,9},{5,13},{9,1},{13,5},{2,10},{6,14},... | collective-permute-start | bytes 49160 | tf_op jit(solution)/shard_map/ppermute | solution.py:412
  72.8 17.6 %collective-permute-start.10 = (bf16[256,1024]{1,0:T(8,128)(2,1)S(1)}, bf16[256,1024]{1,0:T(8,128)(2,1)S(1)}, u32[]{:S(2)}, u32[]{:S(2)}) collective-permute-start(bf16[256,1024]{1,0:T(8,128)(2,1)S(1)} %collective-permute-done.1.va_ref), channel_id=1, source_target_pairs={{4,0},{8,4},{5,1},{9,5},{6,2},{10,6},{7,3},{11,7},{20,16},{24,20},... | collective-permute-start | bytes 1572872 | tf_op jit(solution)/shard_map/ppermute | solution.py:412
  74.1 16.3 %collective-permute-start.9 = (bf16[256,1024]{1,0:T(8,128)(2,1)S(1)}, bf16[256,1024]{1,0:T(8,128)(2,1)S(1)}, u32[]{:S(2)}, u32[]{:S(2)}) collective-permute-start(bf16[256,1024]{1,0:T(8,128)(2,1)S(1)} %collective-permute-done.vb_ref), channel_id=1, source_target_pairs={{4,8},{8,12},{5,9},{9,13},{6,10},{10,14},{7,11},{11,15},{20,24},{2... | collective-permute-start | bytes 1572872 | tf_op jit(solution)/shard_map/ppermute | solution.py:412
  81.6 17.8 %collective-permute-start.14 = (bf16[256,1024]{1,0:T(8,128)(2,1)S(1)}, bf16[256,1024]{1,0:T(8,128)(2,1)S(1)}, u32[]{:S(2)}, u32[]{:S(2)}) collective-permute-start(bf16[256,1024]{1,0:T(8,128)(2,1)S(1)} %collective-permute-done.2.vb_ref), channel_id=1, source_target_pairs={{4,8},{8,12},{5,9},{9,13},{6,10},{10,14},{7,11},{11,15},{20,24},{2... | collective-permute-start | bytes 1572872 | tf_op jit(solution)/shard_map/ppermute | solution.py:412
  82.3 18.1 %collective-permute-start.15 = (bf16[256,1024]{1,0:T(8,128)(2,1)S(1)}, bf16[256,1024]{1,0:T(8,128)(2,1)S(1)}, u32[]{:S(2)}, u32[]{:S(2)}) collective-permute-start(bf16[256,1024]{1,0:T(8,128)(2,1)S(1)} %collective-permute-done.3.va_ref), channel_id=1, source_target_pairs={{4,0},{8,4},{5,1},{9,5},{6,2},{10,6},{7,3},{11,7},{20,16},{24,20},... | collective-permute-start | bytes 1572872 | tf_op jit(solution)/shard_map/ppermute | solution.py:412
  85.9 6.3 %copy-start.9 = (s32[32]{0:T(128)S(1)}, s32[32]{0:T(128)}, u32[]{:S(2)}) copy-start(s32[32]{0:T(128)} %owners.1) | copy-start | bytes 388
  92.8 9.4 %collective-permute-start.11 = (bf16[4,1024]{1,0:T(4,128)(2,1)S(1)}, bf16[4,1024]{1,0:T(4,128)(2,1)S(1)}, u32[]{:S(2)}, u32[]{:S(2)}) collective-permute-start(bf16[4,1024]{1,0:T(4,128)(2,1)S(1)} %get-tuple-element.106), channel_id=1, source_target_pairs={{0,4},{4,8},{8,12},{12,0},{1,5},{5,9},{9,13},{13,1},{2,6},{6,10},{... | collective-permute-start | bytes 24584 | tf_op jit(solution)/shard_map/ppermute | solution.py:412
  94.7 7.5 %collective-permute-start.12 = (bf16[4,1024]{1,0:T(4,128)(2,1)S(1)}, bf16[4,1024]{1,0:T(4,128)(2,1)S(1)}, u32[]{:S(2)}, u32[]{:S(2)}) collective-permute-start(bf16[4,1024]{1,0:T(4,128)(2,1)S(1)} %get-tuple-element.107), channel_id=1, source_target_pairs={{0,8},{4,12},{8,0},{12,4},{1,9},{5,13},{9,1},{13,5},{2,10},{6,14},... | collective-permute-start | bytes 24584 | tf_op jit(solution)/shard_map/ppermute | solution.py:412
  96.7 5.5 %collective-permute-start.13 = (bf16[4,1024]{1,0:T(4,128)(2,1)S(1)}, bf16[4,1024]{1,0:T(4,128)(2,1)S(1)}, u32[]{:S(2)}, u32[]{:S(2)}) collective-permute-start(bf16[4,1024]{1,0:T(4,128)(2,1)S(1)} %get-tuple-element.108), channel_id=1, source_target_pairs={{0,12},{4,0},{8,4},{12,8},{1,13},{5,1},{9,5},{13,9},{2,14},{6,2},{... | collective-permute-start | bytes 24584 | tf_op jit(solution)/shard_map/ppermute | solution.py:412
  (3 other events, 3.1 us)
